TPU v7x, 32 devices: a whole 2x2x4 slice. The times are simulated.
32 devices in a mesh: vox: 8 (over z, y), comp: 4 (over x, core).
Axes of the slice: x: 2, y: 2, z: 4, core: 2. Of those that a mesh axis runs over, the one named last changes fastest.
Arguments:
- data: bfloat16 [2048, 8192], P('comp', 'vox'), may hold values from -108 to 108
- projection: bfloat16 [512, 2048], P(None, 'comp'), may hold values from -0.125 to 0.125
- initial: float32 [512, 512], P('comp'), may hold values from -0.25 to 0.25
Outputs:
- unmixing: float32 [512, 512], P('comp')
- sources: bfloat16 [512, 8192], P('comp', 'vox')
All inputs are finite; a program needn't handle non-finite values.
Results may differ from a plain program's by a relative error of at most 0.008.
Values may be sent and summed in bfloat16 or wider, within the bound.
No kernel may reach another device: no remote copies, remote signals or barrier semaphores. Data moves between devices by JAX's collectives and lax.ppermute only.
A program may use at most 64 MiB of HBM per device.

v0:
```python
import functools

import jax
import jax.numpy as jnp
from jax import lax
from jax.experimental import pallas as pl
from jax.experimental.pallas import tpu as pltpu
from jax.sharding import PartitionSpec as P

ICA_ITERS = 2
AXES = ("vox", "comp")
BF = jnp.bfloat16
F32 = jnp.float32
MIB = 1 << 20


def nn(left, right):
    return jnp.dot(left, right, preferred_element_type=F32)


def nt(left, right):
    return lax.dot_general(
        left, right, (((1,), (1,)), ((), ())), preferred_element_type=F32
    )


def rounded(x):
    return lax.reduce_precision(x, 8, 7)


def flip(x, mask):
    count = lax.axis_size("vox") * lax.axis_size("comp")
    return lax.ppermute(x, AXES, [(i, i ^ mask) for i in range(count)])


def sum_over(x, masks):
    for k in range(0, len(masks), 2):
        sent = x.astype(BF)
        x = rounded(x) + flip(sent, masks[k]).astype(F32)
        if k + 1 < len(masks):
            x = x + (
                flip(sent, masks[k + 1]).astype(F32)
                + flip(sent, masks[k] | masks[k + 1]).astype(F32)
            )
    return x


def spread(x, across, near):
    return jnp.stack([x, flip(x, near), flip(x, across), flip(x, across | near)])


VMEM = pl.BlockSpec(memory_space=pltpu.VMEM)
SMEM = pl.BlockSpec(memory_space=pltpu.SMEM)
ANY = pl.BlockSpec(memory_space=pl.ANY)


def run(kernel, outs, args, specs=None, scratch=(), limit=24):
    return pl.pallas_call(
        kernel,
        out_shape=outs,
        in_specs=specs or [SMEM] + [VMEM] * (len(args) - 1),
        out_specs=jax.tree.map(lambda _: VMEM, outs),
        scratch_shapes=list(scratch),
        compiler_params=pltpu.CompilerParams(vmem_limit_bytes=limit * MIB),
    )(*args)


def shape(dims, dtype):
    return jax.ShapeDtypeStruct(dims, dtype)


def project_kernel(away, at, left_ref, right_ref, other_left_ref, other_right_ref, out_ref):
    size = other_right_ref.shape[1]
    across = 1 - at[1] if away else at[1]
    start = pl.multiple_of((across * 2 + at[0]) * size, size)
    total = nn(left_ref[...], right_ref[:, pl.ds(start, size)])
    total += nn(other_left_ref[...], other_right_ref[...])
    out_ref[...] = total.astype(out_ref.dtype)


def covar_kernel(at, here_ref, there_ref, own_ref, y_ref, x_ref, xy_ref, both, pack):
    rows, size = here_ref.shape
    block = rows // 4
    both[:, :size] = here_ref[...]
    both[:, size:] = there_ref[...]

    def part(k):
        return both[pl.ds(pl.multiple_of(k * block, block), block), :]

    low = at[0]
    first, second = part(2 * low), part(2 * low + 1)
    third = part(2 - 2 * low)
    pack[0 * block : 1 * block] = nt(first, first)
    pack[1 * block : 2 * block] = nt(first, second)
    pack[2 * block : 3 * block] = nt(second, second)
    pack[3 * block : 4 * block] = nt(second, third)
    pack[4 * block : 5 * block] = nt(part(low), part(2 + low))
    piece = own_ref.shape[0]

    def quarter(i, j):
        return pack[pl.ds(pl.multiple_of((2 * i + j) * piece, piece), piece), :]

    ax, ay = at[1], at[2]
    own_ref[...] = quarter(ax, ay)
    y_ref[...] = quarter(ax, 1 - ay).astype(BF)
    x_ref[...] = quarter(1 - ax, ay).astype(BF)
    xy_ref[...] = quarter(1 - ax, 1 - ay).astype(BF)


def whiten_kernel(voxels, at, mine_ref, other_ref, out_ref, packs, covar):
    piece = mine_ref.shape[1]
    block = mine_ref.shape[2]
    rows = covar.shape[0]
    low, ax, ay = at[0], at[1], at[2]
    for k in range(4):
        i, j = ax ^ (k >> 1), ay ^ (k & 1)
        place = pl.ds(pl.multiple_of((2 * i + j) * piece, piece), piece)
        packs[low, place, :] = mine_ref[k].astype(F32)
        packs[1 - low, place, :] = other_ref[k].astype(F32)

    def put(i, j, core, k):
        value = packs[core, k * block : (k + 1) * block, :]
        covar[i * block : (i + 1) * block, j * block : (j + 1) * block] = value
        if i != j:
            covar[j * block : (j + 1) * block, i * block : (i + 1) * block] = value.T

    for core in (0, 1):
        a, b, c = 2 * core, 2 * core + 1, 2 - 2 * core
        put(a, a, core, 0)
        put(a, b, core, 1)
        put(b, b, core, 2)
        put(b, c, core, 3)
        put(core, 2 + core, core, 4)

    y = covar[...] / voxels
    cscale = jnp.sqrt(jnp.sum(y * y) + 1e-06)
    y = y / cscale
    eye = (
        lax.broadcasted_iota(jnp.int32, (rows, rows), 0)
        == lax.broadcasted_iota(jnp.int32, (rows, rows), 1)
    ).astype(F32)
    yb = y.astype(BF)
    square = nn(yb, yb)
    squared = square.astype(BF)
    rest = -2.4375 * y + 1.6875 * square
    rest += nn(squared, (0.0625 * square - 0.5625 * y).astype(BF))
    restb = rest.astype(BF)
    left = 2.25 * y + nn(yb, restb)
    right = 4.5 * rest + nn(restb, restb)
    z3 = 3.375 * eye + 1.5 * rest - 0.5 * (
        5.0625 * left + nn(left.astype(BF), right.astype(BF))
    )
    out_ref[...] = (z3 / jnp.sqrt(cscale)).astype(BF)


def step(weights, block):
    bent = jnp.tanh(nn(weights.astype(BF), block))
    pulled = nt(bent.astype(BF), block)
    return pulled, jnp.sum(1.0 - bent * bent, axis=1, keepdims=True)


def apply_kernel(whiten_ref, block_ref, weights_ref, white_ref, newer_ref, total, slope):
    turn = pl.program_id(0)

    @pl.when(turn == 0)
    def _():
        total[...] = jnp.zeros_like(total)
        slope[...] = jnp.zeros_like(slope)

    weights = weights_ref[...]
    for k in range(block_ref.shape[0]):
        white = nn(whiten_ref[...], block_ref[k]).astype(BF)
        white_ref[k] = white
        pulled, part = step(weights, white)
        total[...] += pulled
        slope[...] += part

    @pl.when(turn == pl.num_programs(0) - 1)
    def _():
        newer_ref[...] = total[...] - slope[...] * weights


def decor_kernel(last, at, mine_ref, other_ref, white_ref, *refs):
    outs, (newer, lower, white, sem) = refs[:-4], refs[-4:]
    count = mine_ref.shape[1]
    low, ax, ay = at[0], at[1], at[2]
    chunks = white.shape[0]
    source = white_ref.at[pl.ds(ay * chunks, chunks)] if last else white_ref
    copy = pltpu.make_async_copy(source, white, sem)
    copy.start()
    for k in range(4):
        i, j = ax ^ (k >> 1), ay ^ (k & 1)
        for ref, core in ((mine_ref, low), (other_ref, 1 - low)):
            start = pl.multiple_of((4 * i + 2 * core + j) * count, count)
            lower[pl.ds(start, count), :] = ref[k]

    raw = lower[...]
    gram = nt(raw, raw)
    gscale = jnp.sqrt(jnp.sum(gram * gram) + 1e-06)
    gram = (gram / gscale).astype(BF)
    value = (1.5 * raw.astype(F32) - 0.5 * nn(gram, raw)) / jnp.sqrt(gscale)
    raw = value.astype(BF)
    gram = nt(raw, raw).astype(BF)
    newer[...] = 1.5 * value - 0.5 * nn(gram, raw)
    lower[...] = newer[...].astype(BF)
    start = pl.multiple_of((4 * ax + 2 * low) * count, count)
    size = 2 * count
    if not last:
        start = pl.multiple_of(start + ay * count, count)
        size = count
    raw = lower[...]
    gram = nt(lower[pl.ds(start, size), :], raw).astype(BF)
    weights = 1.5 * newer[pl.ds(start, size), :] - 0.5 * nn(gram, raw)
    copy.wait()
    if last:
        outs[0][...] = weights
        width = white.shape[2]
        for k in range(chunks):
            outs[1][:, k * width : (k + 1) * width] = nn(
                weights.astype(BF), white[k]
            ).astype(BF)
    else:
        total, slope = step(weights, white[0])
        for k in range(1, chunks):
            pulled, part = step(weights, white[k])
            total += pulled
            slope += part
        outs[0][...] = total - slope * weights


def shards(data, projection, initial):
    comps = lax.axis_size("comp")
    voxels = data.shape[1] * lax.axis_size("vox")
    vox, comp = lax.axis_index("vox"), lax.axis_index("comp")
    index = vox * comps + comp
    all_bits = (lax.axis_size("vox") * comps).bit_length() - 1
    low, across, near = 1, 2, comps
    far = [1 << k for k in range(near.bit_length(), all_bits)]
    at = jnp.stack([comp & 1, comp >> 1, vox & 1]).astype(jnp.int32)
    rows = projection.shape[0]
    size = data.shape[1] // comps

    def columns(x):
        start = (x * 2 + (1 - at[0])) * size
        return flip(lax.dynamic_slice_in_dim(data, start, size, 1), low)

    other = flip(projection, low)
    sent = run(
        functools.partial(project_kernel, True),
        shape((rows, size), BF),
        (at, projection, data, other, columns(1 - at[1])),
    )
    kept = run(
        functools.partial(project_kernel, False),
        shape((rows, size), F32),
        (at, projection, data, other, columns(at[1])),
    )
    reduced = (kept + flip(sent, across).astype(F32)).astype(BF)

    near_size = comps * 2
    groups = [
        list(range(g, g + near_size)) for g in range(0, 1 << all_bits, near_size)
    ]
    gathered = lax.all_gather(reduced, AXES, axis=0, axis_index_groups=groups)

    block = rows // 4
    piece = 5 * block // 4
    small = shape((piece, block), BF)
    own, by, bx, bxy = run(
        covar_kernel,
        (shape((piece, block), F32), small, small, small),
        (at, reduced, flip(reduced, low)),
        scratch=[pltpu.VMEM((rows, 2 * size), BF), pltpu.VMEM((5 * block, block), F32)],
    )
    own = own + flip(by, near).astype(F32)
    own = own + flip(bx, across).astype(F32)
    own = own + flip(bxy, across | near).astype(F32)
    packed = spread(sum_over(own, far).astype(BF), across, near)
    whiten = run(
        functools.partial(whiten_kernel, voxels),
        shape((rows, rows), BF),
        (at, packed, flip(packed, low)),
        scratch=[pltpu.VMEM((2, 5 * block, block), F32), pltpu.VMEM((rows, rows), F32)],
    )

    count = initial.shape[0] // 2
    weights = lax.dynamic_slice_in_dim(initial, at[2] * count, count, 0)
    steps = 4
    per = near_size // steps
    whitened, newer = pl.pallas_call(
        apply_kernel,
        grid=(steps,),
        out_shape=(shape((near_size, rows, size), BF), shape((count, rows), F32)),
        in_specs=[
            pl.BlockSpec((rows, rows), lambda i: (0, 0)),
            pl.BlockSpec((per, rows, size), lambda i: (i, 0, 0)),
            pl.BlockSpec((count, rows), lambda i: (0, 0)),
        ],
        out_specs=(
            pl.BlockSpec((per, rows, size), lambda i: (i, 0, 0)),
            pl.BlockSpec((count, rows), lambda i: (0, 0)),
        ),
        scratch_shapes=[pltpu.VMEM((count, rows), F32), pltpu.VMEM((count, 1), F32)],
        compiler_params=pltpu.CompilerParams(vmem_limit_bytes=24 * MIB),
    )(whiten, gathered, weights)

    for turn in range(ICA_ITERS):
        last = turn == ICA_ITERS - 1
        stacked = spread(sum_over(newer, far).astype(BF), across, near)
        chunks = comps if last else near_size
        outs = (
            (shape((2 * count, rows), F32), shape((2 * count, data.shape[1]), BF))
            if last
            else shape((count, rows), F32)
        )
        newer = run(
            functools.partial(decor_kernel, last),
            outs,
            (at, stacked, flip(stacked, low), whitened),
            specs=[SMEM, VMEM, VMEM, ANY],
            scratch=[
                pltpu.VMEM((rows, rows), F32),
                pltpu.VMEM((rows, rows), BF),
                pltpu.VMEM((chunks, rows, size), BF),
                pltpu.SemaphoreType.DMA,
            ],
        )
    return newer


def solution(mesh):
    return jax.shard_map(
        shards,
        mesh=mesh,
        in_specs=(P("comp", "vox"), P(None, "comp"), P("comp", None)),
        out_specs=(P("comp", None), P("comp", "vox")),
        check_vma=False,
    )
```

profile of v0, /device:TPU:0, one launch (start us, length us, event | category | flops | bytes accessed | tf_op | source)
XLA Modules:
  0.0 112.8 jit_solution(18269532453549813838)
XLA Ops:
  7.2 0.5 collective-permute-start
  7.7 1.1 constant_dynamic-slice_fusion.1
  8.8 0.1 collective-permute-start.2
  8.9 0.5 collective-permute-start.1
  9.4 0.1 pad_add_fusion.at
  9.5 0.9 collective-permute-done.2.other_right_ref
  10.4 1.2 %copy-done.1 = bf16[512,1024]{1,0:T(8,128)(2,1)S(1)} copy-done((bf16[512,1024]{1,0:T(8,128)(2,1)S(1)}, bf16[512,1024]{1,0:T(8,128)(2,1)}, u32[]{:S(2)}) %copy-start.1) | copy-done | bytes 1048600
  11.6 1.0 copy-done.4
  12.7 1.0 shard_map.51
  13.7 2.7 %collective-permute-start.3 = (bf16[512,256]{1,0:T(8,128)(2,1)S(1)}, bf16[512,256]{1,0:T(8,128)(2,1)S(1)}, u32[]{:S(2)}, u32[]{:S(2)}) collective-permute-start(bf16[512,256]{1,0:T(8,128)(2,1)S(1)} %shard_map.51), channel_id=1, source_target_pairs={{0,2},{1,3},{2,0},{3,1},{4,6},{5,7},{6,4},{7,5},{8,10},{9,11},{10,... | collective-permute-start | bytes 786440 | tf_op jit(solution)/shard_map/ppermute | solution.py:33
  16.4 1.0 shard_map.50
  17.4 5.8 %collective-permute-done.3 = bf16[512,256]{1,0:T(8,128)(2,1)S(1)} collective-permute-done((bf16[512,256]{1,0:T(8,128)(2,1)S(1)}, bf16[512,256]{1,0:T(8,128)(2,1)S(1)}, u32[]{:S(2)}, u32[]{:S(2)}) %collective-permute-start.3) | collective-permute-done | bytes 262176 | tf_op jit(solution)/shard_map/ppermute | solution.py:33
  23.2 0.8 add_convert_fusion.here_ref
  24.0 0.1 collective-permute-start.4
  24.1 1.7 %collective-permute-done.4.there_ref = bf16[512,256]{1,0:T(8,128)(2,1)S(1)} collective-permute-done((bf16[512,256]{1,0:T(8,128)(2,1)}, bf16[512,256]{1,0:T(8,128)(2,1)S(1)}, u32[]{:S(2)}, u32[]{:S(2)}) %collective-permute-start.4) | collective-permute-done | bytes 262176 | tf_op jit(solution)/shard_map/ppermute | solution.py:33
  25.8 0.9 copy-done.2
  26.8 0.9 shard_map.52
  27.7 1.8 %collective-permute-start.5 = (bf16[160,128]{1,0:T(8,128)(2,1)S(1)}, bf16[160,128]{1,0:T(8,128)(2,1)S(1)}, u32[]{:S(2)}, u32[]{:S(2)}) collective-permute-start(bf16[160,128]{1,0:T(8,128)(2,1)S(1)} %get-tuple-element.9), channel_id=1, source_target_pairs={{0,4},{1,5},{2,6},{3,7},{4,0},{5,1},{6,2},{7,3},{8,12},{9,13},{10,... | collective-permute-start | bytes 122888 | tf_op jit(solution)/shard_map/ppermute | solution.py:33
  29.5 1.5 %collective-permute-start.6 = (bf16[160,128]{1,0:T(8,128)(2,1)S(1)}, bf16[160,128]{1,0:T(8,128)(2,1)S(1)}, u32[]{:S(2)}, u32[]{:S(2)}) collective-permute-start(bf16[160,128]{1,0:T(8,128)(2,1)S(1)} %get-tuple-element.10), channel_id=1, source_target_pairs={{0,2},{1,3},{2,0},{3,1},{4,6},{5,7},{6,4},{7,5},{8,10},{9,11},{10,... | collective-permute-start | bytes 122888 | tf_op jit(solution)/shard_map/ppermute | solution.py:33
  31.0 0.2 collective-permute-start.7
  31.3 0.5 collective-permute-done.5
  31.8 2.1 %collective-permute-done.6 = bf16[160,128]{1,0:T(8,128)(2,1)S(1)} collective-permute-done((bf16[160,128]{1,0:T(8,128)(2,1)S(1)}, bf16[160,128]{1,0:T(8,128)(2,1)S(1)}, u32[]{:S(2)}, u32[]{:S(2)}) %collective-permute-start.6) | collective-permute-done | bytes 40992 | tf_op jit(solution)/shard_map/ppermute | solution.py:33
  33.9 2.0 %collective-permute-done.7 = bf16[160,128]{1,0:T(8,128)(2,1)S(1)} collective-permute-done((bf16[160,128]{1,0:T(8,128)(2,1)S(1)}, bf16[160,128]{1,0:T(8,128)(2,1)S(1)}, u32[]{:S(2)}, u32[]{:S(2)}) %collective-permute-start.7) | collective-permute-done | bytes 40992 | tf_op jit(solution)/shard_map/ppermute | solution.py:33
  36.0 3.7 %collective-permute-start.10 = (bf16[160,128]{1,0:T(8,128)(2,1)S(1)}, bf16[160,128]{1,0:T(8,128)(2,1)S(1)}, u32[]{:S(2)}, u32[]{:S(2)}) collective-permute-start(bf16[160,128]{1,0:T(8,128)(2,1)S(1)} %fusion), channel_id=1, source_target_pairs={{0,24},{1,25},{2,26},{3,27},{4,28},{5,29},{6,30},{7,31},{8,16},{9,... | collective-permute-start | bytes 122888 | tf_op jit(solution)/shard_map/ppermute | solution.py:33
  39.7 0.8 collective-permute-start.8
  40.4 1.5 %collective-permute-done.10 = bf16[160,128]{1,0:T(8,128)(2,1)S(1)} collective-permute-done((bf16[160,128]{1,0:T(8,128)(2,1)S(1)}, bf16[160,128]{1,0:T(8,128)(2,1)S(1)}, u32[]{:S(2)}, u32[]{:S(2)}) %collective-permute-start.10) | collective-permute-done | bytes 40992 | tf_op jit(solution)/shard_map/ppermute | solution.py:33
  41.9 2.6 %collective-permute-done.9 = bf16[160,128]{1,0:T(8,128)(2,1)S(1)} collective-permute-done((bf16[160,128]{1,0:T(8,128)(2,1)S(1)}, bf16[160,128]{1,0:T(8,128)(2,1)S(1)}, u32[]{:S(2)}, u32[]{:S(2)}) %collective-permute-start.9) | collective-permute-done | bytes 40992 | tf_op jit(solution)/shard_map/ppermute | solution.py:33
  44.6 0.5 collective-permute-start.13
  45.1 1.5 %collective-permute-start.12 = (bf16[160,128]{1,0:T(8,128)(2,1)S(1)}, bf16[160,128]{1,0:T(8,128)(2,1)S(1)}, u32[]{:S(2)}, u32[]{:S(2)}) collective-permute-start(bf16[160,128]{1,0:T(8,128)(2,1)S(1)} %add_convert_fusion.3), channel_id=1, source_target_pairs={{0,2},{1,3},{2,0},{3,1},{4,6},{5,7},{6,4},{7,5},{8,10},{9,11},{10,... | collective-permute-start | bytes 122888 | tf_op jit(solution)/shard_map/ppermute | solution.py:33
  46.7 1.5 %collective-permute-start.11 = (bf16[160,128]{1,0:T(8,128)(2,1)S(1)}, bf16[160,128]{1,0:T(8,128)(2,1)S(1)}, u32[]{:S(2)}, u32[]{:S(2)}) collective-permute-start(bf16[160,128]{1,0:T(8,128)(2,1)S(1)} %add_convert_fusion.3), channel_id=1, source_target_pairs={{0,4},{1,5},{2,6},{3,7},{4,0},{5,1},{6,2},{7,3},{8,12},{9,13},{10,... | collective-permute-start | bytes 122888 | tf_op jit(solution)/shard_map/ppermute | solution.py:33
  48.2 2.2 %collective-permute-done.13 = bf16[160,128]{1,0:T(8,128)(2,1)S(1)} collective-permute-done((bf16[160,128]{1,0:T(8,128)(2,1)S(1)}, bf16[160,128]{1,0:T(8,128)(2,1)S(1)}, u32[]{:S(2)}, u32[]{:S(2)}) %collective-permute-start.13) | collective-permute-done | bytes 40992 | tf_op jit(solution)/shard_map/ppermute | solution.py:33
  50.4 0.3 collective-permute-done.12
  50.7 0.8 collective-permute-done.11
  51.6 0.1 collective-permute-start.14
  51.7 1.3 %collective-permute-done.14.other_ref = bf16[4,160,128]{2,1,0:T(8,128)(2,1)S(1)} collective-permute-done((bf16[4,160,128]{2,1,0:T(8,128)(2,1)S(1)}, bf16[4,160,128]{2,1,0:T(8,128)(2,1)S(1)}, u32[]{:S(2)}, u32[]{:S(2)}) %collective-permute-start.14) | collective-permute-done | bytes 163872 | tf_op jit(solution)/shard_map/ppermute | solution.py:33
  53.1 3.0 %shard_map.53.whiten_ref = bf16[512,512]{1,0:T(8,128)(2,1)S(1)} custom-call(s32[3]{0:T(128)S(1)} %pad_add_fusion.at, bf16[4,160,128]{2,1,0:T(8,128)(2,1)S(1)} %pad_maximum_fusion.2.mine_ref, bf16[4,160,128]{2,1,0:T(8,128)(2,1)S(1)} %collective-permute-done.14.other_ref), custom_call_target="tpu_custom_call" | custom-call | tf_op jit(solution)/shard_map/pallas_call | solution.py:58
  56.1 1.6 %copy-done.3 = bf16[4096,256]{1,0:T(8,128)(2,1)S(1)} copy-done((bf16[4096,256]{1,0:T(8,128)(2,1)S(1)}, bf16[4096,256]{1,0:T(8,128)(2,1)}, u32[]{:S(2)}) %copy-start.3) | copy-done | bytes 2097176
  57.7 5.0 %shard_map.54 = (bf16[8,512,256]{2,1,0:T(8,128)(2,1)S(1)}, f32[64,512]{1,0:T(8,128)S(1)}) custom-call(bf16[512,512]{1,0:T(8,128)(2,1)S(1)} %shard_map.53.whiten_ref, bf16[8,512,256]{2,1,0:T(8,128)(2,1)S(1)} %bitcast.16, f32[64,512]{1,0:T(8,128)S(1)} %constant_dynamic-slice_fusion.weights_ref), custom_call_target="tpu_custom_call" | custom-call | tf_op jit(solution)/shard_map/pallas_call | solution.py:290
  62.7 1.8 %collective-permute-start.17 = (bf16[64,512]{1,0:T(8,128)(2,1)S(1)}, bf16[64,512]{1,0:T(8,128)(2,1)S(1)}, u32[]{:S(2)}, u32[]{:S(2)}) collective-permute-start(bf16[64,512]{1,0:T(8,128)(2,1)S(1)} %convert_element_type.70), channel_id=1, source_target_pairs={{0,24},{1,25},{2,26},{3,27},{4,28},{5,29},{6,30},{7,31},{8,16},{9,... | collective-permute-start | bytes 196616 | tf_op jit(solution)/shard_map/ppermute | solution.py:33
  64.4 0.4 collective-permute-start.16
  64.9 2.3 %collective-permute-start.15 = (bf16[64,512]{1,0:T(8,128)(2,1)S(1)}, bf16[64,512]{1,0:T(8,128)(2,1)S(1)}, u32[]{:S(2)}, u32[]{:S(2)}) collective-permute-start(bf16[64,512]{1,0:T(8,128)(2,1)S(1)} %convert_element_type.70), channel_id=1, source_target_pairs={{0,8},{1,9},{2,10},{3,11},{4,12},{5,13},{6,14},{7,15},{8,0},{9,1},... | collective-permute-start | bytes 196616 | tf_op jit(solution)/shard_map/ppermute | solution.py:33
  67.1 2.3 %collective-permute-done.17 = bf16[64,512]{1,0:T(8,128)(2,1)S(1)} collective-permute-done((bf16[64,512]{1,0:T(8,128)(2,1)S(1)}, bf16[64,512]{1,0:T(8,128)(2,1)S(1)}, u32[]{:S(2)}, u32[]{:S(2)}) %collective-permute-start.17) | collective-permute-done | bytes 65568 | tf_op jit(solution)/shard_map/ppermute | solution.py:33
  69.5 2.0 %collective-permute-done.16 = bf16[64,512]{1,0:T(8,128)(2,1)S(1)} collective-permute-done((bf16[64,512]{1,0:T(8,128)(2,1)S(1)}, bf16[64,512]{1,0:T(8,128)(2,1)S(1)}, u32[]{:S(2)}, u32[]{:S(2)}) %collective-permute-start.16) | collective-permute-done | bytes 65568 | tf_op jit(solution)/shard_map/ppermute | solution.py:33
  71.5 1.5 %collective-permute-start.20 = (bf16[64,512]{1,0:T(8,128)(2,1)S(1)}, bf16[64,512]{1,0:T(8,128)(2,1)S(1)}, u32[]{:S(2)}, u32[]{:S(2)}) collective-permute-start(bf16[64,512]{1,0:T(8,128)(2,1)S(1)} %add_convert_fusion.2), channel_id=1, source_target_pairs={{0,6},{1,7},{2,4},{3,5},{4,2},{5,3},{6,0},{7,1},{8,14},{9,15},{10,... | collective-permute-start | bytes 196616 | tf_op jit(solution)/shard_map/ppermute | solution.py:33
  73.0 1.5 %collective-permute-start.19 = (bf16[64,512]{1,0:T(8,128)(2,1)S(1)}, bf16[64,512]{1,0:T(8,128)(2,1)S(1)}, u32[]{:S(2)}, u32[]{:S(2)}) collective-permute-start(bf16[64,512]{1,0:T(8,128)(2,1)S(1)} %add_convert_fusion.2), channel_id=1, source_target_pairs={{0,2},{1,3},{2,0},{3,1},{4,6},{5,7},{6,4},{7,5},{8,10},{9,11},{10,... | collective-permute-start | bytes 196616 | tf_op jit(solution)/shard_map/ppermute | solution.py:33
  74.5 0.6 collective-permute-start.18
  75.1 2.2 %collective-permute-done.20 = bf16[64,512]{1,0:T(8,128)(2,1)S(1)} collective-permute-done((bf16[64,512]{1,0:T(8,128)(2,1)S(1)}, bf16[64,512]{1,0:T(8,128)(2,1)S(1)}, u32[]{:S(2)}, u32[]{:S(2)}) %collective-permute-start.20) | collective-permute-done | bytes 65568 | tf_op jit(solution)/shard_map/ppermute | solution.py:33
  77.3 0.6 collective-permute-done.19
  77.9 0.9 collective-permute-done.18
  78.8 0.1 collective-permute-start.21
  78.9 1.5 %collective-permute-done.21.other_ref = bf16[4,64,512]{2,1,0:T(8,128)(2,1)S(1)} collective-permute-done((bf16[4,64,512]{2,1,0:T(8,128)(2,1)S(1)}, bf16[4,64,512]{2,1,0:T(8,128)(2,1)S(1)}, u32[]{:S(2)}, u32[]{:S(2)}) %collective-permute-start.21) | collective-permute-done | bytes 262176 | tf_op jit(solution)/shard_map/ppermute | solution.py:33
  80.4 4.6 %shard_map.55 = f32[64,512]{1,0:T(8,128)S(1)} custom-call(s32[3]{0:T(128)S(1)} %pad_add_fusion.at, bf16[4,64,512]{2,1,0:T(8,128)(2,1)S(1)} %pad_maximum_fusion.mine_ref, bf16[4,64,512]{2,1,0:T(8,128)(2,1)S(1)} %collective-permute-done.21.other_ref, bf16[8,512,256]{2,1,0:T(8,128)(2,1)S(1)} %get-tuple-element.13.white_ref), custom_call_target="tpu_custom_call" | custom-call | tf_op jit(solution)/shard_map/pallas_call | solution.py:58
  85.1 2.6 %collective-permute-start.24 = (bf16[64,512]{1,0:T(8,128)(2,1)S(1)}, bf16[64,512]{1,0:T(8,128)(2,1)S(1)}, u32[]{:S(2)}, u32[]{:S(2)}) collective-permute-start(bf16[64,512]{1,0:T(8,128)(2,1)S(1)} %convert_element_type.75), channel_id=1, source_target_pairs={{0,24},{1,25},{2,26},{3,27},{4,28},{5,29},{6,30},{7,31},{8,16},{9,... | collective-permute-start | bytes 196616 | tf_op jit(solution)/shard_map/ppermute | solution.py:33
  87.7 1.8 %collective-permute-start.22 = (bf16[64,512]{1,0:T(8,128)(2,1)S(1)}, bf16[64,512]{1,0:T(8,128)(2,1)S(1)}, u32[]{:S(2)}, u32[]{:S(2)}) collective-permute-start(bf16[64,512]{1,0:T(8,128)(2,1)S(1)} %convert_element_type.75), channel_id=1, source_target_pairs={{0,8},{1,9},{2,10},{3,11},{4,12},{5,13},{6,14},{7,15},{8,0},{9,1},... | collective-permute-start | bytes 196616 | tf_op jit(solution)/shard_map/ppermute | solution.py:33
  89.5 2.3 %collective-permute-done.24 = bf16[64,512]{1,0:T(8,128)(2,1)S(1)} collective-permute-done((bf16[64,512]{1,0:T(8,128)(2,1)S(1)}, bf16[64,512]{1,0:T(8,128)(2,1)S(1)}, u32[]{:S(2)}, u32[]{:S(2)}) %collective-permute-start.24) | collective-permute-done | bytes 65568 | tf_op jit(solution)/shard_map/ppermute | solution.py:33
  91.9 2.0 %collective-permute-done.23 = bf16[64,512]{1,0:T(8,128)(2,1)S(1)} collective-permute-done((bf16[64,512]{1,0:T(8,128)(2,1)S(1)}, bf16[64,512]{1,0:T(8,128)(2,1)S(1)}, u32[]{:S(2)}, u32[]{:S(2)}) %collective-permute-start.23) | collective-permute-done | bytes 65568 | tf_op jit(solution)/shard_map/ppermute | solution.py:33
  93.9 0.7 collective-permute-start.27
  94.7 1.3 %collective-permute-start.26 = (bf16[64,512]{1,0:T(8,128)(2,1)S(1)}, bf16[64,512]{1,0:T(8,128)(2,1)S(1)}, u32[]{:S(2)}, u32[]{:S(2)}) collective-permute-start(bf16[64,512]{1,0:T(8,128)(2,1)S(1)} %add_convert_fusion.1), channel_id=1, source_target_pairs={{0,2},{1,3},{2,0},{3,1},{4,6},{5,7},{6,4},{7,5},{8,10},{9,11},{10,... | collective-permute-start | bytes 196616 | tf_op jit(solution)/shard_map/ppermute | solution.py:33
  96.0 1.5 %collective-permute-start.25 = (bf16[64,512]{1,0:T(8,128)(2,1)S(1)}, bf16[64,512]{1,0:T(8,128)(2,1)S(1)}, u32[]{:S(2)}, u32[]{:S(2)}) collective-permute-start(bf16[64,512]{1,0:T(8,128)(2,1)S(1)} %add_convert_fusion.1), channel_id=1, source_target_pairs={{0,4},{1,5},{2,6},{3,7},{4,0},{5,1},{6,2},{7,3},{8,12},{9,13},{10,... | collective-permute-start | bytes 196616 | tf_op jit(solution)/shard_map/ppermute | solution.py:33
  97.5 2.1 %collective-permute-done.27 = bf16[64,512]{1,0:T(8,128)(2,1)S(1)} collective-permute-done((bf16[64,512]{1,0:T(8,128)(2,1)S(1)}, bf16[64,512]{1,0:T(8,128)(2,1)S(1)}, u32[]{:S(2)}, u32[]{:S(2)}) %collective-permute-start.27) | collective-permute-done | bytes 65568 | tf_op jit(solution)/shard_map/ppermute | solution.py:33
  99.6 0.7 collective-permute-done.25
  100.4 0.1 collective-permute-start.28
  100.4 1.5 %collective-permute-done.28.other_ref = bf16[4,64,512]{2,1,0:T(8,128)(2,1)S(1)} collective-permute-done((bf16[4,64,512]{2,1,0:T(8,128)(2,1)S(1)}, bf16[4,64,512]{2,1,0:T(8,128)(2,1)S(1)}, u32[]{:S(2)}, u32[]{:S(2)}) %collective-permute-start.28) | collective-permute-done | bytes 262176 | tf_op jit(solution)/shard_map/ppermute | solution.py:33
  102.0 4.0 %shard_map.56 = (f32[128,512]{1,0:T(8,128)}, bf16[128,1024]{1,0:T(8,128)(2,1)}) custom-call(s32[3]{0:T(128)S(1)} %pad_add_fusion.at, bf16[4,64,512]{2,1,0:T(8,128)(2,1)S(1)} %pad_maximum_fusion.1.mine_ref, bf16[4,64,512]{2,1,0:T(8,128)(2,1)S(1)} %collective-permute-done.28.other_ref, bf16[8,512,256]{2,1,0:T(8,128)(2,1)S(1)} %get-tuple-element.13.white_ref), custom_call_target="tpu_custom_call" | custom-call | tf_op jit(solution)/shard_map/pallas_call | solution.py:58
  (27 shorter events, 0.4 us)
Async XLA Ops:
  7.2 44.5 %copy-start = (f32[128,512]{1,0:T(8,128)S(1)}, f32[128,512]{1,0:T(8,128)}, u32[]{:S(2)}) copy-start(f32[128,512]{1,0:T(8,128)} %param.5) | copy-start | bytes 786436
  7.2 48.9 %all-gather.3.cloned.1.call-start = ((), (), s32[]{:S(2)}) async-start(), calls=%async_computation | async-start | bytes 2359296 | tf_op jit(solution)/shard_map/all_gather | solution.py:264
  7.2 3.2 %collective-permute-start = (bf16[512,512]{1,0:T(8,128)(2,1)}, bf16[512,512]{1,0:T(8,128)(2,1)S(1)}, u32[]{:S(2)}, u32[]{:S(2)}) collective-permute-start(bf16[512,512]{1,0:T(8,128)(2,1)} %left_ref.3), channel_id=1, source_target_pairs={{0,1},{1,0},{2,3},{3,2},{4,5},{5,4},{6,7},{7,6},{8,9},{9,8},{10,11... | collective-permute-start | bytes 1572872 | tf_op jit(solution)/shard_map/ppermute | solution.py:33
  8.8 1.6 %collective-permute-start.2 = (bf16[512,256]{1,0:T(8,128)(2,1)S(1)}, bf16[512,256]{1,0:T(8,128)(2,1)S(1)}, u32[]{:S(2)}, u32[]{:S(2)}) collective-permute-start(bf16[512,256]{1,0:T(8,128)(2,1)S(1)} %get-tuple-element.14), channel_id=1, source_target_pairs={{0,1},{1,0},{2,3},{3,2},{4,5},{5,4},{6,7},{7,6},{8,9},{9,8},{10,11... | collective-permute-start | bytes 786440 | tf_op jit(solution)/shard_map/ppermute | solution.py:33
  8.9 7.5 %collective-permute-start.1 = (bf16[512,256]{1,0:T(8,128)(2,1)S(1)}, bf16[512,256]{1,0:T(8,128)(2,1)S(1)}, u32[]{:S(2)}, u32[]{:S(2)}) collective-permute-start(bf16[512,256]{1,0:T(8,128)(2,1)S(1)} %get-tuple-element.15), channel_id=1, source_target_pairs={{0,1},{1,0},{2,3},{3,2},{4,5},{5,4},{6,7},{7,6},{8,9},{9,8},{10,11... | collective-permute-start | bytes 786440 | tf_op jit(solution)/shard_map/ppermute | solution.py:33
  10.4 1.2 %copy-start.1 = (bf16[512,1024]{1,0:T(8,128)(2,1)S(1)}, bf16[512,1024]{1,0:T(8,128)(2,1)}, u32[]{:S(2)}) copy-start(bf16[512,1024]{1,0:T(8,128)(2,1)} %right_ref.3) | copy-start | bytes 3145732
  11.6 1.0 copy-start.4
  13.7 9.5 %collective-permute-start.3 = (bf16[512,256]{1,0:T(8,128)(2,1)S(1)}, bf16[512,256]{1,0:T(8,128)(2,1)S(1)}, u32[]{:S(2)}, u32[]{:S(2)}) collective-permute-start(bf16[512,256]{1,0:T(8,128)(2,1)S(1)} %shard_map.51), channel_id=1, source_target_pairs={{0,2},{1,3},{2,0},{3,1},{4,6},{5,7},{6,4},{7,5},{8,10},{9,11},{10,... | collective-permute-start | bytes 786440 | tf_op jit(solution)/shard_map/ppermute | solution.py:33
  24.0 1.8 %collective-permute-start.4 = (bf16[512,256]{1,0:T(8,128)(2,1)}, bf16[512,256]{1,0:T(8,128)(2,1)S(1)}, u32[]{:S(2)}, u32[]{:S(2)}) collective-permute-start(bf16[512,256]{1,0:T(8,128)(2,1)} %add_convert_fusion.here_ref), channel_id=1, source_target_pairs={{0,1},{1,0},{2,3},{3,2},{4,5},{5,4},{6,7},{7,6},{8,9},{9,8},{10,11... | collective-permute-start | bytes 786440 | tf_op jit(solution)/shard_map/ppermute | solution.py:33
  25.8 1.0 copy-start.2
  27.7 4.1 %collective-permute-start.5 = (bf16[160,128]{1,0:T(8,128)(2,1)S(1)}, bf16[160,128]{1,0:T(8,128)(2,1)S(1)}, u32[]{:S(2)}, u32[]{:S(2)}) collective-permute-start(bf16[160,128]{1,0:T(8,128)(2,1)S(1)} %get-tuple-element.9), channel_id=1, source_target_pairs={{0,4},{1,5},{2,6},{3,7},{4,0},{5,1},{6,2},{7,3},{8,12},{9,13},{10,... | collective-permute-start | bytes 122888 | tf_op jit(solution)/shard_map/ppermute | solution.py:33
  29.5 4.4 %collective-permute-start.6 = (bf16[160,128]{1,0:T(8,128)(2,1)S(1)}, bf16[160,128]{1,0:T(8,128)(2,1)S(1)}, u32[]{:S(2)}, u32[]{:S(2)}) collective-permute-start(bf16[160,128]{1,0:T(8,128)(2,1)S(1)} %get-tuple-element.10), channel_id=1, source_target_pairs={{0,2},{1,3},{2,0},{3,1},{4,6},{5,7},{6,4},{7,5},{8,10},{9,11},{10,... | collective-permute-start | bytes 122888 | tf_op jit(solution)/shard_map/ppermute | solution.py:33
  31.0 4.9 %collective-permute-start.7 = (bf16[160,128]{1,0:T(8,128)(2,1)S(1)}, bf16[160,128]{1,0:T(8,128)(2,1)S(1)}, u32[]{:S(2)}, u32[]{:S(2)}) collective-permute-start(bf16[160,128]{1,0:T(8,128)(2,1)S(1)} %get-tuple-element.11), channel_id=1, source_target_pairs={{0,6},{1,7},{2,4},{3,5},{4,2},{5,3},{6,0},{7,1},{8,14},{9,15},{10,... | collective-permute-start | bytes 122888 | tf_op jit(solution)/shard_map/ppermute | solution.py:33
  36.0 6.0 %collective-permute-start.10 = (bf16[160,128]{1,0:T(8,128)(2,1)S(1)}, bf16[160,128]{1,0:T(8,128)(2,1)S(1)}, u32[]{:S(2)}, u32[]{:S(2)}) collective-permute-start(bf16[160,128]{1,0:T(8,128)(2,1)S(1)} %fusion), channel_id=1, source_target_pairs={{0,24},{1,25},{2,26},{3,27},{4,28},{5,29},{6,30},{7,31},{8,16},{9,... | collective-permute-start | bytes 122888 | tf_op jit(solution)/shard_map/ppermute | solution.py:33
  39.7 4.9 %collective-permute-start.9 = (bf16[160,128]{1,0:T(8,128)(2,1)S(1)}, bf16[160,128]{1,0:T(8,128)(2,1)S(1)}, u32[]{:S(2)}, u32[]{:S(2)}) collective-permute-start(bf16[160,128]{1,0:T(8,128)(2,1)S(1)} %fusion), channel_id=1, source_target_pairs={{0,16},{1,17},{2,18},{3,19},{4,20},{5,21},{6,22},{7,23},{8,24},{9,... | collective-permute-start | bytes 122888 | tf_op jit(solution)/shard_map/ppermute | solution.py:33
  39.7 4.9 %collective-permute-start.8 = (bf16[160,128]{1,0:T(8,128)(2,1)S(1)}, bf16[160,128]{1,0:T(8,128)(2,1)S(1)}, u32[]{:S(2)}, u32[]{:S(2)}) collective-permute-start(bf16[160,128]{1,0:T(8,128)(2,1)S(1)} %fusion), channel_id=1, source_target_pairs={{0,8},{1,9},{2,10},{3,11},{4,12},{5,13},{6,14},{7,15},{8,0},{9,1},... | collective-permute-start | bytes 122888 | tf_op jit(solution)/shard_map/ppermute | solution.py:33
  44.6 5.8 %collective-permute-start.13 = (bf16[160,128]{1,0:T(8,128)(2,1)S(1)}, bf16[160,128]{1,0:T(8,128)(2,1)S(1)}, u32[]{:S(2)}, u32[]{:S(2)}) collective-permute-start(bf16[160,128]{1,0:T(8,128)(2,1)S(1)} %add_convert_fusion.3), channel_id=1, source_target_pairs={{0,6},{1,7},{2,4},{3,5},{4,2},{5,3},{6,0},{7,1},{8,14},{9,15},{10,... | collective-permute-start | bytes 122888 | tf_op jit(solution)/shard_map/ppermute | solution.py:33
  45.1 5.6 %collective-permute-start.12 = (bf16[160,128]{1,0:T(8,128)(2,1)S(1)}, bf16[160,128]{1,0:T(8,128)(2,1)S(1)}, u32[]{:S(2)}, u32[]{:S(2)}) collective-permute-start(bf16[160,128]{1,0:T(8,128)(2,1)S(1)} %add_convert_fusion.3), channel_id=1, source_target_pairs={{0,2},{1,3},{2,0},{3,1},{4,6},{5,7},{6,4},{7,5},{8,10},{9,11},{10,... | collective-permute-start | bytes 122888 | tf_op jit(solution)/shard_map/ppermute | solution.py:33
  46.7 4.9 %collective-permute-start.11 = (bf16[160,128]{1,0:T(8,128)(2,1)S(1)}, bf16[160,128]{1,0:T(8,128)(2,1)S(1)}, u32[]{:S(2)}, u32[]{:S(2)}) collective-permute-start(bf16[160,128]{1,0:T(8,128)(2,1)S(1)} %add_convert_fusion.3), channel_id=1, source_target_pairs={{0,4},{1,5},{2,6},{3,7},{4,0},{5,1},{6,2},{7,3},{8,12},{9,13},{10,... | collective-permute-start | bytes 122888 | tf_op jit(solution)/shard_map/ppermute | solution.py:33
  51.6 1.5 %collective-permute-start.14 = (bf16[4,160,128]{2,1,0:T(8,128)(2,1)S(1)}, bf16[4,160,128]{2,1,0:T(8,128)(2,1)S(1)}, u32[]{:S(2)}, u32[]{:S(2)}) collective-permute-start(bf16[4,160,128]{2,1,0:T(8,128)(2,1)S(1)} %pad_maximum_fusion.2.mine_ref), channel_id=1, source_target_pairs={{0,1},{1,0},{2,3},{3,2},{4,5},{5,4},{6,7},{7,6},{8,9},{9,8},{10,11... | collective-permute-start | bytes 491528 | tf_op jit(solution)/shard_map/ppermute | solution.py:33
  56.1 1.6 %copy-start.3 = (bf16[4096,256]{1,0:T(8,128)(2,1)S(1)}, bf16[4096,256]{1,0:T(8,128)(2,1)}, u32[]{:S(2)}) copy-start(bf16[4096,256]{1,0:T(8,128)(2,1)} %all-gather.3.cloned.1.call-done) | copy-start | bytes 6291460
  62.7 6.8 %collective-permute-start.17 = (bf16[64,512]{1,0:T(8,128)(2,1)S(1)}, bf16[64,512]{1,0:T(8,128)(2,1)S(1)}, u32[]{:S(2)}, u32[]{:S(2)}) collective-permute-start(bf16[64,512]{1,0:T(8,128)(2,1)S(1)} %convert_element_type.70), channel_id=1, source_target_pairs={{0,24},{1,25},{2,26},{3,27},{4,28},{5,29},{6,30},{7,31},{8,16},{9,... | collective-permute-start | bytes 196616 | tf_op jit(solution)/shard_map/ppermute | solution.py:33
  64.4 7.0 %collective-permute-start.16 = (bf16[64,512]{1,0:T(8,128)(2,1)S(1)}, bf16[64,512]{1,0:T(8,128)(2,1)S(1)}, u32[]{:S(2)}, u32[]{:S(2)}) collective-permute-start(bf16[64,512]{1,0:T(8,128)(2,1)S(1)} %convert_element_type.70), channel_id=1, source_target_pairs={{0,16},{1,17},{2,18},{3,19},{4,20},{5,21},{6,22},{7,23},{8,24},{9,... | collective-permute-start | bytes 196616 | tf_op jit(solution)/shard_map/ppermute | solution.py:33
  64.9 6.6 %collective-permute-start.15 = (bf16[64,512]{1,0:T(8,128)(2,1)S(1)}, bf16[64,512]{1,0:T(8,128)(2,1)S(1)}, u32[]{:S(2)}, u32[]{:S(2)}) collective-permute-start(bf16[64,512]{1,0:T(8,128)(2,1)S(1)} %convert_element_type.70), channel_id=1, source_target_pairs={{0,8},{1,9},{2,10},{3,11},{4,12},{5,13},{6,14},{7,15},{8,0},{9,1},... | collective-permute-start | bytes 196616 | tf_op jit(solution)/shard_map/ppermute | solution.py:33
  71.5 5.8 %collective-permute-start.20 = (bf16[64,512]{1,0:T(8,128)(2,1)S(1)}, bf16[64,512]{1,0:T(8,128)(2,1)S(1)}, u32[]{:S(2)}, u32[]{:S(2)}) collective-permute-start(bf16[64,512]{1,0:T(8,128)(2,1)S(1)} %add_convert_fusion.2), channel_id=1, source_target_pairs={{0,6},{1,7},{2,4},{3,5},{4,2},{5,3},{6,0},{7,1},{8,14},{9,15},{10,... | collective-permute-start | bytes 196616 | tf_op jit(solution)/shard_map/ppermute | solution.py:33
  73.0 4.9 %collective-permute-start.19 = (bf16[64,512]{1,0:T(8,128)(2,1)S(1)}, bf16[64,512]{1,0:T(8,128)(2,1)S(1)}, u32[]{:S(2)}, u32[]{:S(2)}) collective-permute-start(bf16[64,512]{1,0:T(8,128)(2,1)S(1)} %add_convert_fusion.2), channel_id=1, source_target_pairs={{0,2},{1,3},{2,0},{3,1},{4,6},{5,7},{6,4},{7,5},{8,10},{9,11},{10,... | collective-permute-start | bytes 196616 | tf_op jit(solution)/shard_map/ppermute | solution.py:33
  74.5 4.3 %collective-permute-start.18 = (bf16[64,512]{1,0:T(8,128)(2,1)S(1)}, bf16[64,512]{1,0:T(8,128)(2,1)S(1)}, u32[]{:S(2)}, u32[]{:S(2)}) collective-permute-start(bf16[64,512]{1,0:T(8,128)(2,1)S(1)} %add_convert_fusion.2), channel_id=1, source_target_pairs={{0,4},{1,5},{2,6},{3,7},{4,0},{5,1},{6,2},{7,3},{8,12},{9,13},{10,... | collective-permute-start | bytes 196616 | tf_op jit(solution)/shard_map/ppermute | solution.py:33
  78.8 1.6 %collective-permute-start.21 = (bf16[4,64,512]{2,1,0:T(8,128)(2,1)S(1)}, bf16[4,64,512]{2,1,0:T(8,128)(2,1)S(1)}, u32[]{:S(2)}, u32[]{:S(2)}) collective-permute-start(bf16[4,64,512]{2,1,0:T(8,128)(2,1)S(1)} %pad_maximum_fusion.mine_ref), channel_id=1, source_target_pairs={{0,1},{1,0},{2,3},{3,2},{4,5},{5,4},{6,7},{7,6},{8,9},{9,8},{10,11... | collective-permute-start | bytes 786440 | tf_op jit(solution)/shard_map/ppermute | solution.py:33
  85.1 6.8 %collective-permute-start.24 = (bf16[64,512]{1,0:T(8,128)(2,1)S(1)}, bf16[64,512]{1,0:T(8,128)(2,1)S(1)}, u32[]{:S(2)}, u32[]{:S(2)}) collective-permute-start(bf16[64,512]{1,0:T(8,128)(2,1)S(1)} %convert_element_type.75), channel_id=1, source_target_pairs={{0,24},{1,25},{2,26},{3,27},{4,28},{5,29},{6,30},{7,31},{8,16},{9,... | collective-permute-start | bytes 196616 | tf_op jit(solution)/shard_map/ppermute | solution.py:33
  87.7 6.2 %collective-permute-start.23 = (bf16[64,512]{1,0:T(8,128)(2,1)S(1)}, bf16[64,512]{1,0:T(8,128)(2,1)S(1)}, u32[]{:S(2)}, u32[]{:S(2)}) collective-permute-start(bf16[64,512]{1,0:T(8,128)(2,1)S(1)} %convert_element_type.75), channel_id=1, source_target_pairs={{0,16},{1,17},{2,18},{3,19},{4,20},{5,21},{6,22},{7,23},{8,24},{9,... | collective-permute-start | bytes 196616 | tf_op jit(solution)/shard_map/ppermute | solution.py:33
  87.7 6.2 %collective-permute-start.22 = (bf16[64,512]{1,0:T(8,128)(2,1)S(1)}, bf16[64,512]{1,0:T(8,128)(2,1)S(1)}, u32[]{:S(2)}, u32[]{:S(2)}) collective-permute-start(bf16[64,512]{1,0:T(8,128)(2,1)S(1)} %convert_element_type.75), channel_id=1, source_target_pairs={{0,8},{1,9},{2,10},{3,11},{4,12},{5,13},{6,14},{7,15},{8,0},{9,1},... | collective-permute-start | bytes 196616 | tf_op jit(solution)/shard_map/ppermute | solution.py:33
  93.9 5.7 %collective-permute-start.27 = (bf16[64,512]{1,0:T(8,128)(2,1)S(1)}, bf16[64,512]{1,0:T(8,128)(2,1)S(1)}, u32[]{:S(2)}, u32[]{:S(2)}) collective-permute-start(bf16[64,512]{1,0:T(8,128)(2,1)S(1)} %add_convert_fusion.1), channel_id=1, source_target_pairs={{0,6},{1,7},{2,4},{3,5},{4,2},{5,3},{6,0},{7,1},{8,14},{9,15},{10,... | collective-permute-start | bytes 196616 | tf_op jit(solution)/shard_map/ppermute | solution.py:33
  94.7 4.9 %collective-permute-start.26 = (bf16[64,512]{1,0:T(8,128)(2,1)S(1)}, bf16[64,512]{1,0:T(8,128)(2,1)S(1)}, u32[]{:S(2)}, u32[]{:S(2)}) collective-permute-start(bf16[64,512]{1,0:T(8,128)(2,1)S(1)} %add_convert_fusion.1), channel_id=1, source_target_pairs={{0,2},{1,3},{2,0},{3,1},{4,6},{5,7},{6,4},{7,5},{8,10},{9,11},{10,... | collective-permute-start | bytes 196616 | tf_op jit(solution)/shard_map/ppermute | solution.py:33
  96.0 4.3 %collective-permute-start.25 = (bf16[64,512]{1,0:T(8,128)(2,1)S(1)}, bf16[64,512]{1,0:T(8,128)(2,1)S(1)}, u32[]{:S(2)}, u32[]{:S(2)}) collective-permute-start(bf16[64,512]{1,0:T(8,128)(2,1)S(1)} %add_convert_fusion.1), channel_id=1, source_target_pairs={{0,4},{1,5},{2,6},{3,7},{4,0},{5,1},{6,2},{7,3},{8,12},{9,13},{10,... | collective-permute-start | bytes 196616 | tf_op jit(solution)/shard_map/ppermute | solution.py:33
  100.4 1.6 %collective-permute-start.28 = (bf16[4,64,512]{2,1,0:T(8,128)(2,1)S(1)}, bf16[4,64,512]{2,1,0:T(8,128)(2,1)S(1)}, u32[]{:S(2)}, u32[]{:S(2)}) collective-permute-start(bf16[4,64,512]{2,1,0:T(8,128)(2,1)S(1)} %pad_maximum_fusion.1.mine_ref), channel_id=1, source_target_pairs={{0,1},{1,0},{2,3},{3,2},{4,5},{5,4},{6,7},{7,6},{8,9},{9,8},{10,11... | collective-permute-start | bytes 786440 | tf_op jit(solution)/shard_map/ppermute | solution.py:33
Sparse Core Ops, SparseCore 0:
  24.1 30.6 all-gather.2
where the time goes:
time: 113 us
  waiting for transfers between devices  40.4 us (36%)
  starting transfers between devices  31.7 us (28%)
  Pallas kernels  19.5 us (17%)
  between operations  14.2 us (13%)
  local copies, waits for them, and re-layouts  5.89 us (5%)
    ppermute x29, waiting for transfers between devices, flip(): return lax.ppermute(x, AXES, [(i, i ^ mask) for i in range(count)])  40.4 us
    ppermute x29, starting transfers between devices, flip(): return lax.ppermute(x, AXES, [(i, i ^ mask) for i in range(count)])  31.7 us
    pallas_call x6, Pallas kernels, run(): pl.pallas_call(kernel, out_shape=outs, in_specs=specs or [SMEM] + [VMEM]...  14.5 us
    pallas_call x1, Pallas kernels, shards(): pl.pallas_call(apply_kernel, grid=(steps,), out_shape=(shape((near_size,...  4.97 us
    unnamed x10, local copies, waits for them, and re-layouts  4.81 us
  transfers between devices with their start and end apart: 30, of which 23 were waited for; matrix products, arithmetic and copies ran while one was open for 1% of the time, Pallas kernels for 5%

commit v1 on v0

--- a/solution.py
+++ b/solution.py
@@ -159,35 +159,34 @@
     return pulled, jnp.sum(1.0 - bent * bent, axis=1, keepdims=True)
 
 
-def apply_kernel(whiten_ref, block_ref, weights_ref, white_ref, newer_ref, total, slope):
-    turn = pl.program_id(0)
-
-    @pl.when(turn == 0)
-    def _():
-        total[...] = jnp.zeros_like(total)
-        slope[...] = jnp.zeros_like(slope)
-
+def apply_kernel(part, whiten_ref, *refs):
+    blocks, (weights_ref, white_ref, total_ref, slope_ref) = refs[:4], refs[-4:]
     weights = weights_ref[...]
-    for k in range(block_ref.shape[0]):
-        white = nn(whiten_ref[...], block_ref[k]).astype(BF)
+    total, slope = refs[4][...] if part else 0.0, refs[5][...] if part else 0.0
+    for k in range(4):
+        white = nn(whiten_ref[...], blocks[k][...]).astype(BF)
         white_ref[k] = white
-        pulled, part = step(weights, white)
-        total[...] += pulled
-        slope[...] += part
-
-    @pl.when(turn == pl.num_programs(0) - 1)
-    def _():
-        newer_ref[...] = total[...] - slope[...] * weights
-
-
-def decor_kernel(last, at, mine_ref, other_ref, white_ref, *refs):
-    outs, (newer, lower, white, sem) = refs[:-4], refs[-4:]
+        pulled, sums = step(weights, white)
+        total += pulled
+        slope += sums
+    if part:
+        total -= slope * weights
+    total_ref[...] = total
+    slope_ref[...] = slope
+
+
+def decor_kernel(last, at, mine_ref, other_ref, *refs):
+    sources = 1 if last else 2
+    whites, outs, (newer, lower, white, sem) = refs[:sources], refs[sources:-4], refs[-4:]
     count = mine_ref.shape[1]
     low, ax, ay = at[0], at[1], at[2]
     chunks = white.shape[0]
-    source = white_ref.at[pl.ds(ay * chunks, chunks)] if last else white_ref
-    copy = pltpu.make_async_copy(source, white, sem)
-    copy.start()
+    copies = [
+        pltpu.make_async_copy(ref, white.at[pl.ds(4 * k, 4)], sem.at[k])
+        for k, ref in enumerate(whites)
+    ]
+    for copy in copies:
+        copy.start()
     for k in range(4):
         i, j = ax ^ (k >> 1), ay ^ (k & 1)
         for ref, core in ((mine_ref, low), (other_ref, 1 - low)):
@@ -211,12 +210,14 @@
     raw = lower[...]
     gram = nt(lower[pl.ds(start, size), :], raw).astype(BF)
     weights = 1.5 * newer[pl.ds(start, size), :] - 0.5 * nn(gram, raw)
-    copy.wait()
+    for copy in copies:
+        copy.wait()
     if last:
         outs[0][...] = weights
         width = white.shape[2]
         for k in range(chunks):
-            outs[1][:, k * width : (k + 1) * width] = nn(
+            place = 2 * (ax ^ (k >> 1)) + (low ^ (k & 1))
+            outs[1][:, pl.ds(pl.multiple_of(place * width, width), width)] = nn(
                 weights.astype(BF), white[k]
             ).astype(BF)
     else:
@@ -257,25 +258,26 @@
     )
     reduced = (kept + flip(sent, across).astype(F32)).astype(BF)
 
-    near_size = comps * 2
-    groups = [
-        list(range(g, g + near_size)) for g in range(0, 1 << all_bits, near_size)
-    ]
-    gathered = lax.all_gather(reduced, AXES, axis=0, axis_index_groups=groups)
-
     block = rows // 4
     piece = 5 * block // 4
     small = shape((piece, block), BF)
+    there = flip(reduced, low)
     own, by, bx, bxy = run(
         covar_kernel,
         (shape((piece, block), F32), small, small, small),
-        (at, reduced, flip(reduced, low)),
+        (at, reduced, there),
         scratch=[pltpu.VMEM((rows, 2 * size), BF), pltpu.VMEM((5 * block, block), F32)],
     )
     own = own + flip(by, near).astype(F32)
     own = own + flip(bx, across).astype(F32)
     own = own + flip(bxy, across | near).astype(F32)
-    packed = spread(sum_over(own, far).astype(BF), across, near)
+
+    reduced, own = lax.optimization_barrier((reduced, own))
+    at_x, at_y = flip(reduced, across), flip(reduced, near)
+    packed = sum_over(own, far).astype(BF)
+    packed = spread(packed, across, near)
+    packed, reduced, at_x, at_y = lax.optimization_barrier((packed, reduced, at_x, at_y))
+    at_xy = flip(reduced, across | near)
     whiten = run(
         functools.partial(whiten_kernel, voxels),
         shape((rows, rows), BF),
@@ -285,29 +287,31 @@
 
     count = initial.shape[0] // 2
     weights = lax.dynamic_slice_in_dim(initial, at[2] * count, count, 0)
-    steps = 4
-    per = near_size // steps
-    whitened, newer = pl.pallas_call(
-        apply_kernel,
-        grid=(steps,),
-        out_shape=(shape((near_size, rows, size), BF), shape((count, rows), F32)),
-        in_specs=[
-            pl.BlockSpec((rows, rows), lambda i: (0, 0)),
-            pl.BlockSpec((per, rows, size), lambda i: (i, 0, 0)),
-            pl.BlockSpec((count, rows), lambda i: (0, 0)),
-        ],
-        out_specs=(
-            pl.BlockSpec((per, rows, size), lambda i: (i, 0, 0)),
-            pl.BlockSpec((count, rows), lambda i: (0, 0)),
-        ),
-        scratch_shapes=[pltpu.VMEM((count, rows), F32), pltpu.VMEM((count, 1), F32)],
-        compiler_params=pltpu.CompilerParams(vmem_limit_bytes=24 * MIB),
-    )(whiten, gathered, weights)
+    outs = (
+        shape((4, rows, size), BF),
+        shape((count, rows), F32),
+        shape((count, 1), F32),
+    )
+    blocks = (reduced, there, at_x, flip(at_x, low))
+    white_here, total, slope = run(
+        functools.partial(apply_kernel, False),
+        outs,
+        (whiten, *blocks, weights),
+        specs=[VMEM] * 6,
+    )
+    blocks = (at_y, flip(at_y, low), at_xy, flip(at_xy, low))
+    white_there, newer, _ = run(
+        functools.partial(apply_kernel, True),
+        outs,
+        (whiten, *blocks, total, slope, weights),
+        specs=[VMEM] * 8,
+    )
+    whites = (white_here, white_there)
 
     for turn in range(ICA_ITERS):
         last = turn == ICA_ITERS - 1
         stacked = spread(sum_over(newer, far).astype(BF), across, near)
-        chunks = comps if last else near_size
+        used = whites[:1] if last else whites
         outs = (
             (shape((2 * count, rows), F32), shape((2 * count, data.shape[1]), BF))
             if last
@@ -316,13 +320,13 @@
         newer = run(
             functools.partial(decor_kernel, last),
             outs,
-            (at, stacked, flip(stacked, low), whitened),
-            specs=[SMEM, VMEM, VMEM, ANY],
+            (at, stacked, flip(stacked, low), *used),
+            specs=[SMEM, VMEM, VMEM] + [ANY] * len(used),
             scratch=[
                 pltpu.VMEM((rows, rows), F32),
                 pltpu.VMEM((rows, rows), BF),
-                pltpu.VMEM((chunks, rows, size), BF),
-                pltpu.SemaphoreType.DMA,
+                pltpu.VMEM((4 * len(used), rows, size), BF),
+                pltpu.SemaphoreType.DMA((2,)),
             ],
         )
     return newer

time: 113 us -> 104 us (0.920)
  between operations: 14.2 us -> 0.99 us
  starting transfers between devices: 31.7 us -> 38.4 us
  local copies, waits for them, and re-layouts: 5.89 us -> 2.13 us
  waiting for transfers between devices: 40.4 us -> 42.7 us
    ppermute x29 -> x35, starting transfers between devices: 31.7 us -> 38.4 us  [flip(): return lax.ppermute(x, AXES, [(i, i ^ mask) for i in range(count)])]
    pallas_call x6 -> x8, Pallas kernels: 14.5 us -> 19.6 us  [run(): pl.pallas_call(kernel, out_shape=outs, in_specs=specs or [SMEM] + [VMEM]...]
    pallas_call x1 -> x0, Pallas kernels: 4.97 us -> none  [shards(): pl.pallas_call(apply_kernel, grid=(steps,), out_shape=(shape((near_size,...]
    unnamed x10 -> x6, local copies, waits for them, and re-layouts: 4.81 us -> 1.05 us
    ppermute x29 -> x35, waiting for transfers between devices: 40.4 us -> 42.7 us  [flip(): return lax.ppermute(x, AXES, [(i, i ^ mask) for i in range(count)])]
  transfers between devices with their start and end apart: 30 -> 35, of which waited for: 23 -> 23; matrix products, arithmetic and copies ran while one was open for 1% -> 1% of each run, Pallas kernels for 5% -> 7%
where the time goes in v1:
time: 104 us
  waiting for transfers between devices  42.7 us (41%)
  starting transfers between devices  38.4 us (37%)
  Pallas kernels  19.6 us (19%)
  local copies, waits for them, and re-layouts  2.13 us (2%)
    ppermute x35, waiting for transfers between devices, flip(): return lax.ppermute(x, AXES, [(i, i ^ mask) for i in range(count)])  42.7 us
    ppermute x35, starting transfers between devices, flip(): return lax.ppermute(x, AXES, [(i, i ^ mask) for i in range(count)])  38.4 us
    pallas_call x8, Pallas kernels, run(): pl.pallas_call(kernel, out_shape=outs, in_specs=specs or [SMEM] + [VMEM]...  19.6 us
  transfers between devices with their start and end apart: 35, of which 23 were waited for; matrix products, arithmetic and copies ran while one was open for 1% of the time, Pallas kernels for 7%

profile of v1, /device:TPU:0, one launch (start us, length us, event | category | flops | bytes accessed | tf_op | source)
XLA Modules:
  0.0 104.3 jit_solution(18191491029737132072)
XLA Ops:
  0.7 0.5 collective-permute-start
  1.2 1.1 %constant_dynamic-slice_fusion.1 = (bf16[512,256]{1,0:T(8,128)(2,1)S(1)}, bf16[512,256]{1,0:T(8,128)(2,1)S(1)}) fusion(bf16[512,1024]{1,0:T(8,128)(2,1)} %right_ref.3, s32[]{:T(128)S(6)} %select_n.10, s32[]{:T(128)S(6)} %select_n.9), kind=kLoop, calls=%fused_computation.9 | loop fusion | bytes 1048584 | tf_op jit(solution)/shard_map/dynamic_slice | solution.py:246
  2.2 0.2 collective-permute-start.2
  2.5 0.3 collective-permute-start.1
  2.8 0.1 pad_add_fusion.at
  2.9 0.9 collective-permute-done.2.other_right_ref
  3.9 1.0 copy-done.2
  4.9 1.0 shard_map.51
  5.9 2.7 %collective-permute-start.3 = (bf16[512,256]{1,0:T(8,128)(2,1)S(1)}, bf16[512,256]{1,0:T(8,128)(2,1)S(1)}, u32[]{:S(2)}, u32[]{:S(2)}) collective-permute-start(bf16[512,256]{1,0:T(8,128)(2,1)S(1)} %shard_map.51), channel_id=1, source_target_pairs={{0,2},{1,3},{2,0},{3,1},{4,6},{5,7},{6,4},{7,5},{8,10},{9,11},{10,... | collective-permute-start | bytes 786440 | tf_op jit(solution)/shard_map/ppermute | solution.py:33
  8.6 1.0 shard_map.50
  9.6 5.8 %collective-permute-done.3 = bf16[512,256]{1,0:T(8,128)(2,1)S(1)} collective-permute-done((bf16[512,256]{1,0:T(8,128)(2,1)S(1)}, bf16[512,256]{1,0:T(8,128)(2,1)S(1)}, u32[]{:S(2)}, u32[]{:S(2)}) %collective-permute-start.3) | collective-permute-done | bytes 262176 | tf_op jit(solution)/shard_map/ppermute | solution.py:33
  15.5 0.1 collective-permute-start.4
  15.6 1.5 %collective-permute-done.4.there_ref.refs_1_ = bf16[512,256]{1,0:T(8,128)(2,1)S(1)} collective-permute-done((bf16[512,256]{1,0:T(8,128)(2,1)S(1)}, bf16[512,256]{1,0:T(8,128)(2,1)S(1)}, u32[]{:S(2)}, u32[]{:S(2)}) %collective-permute-start.4) | collective-permute-done | bytes 262176 | tf_op jit(solution)/shard_map/ppermute | solution.py:33
  17.1 0.9 shard_map.52
  18.0 1.8 %collective-permute-start.5 = (bf16[160,128]{1,0:T(8,128)(2,1)S(1)}, bf16[160,128]{1,0:T(8,128)(2,1)S(1)}, u32[]{:S(2)}, u32[]{:S(2)}) collective-permute-start(bf16[160,128]{1,0:T(8,128)(2,1)S(1)} %get-tuple-element.18), channel_id=1, source_target_pairs={{0,4},{1,5},{2,6},{3,7},{4,0},{5,1},{6,2},{7,3},{8,12},{9,13},{10,... | collective-permute-start | bytes 122888 | tf_op jit(solution)/shard_map/ppermute | solution.py:33
  19.9 1.5 %collective-permute-start.6 = (bf16[160,128]{1,0:T(8,128)(2,1)S(1)}, bf16[160,128]{1,0:T(8,128)(2,1)S(1)}, u32[]{:S(2)}, u32[]{:S(2)}) collective-permute-start(bf16[160,128]{1,0:T(8,128)(2,1)S(1)} %get-tuple-element.19), channel_id=1, source_target_pairs={{0,2},{1,3},{2,0},{3,1},{4,6},{5,7},{6,4},{7,5},{8,10},{9,11},{10,... | collective-permute-start | bytes 122888 | tf_op jit(solution)/shard_map/ppermute | solution.py:33
  21.4 0.2 collective-permute-start.7
  21.6 0.5 collective-permute-done.5
  22.1 2.2 %collective-permute-done.6 = bf16[160,128]{1,0:T(8,128)(2,1)S(1)} collective-permute-done((bf16[160,128]{1,0:T(8,128)(2,1)S(1)}, bf16[160,128]{1,0:T(8,128)(2,1)S(1)}, u32[]{:S(2)}, u32[]{:S(2)}) %collective-permute-start.6) | collective-permute-done | bytes 40992 | tf_op jit(solution)/shard_map/ppermute | solution.py:33
  24.3 2.0 %collective-permute-done.7 = bf16[160,128]{1,0:T(8,128)(2,1)S(1)} collective-permute-done((bf16[160,128]{1,0:T(8,128)(2,1)S(1)}, bf16[160,128]{1,0:T(8,128)(2,1)S(1)}, u32[]{:S(2)}, u32[]{:S(2)}) %collective-permute-start.7) | collective-permute-done | bytes 40992 | tf_op jit(solution)/shard_map/ppermute | solution.py:33
  26.3 3.7 %collective-permute-start.10 = (bf16[160,128]{1,0:T(8,128)(2,1)S(1)}, bf16[160,128]{1,0:T(8,128)(2,1)S(1)}, u32[]{:S(2)}, u32[]{:S(2)}) collective-permute-start(bf16[160,128]{1,0:T(8,128)(2,1)S(1)} %convert_element_type.65), channel_id=1, source_target_pairs={{0,24},{1,25},{2,26},{3,27},{4,28},{5,29},{6,30},{7,31},{8,16},{9,... | collective-permute-start | bytes 122888 | tf_op jit(solution)/shard_map/ppermute | solution.py:33
  30.0 0.8 collective-permute-start.8
  30.8 0.5 collective-permute-start.15
  31.3 0.5 collective-permute-start.14
  31.8 0.5 collective-permute-done.10
  32.3 2.6 %collective-permute-done.9 = bf16[160,128]{1,0:T(8,128)(2,1)S(1)} collective-permute-done((bf16[160,128]{1,0:T(8,128)(2,1)S(1)}, bf16[160,128]{1,0:T(8,128)(2,1)S(1)}, u32[]{:S(2)}, u32[]{:S(2)}) %collective-permute-start.9) | collective-permute-done | bytes 40992 | tf_op jit(solution)/shard_map/ppermute | solution.py:33
  34.9 0.6 collective-permute-start.13
  35.5 1.5 %collective-permute-start.12 = (bf16[160,128]{1,0:T(8,128)(2,1)S(1)}, bf16[160,128]{1,0:T(8,128)(2,1)S(1)}, u32[]{:S(2)}, u32[]{:S(2)}) collective-permute-start(bf16[160,128]{1,0:T(8,128)(2,1)S(1)} %add_convert_fusion.3), channel_id=1, source_target_pairs={{0,2},{1,3},{2,0},{3,1},{4,6},{5,7},{6,4},{7,5},{8,10},{9,11},{10,... | collective-permute-start | bytes 122888 | tf_op jit(solution)/shard_map/ppermute | solution.py:33
  36.9 1.5 %collective-permute-start.11 = (bf16[160,128]{1,0:T(8,128)(2,1)S(1)}, bf16[160,128]{1,0:T(8,128)(2,1)S(1)}, u32[]{:S(2)}, u32[]{:S(2)}) collective-permute-start(bf16[160,128]{1,0:T(8,128)(2,1)S(1)} %add_convert_fusion.3), channel_id=1, source_target_pairs={{0,4},{1,5},{2,6},{3,7},{4,0},{5,1},{6,2},{7,3},{8,12},{9,13},{10,... | collective-permute-start | bytes 122888 | tf_op jit(solution)/shard_map/ppermute | solution.py:33
  38.5 1.4 %collective-permute-done.13 = bf16[160,128]{1,0:T(8,128)(2,1)S(1)} collective-permute-done((bf16[160,128]{1,0:T(8,128)(2,1)S(1)}, bf16[160,128]{1,0:T(8,128)(2,1)S(1)}, u32[]{:S(2)}, u32[]{:S(2)}) %collective-permute-start.13) | collective-permute-done | bytes 40992 | tf_op jit(solution)/shard_map/ppermute | solution.py:33
  39.9 1.0 collective-permute-done.11
  41.0 4.4 %collective-permute-start.18 = (bf16[512,256]{1,0:T(8,128)(2,1)S(1)}, bf16[512,256]{1,0:T(8,128)(2,1)S(1)}, u32[]{:S(2)}, u32[]{:S(2)}) collective-permute-start(bf16[512,256]{1,0:T(8,128)(2,1)S(1)} %add_convert_fusion.here_ref.refs_0_), channel_id=1, source_target_pairs={{0,6},{1,7},{2,4},{3,5},{4,2},{5,3},{6,0},{7,1},{8,14},{9,15},{10,... | collective-permute-start | bytes 786440 | tf_op jit(solution)/shard_map/ppermute | solution.py:33
  45.4 0.5 collective-permute-start.17
  45.9 3.8 %collective-permute-done.18.refs_2_ = bf16[512,256]{1,0:T(8,128)(2,1)S(1)} collective-permute-done((bf16[512,256]{1,0:T(8,128)(2,1)S(1)}, bf16[512,256]{1,0:T(8,128)(2,1)S(1)}, u32[]{:S(2)}, u32[]{:S(2)}) %collective-permute-start.18) | collective-permute-done | bytes 262176 | tf_op jit(solution)/shard_map/ppermute | solution.py:33
  49.7 0.5 collective-permute-start.16
  50.2 1.2 %collective-permute-done.16.other_ref = bf16[4,160,128]{2,1,0:T(8,128)(2,1)S(1)} collective-permute-done((bf16[4,160,128]{2,1,0:T(8,128)(2,1)S(1)}, bf16[4,160,128]{2,1,0:T(8,128)(2,1)S(1)}, u32[]{:S(2)}, u32[]{:S(2)}) %collective-permute-start.16) | collective-permute-done | bytes 163872 | tf_op jit(solution)/shard_map/ppermute | solution.py:33
  51.5 3.0 %shard_map.53.whiten_ref = bf16[512,512]{1,0:T(8,128)(2,1)S(1)} custom-call(s32[3]{0:T(128)S(1)} %pad_add_fusion.at, bf16[4,160,128]{2,1,0:T(8,128)(2,1)S(1)} %pad_maximum_fusion.2.mine_ref, bf16[4,160,128]{2,1,0:T(8,128)(2,1)S(1)} %collective-permute-done.16.other_ref), custom_call_target="tpu_custom_call" | custom-call | tf_op jit(solution)/shard_map/pallas_call | solution.py:58
  54.5 2.3 %shard_map.54 = (bf16[4,512,256]{2,1,0:T(8,128)(2,1)S(1)}, f32[64,512]{1,0:T(8,128)S(1)}, f32[64,1]{1,0:T(8,128)S(1)}) custom-call(bf16[512,512]{1,0:T(8,128)(2,1)S(1)} %shard_map.53.whiten_ref, bf16[512,256]{1,0:T(8,128)(2,1)S(1)} %add_convert_fusion.here_ref.refs_0_, bf16[512,256]{1,0:T(8,128)(2,1)S(1)} %collective-permute-done.4.there_ref.refs_1_, ...), custom_call_target="tpu_custom_call" | custom-call | tf_op jit(solution)/shard_map/pallas_call | solution.py:58
  56.8 2.6 %shard_map.55 = (bf16[4,512,256]{2,1,0:T(8,128)(2,1)S(1)}, f32[64,512]{1,0:T(8,128)S(1)}, f32[64,1]{1,0:T(8,128)}) custom-call(bf16[512,512]{1,0:T(8,128)(2,1)S(1)} %shard_map.53.whiten_ref, bf16[512,256]{1,0:T(8,128)(2,1)S(1)} %collective-permute-done.15.refs_0_, bf16[512,256]{1,0:T(8,128)(2,1)S(1)} %collective-permute-done.17.refs_1_, ...), custom_call_target="tpu_custom_call" | custom-call | tf_op jit(solution)/shard_map/pallas_call | solution.py:58
  59.4 0.7 collective-permute-start.23
  60.1 1.8 %collective-permute-start.22 = (bf16[64,512]{1,0:T(8,128)(2,1)S(1)}, bf16[64,512]{1,0:T(8,128)(2,1)S(1)}, u32[]{:S(2)}, u32[]{:S(2)}) collective-permute-start(bf16[64,512]{1,0:T(8,128)(2,1)S(1)} %convert_element_type.70), channel_id=1, source_target_pairs={{0,16},{1,17},{2,18},{3,19},{4,20},{5,21},{6,22},{7,23},{8,24},{9,... | collective-permute-start | bytes 196616 | tf_op jit(solution)/shard_map/ppermute | solution.py:33
  61.9 2.0 %collective-permute-start.21 = (bf16[64,512]{1,0:T(8,128)(2,1)S(1)}, bf16[64,512]{1,0:T(8,128)(2,1)S(1)}, u32[]{:S(2)}, u32[]{:S(2)}) collective-permute-start(bf16[64,512]{1,0:T(8,128)(2,1)S(1)} %convert_element_type.70), channel_id=1, source_target_pairs={{0,8},{1,9},{2,10},{3,11},{4,12},{5,13},{6,14},{7,15},{8,0},{9,1},... | collective-permute-start | bytes 196616 | tf_op jit(solution)/shard_map/ppermute | solution.py:33
  63.9 2.1 %collective-permute-done.23 = bf16[64,512]{1,0:T(8,128)(2,1)S(1)} collective-permute-done((bf16[64,512]{1,0:T(8,128)(2,1)S(1)}, bf16[64,512]{1,0:T(8,128)(2,1)S(1)}, u32[]{:S(2)}, u32[]{:S(2)}) %collective-permute-start.23) | collective-permute-done | bytes 65568 | tf_op jit(solution)/shard_map/ppermute | solution.py:33
  66.0 2.5 %collective-permute-done.22 = bf16[64,512]{1,0:T(8,128)(2,1)S(1)} collective-permute-done((bf16[64,512]{1,0:T(8,128)(2,1)S(1)}, bf16[64,512]{1,0:T(8,128)(2,1)S(1)}, u32[]{:S(2)}, u32[]{:S(2)}) %collective-permute-start.22) | collective-permute-done | bytes 65568 | tf_op jit(solution)/shard_map/ppermute | solution.py:33
  68.5 2.7 %collective-permute-start.26 = (bf16[64,512]{1,0:T(8,128)(2,1)S(1)}, bf16[64,512]{1,0:T(8,128)(2,1)S(1)}, u32[]{:S(2)}, u32[]{:S(2)}) collective-permute-start(bf16[64,512]{1,0:T(8,128)(2,1)S(1)} %add_convert_fusion.2), channel_id=1, source_target_pairs={{0,6},{1,7},{2,4},{3,5},{4,2},{5,3},{6,0},{7,1},{8,14},{9,15},{10,... | collective-permute-start | bytes 196616 | tf_op jit(solution)/shard_map/ppermute | solution.py:33
  71.2 1.3 %collective-permute-start.25 = (bf16[64,512]{1,0:T(8,128)(2,1)S(1)}, bf16[64,512]{1,0:T(8,128)(2,1)S(1)}, u32[]{:S(2)}, u32[]{:S(2)}) collective-permute-start(bf16[64,512]{1,0:T(8,128)(2,1)S(1)} %add_convert_fusion.2), channel_id=1, source_target_pairs={{0,2},{1,3},{2,0},{3,1},{4,6},{5,7},{6,4},{7,5},{8,10},{9,11},{10,... | collective-permute-start | bytes 196616 | tf_op jit(solution)/shard_map/ppermute | solution.py:33
  72.5 1.5 %collective-permute-done.26 = bf16[64,512]{1,0:T(8,128)(2,1)S(1)} collective-permute-done((bf16[64,512]{1,0:T(8,128)(2,1)S(1)}, bf16[64,512]{1,0:T(8,128)(2,1)S(1)}, u32[]{:S(2)}, u32[]{:S(2)}) %collective-permute-start.26) | collective-permute-done | bytes 65568 | tf_op jit(solution)/shard_map/ppermute | solution.py:33
  74.0 1.5 %collective-permute-done.25 = bf16[64,512]{1,0:T(8,128)(2,1)S(1)} collective-permute-done((bf16[64,512]{1,0:T(8,128)(2,1)S(1)}, bf16[64,512]{1,0:T(8,128)(2,1)S(1)}, u32[]{:S(2)}, u32[]{:S(2)}) %collective-permute-start.25) | collective-permute-done | bytes 65568 | tf_op jit(solution)/shard_map/ppermute | solution.py:33
  75.4 1.3 %collective-permute-done.24 = bf16[64,512]{1,0:T(8,128)(2,1)S(1)} collective-permute-done((bf16[64,512]{1,0:T(8,128)(2,1)S(1)}, bf16[64,512]{1,0:T(8,128)(2,1)S(1)}, u32[]{:S(2)}, u32[]{:S(2)}) %collective-permute-start.24) | collective-permute-done | bytes 65568 | tf_op jit(solution)/shard_map/ppermute | solution.py:33
  76.8 0.1 collective-permute-start.27
  76.9 1.5 %collective-permute-done.27.other_ref = bf16[4,64,512]{2,1,0:T(8,128)(2,1)S(1)} collective-permute-done((bf16[4,64,512]{2,1,0:T(8,128)(2,1)S(1)}, bf16[4,64,512]{2,1,0:T(8,128)(2,1)S(1)}, u32[]{:S(2)}, u32[]{:S(2)}) %collective-permute-start.27) | collective-permute-done | bytes 262176 | tf_op jit(solution)/shard_map/ppermute | solution.py:33
  78.4 4.8 %shard_map.56 = f32[64,512]{1,0:T(8,128)S(1)} custom-call(s32[3]{0:T(128)S(1)} %pad_add_fusion.at, bf16[4,64,512]{2,1,0:T(8,128)(2,1)S(1)} %pad_maximum_fusion.mine_ref, bf16[4,64,512]{2,1,0:T(8,128)(2,1)S(1)} %collective-permute-done.27.other_ref, bf16[4,512,256]{2,1,0:T(8,128)(2,1)S(1)} %get-tuple-element.30.refs_0_, ...), custom_call_target="tpu_custom_call" | custom-call | tf_op jit(solution)/shard_map/pallas_call | solution.py:58
  83.3 2.1 %collective-permute-start.30 = (bf16[64,512]{1,0:T(8,128)(2,1)S(1)}, bf16[64,512]{1,0:T(8,128)(2,1)S(1)}, u32[]{:S(2)}, u32[]{:S(2)}) collective-permute-start(bf16[64,512]{1,0:T(8,128)(2,1)S(1)} %convert_element_type.75), channel_id=1, source_target_pairs={{0,24},{1,25},{2,26},{3,27},{4,28},{5,29},{6,30},{7,31},{8,16},{9,... | collective-permute-start | bytes 196616 | tf_op jit(solution)/shard_map/ppermute | solution.py:33
  85.3 2.4 %collective-permute-start.28 = (bf16[64,512]{1,0:T(8,128)(2,1)S(1)}, bf16[64,512]{1,0:T(8,128)(2,1)S(1)}, u32[]{:S(2)}, u32[]{:S(2)}) collective-permute-start(bf16[64,512]{1,0:T(8,128)(2,1)S(1)} %convert_element_type.75), channel_id=1, source_target_pairs={{0,8},{1,9},{2,10},{3,11},{4,12},{5,13},{6,14},{7,15},{8,0},{9,1},... | collective-permute-start | bytes 196616 | tf_op jit(solution)/shard_map/ppermute | solution.py:33
  87.7 2.4 %collective-permute-done.30 = bf16[64,512]{1,0:T(8,128)(2,1)S(1)} collective-permute-done((bf16[64,512]{1,0:T(8,128)(2,1)S(1)}, bf16[64,512]{1,0:T(8,128)(2,1)S(1)}, u32[]{:S(2)}, u32[]{:S(2)}) %collective-permute-start.30) | collective-permute-done | bytes 65568 | tf_op jit(solution)/shard_map/ppermute | solution.py:33
  90.1 2.0 %collective-permute-done.29 = bf16[64,512]{1,0:T(8,128)(2,1)S(1)} collective-permute-done((bf16[64,512]{1,0:T(8,128)(2,1)S(1)}, bf16[64,512]{1,0:T(8,128)(2,1)S(1)}, u32[]{:S(2)}, u32[]{:S(2)}) %collective-permute-start.29) | collective-permute-done | bytes 65568 | tf_op jit(solution)/shard_map/ppermute | solution.py:33
  92.1 0.5 collective-permute-start.33
  92.6 1.1 %collective-permute-start.32 = (bf16[64,512]{1,0:T(8,128)(2,1)S(1)}, bf16[64,512]{1,0:T(8,128)(2,1)S(1)}, u32[]{:S(2)}, u32[]{:S(2)}) collective-permute-start(bf16[64,512]{1,0:T(8,128)(2,1)S(1)} %add_convert_fusion.1), channel_id=1, source_target_pairs={{0,2},{1,3},{2,0},{3,1},{4,6},{5,7},{6,4},{7,5},{8,10},{9,11},{10,... | collective-permute-start | bytes 196616 | tf_op jit(solution)/shard_map/ppermute | solution.py:33
  93.8 1.9 %collective-permute-start.31 = (bf16[64,512]{1,0:T(8,128)(2,1)S(1)}, bf16[64,512]{1,0:T(8,128)(2,1)S(1)}, u32[]{:S(2)}, u32[]{:S(2)}) collective-permute-start(bf16[64,512]{1,0:T(8,128)(2,1)S(1)} %add_convert_fusion.1), channel_id=1, source_target_pairs={{0,4},{1,5},{2,6},{3,7},{4,0},{5,1},{6,2},{7,3},{8,12},{9,13},{10,... | collective-permute-start | bytes 196616 | tf_op jit(solution)/shard_map/ppermute | solution.py:33
  95.7 2.1 %collective-permute-done.33 = bf16[64,512]{1,0:T(8,128)(2,1)S(1)} collective-permute-done((bf16[64,512]{1,0:T(8,128)(2,1)S(1)}, bf16[64,512]{1,0:T(8,128)(2,1)S(1)}, u32[]{:S(2)}, u32[]{:S(2)}) %collective-permute-start.33) | collective-permute-done | bytes 65568 | tf_op jit(solution)/shard_map/ppermute | solution.py:33
  97.8 0.7 collective-permute-done.31
  98.5 0.1 collective-permute-start.34
  98.6 1.5 %collective-permute-done.34.other_ref = bf16[4,64,512]{2,1,0:T(8,128)(2,1)S(1)} collective-permute-done((bf16[4,64,512]{2,1,0:T(8,128)(2,1)S(1)}, bf16[4,64,512]{2,1,0:T(8,128)(2,1)S(1)}, u32[]{:S(2)}, u32[]{:S(2)}) %collective-permute-start.34) | collective-permute-done | bytes 262176 | tf_op jit(solution)/shard_map/ppermute | solution.py:33
  100.1 4.0 %shard_map.57 = (f32[128,512]{1,0:T(8,128)}, bf16[128,1024]{1,0:T(8,128)(2,1)}) custom-call(s32[3]{0:T(128)S(1)} %pad_add_fusion.at, bf16[4,64,512]{2,1,0:T(8,128)(2,1)S(1)} %pad_maximum_fusion.1.mine_ref, bf16[4,64,512]{2,1,0:T(8,128)(2,1)S(1)} %collective-permute-done.34.other_ref, bf16[4,512,256]{2,1,0:T(8,128)(2,1)S(1)} %get-tuple-element.30.refs_0_), custom_call_target="tpu_custom_call" | custom-call | tf_op jit(solution)/shard_map/pallas_call | solution.py:58
  (34 shorter events, 0.4 us)
Async XLA Ops:
  0.6 49.6 %copy-start = (f32[128,512]{1,0:T(8,128)S(1)}, f32[128,512]{1,0:T(8,128)}, u32[]{:S(2)}) copy-start(f32[128,512]{1,0:T(8,128)} %param.5) | copy-start | bytes 786436
  0.6 3.2 %copy-start.1 = (bf16[512,1024]{1,0:T(8,128)(2,1)S(1)}, bf16[512,1024]{1,0:T(8,128)(2,1)}, u32[]{:S(2)}) copy-start(bf16[512,1024]{1,0:T(8,128)(2,1)} %right_ref.3) | copy-start | bytes 3145732
  0.7 3.2 %collective-permute-start = (bf16[512,512]{1,0:T(8,128)(2,1)}, bf16[512,512]{1,0:T(8,128)(2,1)S(1)}, u32[]{:S(2)}, u32[]{:S(2)}) collective-permute-start(bf16[512,512]{1,0:T(8,128)(2,1)} %left_ref.3), channel_id=1, source_target_pairs={{0,1},{1,0},{2,3},{3,2},{4,5},{5,4},{6,7},{7,6},{8,9},{9,8},{10,11... | collective-permute-start | bytes 1572872 | tf_op jit(solution)/shard_map/ppermute | solution.py:33
  2.2 1.6 %collective-permute-start.2 = (bf16[512,256]{1,0:T(8,128)(2,1)S(1)}, bf16[512,256]{1,0:T(8,128)(2,1)S(1)}, u32[]{:S(2)}, u32[]{:S(2)}) collective-permute-start(bf16[512,256]{1,0:T(8,128)(2,1)S(1)} %get-tuple-element.32), channel_id=1, source_target_pairs={{0,1},{1,0},{2,3},{3,2},{4,5},{5,4},{6,7},{7,6},{8,9},{9,8},{10,11... | collective-permute-start | bytes 786440 | tf_op jit(solution)/shard_map/ppermute | solution.py:33
  2.5 6.1 %collective-permute-start.1 = (bf16[512,256]{1,0:T(8,128)(2,1)S(1)}, bf16[512,256]{1,0:T(8,128)(2,1)S(1)}, u32[]{:S(2)}, u32[]{:S(2)}) collective-permute-start(bf16[512,256]{1,0:T(8,128)(2,1)S(1)} %get-tuple-element.33), channel_id=1, source_target_pairs={{0,1},{1,0},{2,3},{3,2},{4,5},{5,4},{6,7},{7,6},{8,9},{9,8},{10,11... | collective-permute-start | bytes 786440 | tf_op jit(solution)/shard_map/ppermute | solution.py:33
  3.9 1.0 %copy-start.2 = (bf16[512,512]{1,0:T(8,128)(2,1)S(1)}, bf16[512,512]{1,0:T(8,128)(2,1)}, u32[]{:S(2)}) copy-start(bf16[512,512]{1,0:T(8,128)(2,1)} %left_ref.3) | copy-start | bytes 1572868
  5.9 9.5 %collective-permute-start.3 = (bf16[512,256]{1,0:T(8,128)(2,1)S(1)}, bf16[512,256]{1,0:T(8,128)(2,1)S(1)}, u32[]{:S(2)}, u32[]{:S(2)}) collective-permute-start(bf16[512,256]{1,0:T(8,128)(2,1)S(1)} %shard_map.51), channel_id=1, source_target_pairs={{0,2},{1,3},{2,0},{3,1},{4,6},{5,7},{6,4},{7,5},{8,10},{9,11},{10,... | collective-permute-start | bytes 786440 | tf_op jit(solution)/shard_map/ppermute | solution.py:33
  15.5 1.6 %collective-permute-start.4 = (bf16[512,256]{1,0:T(8,128)(2,1)S(1)}, bf16[512,256]{1,0:T(8,128)(2,1)S(1)}, u32[]{:S(2)}, u32[]{:S(2)}) collective-permute-start(bf16[512,256]{1,0:T(8,128)(2,1)S(1)} %add_convert_fusion.here_ref.refs_0_), channel_id=1, source_target_pairs={{0,1},{1,0},{2,3},{3,2},{4,5},{5,4},{6,7},{7,6},{8,9},{9,8},{10,11... | collective-permute-start | bytes 786440 | tf_op jit(solution)/shard_map/ppermute | solution.py:33
  18.0 4.1 %collective-permute-start.5 = (bf16[160,128]{1,0:T(8,128)(2,1)S(1)}, bf16[160,128]{1,0:T(8,128)(2,1)S(1)}, u32[]{:S(2)}, u32[]{:S(2)}) collective-permute-start(bf16[160,128]{1,0:T(8,128)(2,1)S(1)} %get-tuple-element.18), channel_id=1, source_target_pairs={{0,4},{1,5},{2,6},{3,7},{4,0},{5,1},{6,2},{7,3},{8,12},{9,13},{10,... | collective-permute-start | bytes 122888 | tf_op jit(solution)/shard_map/ppermute | solution.py:33
  19.9 4.4 %collective-permute-start.6 = (bf16[160,128]{1,0:T(8,128)(2,1)S(1)}, bf16[160,128]{1,0:T(8,128)(2,1)S(1)}, u32[]{:S(2)}, u32[]{:S(2)}) collective-permute-start(bf16[160,128]{1,0:T(8,128)(2,1)S(1)} %get-tuple-element.19), channel_id=1, source_target_pairs={{0,2},{1,3},{2,0},{3,1},{4,6},{5,7},{6,4},{7,5},{8,10},{9,11},{10,... | collective-permute-start | bytes 122888 | tf_op jit(solution)/shard_map/ppermute | solution.py:33
  21.4 4.9 %collective-permute-start.7 = (bf16[160,128]{1,0:T(8,128)(2,1)S(1)}, bf16[160,128]{1,0:T(8,128)(2,1)S(1)}, u32[]{:S(2)}, u32[]{:S(2)}) collective-permute-start(bf16[160,128]{1,0:T(8,128)(2,1)S(1)} %get-tuple-element.20), channel_id=1, source_target_pairs={{0,6},{1,7},{2,4},{3,5},{4,2},{5,3},{6,0},{7,1},{8,14},{9,15},{10,... | collective-permute-start | bytes 122888 | tf_op jit(solution)/shard_map/ppermute | solution.py:33
  26.3 6.0 %collective-permute-start.10 = (bf16[160,128]{1,0:T(8,128)(2,1)S(1)}, bf16[160,128]{1,0:T(8,128)(2,1)S(1)}, u32[]{:S(2)}, u32[]{:S(2)}) collective-permute-start(bf16[160,128]{1,0:T(8,128)(2,1)S(1)} %convert_element_type.65), channel_id=1, source_target_pairs={{0,24},{1,25},{2,26},{3,27},{4,28},{5,29},{6,30},{7,31},{8,16},{9,... | collective-permute-start | bytes 122888 | tf_op jit(solution)/shard_map/ppermute | solution.py:33
  30.0 4.9 %collective-permute-start.9 = (bf16[160,128]{1,0:T(8,128)(2,1)S(1)}, bf16[160,128]{1,0:T(8,128)(2,1)S(1)}, u32[]{:S(2)}, u32[]{:S(2)}) collective-permute-start(bf16[160,128]{1,0:T(8,128)(2,1)S(1)} %convert_element_type.65), channel_id=1, source_target_pairs={{0,16},{1,17},{2,18},{3,19},{4,20},{5,21},{6,22},{7,23},{8,24},{9,... | collective-permute-start | bytes 122888 | tf_op jit(solution)/shard_map/ppermute | solution.py:33
  30.0 4.9 %collective-permute-start.8 = (bf16[160,128]{1,0:T(8,128)(2,1)S(1)}, bf16[160,128]{1,0:T(8,128)(2,1)S(1)}, u32[]{:S(2)}, u32[]{:S(2)}) collective-permute-start(bf16[160,128]{1,0:T(8,128)(2,1)S(1)} %convert_element_type.65), channel_id=1, source_target_pairs={{0,8},{1,9},{2,10},{3,11},{4,12},{5,13},{6,14},{7,15},{8,0},{9,1},... | collective-permute-start | bytes 122888 | tf_op jit(solution)/shard_map/ppermute | solution.py:33
  30.8 10.2 %collective-permute-start.15 = (bf16[512,256]{1,0:T(8,128)(2,1)S(1)}, bf16[512,256]{1,0:T(8,128)(2,1)S(1)}, u32[]{:S(2)}, u32[]{:S(2)}) collective-permute-start(bf16[512,256]{1,0:T(8,128)(2,1)S(1)} %add_convert_fusion.here_ref.refs_0_), channel_id=1, source_target_pairs={{0,4},{1,5},{2,6},{3,7},{4,0},{5,1},{6,2},{7,3},{8,12},{9,13},{10,... | collective-permute-start | bytes 786440 | tf_op jit(solution)/shard_map/ppermute | solution.py:33
  31.3 9.7 %collective-permute-start.14 = (bf16[512,256]{1,0:T(8,128)(2,1)S(1)}, bf16[512,256]{1,0:T(8,128)(2,1)S(1)}, u32[]{:S(2)}, u32[]{:S(2)}) collective-permute-start(bf16[512,256]{1,0:T(8,128)(2,1)S(1)} %add_convert_fusion.here_ref.refs_0_), channel_id=1, source_target_pairs={{0,2},{1,3},{2,0},{3,1},{4,6},{5,7},{6,4},{7,5},{8,10},{9,11},{10,... | collective-permute-start | bytes 786440 | tf_op jit(solution)/shard_map/ppermute | solution.py:33
  34.9 5.0 %collective-permute-start.13 = (bf16[160,128]{1,0:T(8,128)(2,1)S(1)}, bf16[160,128]{1,0:T(8,128)(2,1)S(1)}, u32[]{:S(2)}, u32[]{:S(2)}) collective-permute-start(bf16[160,128]{1,0:T(8,128)(2,1)S(1)} %add_convert_fusion.3), channel_id=1, source_target_pairs={{0,6},{1,7},{2,4},{3,5},{4,2},{5,3},{6,0},{7,1},{8,14},{9,15},{10,... | collective-permute-start | bytes 122888 | tf_op jit(solution)/shard_map/ppermute | solution.py:33
  35.5 4.5 %collective-permute-start.12 = (bf16[160,128]{1,0:T(8,128)(2,1)S(1)}, bf16[160,128]{1,0:T(8,128)(2,1)S(1)}, u32[]{:S(2)}, u32[]{:S(2)}) collective-permute-start(bf16[160,128]{1,0:T(8,128)(2,1)S(1)} %add_convert_fusion.3), channel_id=1, source_target_pairs={{0,2},{1,3},{2,0},{3,1},{4,6},{5,7},{6,4},{7,5},{8,10},{9,11},{10,... | collective-permute-start | bytes 122888 | tf_op jit(solution)/shard_map/ppermute | solution.py:33
  36.9 4.0 %collective-permute-start.11 = (bf16[160,128]{1,0:T(8,128)(2,1)S(1)}, bf16[160,128]{1,0:T(8,128)(2,1)S(1)}, u32[]{:S(2)}, u32[]{:S(2)}) collective-permute-start(bf16[160,128]{1,0:T(8,128)(2,1)S(1)} %add_convert_fusion.3), channel_id=1, source_target_pairs={{0,4},{1,5},{2,6},{3,7},{4,0},{5,1},{6,2},{7,3},{8,12},{9,13},{10,... | collective-permute-start | bytes 122888 | tf_op jit(solution)/shard_map/ppermute | solution.py:33
  41.0 8.7 %collective-permute-start.18 = (bf16[512,256]{1,0:T(8,128)(2,1)S(1)}, bf16[512,256]{1,0:T(8,128)(2,1)S(1)}, u32[]{:S(2)}, u32[]{:S(2)}) collective-permute-start(bf16[512,256]{1,0:T(8,128)(2,1)S(1)} %add_convert_fusion.here_ref.refs_0_), channel_id=1, source_target_pairs={{0,6},{1,7},{2,4},{3,5},{4,2},{5,3},{6,0},{7,1},{8,14},{9,15},{10,... | collective-permute-start | bytes 786440 | tf_op jit(solution)/shard_map/ppermute | solution.py:33
  45.4 9.1 %collective-permute-start.20 = (bf16[512,256]{1,0:T(8,128)(2,1)S(1)}, bf16[512,256]{1,0:T(8,128)(2,1)S(1)}, u32[]{:S(2)}, u32[]{:S(2)}) collective-permute-start(bf16[512,256]{1,0:T(8,128)(2,1)S(1)} %collective-permute-done.14.refs_2_), channel_id=1, source_target_pairs={{0,1},{1,0},{2,3},{3,2},{4,5},{5,4},{6,7},{7,6},{8,9},{9,8},{10,11... | collective-permute-start | bytes 786440 | tf_op jit(solution)/shard_map/ppermute | solution.py:33
  45.4 11.4 %collective-permute-start.17 = (bf16[512,256]{1,0:T(8,128)(2,1)S(1)}, bf16[512,256]{1,0:T(8,128)(2,1)S(1)}, u32[]{:S(2)}, u32[]{:S(2)}) collective-permute-start(bf16[512,256]{1,0:T(8,128)(2,1)S(1)} %collective-permute-done.15.refs_0_), channel_id=1, source_target_pairs={{0,1},{1,0},{2,3},{3,2},{4,5},{5,4},{6,7},{7,6},{8,9},{9,8},{10,11... | collective-permute-start | bytes 786440 | tf_op jit(solution)/shard_map/ppermute | solution.py:33
  49.7 7.1 %collective-permute-start.19 = (bf16[512,256]{1,0:T(8,128)(2,1)S(1)}, bf16[512,256]{1,0:T(8,128)(2,1)S(1)}, u32[]{:S(2)}, u32[]{:S(2)}) collective-permute-start(bf16[512,256]{1,0:T(8,128)(2,1)S(1)} %collective-permute-done.18.refs_2_), channel_id=1, source_target_pairs={{0,1},{1,0},{2,3},{3,2},{4,5},{5,4},{6,7},{7,6},{8,9},{9,8},{10,11... | collective-permute-start | bytes 786440 | tf_op jit(solution)/shard_map/ppermute | solution.py:33
  49.7 1.8 %collective-permute-start.16 = (bf16[4,160,128]{2,1,0:T(8,128)(2,1)S(1)}, bf16[4,160,128]{2,1,0:T(8,128)(2,1)S(1)}, u32[]{:S(2)}, u32[]{:S(2)}) collective-permute-start(bf16[4,160,128]{2,1,0:T(8,128)(2,1)S(1)} %pad_maximum_fusion.2.mine_ref), channel_id=1, source_target_pairs={{0,1},{1,0},{2,3},{3,2},{4,5},{5,4},{6,7},{7,6},{8,9},{9,8},{10,11... | collective-permute-start | bytes 491528 | tf_op jit(solution)/shard_map/ppermute | solution.py:33
  59.4 6.6 %collective-permute-start.23 = (bf16[64,512]{1,0:T(8,128)(2,1)S(1)}, bf16[64,512]{1,0:T(8,128)(2,1)S(1)}, u32[]{:S(2)}, u32[]{:S(2)}) collective-permute-start(bf16[64,512]{1,0:T(8,128)(2,1)S(1)} %convert_element_type.70), channel_id=1, source_target_pairs={{0,24},{1,25},{2,26},{3,27},{4,28},{5,29},{6,30},{7,31},{8,16},{9,... | collective-permute-start | bytes 196616 | tf_op jit(solution)/shard_map/ppermute | solution.py:33
  60.1 8.4 %collective-permute-start.22 = (bf16[64,512]{1,0:T(8,128)(2,1)S(1)}, bf16[64,512]{1,0:T(8,128)(2,1)S(1)}, u32[]{:S(2)}, u32[]{:S(2)}) collective-permute-start(bf16[64,512]{1,0:T(8,128)(2,1)S(1)} %convert_element_type.70), channel_id=1, source_target_pairs={{0,16},{1,17},{2,18},{3,19},{4,20},{5,21},{6,22},{7,23},{8,24},{9,... | collective-permute-start | bytes 196616 | tf_op jit(solution)/shard_map/ppermute | solution.py:33
  61.9 6.5 %collective-permute-start.21 = (bf16[64,512]{1,0:T(8,128)(2,1)S(1)}, bf16[64,512]{1,0:T(8,128)(2,1)S(1)}, u32[]{:S(2)}, u32[]{:S(2)}) collective-permute-start(bf16[64,512]{1,0:T(8,128)(2,1)S(1)} %convert_element_type.70), channel_id=1, source_target_pairs={{0,8},{1,9},{2,10},{3,11},{4,12},{5,13},{6,14},{7,15},{8,0},{9,1},... | collective-permute-start | bytes 196616 | tf_op jit(solution)/shard_map/ppermute | solution.py:33
  68.5 5.4 %collective-permute-start.26 = (bf16[64,512]{1,0:T(8,128)(2,1)S(1)}, bf16[64,512]{1,0:T(8,128)(2,1)S(1)}, u32[]{:S(2)}, u32[]{:S(2)}) collective-permute-start(bf16[64,512]{1,0:T(8,128)(2,1)S(1)} %add_convert_fusion.2), channel_id=1, source_target_pairs={{0,6},{1,7},{2,4},{3,5},{4,2},{5,3},{6,0},{7,1},{8,14},{9,15},{10,... | collective-permute-start | bytes 196616 | tf_op jit(solution)/shard_map/ppermute | solution.py:33
  71.2 4.3 %collective-permute-start.25 = (bf16[64,512]{1,0:T(8,128)(2,1)S(1)}, bf16[64,512]{1,0:T(8,128)(2,1)S(1)}, u32[]{:S(2)}, u32[]{:S(2)}) collective-permute-start(bf16[64,512]{1,0:T(8,128)(2,1)S(1)} %add_convert_fusion.2), channel_id=1, source_target_pairs={{0,2},{1,3},{2,0},{3,1},{4,6},{5,7},{6,4},{7,5},{8,10},{9,11},{10,... | collective-permute-start | bytes 196616 | tf_op jit(solution)/shard_map/ppermute | solution.py:33
  72.5 4.3 %collective-permute-start.24 = (bf16[64,512]{1,0:T(8,128)(2,1)S(1)}, bf16[64,512]{1,0:T(8,128)(2,1)S(1)}, u32[]{:S(2)}, u32[]{:S(2)}) collective-permute-start(bf16[64,512]{1,0:T(8,128)(2,1)S(1)} %add_convert_fusion.2), channel_id=1, source_target_pairs={{0,4},{1,5},{2,6},{3,7},{4,0},{5,1},{6,2},{7,3},{8,12},{9,13},{10,... | collective-permute-start | bytes 196616 | tf_op jit(solution)/shard_map/ppermute | solution.py:33
  76.8 1.6 %collective-permute-start.27 = (bf16[4,64,512]{2,1,0:T(8,128)(2,1)S(1)}, bf16[4,64,512]{2,1,0:T(8,128)(2,1)S(1)}, u32[]{:S(2)}, u32[]{:S(2)}) collective-permute-start(bf16[4,64,512]{2,1,0:T(8,128)(2,1)S(1)} %pad_maximum_fusion.mine_ref), channel_id=1, source_target_pairs={{0,1},{1,0},{2,3},{3,2},{4,5},{5,4},{6,7},{7,6},{8,9},{9,8},{10,11... | collective-permute-start | bytes 786440 | tf_op jit(solution)/shard_map/ppermute | solution.py:33
  83.3 6.8 %collective-permute-start.30 = (bf16[64,512]{1,0:T(8,128)(2,1)S(1)}, bf16[64,512]{1,0:T(8,128)(2,1)S(1)}, u32[]{:S(2)}, u32[]{:S(2)}) collective-permute-start(bf16[64,512]{1,0:T(8,128)(2,1)S(1)} %convert_element_type.75), channel_id=1, source_target_pairs={{0,24},{1,25},{2,26},{3,27},{4,28},{5,29},{6,30},{7,31},{8,16},{9,... | collective-permute-start | bytes 196616 | tf_op jit(solution)/shard_map/ppermute | solution.py:33
  85.3 6.7 %collective-permute-start.29 = (bf16[64,512]{1,0:T(8,128)(2,1)S(1)}, bf16[64,512]{1,0:T(8,128)(2,1)S(1)}, u32[]{:S(2)}, u32[]{:S(2)}) collective-permute-start(bf16[64,512]{1,0:T(8,128)(2,1)S(1)} %convert_element_type.75), channel_id=1, source_target_pairs={{0,16},{1,17},{2,18},{3,19},{4,20},{5,21},{6,22},{7,23},{8,24},{9,... | collective-permute-start | bytes 196616 | tf_op jit(solution)/shard_map/ppermute | solution.py:33
  85.3 6.7 %collective-permute-start.28 = (bf16[64,512]{1,0:T(8,128)(2,1)S(1)}, bf16[64,512]{1,0:T(8,128)(2,1)S(1)}, u32[]{:S(2)}, u32[]{:S(2)}) collective-permute-start(bf16[64,512]{1,0:T(8,128)(2,1)S(1)} %convert_element_type.75), channel_id=1, source_target_pairs={{0,8},{1,9},{2,10},{3,11},{4,12},{5,13},{6,14},{7,15},{8,0},{9,1},... | collective-permute-start | bytes 196616 | tf_op jit(solution)/shard_map/ppermute | solution.py:33
  92.1 5.7 %collective-permute-start.33 = (bf16[64,512]{1,0:T(8,128)(2,1)S(1)}, bf16[64,512]{1,0:T(8,128)(2,1)S(1)}, u32[]{:S(2)}, u32[]{:S(2)}) collective-permute-start(bf16[64,512]{1,0:T(8,128)(2,1)S(1)} %add_convert_fusion.1), channel_id=1, source_target_pairs={{0,6},{1,7},{2,4},{3,5},{4,2},{5,3},{6,0},{7,1},{8,14},{9,15},{10,... | collective-permute-start | bytes 196616 | tf_op jit(solution)/shard_map/ppermute | solution.py:33
  92.6 5.2 %collective-permute-start.32 = (bf16[64,512]{1,0:T(8,128)(2,1)S(1)}, bf16[64,512]{1,0:T(8,128)(2,1)S(1)}, u32[]{:S(2)}, u32[]{:S(2)}) collective-permute-start(bf16[64,512]{1,0:T(8,128)(2,1)S(1)} %add_convert_fusion.1), channel_id=1, source_target_pairs={{0,2},{1,3},{2,0},{3,1},{4,6},{5,7},{6,4},{7,5},{8,10},{9,11},{10,... | collective-permute-start | bytes 196616 | tf_op jit(solution)/shard_map/ppermute | solution.py:33
  93.8 4.7 %collective-permute-start.31 = (bf16[64,512]{1,0:T(8,128)(2,1)S(1)}, bf16[64,512]{1,0:T(8,128)(2,1)S(1)}, u32[]{:S(2)}, u32[]{:S(2)}) collective-permute-start(bf16[64,512]{1,0:T(8,128)(2,1)S(1)} %add_convert_fusion.1), channel_id=1, source_target_pairs={{0,4},{1,5},{2,6},{3,7},{4,0},{5,1},{6,2},{7,3},{8,12},{9,13},{10,... | collective-permute-start | bytes 196616 | tf_op jit(solution)/shard_map/ppermute | solution.py:33
  98.5 1.6 %collective-permute-start.34 = (bf16[4,64,512]{2,1,0:T(8,128)(2,1)S(1)}, bf16[4,64,512]{2,1,0:T(8,128)(2,1)S(1)}, u32[]{:S(2)}, u32[]{:S(2)}) collective-permute-start(bf16[4,64,512]{2,1,0:T(8,128)(2,1)S(1)} %pad_maximum_fusion.1.mine_ref), channel_id=1, source_target_pairs={{0,1},{1,0},{2,3},{3,2},{4,5},{5,4},{6,7},{7,6},{8,9},{9,8},{10,11... | collective-permute-start | bytes 786440 | tf_op jit(solution)/shard_map/ppermute | solution.py:33

commit v2 on v1

--- a/solution.py
+++ b/solution.py
@@ -69,13 +69,15 @@
     return jax.ShapeDtypeStruct(dims, dtype)
 
 
-def project_kernel(away, at, left_ref, right_ref, other_left_ref, other_right_ref, out_ref):
-    size = other_right_ref.shape[1]
-    across = 1 - at[1] if away else at[1]
-    start = pl.multiple_of((across * 2 + at[0]) * size, size)
-    total = nn(left_ref[...], right_ref[:, pl.ds(start, size)])
-    total += nn(other_left_ref[...], other_right_ref[...])
-    out_ref[...] = total.astype(out_ref.dtype)
+def own_kernel(at, left_ref, right_ref, out_ref):
+    size = out_ref.shape[2]
+    for k, across in enumerate((1 - at[1], at[1])):
+        start = pl.multiple_of((across * 2 + at[0]) * size, size)
+        out_ref[k] = nn(left_ref[...], right_ref[:, pl.ds(start, size)])
+
+
+def project_kernel(k, left_ref, right_ref, part_ref, out_ref):
+    out_ref[...] = (part_ref[k] + nn(left_ref[...], right_ref[...])).astype(out_ref.dtype)
 
 
 def covar_kernel(at, here_ref, there_ref, own_ref, y_ref, x_ref, xy_ref, both, pack):
@@ -115,26 +117,29 @@
     for k in range(4):
         i, j = ax ^ (k >> 1), ay ^ (k & 1)
         place = pl.ds(pl.multiple_of((2 * i + j) * piece, piece), piece)
-        packs[low, place, :] = mine_ref[k].astype(F32)
-        packs[1 - low, place, :] = other_ref[k].astype(F32)
+        packs[low, place, :] = mine_ref[k].astype(F32) * (1.0 / voxels)
+        packs[1 - low, place, :] = other_ref[k].astype(F32) * (1.0 / voxels)
+
+    squares = jnp.zeros((block, block), F32)
 
     def put(i, j, core, k):
         value = packs[core, k * block : (k + 1) * block, :]
         covar[i * block : (i + 1) * block, j * block : (j + 1) * block] = value
-        if i != j:
-            covar[j * block : (j + 1) * block, i * block : (i + 1) * block] = value.T
+        if i == j:
+            return value * value
+        covar[j * block : (j + 1) * block, i * block : (i + 1) * block] = value.T
+        return 2.0 * (value * value)
 
     for core in (0, 1):
         a, b, c = 2 * core, 2 * core + 1, 2 - 2 * core
-        put(a, a, core, 0)
-        put(a, b, core, 1)
-        put(b, b, core, 2)
-        put(b, c, core, 3)
-        put(core, 2 + core, core, 4)
-
-    y = covar[...] / voxels
-    cscale = jnp.sqrt(jnp.sum(y * y) + 1e-06)
-    y = y / cscale
+        squares += put(a, a, core, 0)
+        squares += put(a, b, core, 1)
+        squares += put(b, b, core, 2)
+        squares += put(b, c, core, 3)
+        squares += put(core, 2 + core, core, 4)
+
+    cscale = jnp.sqrt(jnp.sum(squares, keepdims=True) + 1e-06)
+    y = covar[...] * (1.0 / cscale)
     eye = (
         lax.broadcasted_iota(jnp.int32, (rows, rows), 0)
         == lax.broadcasted_iota(jnp.int32, (rows, rows), 1)
@@ -150,27 +155,30 @@
     z3 = 3.375 * eye + 1.5 * rest - 0.5 * (
         5.0625 * left + nn(left.astype(BF), right.astype(BF))
     )
-    out_ref[...] = (z3 / jnp.sqrt(cscale)).astype(BF)
-
-
-def step(weights, block):
-    bent = jnp.tanh(nn(weights.astype(BF), block))
-    pulled = nt(bent.astype(BF), block)
-    return pulled, jnp.sum(1.0 - bent * bent, axis=1, keepdims=True)
+    out_ref[...] = (z3 * lax.rsqrt(cscale)).astype(BF)
+
+
+def step(weights, blocks):
+    low = weights.astype(BF)
+    bents = [jnp.tanh(nn(low, block)) for block in blocks]
+    pulled = nt(bents[0].astype(BF), blocks[0])
+    slopes = 1.0 - bents[0] * bents[0]
+    for bent, block in zip(bents[1:], blocks[1:]):
+        pulled += nt(bent.astype(BF), block)
+        slopes += 1.0 - bent * bent
+    return pulled, jnp.sum(slopes, axis=1, keepdims=True)
 
 
 def apply_kernel(part, whiten_ref, *refs):
     blocks, (weights_ref, white_ref, total_ref, slope_ref) = refs[:4], refs[-4:]
     weights = weights_ref[...]
-    total, slope = refs[4][...] if part else 0.0, refs[5][...] if part else 0.0
-    for k in range(4):
-        white = nn(whiten_ref[...], blocks[k][...]).astype(BF)
+    whites = [nn(whiten_ref[...], block[...]).astype(BF) for block in blocks]
+    for k, white in enumerate(whites):
         white_ref[k] = white
-        pulled, sums = step(weights, white)
-        total += pulled
-        slope += sums
+    total, slope = step(weights, whites)
     if part:
-        total -= slope * weights
+        slope += refs[5][...]
+        total += refs[4][...] - slope * weights
     total_ref[...] = total
     slope_ref[...] = slope
 
@@ -195,9 +203,9 @@
 
     raw = lower[...]
     gram = nt(raw, raw)
-    gscale = jnp.sqrt(jnp.sum(gram * gram) + 1e-06)
-    gram = (gram / gscale).astype(BF)
-    value = (1.5 * raw.astype(F32) - 0.5 * nn(gram, raw)) / jnp.sqrt(gscale)
+    gscale = jnp.sqrt(jnp.sum(gram * gram, keepdims=True) + 1e-06)
+    value = 1.5 * raw.astype(F32) - (0.5 / gscale) * nn(gram.astype(BF), raw)
+    value = value * lax.rsqrt(gscale)
     raw = value.astype(BF)
     gram = nt(raw, raw).astype(BF)
     newer[...] = 1.5 * value - 0.5 * nn(gram, raw)
@@ -221,11 +229,7 @@
                 weights.astype(BF), white[k]
             ).astype(BF)
     else:
-        total, slope = step(weights, white[0])
-        for k in range(1, chunks):
-            pulled, part = step(weights, white[k])
-            total += pulled
-            slope += part
+        total, slope = step(weights, [white[k] for k in range(chunks)])
         outs[0][...] = total - slope * weights
 
 
@@ -241,20 +245,25 @@
     rows = projection.shape[0]
     size = data.shape[1] // comps
 
-    def columns(x):
+    def columns(data, x):
         start = (x * 2 + (1 - at[0])) * size
-        return flip(lax.dynamic_slice_in_dim(data, start, size, 1), low)
+        return lax.dynamic_slice_in_dim(data, start, size, 1)
 
     other = flip(projection, low)
+    away, rest = lax.optimization_barrier((columns(data, 1 - at[1]), data))
+    away, stay = flip(away, low), flip(columns(rest, at[1]), low)
+    part = run(own_kernel, shape((2, rows, size), F32), (at, projection, data))
     sent = run(
-        functools.partial(project_kernel, True),
+        functools.partial(project_kernel, 0),
         shape((rows, size), BF),
-        (at, projection, data, other, columns(1 - at[1])),
+        (other, away, part),
+        specs=[VMEM] * 3,
     )
     kept = run(
-        functools.partial(project_kernel, False),
+        functools.partial(project_kernel, 1),
         shape((rows, size), F32),
-        (at, projection, data, other, columns(at[1])),
+        (other, stay, part),
+        specs=[VMEM] * 3,
     )
     reduced = (kept + flip(sent, across).astype(F32)).astype(BF)
 
@@ -275,15 +284,19 @@
     reduced, own = lax.optimization_barrier((reduced, own))
     at_x, at_y = flip(reduced, across), flip(reduced, near)
     packed = sum_over(own, far).astype(BF)
+    packed, reduced = lax.optimization_barrier((packed, reduced))
+    at_xy = flip(reduced, across | near)
     packed = spread(packed, across, near)
-    packed, reduced, at_x, at_y = lax.optimization_barrier((packed, reduced, at_x, at_y))
-    at_xy = flip(reduced, across | near)
+    mate = flip(packed, low)
+    mate, at_x, at_y = lax.optimization_barrier((mate, at_x, at_y))
+    at_xc, at_yc = flip(at_x, low), flip(at_y, low)
     whiten = run(
         functools.partial(whiten_kernel, voxels),
         shape((rows, rows), BF),
-        (at, packed, flip(packed, low)),
+        (at, packed, mate),
         scratch=[pltpu.VMEM((2, 5 * block, block), F32), pltpu.VMEM((rows, rows), F32)],
     )
+    whiten, at_xy = lax.optimization_barrier((whiten, at_xy))
 
     count = initial.shape[0] // 2
     weights = lax.dynamic_slice_in_dim(initial, at[2] * count, count, 0)
@@ -292,14 +305,14 @@
         shape((count, rows), F32),
         shape((count, 1), F32),
     )
-    blocks = (reduced, there, at_x, flip(at_x, low))
+    blocks = (reduced, there, at_x, at_xc)
     white_here, total, slope = run(
         functools.partial(apply_kernel, False),
         outs,
         (whiten, *blocks, weights),
         specs=[VMEM] * 6,
     )
-    blocks = (at_y, flip(at_y, low), at_xy, flip(at_xy, low))
+    blocks = (at_y, at_yc, at_xy, flip(at_xy, low))
     white_there, newer, _ = run(
         functools.partial(apply_kernel, True),
         outs,

time: 104 us -> 98 us (0.942)
  Pallas kernels: 19.6 us -> 15.7 us
  starting transfers between devices: 38.4 us -> 35 us
    pallas_call x8 -> x9, Pallas kernels: 19.6 us -> 15.7 us  [run(): pl.pallas_call(kernel, out_shape=outs, in_specs=specs or [SMEM] + [VMEM]...]
    ppermute x35, starting transfers between devices: 38.4 us -> 35 us  [flip(): return lax.ppermute(x, AXES, [(i, i ^ mask) for i in range(count)])]
  transfers between devices with their start and end apart: 35 -> 35, of which waited for: 23 -> 24; matrix products, arithmetic and copies ran while one was open for 1% -> 2% of each run, Pallas kernels for 7% -> 6%
where the time goes in v2:
time: 98 us; the launch traced here: 97.8 us
  waiting for transfers between devices  42.8 us (44%)
  starting transfers between devices  35 us (36%)
  Pallas kernels  15.7 us (16%)
  local copies, waits for them, and re-layouts  3 us (3%)
    ppermute x35, waiting for transfers between devices, flip(): return lax.ppermute(x, AXES, [(i, i ^ mask) for i in range(count)])  42.8 us
    ppermute x35, starting transfers between devices, flip(): return lax.ppermute(x, AXES, [(i, i ^ mask) for i in range(count)])  35 us
    pallas_call x9, Pallas kernels, run(): pl.pallas_call(kernel, out_shape=outs, in_specs=specs or [SMEM] + [VMEM]...  15.7 us
  transfers between devices with their start and end apart: 35, of which 24 were waited for; matrix products, arithmetic and copies ran while one was open for 2% of the time, Pallas kernels for 6%

profile of v2, /device:TPU:0, one launch (start us, length us, event | category | flops | bytes accessed | tf_op | source)
XLA Modules:
  0.0 97.8 jit_solution(6004034455953264776)
XLA Ops:
  0.7 0.5 collective-permute-start
  1.2 1.0 constant_dynamic-slice_fusion.2
  2.1 0.2 collective-permute-start.2
  2.4 1.0 constant_dynamic-slice_fusion.1
  3.3 0.4 collective-permute-start.1
  3.8 0.1 pad_add_fusion.at
  3.8 1.0 %copy-done.2 = bf16[512,512]{1,0:T(8,128)(2,1)S(1)} copy-done((bf16[512,512]{1,0:T(8,128)(2,1)S(1)}, bf16[512,512]{1,0:T(8,128)(2,1)}, u32[]{:S(2)}) %copy-start.2) | copy-done | bytes 524312
  4.9 1.0 %shard_map.50.part_ref = f32[2,512,256]{2,1,0:T(8,128)S(1)} custom-call(s32[3]{0:T(128)S(1)} %pad_add_fusion.at, bf16[512,512]{1,0:T(8,128)(2,1)S(1)} %copy-done.2, bf16[512,1024]{1,0:T(8,128)(2,1)S(1)} %copy-done.1), custom_call_target="tpu_custom_call" | custom-call | tf_op jit(solution)/shard_map/pallas_call | solution.py:58
  5.9 0.3 shard_map.52
  6.2 2.7 %collective-permute-start.3 = (bf16[512,256]{1,0:T(8,128)(2,1)S(1)}, bf16[512,256]{1,0:T(8,128)(2,1)S(1)}, u32[]{:S(2)}, u32[]{:S(2)}) collective-permute-start(bf16[512,256]{1,0:T(8,128)(2,1)S(1)} %shard_map.52), channel_id=1, source_target_pairs={{0,2},{1,3},{2,0},{3,1},{4,6},{5,7},{6,4},{7,5},{8,10},{9,11},{10,... | collective-permute-start | bytes 786440 | tf_op jit(solution)/shard_map/ppermute | solution.py:33
  8.9 0.3 shard_map.51
  9.2 6.5 %collective-permute-done.3 = bf16[512,256]{1,0:T(8,128)(2,1)S(1)} collective-permute-done((bf16[512,256]{1,0:T(8,128)(2,1)S(1)}, bf16[512,256]{1,0:T(8,128)(2,1)S(1)}, u32[]{:S(2)}, u32[]{:S(2)}) %collective-permute-start.3) | collective-permute-done | bytes 262176 | tf_op jit(solution)/shard_map/ppermute | solution.py:33
  15.9 1.5 %collective-permute-done.4.there_ref.refs_1_ = bf16[512,256]{1,0:T(8,128)(2,1)S(1)} collective-permute-done((bf16[512,256]{1,0:T(8,128)(2,1)S(1)}, bf16[512,256]{1,0:T(8,128)(2,1)S(1)}, u32[]{:S(2)}, u32[]{:S(2)}) %collective-permute-start.4) | collective-permute-done | bytes 262176 | tf_op jit(solution)/shard_map/ppermute | solution.py:33
  17.4 0.9 shard_map.53
  18.3 1.8 %collective-permute-start.5 = (bf16[160,128]{1,0:T(8,128)(2,1)S(1)}, bf16[160,128]{1,0:T(8,128)(2,1)S(1)}, u32[]{:S(2)}, u32[]{:S(2)}) collective-permute-start(bf16[160,128]{1,0:T(8,128)(2,1)S(1)} %get-tuple-element.25), channel_id=1, source_target_pairs={{0,4},{1,5},{2,6},{3,7},{4,0},{5,1},{6,2},{7,3},{8,12},{9,13},{10,... | collective-permute-start | bytes 122888 | tf_op jit(solution)/shard_map/ppermute | solution.py:33
  20.2 1.5 %collective-permute-start.6 = (bf16[160,128]{1,0:T(8,128)(2,1)S(1)}, bf16[160,128]{1,0:T(8,128)(2,1)S(1)}, u32[]{:S(2)}, u32[]{:S(2)}) collective-permute-start(bf16[160,128]{1,0:T(8,128)(2,1)S(1)} %get-tuple-element.26), channel_id=1, source_target_pairs={{0,2},{1,3},{2,0},{3,1},{4,6},{5,7},{6,4},{7,5},{8,10},{9,11},{10,... | collective-permute-start | bytes 122888 | tf_op jit(solution)/shard_map/ppermute | solution.py:33
  21.7 0.2 collective-permute-start.7
  21.9 0.5 collective-permute-done.5
  22.4 2.2 %collective-permute-done.6 = bf16[160,128]{1,0:T(8,128)(2,1)S(1)} collective-permute-done((bf16[160,128]{1,0:T(8,128)(2,1)S(1)}, bf16[160,128]{1,0:T(8,128)(2,1)S(1)}, u32[]{:S(2)}, u32[]{:S(2)}) %collective-permute-start.6) | collective-permute-done | bytes 40992 | tf_op jit(solution)/shard_map/ppermute | solution.py:33
  24.5 2.0 %collective-permute-done.7 = bf16[160,128]{1,0:T(8,128)(2,1)S(1)} collective-permute-done((bf16[160,128]{1,0:T(8,128)(2,1)S(1)}, bf16[160,128]{1,0:T(8,128)(2,1)S(1)}, u32[]{:S(2)}, u32[]{:S(2)}) %collective-permute-start.7) | collective-permute-done | bytes 40992 | tf_op jit(solution)/shard_map/ppermute | solution.py:33
  26.6 3.7 %collective-permute-start.10 = (bf16[160,128]{1,0:T(8,128)(2,1)S(1)}, bf16[160,128]{1,0:T(8,128)(2,1)S(1)}, u32[]{:S(2)}, u32[]{:S(2)}) collective-permute-start(bf16[160,128]{1,0:T(8,128)(2,1)S(1)} %convert_element_type.65), channel_id=1, source_target_pairs={{0,24},{1,25},{2,26},{3,27},{4,28},{5,29},{6,30},{7,31},{8,16},{9,... | collective-permute-start | bytes 122888 | tf_op jit(solution)/shard_map/ppermute | solution.py:33
  30.3 0.8 collective-permute-start.8
  31.1 1.5 %collective-permute-done.10 = bf16[160,128]{1,0:T(8,128)(2,1)S(1)} collective-permute-done((bf16[160,128]{1,0:T(8,128)(2,1)S(1)}, bf16[160,128]{1,0:T(8,128)(2,1)S(1)}, u32[]{:S(2)}, u32[]{:S(2)}) %collective-permute-start.10) | collective-permute-done | bytes 40992 | tf_op jit(solution)/shard_map/ppermute | solution.py:33
  32.6 2.6 %collective-permute-done.9 = bf16[160,128]{1,0:T(8,128)(2,1)S(1)} collective-permute-done((bf16[160,128]{1,0:T(8,128)(2,1)S(1)}, bf16[160,128]{1,0:T(8,128)(2,1)S(1)}, u32[]{:S(2)}, u32[]{:S(2)}) %collective-permute-start.9) | collective-permute-done | bytes 40992 | tf_op jit(solution)/shard_map/ppermute | solution.py:33
  35.2 0.5 collective-permute-start.13
  35.7 1.5 %collective-permute-start.12 = (bf16[160,128]{1,0:T(8,128)(2,1)S(1)}, bf16[160,128]{1,0:T(8,128)(2,1)S(1)}, u32[]{:S(2)}, u32[]{:S(2)}) collective-permute-start(bf16[160,128]{1,0:T(8,128)(2,1)S(1)} %add_convert_fusion.3), channel_id=1, source_target_pairs={{0,2},{1,3},{2,0},{3,1},{4,6},{5,7},{6,4},{7,5},{8,10},{9,11},{10,... | collective-permute-start | bytes 122888 | tf_op jit(solution)/shard_map/ppermute | solution.py:33
  37.2 1.5 %collective-permute-start.11 = (bf16[160,128]{1,0:T(8,128)(2,1)S(1)}, bf16[160,128]{1,0:T(8,128)(2,1)S(1)}, u32[]{:S(2)}, u32[]{:S(2)}) collective-permute-start(bf16[160,128]{1,0:T(8,128)(2,1)S(1)} %add_convert_fusion.3), channel_id=1, source_target_pairs={{0,4},{1,5},{2,6},{3,7},{4,0},{5,1},{6,2},{7,3},{8,12},{9,13},{10,... | collective-permute-start | bytes 122888 | tf_op jit(solution)/shard_map/ppermute | solution.py:33
  38.8 0.5 collective-permute-start.16
  39.3 0.5 collective-permute-start.15
  39.8 0.7 collective-permute-done.13
  40.5 1.7 %collective-permute-start.17 = (bf16[512,256]{1,0:T(8,128)(2,1)S(1)}, bf16[512,256]{1,0:T(8,128)(2,1)S(1)}, u32[]{:S(2)}, u32[]{:S(2)}) collective-permute-start(bf16[512,256]{1,0:T(8,128)(2,1)S(1)} %add_convert_fusion.here_ref.refs_0_), channel_id=1, source_target_pairs={{0,6},{1,7},{2,4},{3,5},{4,2},{5,3},{6,0},{7,1},{8,14},{9,15},{10,... | collective-permute-start | bytes 786440 | tf_op jit(solution)/shard_map/ppermute | solution.py:33
  42.4 1.4 %collective-permute-done.14.other_ref = bf16[4,160,128]{2,1,0:T(8,128)(2,1)S(1)} collective-permute-done((bf16[4,160,128]{2,1,0:T(8,128)(2,1)S(1)}, bf16[4,160,128]{2,1,0:T(8,128)(2,1)S(1)}, u32[]{:S(2)}, u32[]{:S(2)}) %collective-permute-start.14) | collective-permute-done | bytes 163872 | tf_op jit(solution)/shard_map/ppermute | solution.py:33
  43.7 4.2 %collective-permute-done.16.refs_0_ = bf16[512,256]{1,0:T(8,128)(2,1)S(1)} collective-permute-done((bf16[512,256]{1,0:T(8,128)(2,1)S(1)}, bf16[512,256]{1,0:T(8,128)(2,1)S(1)}, u32[]{:S(2)}, u32[]{:S(2)}) %collective-permute-start.16) | collective-permute-done | bytes 262176 | tf_op jit(solution)/shard_map/ppermute | solution.py:33
  47.9 2.7 %shard_map.54.whiten_ref = bf16[512,512]{1,0:T(8,128)(2,1)S(1)} custom-call(s32[3]{0:T(128)S(1)} %pad_add_fusion.at, bf16[4,160,128]{2,1,0:T(8,128)(2,1)S(1)} %pad_maximum_fusion.2.mine_ref, bf16[4,160,128]{2,1,0:T(8,128)(2,1)S(1)} %collective-permute-done.14.other_ref), custom_call_target="tpu_custom_call" | custom-call | tf_op jit(solution)/shard_map/pallas_call | solution.py:58
  50.7 0.5 collective-permute-start.20
  51.2 0.1 collective-permute-done.17.refs_2_
  51.3 1.3 %collective-permute-done.20.refs_3_ = bf16[512,256]{1,0:T(8,128)(2,1)S(1)} collective-permute-done((bf16[512,256]{1,0:T(8,128)(2,1)S(1)}, bf16[512,256]{1,0:T(8,128)(2,1)S(1)}, u32[]{:S(2)}, u32[]{:S(2)}) %collective-permute-start.20) | collective-permute-done | bytes 262176 | tf_op jit(solution)/shard_map/ppermute | solution.py:33
  52.6 1.2 %shard_map.55 = (bf16[4,512,256]{2,1,0:T(8,128)(2,1)S(1)}, f32[64,512]{1,0:T(8,128)S(1)}, f32[64,1]{1,0:T(8,128)S(1)}) custom-call(bf16[512,512]{1,0:T(8,128)(2,1)S(1)} %shard_map.54.whiten_ref, bf16[512,256]{1,0:T(8,128)(2,1)S(1)} %add_convert_fusion.here_ref.refs_0_, bf16[512,256]{1,0:T(8,128)(2,1)S(1)} %collective-permute-done.4.there_ref.refs_1_, ...), custom_call_target="tpu_custom_call" | custom-call | tf_op jit(solution)/shard_map/pallas_call | solution.py:58
  53.8 1.6 %shard_map.56 = (bf16[4,512,256]{2,1,0:T(8,128)(2,1)S(1)}, f32[64,512]{1,0:T(8,128)S(1)}, f32[64,1]{1,0:T(8,128)}) custom-call(bf16[512,512]{1,0:T(8,128)(2,1)S(1)} %shard_map.54.whiten_ref, bf16[512,256]{1,0:T(8,128)(2,1)S(1)} %collective-permute-done.16.refs_0_, bf16[512,256]{1,0:T(8,128)(2,1)S(1)} %collective-permute-done.18.refs_1_, ...), custom_call_target="tpu_custom_call" | custom-call | tf_op jit(solution)/shard_map/pallas_call | solution.py:58
  55.5 1.5 %collective-permute-start.23 = (bf16[64,512]{1,0:T(8,128)(2,1)S(1)}, bf16[64,512]{1,0:T(8,128)(2,1)S(1)}, u32[]{:S(2)}, u32[]{:S(2)}) collective-permute-start(bf16[64,512]{1,0:T(8,128)(2,1)S(1)} %convert_element_type.70), channel_id=1, source_target_pairs={{0,24},{1,25},{2,26},{3,27},{4,28},{5,29},{6,30},{7,31},{8,16},{9,... | collective-permute-start | bytes 196616 | tf_op jit(solution)/shard_map/ppermute | solution.py:33
  57.0 0.4 collective-permute-start.22
  57.4 2.5 %collective-permute-start.21 = (bf16[64,512]{1,0:T(8,128)(2,1)S(1)}, bf16[64,512]{1,0:T(8,128)(2,1)S(1)}, u32[]{:S(2)}, u32[]{:S(2)}) collective-permute-start(bf16[64,512]{1,0:T(8,128)(2,1)S(1)} %convert_element_type.70), channel_id=1, source_target_pairs={{0,8},{1,9},{2,10},{3,11},{4,12},{5,13},{6,14},{7,15},{8,0},{9,1},... | collective-permute-start | bytes 196616 | tf_op jit(solution)/shard_map/ppermute | solution.py:33
  59.9 2.4 %collective-permute-done.23 = bf16[64,512]{1,0:T(8,128)(2,1)S(1)} collective-permute-done((bf16[64,512]{1,0:T(8,128)(2,1)S(1)}, bf16[64,512]{1,0:T(8,128)(2,1)S(1)}, u32[]{:S(2)}, u32[]{:S(2)}) %collective-permute-start.23) | collective-permute-done | bytes 65568 | tf_op jit(solution)/shard_map/ppermute | solution.py:33
  62.3 2.0 %collective-permute-done.22 = bf16[64,512]{1,0:T(8,128)(2,1)S(1)} collective-permute-done((bf16[64,512]{1,0:T(8,128)(2,1)S(1)}, bf16[64,512]{1,0:T(8,128)(2,1)S(1)}, u32[]{:S(2)}, u32[]{:S(2)}) %collective-permute-start.22) | collective-permute-done | bytes 65568 | tf_op jit(solution)/shard_map/ppermute | solution.py:33
  64.3 1.3 %collective-permute-start.26 = (bf16[64,512]{1,0:T(8,128)(2,1)S(1)}, bf16[64,512]{1,0:T(8,128)(2,1)S(1)}, u32[]{:S(2)}, u32[]{:S(2)}) collective-permute-start(bf16[64,512]{1,0:T(8,128)(2,1)S(1)} %add_convert_fusion.2), channel_id=1, source_target_pairs={{0,6},{1,7},{2,4},{3,5},{4,2},{5,3},{6,0},{7,1},{8,14},{9,15},{10,... | collective-permute-start | bytes 196616 | tf_op jit(solution)/shard_map/ppermute | solution.py:33
  65.6 1.3 %collective-permute-start.25 = (bf16[64,512]{1,0:T(8,128)(2,1)S(1)}, bf16[64,512]{1,0:T(8,128)(2,1)S(1)}, u32[]{:S(2)}, u32[]{:S(2)}) collective-permute-start(bf16[64,512]{1,0:T(8,128)(2,1)S(1)} %add_convert_fusion.2), channel_id=1, source_target_pairs={{0,2},{1,3},{2,0},{3,1},{4,6},{5,7},{6,4},{7,5},{8,10},{9,11},{10,... | collective-permute-start | bytes 196616 | tf_op jit(solution)/shard_map/ppermute | solution.py:33
  66.9 0.9 collective-permute-start.24
  67.9 2.2 %collective-permute-done.26 = bf16[64,512]{1,0:T(8,128)(2,1)S(1)} collective-permute-done((bf16[64,512]{1,0:T(8,128)(2,1)S(1)}, bf16[64,512]{1,0:T(8,128)(2,1)S(1)}, u32[]{:S(2)}, u32[]{:S(2)}) %collective-permute-start.26) | collective-permute-done | bytes 65568 | tf_op jit(solution)/shard_map/ppermute | solution.py:33
  70.1 0.2 collective-permute-done.25
  70.3 0.9 collective-permute-done.24
  71.3 1.5 %collective-permute-done.27.other_ref = bf16[4,64,512]{2,1,0:T(8,128)(2,1)S(1)} collective-permute-done((bf16[4,64,512]{2,1,0:T(8,128)(2,1)S(1)}, bf16[4,64,512]{2,1,0:T(8,128)(2,1)S(1)}, u32[]{:S(2)}, u32[]{:S(2)}) %collective-permute-start.27) | collective-permute-done | bytes 262176 | tf_op jit(solution)/shard_map/ppermute | solution.py:33
  72.8 3.9 %shard_map.57 = f32[64,512]{1,0:T(8,128)S(1)} custom-call(s32[3]{0:T(128)S(1)} %pad_add_fusion.at, bf16[4,64,512]{2,1,0:T(8,128)(2,1)S(1)} %pad_maximum_fusion.mine_ref, bf16[4,64,512]{2,1,0:T(8,128)(2,1)S(1)} %collective-permute-done.27.other_ref, bf16[4,512,256]{2,1,0:T(8,128)(2,1)S(1)} %get-tuple-element.40.refs_0_, ...), custom_call_target="tpu_custom_call" | custom-call | tf_op jit(solution)/shard_map/pallas_call | solution.py:58
  76.8 2.0 %collective-permute-start.30 = (bf16[64,512]{1,0:T(8,128)(2,1)S(1)}, bf16[64,512]{1,0:T(8,128)(2,1)S(1)}, u32[]{:S(2)}, u32[]{:S(2)}) collective-permute-start(bf16[64,512]{1,0:T(8,128)(2,1)S(1)} %convert_element_type.75), channel_id=1, source_target_pairs={{0,24},{1,25},{2,26},{3,27},{4,28},{5,29},{6,30},{7,31},{8,16},{9,... | collective-permute-start | bytes 196616 | tf_op jit(solution)/shard_map/ppermute | solution.py:33
  78.8 2.4 %collective-permute-start.28 = (bf16[64,512]{1,0:T(8,128)(2,1)S(1)}, bf16[64,512]{1,0:T(8,128)(2,1)S(1)}, u32[]{:S(2)}, u32[]{:S(2)}) collective-permute-start(bf16[64,512]{1,0:T(8,128)(2,1)S(1)} %convert_element_type.75), channel_id=1, source_target_pairs={{0,8},{1,9},{2,10},{3,11},{4,12},{5,13},{6,14},{7,15},{8,0},{9,1},... | collective-permute-start | bytes 196616 | tf_op jit(solution)/shard_map/ppermute | solution.py:33
  81.2 2.4 %collective-permute-done.30 = bf16[64,512]{1,0:T(8,128)(2,1)S(1)} collective-permute-done((bf16[64,512]{1,0:T(8,128)(2,1)S(1)}, bf16[64,512]{1,0:T(8,128)(2,1)S(1)}, u32[]{:S(2)}, u32[]{:S(2)}) %collective-permute-start.30) | collective-permute-done | bytes 65568 | tf_op jit(solution)/shard_map/ppermute | solution.py:33
  83.6 2.0 %collective-permute-done.29 = bf16[64,512]{1,0:T(8,128)(2,1)S(1)} collective-permute-done((bf16[64,512]{1,0:T(8,128)(2,1)S(1)}, bf16[64,512]{1,0:T(8,128)(2,1)S(1)}, u32[]{:S(2)}, u32[]{:S(2)}) %collective-permute-start.29) | collective-permute-done | bytes 65568 | tf_op jit(solution)/shard_map/ppermute | solution.py:33
  85.6 0.9 collective-permute-start.33
  86.6 1.5 %collective-permute-start.32 = (bf16[64,512]{1,0:T(8,128)(2,1)S(1)}, bf16[64,512]{1,0:T(8,128)(2,1)S(1)}, u32[]{:S(2)}, u32[]{:S(2)}) collective-permute-start(bf16[64,512]{1,0:T(8,128)(2,1)S(1)} %add_convert_fusion.1), channel_id=1, source_target_pairs={{0,2},{1,3},{2,0},{3,1},{4,6},{5,7},{6,4},{7,5},{8,10},{9,11},{10,... | collective-permute-start | bytes 196616 | tf_op jit(solution)/shard_map/ppermute | solution.py:33
  88.1 1.1 %collective-permute-start.31 = (bf16[64,512]{1,0:T(8,128)(2,1)S(1)}, bf16[64,512]{1,0:T(8,128)(2,1)S(1)}, u32[]{:S(2)}, u32[]{:S(2)}) collective-permute-start(bf16[64,512]{1,0:T(8,128)(2,1)S(1)} %add_convert_fusion.1), channel_id=1, source_target_pairs={{0,4},{1,5},{2,6},{3,7},{4,0},{5,1},{6,2},{7,3},{8,12},{9,13},{10,... | collective-permute-start | bytes 196616 | tf_op jit(solution)/shard_map/ppermute | solution.py:33
  89.2 2.2 %collective-permute-done.33 = bf16[64,512]{1,0:T(8,128)(2,1)S(1)} collective-permute-done((bf16[64,512]{1,0:T(8,128)(2,1)S(1)}, bf16[64,512]{1,0:T(8,128)(2,1)S(1)}, u32[]{:S(2)}, u32[]{:S(2)}) %collective-permute-start.33) | collective-permute-done | bytes 65568 | tf_op jit(solution)/shard_map/ppermute | solution.py:33
  91.3 0.1 collective-permute-done.32
  91.5 0.9 collective-permute-done.31
  92.5 1.5 %collective-permute-done.34.other_ref = bf16[4,64,512]{2,1,0:T(8,128)(2,1)S(1)} collective-permute-done((bf16[4,64,512]{2,1,0:T(8,128)(2,1)S(1)}, bf16[4,64,512]{2,1,0:T(8,128)(2,1)S(1)}, u32[]{:S(2)}, u32[]{:S(2)}) %collective-permute-start.34) | collective-permute-done | bytes 262176 | tf_op jit(solution)/shard_map/ppermute | solution.py:33
  94.0 3.8 %shard_map.58 = (f32[128,512]{1,0:T(8,128)}, bf16[128,1024]{1,0:T(8,128)(2,1)}) custom-call(s32[3]{0:T(128)S(1)} %pad_add_fusion.at, bf16[4,64,512]{2,1,0:T(8,128)(2,1)S(1)} %pad_maximum_fusion.1.mine_ref, bf16[4,64,512]{2,1,0:T(8,128)(2,1)S(1)} %collective-permute-done.34.other_ref, bf16[4,512,256]{2,1,0:T(8,128)(2,1)S(1)} %get-tuple-element.40.refs_0_), custom_call_target="tpu_custom_call" | custom-call | tf_op jit(solution)/shard_map/pallas_call | solution.py:58
  (36 shorter events, 0.7 us)
Async XLA Ops:
  0.6 50.7 %copy-start = (f32[128,512]{1,0:T(8,128)S(1)}, f32[128,512]{1,0:T(8,128)}, u32[]{:S(2)}) copy-start(f32[128,512]{1,0:T(8,128)} %param.5) | copy-start | bytes 786436
  0.6 3.2 %copy-start.1 = (bf16[512,1024]{1,0:T(8,128)(2,1)S(1)}, bf16[512,1024]{1,0:T(8,128)(2,1)}, u32[]{:S(2)}) copy-start(bf16[512,1024]{1,0:T(8,128)(2,1)} %right_ref.1) | copy-start | bytes 3145732
  0.7 5.2 %collective-permute-start = (bf16[512,512]{1,0:T(8,128)(2,1)}, bf16[512,512]{1,0:T(8,128)(2,1)S(1)}, u32[]{:S(2)}, u32[]{:S(2)}) collective-permute-start(bf16[512,512]{1,0:T(8,128)(2,1)} %left_ref.1), channel_id=1, source_target_pairs={{0,1},{1,0},{2,3},{3,2},{4,5},{5,4},{6,7},{7,6},{8,9},{9,8},{10,11... | collective-permute-start | bytes 1572872 | tf_op jit(solution)/shard_map/ppermute | solution.py:33
  2.1 3.7 %collective-permute-start.2 = (bf16[512,256]{1,0:T(8,128)(2,1)S(1)}, bf16[512,256]{1,0:T(8,128)(2,1)S(1)}, u32[]{:S(2)}, u32[]{:S(2)}) collective-permute-start(bf16[512,256]{1,0:T(8,128)(2,1)S(1)} %constant_dynamic-slice_fusion.2), channel_id=1, source_target_pairs={{0,1},{1,0},{2,3},{3,2},{4,5},{5,4},{6,7},{7,6},{8,9},{9,8},{10,11... | collective-permute-start | bytes 786440 | tf_op jit(solution)/shard_map/ppermute | solution.py:33
  3.3 5.5 %collective-permute-start.1 = (bf16[512,256]{1,0:T(8,128)(2,1)S(1)}, bf16[512,256]{1,0:T(8,128)(2,1)S(1)}, u32[]{:S(2)}, u32[]{:S(2)}) collective-permute-start(bf16[512,256]{1,0:T(8,128)(2,1)S(1)} %constant_dynamic-slice_fusion.1), channel_id=1, source_target_pairs={{0,1},{1,0},{2,3},{3,2},{4,5},{5,4},{6,7},{7,6},{8,9},{9,8},{10,11... | collective-permute-start | bytes 786440 | tf_op jit(solution)/shard_map/ppermute | solution.py:33
  3.8 1.0 %copy-start.2 = (bf16[512,512]{1,0:T(8,128)(2,1)S(1)}, bf16[512,512]{1,0:T(8,128)(2,1)}, u32[]{:S(2)}) copy-start(bf16[512,512]{1,0:T(8,128)(2,1)} %left_ref.1) | copy-start | bytes 1572868
  6.2 9.5 %collective-permute-start.3 = (bf16[512,256]{1,0:T(8,128)(2,1)S(1)}, bf16[512,256]{1,0:T(8,128)(2,1)S(1)}, u32[]{:S(2)}, u32[]{:S(2)}) collective-permute-start(bf16[512,256]{1,0:T(8,128)(2,1)S(1)} %shard_map.52), channel_id=1, source_target_pairs={{0,2},{1,3},{2,0},{3,1},{4,6},{5,7},{6,4},{7,5},{8,10},{9,11},{10,... | collective-permute-start | bytes 786440 | tf_op jit(solution)/shard_map/ppermute | solution.py:33
  15.8 1.6 %collective-permute-start.4 = (bf16[512,256]{1,0:T(8,128)(2,1)S(1)}, bf16[512,256]{1,0:T(8,128)(2,1)S(1)}, u32[]{:S(2)}, u32[]{:S(2)}) collective-permute-start(bf16[512,256]{1,0:T(8,128)(2,1)S(1)} %add_convert_fusion.here_ref.refs_0_), channel_id=1, source_target_pairs={{0,1},{1,0},{2,3},{3,2},{4,5},{5,4},{6,7},{7,6},{8,9},{9,8},{10,11... | collective-permute-start | bytes 786440 | tf_op jit(solution)/shard_map/ppermute | solution.py:33
  18.3 4.1 %collective-permute-start.5 = (bf16[160,128]{1,0:T(8,128)(2,1)S(1)}, bf16[160,128]{1,0:T(8,128)(2,1)S(1)}, u32[]{:S(2)}, u32[]{:S(2)}) collective-permute-start(bf16[160,128]{1,0:T(8,128)(2,1)S(1)} %get-tuple-element.25), channel_id=1, source_target_pairs={{0,4},{1,5},{2,6},{3,7},{4,0},{5,1},{6,2},{7,3},{8,12},{9,13},{10,... | collective-permute-start | bytes 122888 | tf_op jit(solution)/shard_map/ppermute | solution.py:33
  20.2 4.4 %collective-permute-start.6 = (bf16[160,128]{1,0:T(8,128)(2,1)S(1)}, bf16[160,128]{1,0:T(8,128)(2,1)S(1)}, u32[]{:S(2)}, u32[]{:S(2)}) collective-permute-start(bf16[160,128]{1,0:T(8,128)(2,1)S(1)} %get-tuple-element.26), channel_id=1, source_target_pairs={{0,2},{1,3},{2,0},{3,1},{4,6},{5,7},{6,4},{7,5},{8,10},{9,11},{10,... | collective-permute-start | bytes 122888 | tf_op jit(solution)/shard_map/ppermute | solution.py:33
  21.7 4.9 %collective-permute-start.7 = (bf16[160,128]{1,0:T(8,128)(2,1)S(1)}, bf16[160,128]{1,0:T(8,128)(2,1)S(1)}, u32[]{:S(2)}, u32[]{:S(2)}) collective-permute-start(bf16[160,128]{1,0:T(8,128)(2,1)S(1)} %get-tuple-element.27), channel_id=1, source_target_pairs={{0,6},{1,7},{2,4},{3,5},{4,2},{5,3},{6,0},{7,1},{8,14},{9,15},{10,... | collective-permute-start | bytes 122888 | tf_op jit(solution)/shard_map/ppermute | solution.py:33
  26.6 6.0 %collective-permute-start.10 = (bf16[160,128]{1,0:T(8,128)(2,1)S(1)}, bf16[160,128]{1,0:T(8,128)(2,1)S(1)}, u32[]{:S(2)}, u32[]{:S(2)}) collective-permute-start(bf16[160,128]{1,0:T(8,128)(2,1)S(1)} %convert_element_type.65), channel_id=1, source_target_pairs={{0,24},{1,25},{2,26},{3,27},{4,28},{5,29},{6,30},{7,31},{8,16},{9,... | collective-permute-start | bytes 122888 | tf_op jit(solution)/shard_map/ppermute | solution.py:33
  30.3 4.9 %collective-permute-start.9 = (bf16[160,128]{1,0:T(8,128)(2,1)S(1)}, bf16[160,128]{1,0:T(8,128)(2,1)S(1)}, u32[]{:S(2)}, u32[]{:S(2)}) collective-permute-start(bf16[160,128]{1,0:T(8,128)(2,1)S(1)} %convert_element_type.65), channel_id=1, source_target_pairs={{0,16},{1,17},{2,18},{3,19},{4,20},{5,21},{6,22},{7,23},{8,24},{9,... | collective-permute-start | bytes 122888 | tf_op jit(solution)/shard_map/ppermute | solution.py:33
  30.3 4.9 %collective-permute-start.8 = (bf16[160,128]{1,0:T(8,128)(2,1)S(1)}, bf16[160,128]{1,0:T(8,128)(2,1)S(1)}, u32[]{:S(2)}, u32[]{:S(2)}) collective-permute-start(bf16[160,128]{1,0:T(8,128)(2,1)S(1)} %convert_element_type.65), channel_id=1, source_target_pairs={{0,8},{1,9},{2,10},{3,11},{4,12},{5,13},{6,14},{7,15},{8,0},{9,1},... | collective-permute-start | bytes 122888 | tf_op jit(solution)/shard_map/ppermute | solution.py:33
  35.2 5.3 %collective-permute-start.13 = (bf16[160,128]{1,0:T(8,128)(2,1)S(1)}, bf16[160,128]{1,0:T(8,128)(2,1)S(1)}, u32[]{:S(2)}, u32[]{:S(2)}) collective-permute-start(bf16[160,128]{1,0:T(8,128)(2,1)S(1)} %add_convert_fusion.3), channel_id=1, source_target_pairs={{0,6},{1,7},{2,4},{3,5},{4,2},{5,3},{6,0},{7,1},{8,14},{9,15},{10,... | collective-permute-start | bytes 122888 | tf_op jit(solution)/shard_map/ppermute | solution.py:33
  35.7 6.5 %collective-permute-start.12 = (bf16[160,128]{1,0:T(8,128)(2,1)S(1)}, bf16[160,128]{1,0:T(8,128)(2,1)S(1)}, u32[]{:S(2)}, u32[]{:S(2)}) collective-permute-start(bf16[160,128]{1,0:T(8,128)(2,1)S(1)} %add_convert_fusion.3), channel_id=1, source_target_pairs={{0,2},{1,3},{2,0},{3,1},{4,6},{5,7},{6,4},{7,5},{8,10},{9,11},{10,... | collective-permute-start | bytes 122888 | tf_op jit(solution)/shard_map/ppermute | solution.py:33
  37.2 5.0 %collective-permute-start.11 = (bf16[160,128]{1,0:T(8,128)(2,1)S(1)}, bf16[160,128]{1,0:T(8,128)(2,1)S(1)}, u32[]{:S(2)}, u32[]{:S(2)}) collective-permute-start(bf16[160,128]{1,0:T(8,128)(2,1)S(1)} %add_convert_fusion.3), channel_id=1, source_target_pairs={{0,4},{1,5},{2,6},{3,7},{4,0},{5,1},{6,2},{7,3},{8,12},{9,13},{10,... | collective-permute-start | bytes 122888 | tf_op jit(solution)/shard_map/ppermute | solution.py:33
  38.8 9.2 %collective-permute-start.16 = (bf16[512,256]{1,0:T(8,128)(2,1)S(1)}, bf16[512,256]{1,0:T(8,128)(2,1)S(1)}, u32[]{:S(2)}, u32[]{:S(2)}) collective-permute-start(bf16[512,256]{1,0:T(8,128)(2,1)S(1)} %add_convert_fusion.here_ref.refs_0_), channel_id=1, source_target_pairs={{0,4},{1,5},{2,6},{3,7},{4,0},{5,1},{6,2},{7,3},{8,12},{9,13},{10,... | collective-permute-start | bytes 786440 | tf_op jit(solution)/shard_map/ppermute | solution.py:33
  39.3 8.7 %collective-permute-start.15 = (bf16[512,256]{1,0:T(8,128)(2,1)S(1)}, bf16[512,256]{1,0:T(8,128)(2,1)S(1)}, u32[]{:S(2)}, u32[]{:S(2)}) collective-permute-start(bf16[512,256]{1,0:T(8,128)(2,1)S(1)} %add_convert_fusion.here_ref.refs_0_), channel_id=1, source_target_pairs={{0,2},{1,3},{2,0},{3,1},{4,6},{5,7},{6,4},{7,5},{8,10},{9,11},{10,... | collective-permute-start | bytes 786440 | tf_op jit(solution)/shard_map/ppermute | solution.py:33
  40.5 10.7 %collective-permute-start.17 = (bf16[512,256]{1,0:T(8,128)(2,1)S(1)}, bf16[512,256]{1,0:T(8,128)(2,1)S(1)}, u32[]{:S(2)}, u32[]{:S(2)}) collective-permute-start(bf16[512,256]{1,0:T(8,128)(2,1)S(1)} %add_convert_fusion.here_ref.refs_0_), channel_id=1, source_target_pairs={{0,6},{1,7},{2,4},{3,5},{4,2},{5,3},{6,0},{7,1},{8,14},{9,15},{10,... | collective-permute-start | bytes 786440 | tf_op jit(solution)/shard_map/ppermute | solution.py:33
  42.3 1.5 %collective-permute-start.14 = (bf16[4,160,128]{2,1,0:T(8,128)(2,1)S(1)}, bf16[4,160,128]{2,1,0:T(8,128)(2,1)S(1)}, u32[]{:S(2)}, u32[]{:S(2)}) collective-permute-start(bf16[4,160,128]{2,1,0:T(8,128)(2,1)S(1)} %pad_maximum_fusion.2.mine_ref), channel_id=1, source_target_pairs={{0,1},{1,0},{2,3},{3,2},{4,5},{5,4},{6,7},{7,6},{8,9},{9,8},{10,11... | collective-permute-start | bytes 491528 | tf_op jit(solution)/shard_map/ppermute | solution.py:33
  50.6 3.2 %collective-permute-start.18 = (bf16[512,256]{1,0:T(8,128)(2,1)S(1)}, bf16[512,256]{1,0:T(8,128)(2,1)S(1)}, u32[]{:S(2)}, u32[]{:S(2)}) collective-permute-start(bf16[512,256]{1,0:T(8,128)(2,1)S(1)} %collective-permute-done.16.refs_0_), channel_id=1, source_target_pairs={{0,1},{1,0},{2,3},{3,2},{4,5},{5,4},{6,7},{7,6},{8,9},{9,8},{10,11... | collective-permute-start | bytes 786440 | tf_op jit(solution)/shard_map/ppermute | solution.py:33
  50.7 1.9 %collective-permute-start.20 = (bf16[512,256]{1,0:T(8,128)(2,1)S(1)}, bf16[512,256]{1,0:T(8,128)(2,1)S(1)}, u32[]{:S(2)}, u32[]{:S(2)}) collective-permute-start(bf16[512,256]{1,0:T(8,128)(2,1)S(1)} %collective-permute-done.15.refs_2_), channel_id=1, source_target_pairs={{0,1},{1,0},{2,3},{3,2},{4,5},{5,4},{6,7},{7,6},{8,9},{9,8},{10,11... | collective-permute-start | bytes 786440 | tf_op jit(solution)/shard_map/ppermute | solution.py:33
  51.3 2.5 %collective-permute-start.19 = (bf16[512,256]{1,0:T(8,128)(2,1)S(1)}, bf16[512,256]{1,0:T(8,128)(2,1)S(1)}, u32[]{:S(2)}, u32[]{:S(2)}) collective-permute-start(bf16[512,256]{1,0:T(8,128)(2,1)S(1)} %collective-permute-done.17.refs_2_), channel_id=1, source_target_pairs={{0,1},{1,0},{2,3},{3,2},{4,5},{5,4},{6,7},{7,6},{8,9},{9,8},{10,11... | collective-permute-start | bytes 786440 | tf_op jit(solution)/shard_map/ppermute | solution.py:33
  55.5 6.8 %collective-permute-start.23 = (bf16[64,512]{1,0:T(8,128)(2,1)S(1)}, bf16[64,512]{1,0:T(8,128)(2,1)S(1)}, u32[]{:S(2)}, u32[]{:S(2)}) collective-permute-start(bf16[64,512]{1,0:T(8,128)(2,1)S(1)} %convert_element_type.70), channel_id=1, source_target_pairs={{0,24},{1,25},{2,26},{3,27},{4,28},{5,29},{6,30},{7,31},{8,16},{9,... | collective-permute-start | bytes 196616 | tf_op jit(solution)/shard_map/ppermute | solution.py:33
  57.0 7.3 %collective-permute-start.22 = (bf16[64,512]{1,0:T(8,128)(2,1)S(1)}, bf16[64,512]{1,0:T(8,128)(2,1)S(1)}, u32[]{:S(2)}, u32[]{:S(2)}) collective-permute-start(bf16[64,512]{1,0:T(8,128)(2,1)S(1)} %convert_element_type.70), channel_id=1, source_target_pairs={{0,16},{1,17},{2,18},{3,19},{4,20},{5,21},{6,22},{7,23},{8,24},{9,... | collective-permute-start | bytes 196616 | tf_op jit(solution)/shard_map/ppermute | solution.py:33
  57.4 6.9 %collective-permute-start.21 = (bf16[64,512]{1,0:T(8,128)(2,1)S(1)}, bf16[64,512]{1,0:T(8,128)(2,1)S(1)}, u32[]{:S(2)}, u32[]{:S(2)}) collective-permute-start(bf16[64,512]{1,0:T(8,128)(2,1)S(1)} %convert_element_type.70), channel_id=1, source_target_pairs={{0,8},{1,9},{2,10},{3,11},{4,12},{5,13},{6,14},{7,15},{8,0},{9,1},... | collective-permute-start | bytes 196616 | tf_op jit(solution)/shard_map/ppermute | solution.py:33
  64.3 5.8 %collective-permute-start.26 = (bf16[64,512]{1,0:T(8,128)(2,1)S(1)}, bf16[64,512]{1,0:T(8,128)(2,1)S(1)}, u32[]{:S(2)}, u32[]{:S(2)}) collective-permute-start(bf16[64,512]{1,0:T(8,128)(2,1)S(1)} %add_convert_fusion.2), channel_id=1, source_target_pairs={{0,6},{1,7},{2,4},{3,5},{4,2},{5,3},{6,0},{7,1},{8,14},{9,15},{10,... | collective-permute-start | bytes 196616 | tf_op jit(solution)/shard_map/ppermute | solution.py:33
  65.6 4.7 %collective-permute-start.25 = (bf16[64,512]{1,0:T(8,128)(2,1)S(1)}, bf16[64,512]{1,0:T(8,128)(2,1)S(1)}, u32[]{:S(2)}, u32[]{:S(2)}) collective-permute-start(bf16[64,512]{1,0:T(8,128)(2,1)S(1)} %add_convert_fusion.2), channel_id=1, source_target_pairs={{0,2},{1,3},{2,0},{3,1},{4,6},{5,7},{6,4},{7,5},{8,10},{9,11},{10,... | collective-permute-start | bytes 196616 | tf_op jit(solution)/shard_map/ppermute | solution.py:33
  66.9 4.3 %collective-permute-start.24 = (bf16[64,512]{1,0:T(8,128)(2,1)S(1)}, bf16[64,512]{1,0:T(8,128)(2,1)S(1)}, u32[]{:S(2)}, u32[]{:S(2)}) collective-permute-start(bf16[64,512]{1,0:T(8,128)(2,1)S(1)} %add_convert_fusion.2), channel_id=1, source_target_pairs={{0,4},{1,5},{2,6},{3,7},{4,0},{5,1},{6,2},{7,3},{8,12},{9,13},{10,... | collective-permute-start | bytes 196616 | tf_op jit(solution)/shard_map/ppermute | solution.py:33
  71.2 1.6 %collective-permute-start.27 = (bf16[4,64,512]{2,1,0:T(8,128)(2,1)S(1)}, bf16[4,64,512]{2,1,0:T(8,128)(2,1)S(1)}, u32[]{:S(2)}, u32[]{:S(2)}) collective-permute-start(bf16[4,64,512]{2,1,0:T(8,128)(2,1)S(1)} %pad_maximum_fusion.mine_ref), channel_id=1, source_target_pairs={{0,1},{1,0},{2,3},{3,2},{4,5},{5,4},{6,7},{7,6},{8,9},{9,8},{10,11... | collective-permute-start | bytes 786440 | tf_op jit(solution)/shard_map/ppermute | solution.py:33
  76.8 6.8 %collective-permute-start.30 = (bf16[64,512]{1,0:T(8,128)(2,1)S(1)}, bf16[64,512]{1,0:T(8,128)(2,1)S(1)}, u32[]{:S(2)}, u32[]{:S(2)}) collective-permute-start(bf16[64,512]{1,0:T(8,128)(2,1)S(1)} %convert_element_type.75), channel_id=1, source_target_pairs={{0,24},{1,25},{2,26},{3,27},{4,28},{5,29},{6,30},{7,31},{8,16},{9,... | collective-permute-start | bytes 196616 | tf_op jit(solution)/shard_map/ppermute | solution.py:33
  78.8 6.8 %collective-permute-start.29 = (bf16[64,512]{1,0:T(8,128)(2,1)S(1)}, bf16[64,512]{1,0:T(8,128)(2,1)S(1)}, u32[]{:S(2)}, u32[]{:S(2)}) collective-permute-start(bf16[64,512]{1,0:T(8,128)(2,1)S(1)} %convert_element_type.75), channel_id=1, source_target_pairs={{0,16},{1,17},{2,18},{3,19},{4,20},{5,21},{6,22},{7,23},{8,24},{9,... | collective-permute-start | bytes 196616 | tf_op jit(solution)/shard_map/ppermute | solution.py:33
  78.8 6.8 %collective-permute-start.28 = (bf16[64,512]{1,0:T(8,128)(2,1)S(1)}, bf16[64,512]{1,0:T(8,128)(2,1)S(1)}, u32[]{:S(2)}, u32[]{:S(2)}) collective-permute-start(bf16[64,512]{1,0:T(8,128)(2,1)S(1)} %convert_element_type.75), channel_id=1, source_target_pairs={{0,8},{1,9},{2,10},{3,11},{4,12},{5,13},{6,14},{7,15},{8,0},{9,1},... | collective-permute-start | bytes 196616 | tf_op jit(solution)/shard_map/ppermute | solution.py:33
  85.6 5.7 %collective-permute-start.33 = (bf16[64,512]{1,0:T(8,128)(2,1)S(1)}, bf16[64,512]{1,0:T(8,128)(2,1)S(1)}, u32[]{:S(2)}, u32[]{:S(2)}) collective-permute-start(bf16[64,512]{1,0:T(8,128)(2,1)S(1)} %add_convert_fusion.1), channel_id=1, source_target_pairs={{0,6},{1,7},{2,4},{3,5},{4,2},{5,3},{6,0},{7,1},{8,14},{9,15},{10,... | collective-permute-start | bytes 196616 | tf_op jit(solution)/shard_map/ppermute | solution.py:33
  86.6 4.9 %collective-permute-start.32 = (bf16[64,512]{1,0:T(8,128)(2,1)S(1)}, bf16[64,512]{1,0:T(8,128)(2,1)S(1)}, u32[]{:S(2)}, u32[]{:S(2)}) collective-permute-start(bf16[64,512]{1,0:T(8,128)(2,1)S(1)} %add_convert_fusion.1), channel_id=1, source_target_pairs={{0,2},{1,3},{2,0},{3,1},{4,6},{5,7},{6,4},{7,5},{8,10},{9,11},{10,... | collective-permute-start | bytes 196616 | tf_op jit(solution)/shard_map/ppermute | solution.py:33
  88.1 4.3 %collective-permute-start.31 = (bf16[64,512]{1,0:T(8,128)(2,1)S(1)}, bf16[64,512]{1,0:T(8,128)(2,1)S(1)}, u32[]{:S(2)}, u32[]{:S(2)}) collective-permute-start(bf16[64,512]{1,0:T(8,128)(2,1)S(1)} %add_convert_fusion.1), channel_id=1, source_target_pairs={{0,4},{1,5},{2,6},{3,7},{4,0},{5,1},{6,2},{7,3},{8,12},{9,13},{10,... | collective-permute-start | bytes 196616 | tf_op jit(solution)/shard_map/ppermute | solution.py:33
  92.4 1.6 %collective-permute-start.34 = (bf16[4,64,512]{2,1,0:T(8,128)(2,1)S(1)}, bf16[4,64,512]{2,1,0:T(8,128)(2,1)S(1)}, u32[]{:S(2)}, u32[]{:S(2)}) collective-permute-start(bf16[4,64,512]{2,1,0:T(8,128)(2,1)S(1)} %pad_maximum_fusion.1.mine_ref), channel_id=1, source_target_pairs={{0,1},{1,0},{2,3},{3,2},{4,5},{5,4},{6,7},{7,6},{8,9},{9,8},{10,11... | collective-permute-start | bytes 786440 | tf_op jit(solution)/shard_map/ppermute | solution.py:33

commit v3 on v2

--- a/solution.py
+++ b/solution.py
@@ -184,14 +184,18 @@
 
 
 def decor_kernel(last, at, mine_ref, other_ref, *refs):
-    sources = 1 if last else 2
-    whites, outs, (newer, lower, white, sem) = refs[:sources], refs[sources:-4], refs[-4:]
+    whites, outs, (newer, lower, white, sem) = refs[:2], refs[2:-4], refs[-4:]
     count = mine_ref.shape[1]
     low, ax, ay = at[0], at[1], at[2]
     chunks = white.shape[0]
+    first = 3 if last else 4
     copies = [
-        pltpu.make_async_copy(ref, white.at[pl.ds(4 * k, 4)], sem.at[k])
-        for k, ref in enumerate(whites)
+        pltpu.make_async_copy(
+            ref.at[pl.ds(0, size)], white.at[pl.ds(start, size)], sem.at[k]
+        )
+        for k, (ref, start, size) in enumerate(
+            zip(whites, (0, first), (first, chunks - first))
+        )
     ]
     for copy in copies:
         copy.start()
@@ -245,13 +249,12 @@
     rows = projection.shape[0]
     size = data.shape[1] // comps
 
-    def columns(data, x):
+    def columns(x):
         start = (x * 2 + (1 - at[0])) * size
-        return lax.dynamic_slice_in_dim(data, start, size, 1)
+        return flip(lax.dynamic_slice_in_dim(data, start, size, 1), low)
 
     other = flip(projection, low)
-    away, rest = lax.optimization_barrier((columns(data, 1 - at[1]), data))
-    away, stay = flip(away, low), flip(columns(rest, at[1]), low)
+    away, stay = columns(1 - at[1]), columns(at[1])
     part = run(own_kernel, shape((2, rows, size), F32), (at, projection, data))
     sent = run(
         functools.partial(project_kernel, 0),
@@ -287,9 +290,8 @@
     packed, reduced = lax.optimization_barrier((packed, reduced))
     at_xy = flip(reduced, across | near)
     packed = spread(packed, across, near)
+    packed, at_x, at_y = lax.optimization_barrier((packed, at_x, at_y))
     mate = flip(packed, low)
-    mate, at_x, at_y = lax.optimization_barrier((mate, at_x, at_y))
-    at_xc, at_yc = flip(at_x, low), flip(at_y, low)
     whiten = run(
         functools.partial(whiten_kernel, voxels),
         shape((rows, rows), BF),
@@ -305,14 +307,14 @@
         shape((count, rows), F32),
         shape((count, 1), F32),
     )
-    blocks = (reduced, there, at_x, at_xc)
+    blocks = (reduced, there, at_x, at_y)
     white_here, total, slope = run(
         functools.partial(apply_kernel, False),
         outs,
         (whiten, *blocks, weights),
         specs=[VMEM] * 6,
     )
-    blocks = (at_y, at_yc, at_xy, flip(at_xy, low))
+    blocks = (flip(at_x, low), flip(at_y, low), at_xy, flip(at_xy, low))
     white_there, newer, _ = run(
         functools.partial(apply_kernel, True),
         outs,
@@ -324,7 +326,7 @@
     for turn in range(ICA_ITERS):
         last = turn == ICA_ITERS - 1
         stacked = spread(sum_over(newer, far).astype(BF), across, near)
-        used = whites[:1] if last else whites
+        chunks = 4 if last else 8
         outs = (
             (shape((2 * count, rows), F32), shape((2 * count, data.shape[1]), BF))
             if last
@@ -333,12 +335,12 @@
         newer = run(
             functools.partial(decor_kernel, last),
             outs,
-            (at, stacked, flip(stacked, low), *used),
-            specs=[SMEM, VMEM, VMEM] + [ANY] * len(used),
+            (at, stacked, flip(stacked, low), *whites),
+            specs=[SMEM, VMEM, VMEM] + [ANY] * 2,
             scratch=[
                 pltpu.VMEM((rows, rows), F32),
                 pltpu.VMEM((rows, rows), BF),
-                pltpu.VMEM((4 * len(used), rows, size), BF),
+                pltpu.VMEM((chunks, rows, size), BF),
                 pltpu.SemaphoreType.DMA((2,)),
             ],
         )

time: 98 us -> 92.9 us (0.948)
  waiting for transfers between devices: 42.8 us -> 39.8 us
  starting transfers between devices: 35 us -> 33.9 us
    ppermute x35, waiting for transfers between devices: 42.8 us -> 39.8 us  [flip(): return lax.ppermute(x, AXES, [(i, i ^ mask) for i in range(count)])]
    ppermute x35, starting transfers between devices: 35 us -> 33.9 us  [flip(): return lax.ppermute(x, AXES, [(i, i ^ mask) for i in range(count)])]
  transfers between devices with their start and end apart: 35 -> 35, of which waited for: 24 -> 22; matrix products, arithmetic and copies ran while one was open for 2% -> 1% of each run, Pallas kernels for 6% -> 6%
where the time goes in v3:
time: 92.9 us; the launch traced here: 92.8 us
  waiting for transfers between devices  39.8 us (43%)
  starting transfers between devices  33.9 us (36%)
  Pallas kernels  15.7 us (17%)
  local copies, waits for them, and re-layouts  2.13 us (2%)
    ppermute x35, waiting for transfers between devices, flip(): return lax.ppermute(x, AXES, [(i, i ^ mask) for i in range(count)])  39.8 us
    ppermute x35, starting transfers between devices, flip(): return lax.ppermute(x, AXES, [(i, i ^ mask) for i in range(count)])  33.9 us
    pallas_call x9, Pallas kernels, run(): pl.pallas_call(kernel, out_shape=outs, in_specs=specs or [SMEM] + [VMEM]...  15.7 us
  transfers between devices with their start and end apart: 35, of which 22 were waited for; matrix products, arithmetic and copies ran while one was open for 1% of the time, Pallas kernels for 6%

profile of v3, /device:TPU:0, one launch (start us, length us, event | category | flops | bytes accessed | tf_op | source)
XLA Modules:
  0.0 92.8 jit_solution(7757809057321506281)
XLA Ops:
  0.7 0.5 collective-permute-start
  1.2 1.1 %constant_dynamic-slice_fusion.1 = (bf16[512,256]{1,0:T(8,128)(2,1)S(1)}, bf16[512,256]{1,0:T(8,128)(2,1)S(1)}) fusion(bf16[512,1024]{1,0:T(8,128)(2,1)} %right_ref.1, s32[]{:T(128)S(6)} %select_n.10, s32[]{:T(128)S(6)} %select_n.9), kind=kLoop, calls=%fused_computation.9 | loop fusion | bytes 1048584 | tf_op jit(solution)/shard_map/dynamic_slice | solution.py:254
  2.2 0.2 collective-permute-start.2
  2.5 0.3 collective-permute-start.1
  2.8 0.1 pad_add_fusion.at
  2.9 1.0 %copy-done.2 = bf16[512,512]{1,0:T(8,128)(2,1)S(1)} copy-done((bf16[512,512]{1,0:T(8,128)(2,1)S(1)}, bf16[512,512]{1,0:T(8,128)(2,1)}, u32[]{:S(2)}) %copy-start.2) | copy-done | bytes 524312
  3.9 1.0 %shard_map.50.part_ref = f32[2,512,256]{2,1,0:T(8,128)S(1)} custom-call(s32[3]{0:T(128)S(1)} %pad_add_fusion.at, bf16[512,512]{1,0:T(8,128)(2,1)S(1)} %copy-done.2, bf16[512,1024]{1,0:T(8,128)(2,1)S(1)} %copy-done.1), custom_call_target="tpu_custom_call" | custom-call | tf_op jit(solution)/shard_map/pallas_call | solution.py:58
  5.0 0.3 shard_map.52
  5.3 2.7 %collective-permute-start.3 = (bf16[512,256]{1,0:T(8,128)(2,1)S(1)}, bf16[512,256]{1,0:T(8,128)(2,1)S(1)}, u32[]{:S(2)}, u32[]{:S(2)}) collective-permute-start(bf16[512,256]{1,0:T(8,128)(2,1)S(1)} %shard_map.52), channel_id=1, source_target_pairs={{0,2},{1,3},{2,0},{3,1},{4,6},{5,7},{6,4},{7,5},{8,10},{9,11},{10,... | collective-permute-start | bytes 786440 | tf_op jit(solution)/shard_map/ppermute | solution.py:33
  8.0 0.3 shard_map.51
  8.3 6.5 %collective-permute-done.3 = bf16[512,256]{1,0:T(8,128)(2,1)S(1)} collective-permute-done((bf16[512,256]{1,0:T(8,128)(2,1)S(1)}, bf16[512,256]{1,0:T(8,128)(2,1)S(1)}, u32[]{:S(2)}, u32[]{:S(2)}) %collective-permute-start.3) | collective-permute-done | bytes 262176 | tf_op jit(solution)/shard_map/ppermute | solution.py:33
  14.8 0.1 collective-permute-start.4
  14.9 1.5 %collective-permute-done.4.there_ref.refs_1_ = bf16[512,256]{1,0:T(8,128)(2,1)S(1)} collective-permute-done((bf16[512,256]{1,0:T(8,128)(2,1)S(1)}, bf16[512,256]{1,0:T(8,128)(2,1)S(1)}, u32[]{:S(2)}, u32[]{:S(2)}) %collective-permute-start.4) | collective-permute-done | bytes 262176 | tf_op jit(solution)/shard_map/ppermute | solution.py:33
  16.4 0.9 %shard_map.53 = (f32[160,128]{1,0:T(8,128)S(1)}, bf16[160,128]{1,0:T(8,128)(2,1)S(1)}, bf16[160,128]{1,0:T(8,128)(2,1)S(1)}, bf16[160,128]{1,0:T(8,128)(2,1)S(1)}) custom-call(s32[3]{0:T(128)S(1)} %pad_add_fusion.at, bf16[512,256]{1,0:T(8,128)(2,1)S(1)} %add_convert_fusion.here_ref.refs_0_, bf16[512,256]{1,0:T(8,128)(2,1)S(1)} %collective-permute-done.4.there_ref.refs_1_), custom_call_target="tpu_custom_call" | custom-call | tf_op jit(solution)/shard_map/pallas_call | solution.py:58
  17.4 1.8 %collective-permute-start.5 = (bf16[160,128]{1,0:T(8,128)(2,1)S(1)}, bf16[160,128]{1,0:T(8,128)(2,1)S(1)}, u32[]{:S(2)}, u32[]{:S(2)}) collective-permute-start(bf16[160,128]{1,0:T(8,128)(2,1)S(1)} %get-tuple-element.21), channel_id=1, source_target_pairs={{0,4},{1,5},{2,6},{3,7},{4,0},{5,1},{6,2},{7,3},{8,12},{9,13},{10,... | collective-permute-start | bytes 122888 | tf_op jit(solution)/shard_map/ppermute | solution.py:33
  19.2 1.5 %collective-permute-start.6 = (bf16[160,128]{1,0:T(8,128)(2,1)S(1)}, bf16[160,128]{1,0:T(8,128)(2,1)S(1)}, u32[]{:S(2)}, u32[]{:S(2)}) collective-permute-start(bf16[160,128]{1,0:T(8,128)(2,1)S(1)} %get-tuple-element.22), channel_id=1, source_target_pairs={{0,2},{1,3},{2,0},{3,1},{4,6},{5,7},{6,4},{7,5},{8,10},{9,11},{10,... | collective-permute-start | bytes 122888 | tf_op jit(solution)/shard_map/ppermute | solution.py:33
  20.7 0.2 collective-permute-start.7
  20.9 0.5 collective-permute-done.5
  21.4 2.2 %collective-permute-done.6 = bf16[160,128]{1,0:T(8,128)(2,1)S(1)} collective-permute-done((bf16[160,128]{1,0:T(8,128)(2,1)S(1)}, bf16[160,128]{1,0:T(8,128)(2,1)S(1)}, u32[]{:S(2)}, u32[]{:S(2)}) %collective-permute-start.6) | collective-permute-done | bytes 40992 | tf_op jit(solution)/shard_map/ppermute | solution.py:33
  23.6 2.0 %collective-permute-done.7 = bf16[160,128]{1,0:T(8,128)(2,1)S(1)} collective-permute-done((bf16[160,128]{1,0:T(8,128)(2,1)S(1)}, bf16[160,128]{1,0:T(8,128)(2,1)S(1)}, u32[]{:S(2)}, u32[]{:S(2)}) %collective-permute-start.7) | collective-permute-done | bytes 40992 | tf_op jit(solution)/shard_map/ppermute | solution.py:33
  25.7 3.7 %collective-permute-start.10 = (bf16[160,128]{1,0:T(8,128)(2,1)S(1)}, bf16[160,128]{1,0:T(8,128)(2,1)S(1)}, u32[]{:S(2)}, u32[]{:S(2)}) collective-permute-start(bf16[160,128]{1,0:T(8,128)(2,1)S(1)} %convert_element_type.65), channel_id=1, source_target_pairs={{0,24},{1,25},{2,26},{3,27},{4,28},{5,29},{6,30},{7,31},{8,16},{9,... | collective-permute-start | bytes 122888 | tf_op jit(solution)/shard_map/ppermute | solution.py:33
  29.3 0.8 collective-permute-start.8
  30.1 0.5 collective-permute-start.15
  30.6 0.5 collective-permute-start.14
  31.1 0.5 collective-permute-done.10
  31.6 2.6 %collective-permute-done.9 = bf16[160,128]{1,0:T(8,128)(2,1)S(1)} collective-permute-done((bf16[160,128]{1,0:T(8,128)(2,1)S(1)}, bf16[160,128]{1,0:T(8,128)(2,1)S(1)}, u32[]{:S(2)}, u32[]{:S(2)}) %collective-permute-start.9) | collective-permute-done | bytes 40992 | tf_op jit(solution)/shard_map/ppermute | solution.py:33
  34.3 0.5 collective-permute-start.13
  34.8 1.5 %collective-permute-start.12 = (bf16[160,128]{1,0:T(8,128)(2,1)S(1)}, bf16[160,128]{1,0:T(8,128)(2,1)S(1)}, u32[]{:S(2)}, u32[]{:S(2)}) collective-permute-start(bf16[160,128]{1,0:T(8,128)(2,1)S(1)} %add_convert_fusion.3), channel_id=1, source_target_pairs={{0,2},{1,3},{2,0},{3,1},{4,6},{5,7},{6,4},{7,5},{8,10},{9,11},{10,... | collective-permute-start | bytes 122888 | tf_op jit(solution)/shard_map/ppermute | solution.py:33
  36.3 1.5 %collective-permute-start.11 = (bf16[160,128]{1,0:T(8,128)(2,1)S(1)}, bf16[160,128]{1,0:T(8,128)(2,1)S(1)}, u32[]{:S(2)}, u32[]{:S(2)}) collective-permute-start(bf16[160,128]{1,0:T(8,128)(2,1)S(1)} %add_convert_fusion.3), channel_id=1, source_target_pairs={{0,4},{1,5},{2,6},{3,7},{4,0},{5,1},{6,2},{7,3},{8,12},{9,13},{10,... | collective-permute-start | bytes 122888 | tf_op jit(solution)/shard_map/ppermute | solution.py:33
  37.8 1.4 %collective-permute-done.13 = bf16[160,128]{1,0:T(8,128)(2,1)S(1)} collective-permute-done((bf16[160,128]{1,0:T(8,128)(2,1)S(1)}, bf16[160,128]{1,0:T(8,128)(2,1)S(1)}, u32[]{:S(2)}, u32[]{:S(2)}) %collective-permute-start.13) | collective-permute-done | bytes 40992 | tf_op jit(solution)/shard_map/ppermute | solution.py:33
  39.3 0.4 collective-permute-start.17
  39.7 3.2 %collective-permute-done.11 = bf16[160,128]{1,0:T(8,128)(2,1)S(1)} collective-permute-done((bf16[160,128]{1,0:T(8,128)(2,1)S(1)}, bf16[160,128]{1,0:T(8,128)(2,1)S(1)}, u32[]{:S(2)}, u32[]{:S(2)}) %collective-permute-start.11) | collective-permute-done | bytes 40992 | tf_op jit(solution)/shard_map/ppermute | solution.py:33
  43.0 0.1 collective-permute-start.16
  43.0 0.5 collective-permute-start.18
  43.5 0.1 collective-permute-start.19
  43.6 0.8 collective-permute-done.16.other_ref
  44.4 2.7 %shard_map.54.whiten_ref = bf16[512,512]{1,0:T(8,128)(2,1)S(1)} custom-call(s32[3]{0:T(128)S(1)} %pad_add_fusion.at, bf16[4,160,128]{2,1,0:T(8,128)(2,1)S(1)} %pad_maximum_fusion.2.mine_ref, bf16[4,160,128]{2,1,0:T(8,128)(2,1)S(1)} %collective-permute-done.16.other_ref), custom_call_target="tpu_custom_call" | custom-call | tf_op jit(solution)/shard_map/pallas_call | solution.py:58
  47.1 0.2 collective-permute-start.20
  47.3 1.2 %shard_map.55 = (bf16[4,512,256]{2,1,0:T(8,128)(2,1)S(1)}, f32[64,512]{1,0:T(8,128)S(1)}, f32[64,1]{1,0:T(8,128)S(1)}) custom-call(bf16[512,512]{1,0:T(8,128)(2,1)S(1)} %shard_map.54.whiten_ref, bf16[512,256]{1,0:T(8,128)(2,1)S(1)} %add_convert_fusion.here_ref.refs_0_, bf16[512,256]{1,0:T(8,128)(2,1)S(1)} %collective-permute-done.4.there_ref.refs_1_, ...), custom_call_target="tpu_custom_call" | custom-call | tf_op jit(solution)/shard_map/pallas_call | solution.py:58
  48.5 0.2 collective-permute-done.20.refs_3_
  48.7 1.6 %shard_map.56 = (bf16[4,512,256]{2,1,0:T(8,128)(2,1)S(1)}, f32[64,512]{1,0:T(8,128)S(1)}, f32[64,1]{1,0:T(8,128)}) custom-call(bf16[512,512]{1,0:T(8,128)(2,1)S(1)} %shard_map.54.whiten_ref, bf16[512,256]{1,0:T(8,128)(2,1)S(1)} %collective-permute-done.18.refs_0_, bf16[512,256]{1,0:T(8,128)(2,1)S(1)} %collective-permute-done.19.refs_1_, ...), custom_call_target="tpu_custom_call" | custom-call | tf_op jit(solution)/shard_map/pallas_call | solution.py:58
  50.3 2.5 %collective-permute-start.23 = (bf16[64,512]{1,0:T(8,128)(2,1)S(1)}, bf16[64,512]{1,0:T(8,128)(2,1)S(1)}, u32[]{:S(2)}, u32[]{:S(2)}) collective-permute-start(bf16[64,512]{1,0:T(8,128)(2,1)S(1)} %convert_element_type.70), channel_id=1, source_target_pairs={{0,24},{1,25},{2,26},{3,27},{4,28},{5,29},{6,30},{7,31},{8,16},{9,... | collective-permute-start | bytes 196616 | tf_op jit(solution)/shard_map/ppermute | solution.py:33
  52.8 2.0 %collective-permute-start.21 = (bf16[64,512]{1,0:T(8,128)(2,1)S(1)}, bf16[64,512]{1,0:T(8,128)(2,1)S(1)}, u32[]{:S(2)}, u32[]{:S(2)}) collective-permute-start(bf16[64,512]{1,0:T(8,128)(2,1)S(1)} %convert_element_type.70), channel_id=1, source_target_pairs={{0,8},{1,9},{2,10},{3,11},{4,12},{5,13},{6,14},{7,15},{8,0},{9,1},... | collective-permute-start | bytes 196616 | tf_op jit(solution)/shard_map/ppermute | solution.py:33
  54.8 2.4 %collective-permute-done.23 = bf16[64,512]{1,0:T(8,128)(2,1)S(1)} collective-permute-done((bf16[64,512]{1,0:T(8,128)(2,1)S(1)}, bf16[64,512]{1,0:T(8,128)(2,1)S(1)}, u32[]{:S(2)}, u32[]{:S(2)}) %collective-permute-start.23) | collective-permute-done | bytes 65568 | tf_op jit(solution)/shard_map/ppermute | solution.py:33
  57.2 2.0 %collective-permute-done.22 = bf16[64,512]{1,0:T(8,128)(2,1)S(1)} collective-permute-done((bf16[64,512]{1,0:T(8,128)(2,1)S(1)}, bf16[64,512]{1,0:T(8,128)(2,1)S(1)}, u32[]{:S(2)}, u32[]{:S(2)}) %collective-permute-start.22) | collective-permute-done | bytes 65568 | tf_op jit(solution)/shard_map/ppermute | solution.py:33
  59.3 0.7 collective-permute-start.26
  60.0 1.4 %collective-permute-start.25 = (bf16[64,512]{1,0:T(8,128)(2,1)S(1)}, bf16[64,512]{1,0:T(8,128)(2,1)S(1)}, u32[]{:S(2)}, u32[]{:S(2)}) collective-permute-start(bf16[64,512]{1,0:T(8,128)(2,1)S(1)} %add_convert_fusion.2), channel_id=1, source_target_pairs={{0,2},{1,3},{2,0},{3,1},{4,6},{5,7},{6,4},{7,5},{8,10},{9,11},{10,... | collective-permute-start | bytes 196616 | tf_op jit(solution)/shard_map/ppermute | solution.py:33
  61.5 1.4 %collective-permute-start.24 = (bf16[64,512]{1,0:T(8,128)(2,1)S(1)}, bf16[64,512]{1,0:T(8,128)(2,1)S(1)}, u32[]{:S(2)}, u32[]{:S(2)}) collective-permute-start(bf16[64,512]{1,0:T(8,128)(2,1)S(1)} %add_convert_fusion.2), channel_id=1, source_target_pairs={{0,4},{1,5},{2,6},{3,7},{4,0},{5,1},{6,2},{7,3},{8,12},{9,13},{10,... | collective-permute-start | bytes 196616 | tf_op jit(solution)/shard_map/ppermute | solution.py:33
  62.8 2.1 %collective-permute-done.26 = bf16[64,512]{1,0:T(8,128)(2,1)S(1)} collective-permute-done((bf16[64,512]{1,0:T(8,128)(2,1)S(1)}, bf16[64,512]{1,0:T(8,128)(2,1)S(1)}, u32[]{:S(2)}, u32[]{:S(2)}) %collective-permute-start.26) | collective-permute-done | bytes 65568 | tf_op jit(solution)/shard_map/ppermute | solution.py:33
  65.0 0.8 collective-permute-done.24
  65.9 1.5 %collective-permute-done.27.other_ref = bf16[4,64,512]{2,1,0:T(8,128)(2,1)S(1)} collective-permute-done((bf16[4,64,512]{2,1,0:T(8,128)(2,1)S(1)}, bf16[4,64,512]{2,1,0:T(8,128)(2,1)S(1)}, u32[]{:S(2)}, u32[]{:S(2)}) %collective-permute-start.27) | collective-permute-done | bytes 262176 | tf_op jit(solution)/shard_map/ppermute | solution.py:33
  67.4 3.9 %shard_map.57 = f32[64,512]{1,0:T(8,128)S(1)} custom-call(s32[3]{0:T(128)S(1)} %pad_add_fusion.at, bf16[4,64,512]{2,1,0:T(8,128)(2,1)S(1)} %pad_maximum_fusion.mine_ref, bf16[4,64,512]{2,1,0:T(8,128)(2,1)S(1)} %collective-permute-done.27.other_ref, bf16[4,512,256]{2,1,0:T(8,128)(2,1)S(1)} %get-tuple-element.36.refs_0_, ...), custom_call_target="tpu_custom_call" | custom-call | tf_op jit(solution)/shard_map/pallas_call | solution.py:58
  71.3 2.6 %collective-permute-start.30 = (bf16[64,512]{1,0:T(8,128)(2,1)S(1)}, bf16[64,512]{1,0:T(8,128)(2,1)S(1)}, u32[]{:S(2)}, u32[]{:S(2)}) collective-permute-start(bf16[64,512]{1,0:T(8,128)(2,1)S(1)} %convert_element_type.75), channel_id=1, source_target_pairs={{0,24},{1,25},{2,26},{3,27},{4,28},{5,29},{6,30},{7,31},{8,16},{9,... | collective-permute-start | bytes 196616 | tf_op jit(solution)/shard_map/ppermute | solution.py:33
  74.0 1.8 %collective-permute-start.28 = (bf16[64,512]{1,0:T(8,128)(2,1)S(1)}, bf16[64,512]{1,0:T(8,128)(2,1)S(1)}, u32[]{:S(2)}, u32[]{:S(2)}) collective-permute-start(bf16[64,512]{1,0:T(8,128)(2,1)S(1)} %convert_element_type.75), channel_id=1, source_target_pairs={{0,8},{1,9},{2,10},{3,11},{4,12},{5,13},{6,14},{7,15},{8,0},{9,1},... | collective-permute-start | bytes 196616 | tf_op jit(solution)/shard_map/ppermute | solution.py:33
  75.8 2.3 %collective-permute-done.30 = bf16[64,512]{1,0:T(8,128)(2,1)S(1)} collective-permute-done((bf16[64,512]{1,0:T(8,128)(2,1)S(1)}, bf16[64,512]{1,0:T(8,128)(2,1)S(1)}, u32[]{:S(2)}, u32[]{:S(2)}) %collective-permute-start.30) | collective-permute-done | bytes 65568 | tf_op jit(solution)/shard_map/ppermute | solution.py:33
  78.1 2.0 %collective-permute-done.29 = bf16[64,512]{1,0:T(8,128)(2,1)S(1)} collective-permute-done((bf16[64,512]{1,0:T(8,128)(2,1)S(1)}, bf16[64,512]{1,0:T(8,128)(2,1)S(1)}, u32[]{:S(2)}, u32[]{:S(2)}) %collective-permute-start.29) | collective-permute-done | bytes 65568 | tf_op jit(solution)/shard_map/ppermute | solution.py:33
  80.2 1.5 %collective-permute-start.33 = (bf16[64,512]{1,0:T(8,128)(2,1)S(1)}, bf16[64,512]{1,0:T(8,128)(2,1)S(1)}, u32[]{:S(2)}, u32[]{:S(2)}) collective-permute-start(bf16[64,512]{1,0:T(8,128)(2,1)S(1)} %add_convert_fusion.1), channel_id=1, source_target_pairs={{0,6},{1,7},{2,4},{3,5},{4,2},{5,3},{6,0},{7,1},{8,14},{9,15},{10,... | collective-permute-start | bytes 196616 | tf_op jit(solution)/shard_map/ppermute | solution.py:33
  81.6 1.4 %collective-permute-start.32 = (bf16[64,512]{1,0:T(8,128)(2,1)S(1)}, bf16[64,512]{1,0:T(8,128)(2,1)S(1)}, u32[]{:S(2)}, u32[]{:S(2)}) collective-permute-start(bf16[64,512]{1,0:T(8,128)(2,1)S(1)} %add_convert_fusion.1), channel_id=1, source_target_pairs={{0,2},{1,3},{2,0},{3,1},{4,6},{5,7},{6,4},{7,5},{8,10},{9,11},{10,... | collective-permute-start | bytes 196616 | tf_op jit(solution)/shard_map/ppermute | solution.py:33
  83.1 0.7 collective-permute-start.31
  83.7 2.2 %collective-permute-done.33 = bf16[64,512]{1,0:T(8,128)(2,1)S(1)} collective-permute-done((bf16[64,512]{1,0:T(8,128)(2,1)S(1)}, bf16[64,512]{1,0:T(8,128)(2,1)S(1)}, u32[]{:S(2)}, u32[]{:S(2)}) %collective-permute-start.33) | collective-permute-done | bytes 65568 | tf_op jit(solution)/shard_map/ppermute | solution.py:33
  86.0 0.5 collective-permute-done.32
  86.5 0.9 collective-permute-done.31
  87.5 1.5 %collective-permute-done.34.other_ref = bf16[4,64,512]{2,1,0:T(8,128)(2,1)S(1)} collective-permute-done((bf16[4,64,512]{2,1,0:T(8,128)(2,1)S(1)}, bf16[4,64,512]{2,1,0:T(8,128)(2,1)S(1)}, u32[]{:S(2)}, u32[]{:S(2)}) %collective-permute-start.34) | collective-permute-done | bytes 262176 | tf_op jit(solution)/shard_map/ppermute | solution.py:33
  89.0 3.8 %shard_map.58 = (f32[128,512]{1,0:T(8,128)}, bf16[128,1024]{1,0:T(8,128)(2,1)}) custom-call(s32[3]{0:T(128)S(1)} %pad_add_fusion.at, bf16[4,64,512]{2,1,0:T(8,128)(2,1)S(1)} %pad_maximum_fusion.1.mine_ref, bf16[4,64,512]{2,1,0:T(8,128)(2,1)S(1)} %collective-permute-done.34.other_ref, bf16[4,512,256]{2,1,0:T(8,128)(2,1)S(1)} %get-tuple-element.36.refs_0_, ...), custom_call_target="tpu_custom_call" | custom-call | tf_op jit(solution)/shard_map/pallas_call | solution.py:58
  (35 shorter events, 0.5 us)
Async XLA Ops:
  0.6 46.7 %copy-start = (f32[128,512]{1,0:T(8,128)S(1)}, f32[128,512]{1,0:T(8,128)}, u32[]{:S(2)}) copy-start(f32[128,512]{1,0:T(8,128)} %param.5) | copy-start | bytes 786436
  0.6 2.3 %copy-start.1 = (bf16[512,1024]{1,0:T(8,128)(2,1)S(1)}, bf16[512,1024]{1,0:T(8,128)(2,1)}, u32[]{:S(2)}) copy-start(bf16[512,1024]{1,0:T(8,128)(2,1)} %right_ref.1) | copy-start | bytes 3145732
  0.7 4.3 %collective-permute-start = (bf16[512,512]{1,0:T(8,128)(2,1)}, bf16[512,512]{1,0:T(8,128)(2,1)S(1)}, u32[]{:S(2)}, u32[]{:S(2)}) collective-permute-start(bf16[512,512]{1,0:T(8,128)(2,1)} %left_ref.1), channel_id=1, source_target_pairs={{0,1},{1,0},{2,3},{3,2},{4,5},{5,4},{6,7},{7,6},{8,9},{9,8},{10,11... | collective-permute-start | bytes 1572872 | tf_op jit(solution)/shard_map/ppermute | solution.py:33
  2.2 2.7 %collective-permute-start.2 = (bf16[512,256]{1,0:T(8,128)(2,1)S(1)}, bf16[512,256]{1,0:T(8,128)(2,1)S(1)}, u32[]{:S(2)}, u32[]{:S(2)}) collective-permute-start(bf16[512,256]{1,0:T(8,128)(2,1)S(1)} %get-tuple-element.38), channel_id=1, source_target_pairs={{0,1},{1,0},{2,3},{3,2},{4,5},{5,4},{6,7},{7,6},{8,9},{9,8},{10,11... | collective-permute-start | bytes 786440 | tf_op jit(solution)/shard_map/ppermute | solution.py:33
  2.5 5.5 %collective-permute-start.1 = (bf16[512,256]{1,0:T(8,128)(2,1)S(1)}, bf16[512,256]{1,0:T(8,128)(2,1)S(1)}, u32[]{:S(2)}, u32[]{:S(2)}) collective-permute-start(bf16[512,256]{1,0:T(8,128)(2,1)S(1)} %get-tuple-element.39), channel_id=1, source_target_pairs={{0,1},{1,0},{2,3},{3,2},{4,5},{5,4},{6,7},{7,6},{8,9},{9,8},{10,11... | collective-permute-start | bytes 786440 | tf_op jit(solution)/shard_map/ppermute | solution.py:33
  2.9 1.0 %copy-start.2 = (bf16[512,512]{1,0:T(8,128)(2,1)S(1)}, bf16[512,512]{1,0:T(8,128)(2,1)}, u32[]{:S(2)}) copy-start(bf16[512,512]{1,0:T(8,128)(2,1)} %left_ref.1) | copy-start | bytes 1572868
  5.3 9.5 %collective-permute-start.3 = (bf16[512,256]{1,0:T(8,128)(2,1)S(1)}, bf16[512,256]{1,0:T(8,128)(2,1)S(1)}, u32[]{:S(2)}, u32[]{:S(2)}) collective-permute-start(bf16[512,256]{1,0:T(8,128)(2,1)S(1)} %shard_map.52), channel_id=1, source_target_pairs={{0,2},{1,3},{2,0},{3,1},{4,6},{5,7},{6,4},{7,5},{8,10},{9,11},{10,... | collective-permute-start | bytes 786440 | tf_op jit(solution)/shard_map/ppermute | solution.py:33
  14.8 1.6 %collective-permute-start.4 = (bf16[512,256]{1,0:T(8,128)(2,1)S(1)}, bf16[512,256]{1,0:T(8,128)(2,1)S(1)}, u32[]{:S(2)}, u32[]{:S(2)}) collective-permute-start(bf16[512,256]{1,0:T(8,128)(2,1)S(1)} %add_convert_fusion.here_ref.refs_0_), channel_id=1, source_target_pairs={{0,1},{1,0},{2,3},{3,2},{4,5},{5,4},{6,7},{7,6},{8,9},{9,8},{10,11... | collective-permute-start | bytes 786440 | tf_op jit(solution)/shard_map/ppermute | solution.py:33
  17.4 4.1 %collective-permute-start.5 = (bf16[160,128]{1,0:T(8,128)(2,1)S(1)}, bf16[160,128]{1,0:T(8,128)(2,1)S(1)}, u32[]{:S(2)}, u32[]{:S(2)}) collective-permute-start(bf16[160,128]{1,0:T(8,128)(2,1)S(1)} %get-tuple-element.21), channel_id=1, source_target_pairs={{0,4},{1,5},{2,6},{3,7},{4,0},{5,1},{6,2},{7,3},{8,12},{9,13},{10,... | collective-permute-start | bytes 122888 | tf_op jit(solution)/shard_map/ppermute | solution.py:33
  19.2 4.4 %collective-permute-start.6 = (bf16[160,128]{1,0:T(8,128)(2,1)S(1)}, bf16[160,128]{1,0:T(8,128)(2,1)S(1)}, u32[]{:S(2)}, u32[]{:S(2)}) collective-permute-start(bf16[160,128]{1,0:T(8,128)(2,1)S(1)} %get-tuple-element.22), channel_id=1, source_target_pairs={{0,2},{1,3},{2,0},{3,1},{4,6},{5,7},{6,4},{7,5},{8,10},{9,11},{10,... | collective-permute-start | bytes 122888 | tf_op jit(solution)/shard_map/ppermute | solution.py:33
  20.7 4.9 %collective-permute-start.7 = (bf16[160,128]{1,0:T(8,128)(2,1)S(1)}, bf16[160,128]{1,0:T(8,128)(2,1)S(1)}, u32[]{:S(2)}, u32[]{:S(2)}) collective-permute-start(bf16[160,128]{1,0:T(8,128)(2,1)S(1)} %get-tuple-element.23), channel_id=1, source_target_pairs={{0,6},{1,7},{2,4},{3,5},{4,2},{5,3},{6,0},{7,1},{8,14},{9,15},{10,... | collective-permute-start | bytes 122888 | tf_op jit(solution)/shard_map/ppermute | solution.py:33
  25.7 6.0 %collective-permute-start.10 = (bf16[160,128]{1,0:T(8,128)(2,1)S(1)}, bf16[160,128]{1,0:T(8,128)(2,1)S(1)}, u32[]{:S(2)}, u32[]{:S(2)}) collective-permute-start(bf16[160,128]{1,0:T(8,128)(2,1)S(1)} %convert_element_type.65), channel_id=1, source_target_pairs={{0,24},{1,25},{2,26},{3,27},{4,28},{5,29},{6,30},{7,31},{8,16},{9,... | collective-permute-start | bytes 122888 | tf_op jit(solution)/shard_map/ppermute | solution.py:33
  29.3 4.9 %collective-permute-start.9 = (bf16[160,128]{1,0:T(8,128)(2,1)S(1)}, bf16[160,128]{1,0:T(8,128)(2,1)S(1)}, u32[]{:S(2)}, u32[]{:S(2)}) collective-permute-start(bf16[160,128]{1,0:T(8,128)(2,1)S(1)} %convert_element_type.65), channel_id=1, source_target_pairs={{0,16},{1,17},{2,18},{3,19},{4,20},{5,21},{6,22},{7,23},{8,24},{9,... | collective-permute-start | bytes 122888 | tf_op jit(solution)/shard_map/ppermute | solution.py:33
  29.3 4.9 %collective-permute-start.8 = (bf16[160,128]{1,0:T(8,128)(2,1)S(1)}, bf16[160,128]{1,0:T(8,128)(2,1)S(1)}, u32[]{:S(2)}, u32[]{:S(2)}) collective-permute-start(bf16[160,128]{1,0:T(8,128)(2,1)S(1)} %convert_element_type.65), channel_id=1, source_target_pairs={{0,8},{1,9},{2,10},{3,11},{4,12},{5,13},{6,14},{7,15},{8,0},{9,1},... | collective-permute-start | bytes 122888 | tf_op jit(solution)/shard_map/ppermute | solution.py:33
  30.1 12.8 %collective-permute-start.15 = (bf16[512,256]{1,0:T(8,128)(2,1)S(1)}, bf16[512,256]{1,0:T(8,128)(2,1)S(1)}, u32[]{:S(2)}, u32[]{:S(2)}) collective-permute-start(bf16[512,256]{1,0:T(8,128)(2,1)S(1)} %add_convert_fusion.here_ref.refs_0_), channel_id=1, source_target_pairs={{0,4},{1,5},{2,6},{3,7},{4,0},{5,1},{6,2},{7,3},{8,12},{9,13},{10,... | collective-permute-start | bytes 786440 | tf_op jit(solution)/shard_map/ppermute | solution.py:33
  30.6 12.3 %collective-permute-start.14 = (bf16[512,256]{1,0:T(8,128)(2,1)S(1)}, bf16[512,256]{1,0:T(8,128)(2,1)S(1)}, u32[]{:S(2)}, u32[]{:S(2)}) collective-permute-start(bf16[512,256]{1,0:T(8,128)(2,1)S(1)} %add_convert_fusion.here_ref.refs_0_), channel_id=1, source_target_pairs={{0,2},{1,3},{2,0},{3,1},{4,6},{5,7},{6,4},{7,5},{8,10},{9,11},{10,... | collective-permute-start | bytes 786440 | tf_op jit(solution)/shard_map/ppermute | solution.py:33
  34.3 5.0 %collective-permute-start.13 = (bf16[160,128]{1,0:T(8,128)(2,1)S(1)}, bf16[160,128]{1,0:T(8,128)(2,1)S(1)}, u32[]{:S(2)}, u32[]{:S(2)}) collective-permute-start(bf16[160,128]{1,0:T(8,128)(2,1)S(1)} %add_convert_fusion.3), channel_id=1, source_target_pairs={{0,6},{1,7},{2,4},{3,5},{4,2},{5,3},{6,0},{7,1},{8,14},{9,15},{10,... | collective-permute-start | bytes 122888 | tf_op jit(solution)/shard_map/ppermute | solution.py:33
  34.8 4.9 %collective-permute-start.12 = (bf16[160,128]{1,0:T(8,128)(2,1)S(1)}, bf16[160,128]{1,0:T(8,128)(2,1)S(1)}, u32[]{:S(2)}, u32[]{:S(2)}) collective-permute-start(bf16[160,128]{1,0:T(8,128)(2,1)S(1)} %add_convert_fusion.3), channel_id=1, source_target_pairs={{0,2},{1,3},{2,0},{3,1},{4,6},{5,7},{6,4},{7,5},{8,10},{9,11},{10,... | collective-permute-start | bytes 122888 | tf_op jit(solution)/shard_map/ppermute | solution.py:33
  36.3 6.6 %collective-permute-start.11 = (bf16[160,128]{1,0:T(8,128)(2,1)S(1)}, bf16[160,128]{1,0:T(8,128)(2,1)S(1)}, u32[]{:S(2)}, u32[]{:S(2)}) collective-permute-start(bf16[160,128]{1,0:T(8,128)(2,1)S(1)} %add_convert_fusion.3), channel_id=1, source_target_pairs={{0,4},{1,5},{2,6},{3,7},{4,0},{5,1},{6,2},{7,3},{8,12},{9,13},{10,... | collective-permute-start | bytes 122888 | tf_op jit(solution)/shard_map/ppermute | solution.py:33
  39.3 7.8 %collective-permute-start.17 = (bf16[512,256]{1,0:T(8,128)(2,1)S(1)}, bf16[512,256]{1,0:T(8,128)(2,1)S(1)}, u32[]{:S(2)}, u32[]{:S(2)}) collective-permute-start(bf16[512,256]{1,0:T(8,128)(2,1)S(1)} %add_convert_fusion.here_ref.refs_0_), channel_id=1, source_target_pairs={{0,6},{1,7},{2,4},{3,5},{4,2},{5,3},{6,0},{7,1},{8,14},{9,15},{10,... | collective-permute-start | bytes 786440 | tf_op jit(solution)/shard_map/ppermute | solution.py:33
  43.0 1.5 %collective-permute-start.16 = (bf16[4,160,128]{2,1,0:T(8,128)(2,1)S(1)}, bf16[4,160,128]{2,1,0:T(8,128)(2,1)S(1)}, u32[]{:S(2)}, u32[]{:S(2)}) collective-permute-start(bf16[4,160,128]{2,1,0:T(8,128)(2,1)S(1)} %pad_maximum_fusion.2.mine_ref), channel_id=1, source_target_pairs={{0,1},{1,0},{2,3},{3,2},{4,5},{5,4},{6,7},{7,6},{8,9},{9,8},{10,11... | collective-permute-start | bytes 491528 | tf_op jit(solution)/shard_map/ppermute | solution.py:33
  43.0 5.5 %collective-permute-start.18 = (bf16[512,256]{1,0:T(8,128)(2,1)S(1)}, bf16[512,256]{1,0:T(8,128)(2,1)S(1)}, u32[]{:S(2)}, u32[]{:S(2)}) collective-permute-start(bf16[512,256]{1,0:T(8,128)(2,1)S(1)} %collective-permute-done.14.refs_2_), channel_id=1, source_target_pairs={{0,1},{1,0},{2,3},{3,2},{4,5},{5,4},{6,7},{7,6},{8,9},{9,8},{10,11... | collective-permute-start | bytes 786440 | tf_op jit(solution)/shard_map/ppermute | solution.py:33
  43.5 5.0 %collective-permute-start.19 = (bf16[512,256]{1,0:T(8,128)(2,1)S(1)}, bf16[512,256]{1,0:T(8,128)(2,1)S(1)}, u32[]{:S(2)}, u32[]{:S(2)}) collective-permute-start(bf16[512,256]{1,0:T(8,128)(2,1)S(1)} %collective-permute-done.15.refs_3_), channel_id=1, source_target_pairs={{0,1},{1,0},{2,3},{3,2},{4,5},{5,4},{6,7},{7,6},{8,9},{9,8},{10,11... | collective-permute-start | bytes 786440 | tf_op jit(solution)/shard_map/ppermute | solution.py:33
  47.1 1.6 %collective-permute-start.20 = (bf16[512,256]{1,0:T(8,128)(2,1)S(1)}, bf16[512,256]{1,0:T(8,128)(2,1)S(1)}, u32[]{:S(2)}, u32[]{:S(2)}) collective-permute-start(bf16[512,256]{1,0:T(8,128)(2,1)S(1)} %collective-permute-done.17.refs_2_), channel_id=1, source_target_pairs={{0,1},{1,0},{2,3},{3,2},{4,5},{5,4},{6,7},{7,6},{8,9},{9,8},{10,11... | collective-permute-start | bytes 786440 | tf_op jit(solution)/shard_map/ppermute | solution.py:33
  50.3 6.9 %collective-permute-start.23 = (bf16[64,512]{1,0:T(8,128)(2,1)S(1)}, bf16[64,512]{1,0:T(8,128)(2,1)S(1)}, u32[]{:S(2)}, u32[]{:S(2)}) collective-permute-start(bf16[64,512]{1,0:T(8,128)(2,1)S(1)} %convert_element_type.70), channel_id=1, source_target_pairs={{0,24},{1,25},{2,26},{3,27},{4,28},{5,29},{6,30},{7,31},{8,16},{9,... | collective-permute-start | bytes 196616 | tf_op jit(solution)/shard_map/ppermute | solution.py:33
  52.8 6.4 %collective-permute-start.22 = (bf16[64,512]{1,0:T(8,128)(2,1)S(1)}, bf16[64,512]{1,0:T(8,128)(2,1)S(1)}, u32[]{:S(2)}, u32[]{:S(2)}) collective-permute-start(bf16[64,512]{1,0:T(8,128)(2,1)S(1)} %convert_element_type.70), channel_id=1, source_target_pairs={{0,16},{1,17},{2,18},{3,19},{4,20},{5,21},{6,22},{7,23},{8,24},{9,... | collective-permute-start | bytes 196616 | tf_op jit(solution)/shard_map/ppermute | solution.py:33
  52.8 6.4 %collective-permute-start.21 = (bf16[64,512]{1,0:T(8,128)(2,1)S(1)}, bf16[64,512]{1,0:T(8,128)(2,1)S(1)}, u32[]{:S(2)}, u32[]{:S(2)}) collective-permute-start(bf16[64,512]{1,0:T(8,128)(2,1)S(1)} %convert_element_type.70), channel_id=1, source_target_pairs={{0,8},{1,9},{2,10},{3,11},{4,12},{5,13},{6,14},{7,15},{8,0},{9,1},... | collective-permute-start | bytes 196616 | tf_op jit(solution)/shard_map/ppermute | solution.py:33
  59.3 5.7 %collective-permute-start.26 = (bf16[64,512]{1,0:T(8,128)(2,1)S(1)}, bf16[64,512]{1,0:T(8,128)(2,1)S(1)}, u32[]{:S(2)}, u32[]{:S(2)}) collective-permute-start(bf16[64,512]{1,0:T(8,128)(2,1)S(1)} %add_convert_fusion.2), channel_id=1, source_target_pairs={{0,6},{1,7},{2,4},{3,5},{4,2},{5,3},{6,0},{7,1},{8,14},{9,15},{10,... | collective-permute-start | bytes 196616 | tf_op jit(solution)/shard_map/ppermute | solution.py:33
  60.0 4.9 %collective-permute-start.25 = (bf16[64,512]{1,0:T(8,128)(2,1)S(1)}, bf16[64,512]{1,0:T(8,128)(2,1)S(1)}, u32[]{:S(2)}, u32[]{:S(2)}) collective-permute-start(bf16[64,512]{1,0:T(8,128)(2,1)S(1)} %add_convert_fusion.2), channel_id=1, source_target_pairs={{0,2},{1,3},{2,0},{3,1},{4,6},{5,7},{6,4},{7,5},{8,10},{9,11},{10,... | collective-permute-start | bytes 196616 | tf_op jit(solution)/shard_map/ppermute | solution.py:33
  61.5 4.3 %collective-permute-start.24 = (bf16[64,512]{1,0:T(8,128)(2,1)S(1)}, bf16[64,512]{1,0:T(8,128)(2,1)S(1)}, u32[]{:S(2)}, u32[]{:S(2)}) collective-permute-start(bf16[64,512]{1,0:T(8,128)(2,1)S(1)} %add_convert_fusion.2), channel_id=1, source_target_pairs={{0,4},{1,5},{2,6},{3,7},{4,0},{5,1},{6,2},{7,3},{8,12},{9,13},{10,... | collective-permute-start | bytes 196616 | tf_op jit(solution)/shard_map/ppermute | solution.py:33
  65.8 1.6 %collective-permute-start.27 = (bf16[4,64,512]{2,1,0:T(8,128)(2,1)S(1)}, bf16[4,64,512]{2,1,0:T(8,128)(2,1)S(1)}, u32[]{:S(2)}, u32[]{:S(2)}) collective-permute-start(bf16[4,64,512]{2,1,0:T(8,128)(2,1)S(1)} %pad_maximum_fusion.mine_ref), channel_id=1, source_target_pairs={{0,1},{1,0},{2,3},{3,2},{4,5},{5,4},{6,7},{7,6},{8,9},{9,8},{10,11... | collective-permute-start | bytes 786440 | tf_op jit(solution)/shard_map/ppermute | solution.py:33
  71.3 6.8 %collective-permute-start.30 = (bf16[64,512]{1,0:T(8,128)(2,1)S(1)}, bf16[64,512]{1,0:T(8,128)(2,1)S(1)}, u32[]{:S(2)}, u32[]{:S(2)}) collective-permute-start(bf16[64,512]{1,0:T(8,128)(2,1)S(1)} %convert_element_type.75), channel_id=1, source_target_pairs={{0,24},{1,25},{2,26},{3,27},{4,28},{5,29},{6,30},{7,31},{8,16},{9,... | collective-permute-start | bytes 196616 | tf_op jit(solution)/shard_map/ppermute | solution.py:33
  74.0 6.2 %collective-permute-start.29 = (bf16[64,512]{1,0:T(8,128)(2,1)S(1)}, bf16[64,512]{1,0:T(8,128)(2,1)S(1)}, u32[]{:S(2)}, u32[]{:S(2)}) collective-permute-start(bf16[64,512]{1,0:T(8,128)(2,1)S(1)} %convert_element_type.75), channel_id=1, source_target_pairs={{0,16},{1,17},{2,18},{3,19},{4,20},{5,21},{6,22},{7,23},{8,24},{9,... | collective-permute-start | bytes 196616 | tf_op jit(solution)/shard_map/ppermute | solution.py:33
  74.0 6.2 %collective-permute-start.28 = (bf16[64,512]{1,0:T(8,128)(2,1)S(1)}, bf16[64,512]{1,0:T(8,128)(2,1)S(1)}, u32[]{:S(2)}, u32[]{:S(2)}) collective-permute-start(bf16[64,512]{1,0:T(8,128)(2,1)S(1)} %convert_element_type.75), channel_id=1, source_target_pairs={{0,8},{1,9},{2,10},{3,11},{4,12},{5,13},{6,14},{7,15},{8,0},{9,1},... | collective-permute-start | bytes 196616 | tf_op jit(solution)/shard_map/ppermute | solution.py:33
  80.2 5.8 %collective-permute-start.33 = (bf16[64,512]{1,0:T(8,128)(2,1)S(1)}, bf16[64,512]{1,0:T(8,128)(2,1)S(1)}, u32[]{:S(2)}, u32[]{:S(2)}) collective-permute-start(bf16[64,512]{1,0:T(8,128)(2,1)S(1)} %add_convert_fusion.1), channel_id=1, source_target_pairs={{0,6},{1,7},{2,4},{3,5},{4,2},{5,3},{6,0},{7,1},{8,14},{9,15},{10,... | collective-permute-start | bytes 196616 | tf_op jit(solution)/shard_map/ppermute | solution.py:33
  81.6 4.8 %collective-permute-start.32 = (bf16[64,512]{1,0:T(8,128)(2,1)S(1)}, bf16[64,512]{1,0:T(8,128)(2,1)S(1)}, u32[]{:S(2)}, u32[]{:S(2)}) collective-permute-start(bf16[64,512]{1,0:T(8,128)(2,1)S(1)} %add_convert_fusion.1), channel_id=1, source_target_pairs={{0,2},{1,3},{2,0},{3,1},{4,6},{5,7},{6,4},{7,5},{8,10},{9,11},{10,... | collective-permute-start | bytes 196616 | tf_op jit(solution)/shard_map/ppermute | solution.py:33
  83.1 4.3 %collective-permute-start.31 = (bf16[64,512]{1,0:T(8,128)(2,1)S(1)}, bf16[64,512]{1,0:T(8,128)(2,1)S(1)}, u32[]{:S(2)}, u32[]{:S(2)}) collective-permute-start(bf16[64,512]{1,0:T(8,128)(2,1)S(1)} %add_convert_fusion.1), channel_id=1, source_target_pairs={{0,4},{1,5},{2,6},{3,7},{4,0},{5,1},{6,2},{7,3},{8,12},{9,13},{10,... | collective-permute-start | bytes 196616 | tf_op jit(solution)/shard_map/ppermute | solution.py:33
  87.4 1.6 %collective-permute-start.34 = (bf16[4,64,512]{2,1,0:T(8,128)(2,1)S(1)}, bf16[4,64,512]{2,1,0:T(8,128)(2,1)S(1)}, u32[]{:S(2)}, u32[]{:S(2)}) collective-permute-start(bf16[4,64,512]{2,1,0:T(8,128)(2,1)S(1)} %pad_maximum_fusion.1.mine_ref), channel_id=1, source_target_pairs={{0,1},{1,0},{2,3},{3,2},{4,5},{5,4},{6,7},{7,6},{8,9},{9,8},{10,11... | collective-permute-start | bytes 786440 | tf_op jit(solution)/shard_map/ppermute | solution.py:33

commit v4 on v3

--- a/solution.py
+++ b/solution.py
@@ -51,7 +51,7 @@
 
 VMEM = pl.BlockSpec(memory_space=pltpu.VMEM)
 SMEM = pl.BlockSpec(memory_space=pltpu.SMEM)
-ANY = pl.BlockSpec(memory_space=pl.ANY)
+HBM = pl.BlockSpec(memory_space=pltpu.HBM)
 
 
 def run(kernel, outs, args, specs=None, scratch=(), limit=24):
@@ -69,34 +69,31 @@
     return jax.ShapeDtypeStruct(dims, dtype)
 
 
-def own_kernel(at, left_ref, right_ref, out_ref):
-    size = out_ref.shape[2]
-    for k, across in enumerate((1 - at[1], at[1])):
-        start = pl.multiple_of((across * 2 + at[0]) * size, size)
-        out_ref[k] = nn(left_ref[...], right_ref[:, pl.ds(start, size)])
-
-
-def project_kernel(k, left_ref, right_ref, part_ref, out_ref):
-    out_ref[...] = (part_ref[k] + nn(left_ref[...], right_ref[...])).astype(out_ref.dtype)
-
-
-def covar_kernel(at, here_ref, there_ref, own_ref, y_ref, x_ref, xy_ref, both, pack):
-    rows, size = here_ref.shape
+def project_kernel(left_ref, right_ref, mate_left_ref, mate_right_ref, out_ref):
+    total = nn(left_ref[...], right_ref[...])
+    total += nn(mate_left_ref[...], mate_right_ref[...])
+    out_ref[...] = total.astype(out_ref.dtype)
+
+
+def covar_kernel(at, here_ref, there_ref, own_ref, y_ref, x_ref, xy_ref, pack):
+    rows = here_ref.shape[0]
     block = rows // 4
-    both[:, :size] = here_ref[...]
-    both[:, size:] = there_ref[...]
-
-    def part(k):
-        return both[pl.ds(pl.multiple_of(k * block, block), block), :]
+
+    def put(k, i, j):
+        total = 0.0
+        for ref in (here_ref, there_ref):
+            left = ref[pl.ds(pl.multiple_of(i * block, block), block), :]
+            right = ref[pl.ds(pl.multiple_of(j * block, block), block), :]
+            total += nt(left, right)
+        pack[k * block : (k + 1) * block] = total
 
     low = at[0]
-    first, second = part(2 * low), part(2 * low + 1)
-    third = part(2 - 2 * low)
-    pack[0 * block : 1 * block] = nt(first, first)
-    pack[1 * block : 2 * block] = nt(first, second)
-    pack[2 * block : 3 * block] = nt(second, second)
-    pack[3 * block : 4 * block] = nt(second, third)
-    pack[4 * block : 5 * block] = nt(part(low), part(2 + low))
+    first, second, third = 2 * low, 2 * low + 1, 2 - 2 * low
+    put(0, first, first)
+    put(1, first, second)
+    put(2, second, second)
+    put(3, second, third)
+    put(4, low, 2 + low)
     piece = own_ref.shape[0]
 
     def quarter(i, j):
@@ -249,24 +246,23 @@
     rows = projection.shape[0]
     size = data.shape[1] // comps
 
-    def columns(x):
-        start = (x * 2 + (1 - at[0])) * size
-        return flip(lax.dynamic_slice_in_dim(data, start, size, 1), low)
-
-    other = flip(projection, low)
-    away, stay = columns(1 - at[1]), columns(at[1])
-    part = run(own_kernel, shape((2, rows, size), F32), (at, projection, data))
-    sent = run(
-        functools.partial(project_kernel, 0),
-        shape((rows, size), BF),
-        (other, away, part),
-        specs=[VMEM] * 3,
-    )
-    kept = run(
-        functools.partial(project_kernel, 1),
-        shape((rows, size), F32),
-        (other, stay, part),
-        specs=[VMEM] * 3,
+    mate = flip(projection, low)
+
+    def columns(x, core):
+        return lax.dynamic_slice_in_dim(data, (x * 2 + core) * size, size, 1)
+
+    here, away = at[1], 1 - at[1]
+    other = [columns(x, 1 - at[0]) for x in (away, here)]
+    mine = [columns(x, at[0]) for x in (away, here)]
+    other = [flip(block, low) for block in other]
+    sent, kept = (
+        run(
+            project_kernel,
+            shape((rows, size), kind),
+            (projection, mine[k], mate, other[k]),
+            specs=[VMEM] * 4,
+        )
+        for k, kind in enumerate((BF, F32))
     )
     reduced = (kept + flip(sent, across).astype(F32)).astype(BF)
 
@@ -278,7 +274,7 @@
         covar_kernel,
         (shape((piece, block), F32), small, small, small),
         (at, reduced, there),
-        scratch=[pltpu.VMEM((rows, 2 * size), BF), pltpu.VMEM((5 * block, block), F32)],
+        scratch=[pltpu.VMEM((5 * block, block), F32)],
     )
     own = own + flip(by, near).astype(F32)
     own = own + flip(bx, across).astype(F32)
@@ -298,6 +294,7 @@
         (at, packed, mate),
         scratch=[pltpu.VMEM((2, 5 * block, block), F32), pltpu.VMEM((rows, rows), F32)],
     )
+
     whiten, at_xy = lax.optimization_barrier((whiten, at_xy))
 
     count = initial.shape[0] // 2
@@ -336,7 +333,7 @@
             functools.partial(decor_kernel, last),
             outs,
             (at, stacked, flip(stacked, low), *whites),
-            specs=[SMEM, VMEM, VMEM] + [ANY] * 2,
+            specs=[SMEM, VMEM, VMEM] + [HBM] * 2,
             scratch=[
                 pltpu.VMEM((rows, rows), F32),
                 pltpu.VMEM((rows, rows), BF),

time: 92.9 us -> 92.2 us (level)
    unnamed x6 -> x4, local copies, waits for them, and re-layouts: 1.06 us -> 0.01 us
    pallas_call x9 -> x8, Pallas kernels: 15.7 us -> 15 us  [run(): pl.pallas_call(kernel, out_shape=outs, in_specs=specs or [SMEM] + [VMEM]...]
  transfers between devices with their start and end apart: 35 -> 35, of which waited for: 22 -> 23; matrix products, arithmetic and copies ran while one was open for 1% -> 2% of each run, Pallas kernels for 6% -> 5%
where the time goes in v4:
time: 92.2 us; the launch traced here: 92 us
  waiting for transfers between devices  40.6 us (44%)
  starting transfers between devices  33.9 us (37%)
  Pallas kernels  15 us (16%)
  local copies, waits for them, and re-layouts  1.35 us (1%)
    ppermute x35, waiting for transfers between devices, flip(): return lax.ppermute(x, AXES, [(i, i ^ mask) for i in range(count)])  40.6 us
    ppermute x35, starting transfers between devices, flip(): return lax.ppermute(x, AXES, [(i, i ^ mask) for i in range(count)])  33.9 us
    pallas_call x8, Pallas kernels, run(): pl.pallas_call(kernel, out_shape=outs, in_specs=specs or [SMEM] + [VMEM]...  15 us
  transfers between devices with their start and end apart: 35, of which 23 were waited for; matrix products, arithmetic and copies ran while one was open for 2% of the time, Pallas kernels for 5%

profile of v4, /device:TPU:0, one launch (start us, length us, event | category | flops | bytes accessed | tf_op | source)
XLA Modules:
  0.0 92.0 jit_solution(7004255135331713896)
XLA Ops:
  0.6 0.5 collective-permute-start
  1.2 1.3 %constant_dynamic-slice_fusion.1 = (bf16[512,256]{1,0:T(8,128)(2,1)S(1)}, bf16[512,256]{1,0:T(8,128)(2,1)S(1)}, bf16[512,256]{1,0:T(8,128)(2,1)S(1)}, bf16[512,256]{1,0:T(8,128)(2,1)S(1)}) fusion(bf16[512,1024]{1,0:T(8,128)(2,1)} %param.3, s32[]{:T(128)S(6)} %select_n.18, s32[]{:T(128)S(6)} %select_n.16, s32[]{:T(128)S(6)} %select_n.15, s32[]{:T(128)S(6)} %select_n.17), kind=kLoop, calls=%fused_computation.9 | loop fusion | bytes 2097168 | tf_op jit(solution)/shard_map/dynamic_slice | solution.py:252
  2.5 0.1 collective-permute-start.2
  2.6 0.5 collective-permute-start.1
  3.1 1.0 %collective-permute-done.2.mate_right_ref = bf16[512,256]{1,0:T(8,128)(2,1)S(1)} collective-permute-done((bf16[512,256]{1,0:T(8,128)(2,1)S(1)}, bf16[512,256]{1,0:T(8,128)(2,1)S(1)}, u32[]{:S(2)}, u32[]{:S(2)}) %collective-permute-start.2) | collective-permute-done | bytes 262176 | tf_op jit(solution)/shard_map/ppermute | solution.py:33
  4.1 0.4 shard_map.51
  4.5 2.7 %collective-permute-start.3 = (bf16[512,256]{1,0:T(8,128)(2,1)S(1)}, bf16[512,256]{1,0:T(8,128)(2,1)S(1)}, u32[]{:S(2)}, u32[]{:S(2)}) collective-permute-start(bf16[512,256]{1,0:T(8,128)(2,1)S(1)} %shard_map.51), channel_id=1, source_target_pairs={{0,2},{1,3},{2,0},{3,1},{4,6},{5,7},{6,4},{7,5},{8,10},{9,11},{10,... | collective-permute-start | bytes 786440 | tf_op jit(solution)/shard_map/ppermute | solution.py:33
  7.3 0.4 shard_map.50
  7.7 6.4 %collective-permute-done.3 = bf16[512,256]{1,0:T(8,128)(2,1)S(1)} collective-permute-done((bf16[512,256]{1,0:T(8,128)(2,1)S(1)}, bf16[512,256]{1,0:T(8,128)(2,1)S(1)}, u32[]{:S(2)}, u32[]{:S(2)}) %collective-permute-start.3) | collective-permute-done | bytes 262176 | tf_op jit(solution)/shard_map/ppermute | solution.py:33
  14.1 0.1 collective-permute-start.4
  14.2 0.1 pad_add_fusion.at
  14.3 1.4 %collective-permute-done.4.there_ref.refs_1_ = bf16[512,256]{1,0:T(8,128)(2,1)S(1)} collective-permute-done((bf16[512,256]{1,0:T(8,128)(2,1)S(1)}, bf16[512,256]{1,0:T(8,128)(2,1)S(1)}, u32[]{:S(2)}, u32[]{:S(2)}) %collective-permute-start.4) | collective-permute-done | bytes 262176 | tf_op jit(solution)/shard_map/ppermute | solution.py:33
  15.7 0.9 shard_map.52
  16.6 1.8 %collective-permute-start.5 = (bf16[160,128]{1,0:T(8,128)(2,1)S(1)}, bf16[160,128]{1,0:T(8,128)(2,1)S(1)}, u32[]{:S(2)}, u32[]{:S(2)}) collective-permute-start(bf16[160,128]{1,0:T(8,128)(2,1)S(1)} %get-tuple-element.21), channel_id=1, source_target_pairs={{0,4},{1,5},{2,6},{3,7},{4,0},{5,1},{6,2},{7,3},{8,12},{9,13},{10,... | collective-permute-start | bytes 122888 | tf_op jit(solution)/shard_map/ppermute | solution.py:33
  18.5 1.5 %collective-permute-start.6 = (bf16[160,128]{1,0:T(8,128)(2,1)S(1)}, bf16[160,128]{1,0:T(8,128)(2,1)S(1)}, u32[]{:S(2)}, u32[]{:S(2)}) collective-permute-start(bf16[160,128]{1,0:T(8,128)(2,1)S(1)} %get-tuple-element.22), channel_id=1, source_target_pairs={{0,2},{1,3},{2,0},{3,1},{4,6},{5,7},{6,4},{7,5},{8,10},{9,11},{10,... | collective-permute-start | bytes 122888 | tf_op jit(solution)/shard_map/ppermute | solution.py:33
  20.0 0.2 collective-permute-start.7
  20.2 0.5 collective-permute-done.5
  20.7 2.2 %collective-permute-done.6 = bf16[160,128]{1,0:T(8,128)(2,1)S(1)} collective-permute-done((bf16[160,128]{1,0:T(8,128)(2,1)S(1)}, bf16[160,128]{1,0:T(8,128)(2,1)S(1)}, u32[]{:S(2)}, u32[]{:S(2)}) %collective-permute-start.6) | collective-permute-done | bytes 40992 | tf_op jit(solution)/shard_map/ppermute | solution.py:33
  22.9 2.0 %collective-permute-done.7 = bf16[160,128]{1,0:T(8,128)(2,1)S(1)} collective-permute-done((bf16[160,128]{1,0:T(8,128)(2,1)S(1)}, bf16[160,128]{1,0:T(8,128)(2,1)S(1)}, u32[]{:S(2)}, u32[]{:S(2)}) %collective-permute-start.7) | collective-permute-done | bytes 40992 | tf_op jit(solution)/shard_map/ppermute | solution.py:33
  24.9 3.7 %collective-permute-start.10 = (bf16[160,128]{1,0:T(8,128)(2,1)S(1)}, bf16[160,128]{1,0:T(8,128)(2,1)S(1)}, u32[]{:S(2)}, u32[]{:S(2)}) collective-permute-start(bf16[160,128]{1,0:T(8,128)(2,1)S(1)} %convert_element_type.65), channel_id=1, source_target_pairs={{0,24},{1,25},{2,26},{3,27},{4,28},{5,29},{6,30},{7,31},{8,16},{9,... | collective-permute-start | bytes 122888 | tf_op jit(solution)/shard_map/ppermute | solution.py:33
  28.6 0.8 collective-permute-start.8
  29.4 0.5 collective-permute-start.15
  29.9 0.5 collective-permute-start.14
  30.4 0.5 collective-permute-done.10
  30.9 2.6 %collective-permute-done.9 = bf16[160,128]{1,0:T(8,128)(2,1)S(1)} collective-permute-done((bf16[160,128]{1,0:T(8,128)(2,1)S(1)}, bf16[160,128]{1,0:T(8,128)(2,1)S(1)}, u32[]{:S(2)}, u32[]{:S(2)}) %collective-permute-start.9) | collective-permute-done | bytes 40992 | tf_op jit(solution)/shard_map/ppermute | solution.py:33
  33.5 0.5 collective-permute-start.13
  34.1 1.5 %collective-permute-start.12 = (bf16[160,128]{1,0:T(8,128)(2,1)S(1)}, bf16[160,128]{1,0:T(8,128)(2,1)S(1)}, u32[]{:S(2)}, u32[]{:S(2)}) collective-permute-start(bf16[160,128]{1,0:T(8,128)(2,1)S(1)} %add_convert_fusion.3), channel_id=1, source_target_pairs={{0,2},{1,3},{2,0},{3,1},{4,6},{5,7},{6,4},{7,5},{8,10},{9,11},{10,... | collective-permute-start | bytes 122888 | tf_op jit(solution)/shard_map/ppermute | solution.py:33
  35.6 1.5 %collective-permute-start.11 = (bf16[160,128]{1,0:T(8,128)(2,1)S(1)}, bf16[160,128]{1,0:T(8,128)(2,1)S(1)}, u32[]{:S(2)}, u32[]{:S(2)}) collective-permute-start(bf16[160,128]{1,0:T(8,128)(2,1)S(1)} %add_convert_fusion.3), channel_id=1, source_target_pairs={{0,4},{1,5},{2,6},{3,7},{4,0},{5,1},{6,2},{7,3},{8,12},{9,13},{10,... | collective-permute-start | bytes 122888 | tf_op jit(solution)/shard_map/ppermute | solution.py:33
  37.1 1.4 %collective-permute-done.13 = bf16[160,128]{1,0:T(8,128)(2,1)S(1)} collective-permute-done((bf16[160,128]{1,0:T(8,128)(2,1)S(1)}, bf16[160,128]{1,0:T(8,128)(2,1)S(1)}, u32[]{:S(2)}, u32[]{:S(2)}) %collective-permute-start.13) | collective-permute-done | bytes 40992 | tf_op jit(solution)/shard_map/ppermute | solution.py:33
  38.5 0.4 collective-permute-start.17
  39.0 3.2 %collective-permute-done.11 = bf16[160,128]{1,0:T(8,128)(2,1)S(1)} collective-permute-done((bf16[160,128]{1,0:T(8,128)(2,1)S(1)}, bf16[160,128]{1,0:T(8,128)(2,1)S(1)}, u32[]{:S(2)}, u32[]{:S(2)}) %collective-permute-start.11) | collective-permute-done | bytes 40992 | tf_op jit(solution)/shard_map/ppermute | solution.py:33
  42.2 0.1 collective-permute-start.16
  42.3 0.5 collective-permute-start.18
  42.8 0.1 collective-permute-start.19
  42.9 0.8 collective-permute-done.16.other_ref
  43.7 2.7 %shard_map.53.whiten_ref = bf16[512,512]{1,0:T(8,128)(2,1)S(1)} custom-call(s32[3]{0:T(128)S(1)} %pad_add_fusion.at, bf16[4,160,128]{2,1,0:T(8,128)(2,1)S(1)} %pad_maximum_fusion.2.mine_ref, bf16[4,160,128]{2,1,0:T(8,128)(2,1)S(1)} %collective-permute-done.16.other_ref), custom_call_target="tpu_custom_call" | custom-call | tf_op jit(solution)/shard_map/pallas_call | solution.py:58
  46.4 0.2 collective-permute-start.20
  46.6 1.2 %shard_map.54 = (bf16[4,512,256]{2,1,0:T(8,128)(2,1)S(1)}, f32[64,512]{1,0:T(8,128)S(1)}, f32[64,1]{1,0:T(8,128)S(1)}) custom-call(bf16[512,512]{1,0:T(8,128)(2,1)S(1)} %shard_map.53.whiten_ref, bf16[512,256]{1,0:T(8,128)(2,1)S(1)} %add_convert_fusion.here_ref.refs_0_, bf16[512,256]{1,0:T(8,128)(2,1)S(1)} %collective-permute-done.4.there_ref.refs_1_, ...), custom_call_target="tpu_custom_call" | custom-call | tf_op jit(solution)/shard_map/pallas_call | solution.py:58
  47.8 0.2 collective-permute-done.20.refs_3_
  48.0 1.6 %shard_map.55 = (bf16[4,512,256]{2,1,0:T(8,128)(2,1)S(1)}, f32[64,512]{1,0:T(8,128)S(1)}, f32[64,1]{1,0:T(8,128)}) custom-call(bf16[512,512]{1,0:T(8,128)(2,1)S(1)} %shard_map.53.whiten_ref, bf16[512,256]{1,0:T(8,128)(2,1)S(1)} %collective-permute-done.18.refs_0_, bf16[512,256]{1,0:T(8,128)(2,1)S(1)} %collective-permute-done.19.refs_1_, ...), custom_call_target="tpu_custom_call" | custom-call | tf_op jit(solution)/shard_map/pallas_call | solution.py:58
  49.6 2.5 %collective-permute-start.23 = (bf16[64,512]{1,0:T(8,128)(2,1)S(1)}, bf16[64,512]{1,0:T(8,128)(2,1)S(1)}, u32[]{:S(2)}, u32[]{:S(2)}) collective-permute-start(bf16[64,512]{1,0:T(8,128)(2,1)S(1)} %convert_element_type.70), channel_id=1, source_target_pairs={{0,24},{1,25},{2,26},{3,27},{4,28},{5,29},{6,30},{7,31},{8,16},{9,... | collective-permute-start | bytes 196616 | tf_op jit(solution)/shard_map/ppermute | solution.py:33
  52.1 2.0 %collective-permute-start.21 = (bf16[64,512]{1,0:T(8,128)(2,1)S(1)}, bf16[64,512]{1,0:T(8,128)(2,1)S(1)}, u32[]{:S(2)}, u32[]{:S(2)}) collective-permute-start(bf16[64,512]{1,0:T(8,128)(2,1)S(1)} %convert_element_type.70), channel_id=1, source_target_pairs={{0,8},{1,9},{2,10},{3,11},{4,12},{5,13},{6,14},{7,15},{8,0},{9,1},... | collective-permute-start | bytes 196616 | tf_op jit(solution)/shard_map/ppermute | solution.py:33
  54.1 2.4 %collective-permute-done.23 = bf16[64,512]{1,0:T(8,128)(2,1)S(1)} collective-permute-done((bf16[64,512]{1,0:T(8,128)(2,1)S(1)}, bf16[64,512]{1,0:T(8,128)(2,1)S(1)}, u32[]{:S(2)}, u32[]{:S(2)}) %collective-permute-start.23) | collective-permute-done | bytes 65568 | tf_op jit(solution)/shard_map/ppermute | solution.py:33
  56.5 2.0 %collective-permute-done.22 = bf16[64,512]{1,0:T(8,128)(2,1)S(1)} collective-permute-done((bf16[64,512]{1,0:T(8,128)(2,1)S(1)}, bf16[64,512]{1,0:T(8,128)(2,1)S(1)}, u32[]{:S(2)}, u32[]{:S(2)}) %collective-permute-start.22) | collective-permute-done | bytes 65568 | tf_op jit(solution)/shard_map/ppermute | solution.py:33
  58.5 0.7 collective-permute-start.26
  59.3 1.4 %collective-permute-start.25 = (bf16[64,512]{1,0:T(8,128)(2,1)S(1)}, bf16[64,512]{1,0:T(8,128)(2,1)S(1)}, u32[]{:S(2)}, u32[]{:S(2)}) collective-permute-start(bf16[64,512]{1,0:T(8,128)(2,1)S(1)} %add_convert_fusion.2), channel_id=1, source_target_pairs={{0,2},{1,3},{2,0},{3,1},{4,6},{5,7},{6,4},{7,5},{8,10},{9,11},{10,... | collective-permute-start | bytes 196616 | tf_op jit(solution)/shard_map/ppermute | solution.py:33
  60.7 1.4 %collective-permute-start.24 = (bf16[64,512]{1,0:T(8,128)(2,1)S(1)}, bf16[64,512]{1,0:T(8,128)(2,1)S(1)}, u32[]{:S(2)}, u32[]{:S(2)}) collective-permute-start(bf16[64,512]{1,0:T(8,128)(2,1)S(1)} %add_convert_fusion.2), channel_id=1, source_target_pairs={{0,4},{1,5},{2,6},{3,7},{4,0},{5,1},{6,2},{7,3},{8,12},{9,13},{10,... | collective-permute-start | bytes 196616 | tf_op jit(solution)/shard_map/ppermute | solution.py:33
  62.1 2.1 %collective-permute-done.26 = bf16[64,512]{1,0:T(8,128)(2,1)S(1)} collective-permute-done((bf16[64,512]{1,0:T(8,128)(2,1)S(1)}, bf16[64,512]{1,0:T(8,128)(2,1)S(1)}, u32[]{:S(2)}, u32[]{:S(2)}) %collective-permute-start.26) | collective-permute-done | bytes 65568 | tf_op jit(solution)/shard_map/ppermute | solution.py:33
  64.2 0.8 collective-permute-done.24
  65.1 1.5 %collective-permute-done.27.other_ref = bf16[4,64,512]{2,1,0:T(8,128)(2,1)S(1)} collective-permute-done((bf16[4,64,512]{2,1,0:T(8,128)(2,1)S(1)}, bf16[4,64,512]{2,1,0:T(8,128)(2,1)S(1)}, u32[]{:S(2)}, u32[]{:S(2)}) %collective-permute-start.27) | collective-permute-done | bytes 262176 | tf_op jit(solution)/shard_map/ppermute | solution.py:33
  66.6 3.9 %shard_map.56 = f32[64,512]{1,0:T(8,128)S(1)} custom-call(s32[3]{0:T(128)S(1)} %pad_add_fusion.at, bf16[4,64,512]{2,1,0:T(8,128)(2,1)S(1)} %pad_maximum_fusion.mine_ref, bf16[4,64,512]{2,1,0:T(8,128)(2,1)S(1)} %collective-permute-done.27.other_ref, bf16[4,512,256]{2,1,0:T(8,128)(2,1)S(1)} %get-tuple-element.36.refs_0_, ...), custom_call_target="tpu_custom_call" | custom-call | tf_op jit(solution)/shard_map/pallas_call | solution.py:58
  70.6 2.6 %collective-permute-start.30 = (bf16[64,512]{1,0:T(8,128)(2,1)S(1)}, bf16[64,512]{1,0:T(8,128)(2,1)S(1)}, u32[]{:S(2)}, u32[]{:S(2)}) collective-permute-start(bf16[64,512]{1,0:T(8,128)(2,1)S(1)} %convert_element_type.75), channel_id=1, source_target_pairs={{0,24},{1,25},{2,26},{3,27},{4,28},{5,29},{6,30},{7,31},{8,16},{9,... | collective-permute-start | bytes 196616 | tf_op jit(solution)/shard_map/ppermute | solution.py:33
  73.2 1.8 %collective-permute-start.28 = (bf16[64,512]{1,0:T(8,128)(2,1)S(1)}, bf16[64,512]{1,0:T(8,128)(2,1)S(1)}, u32[]{:S(2)}, u32[]{:S(2)}) collective-permute-start(bf16[64,512]{1,0:T(8,128)(2,1)S(1)} %convert_element_type.75), channel_id=1, source_target_pairs={{0,8},{1,9},{2,10},{3,11},{4,12},{5,13},{6,14},{7,15},{8,0},{9,1},... | collective-permute-start | bytes 196616 | tf_op jit(solution)/shard_map/ppermute | solution.py:33
  75.0 2.3 %collective-permute-done.30 = bf16[64,512]{1,0:T(8,128)(2,1)S(1)} collective-permute-done((bf16[64,512]{1,0:T(8,128)(2,1)S(1)}, bf16[64,512]{1,0:T(8,128)(2,1)S(1)}, u32[]{:S(2)}, u32[]{:S(2)}) %collective-permute-start.30) | collective-permute-done | bytes 65568 | tf_op jit(solution)/shard_map/ppermute | solution.py:33
  77.4 2.0 %collective-permute-done.29 = bf16[64,512]{1,0:T(8,128)(2,1)S(1)} collective-permute-done((bf16[64,512]{1,0:T(8,128)(2,1)S(1)}, bf16[64,512]{1,0:T(8,128)(2,1)S(1)}, u32[]{:S(2)}, u32[]{:S(2)}) %collective-permute-start.29) | collective-permute-done | bytes 65568 | tf_op jit(solution)/shard_map/ppermute | solution.py:33
  79.4 1.5 %collective-permute-start.33 = (bf16[64,512]{1,0:T(8,128)(2,1)S(1)}, bf16[64,512]{1,0:T(8,128)(2,1)S(1)}, u32[]{:S(2)}, u32[]{:S(2)}) collective-permute-start(bf16[64,512]{1,0:T(8,128)(2,1)S(1)} %add_convert_fusion.1), channel_id=1, source_target_pairs={{0,6},{1,7},{2,4},{3,5},{4,2},{5,3},{6,0},{7,1},{8,14},{9,15},{10,... | collective-permute-start | bytes 196616 | tf_op jit(solution)/shard_map/ppermute | solution.py:33
  80.9 1.4 %collective-permute-start.32 = (bf16[64,512]{1,0:T(8,128)(2,1)S(1)}, bf16[64,512]{1,0:T(8,128)(2,1)S(1)}, u32[]{:S(2)}, u32[]{:S(2)}) collective-permute-start(bf16[64,512]{1,0:T(8,128)(2,1)S(1)} %add_convert_fusion.1), channel_id=1, source_target_pairs={{0,2},{1,3},{2,0},{3,1},{4,6},{5,7},{6,4},{7,5},{8,10},{9,11},{10,... | collective-permute-start | bytes 196616 | tf_op jit(solution)/shard_map/ppermute | solution.py:33
  82.3 0.7 collective-permute-start.31
  83.0 2.2 %collective-permute-done.33 = bf16[64,512]{1,0:T(8,128)(2,1)S(1)} collective-permute-done((bf16[64,512]{1,0:T(8,128)(2,1)S(1)}, bf16[64,512]{1,0:T(8,128)(2,1)S(1)}, u32[]{:S(2)}, u32[]{:S(2)}) %collective-permute-start.33) | collective-permute-done | bytes 65568 | tf_op jit(solution)/shard_map/ppermute | solution.py:33
  85.2 0.5 collective-permute-done.32
  85.7 0.9 collective-permute-done.31
  86.6 0.1 collective-permute-start.34
  86.7 1.5 %collective-permute-done.34.other_ref = bf16[4,64,512]{2,1,0:T(8,128)(2,1)S(1)} collective-permute-done((bf16[4,64,512]{2,1,0:T(8,128)(2,1)S(1)}, bf16[4,64,512]{2,1,0:T(8,128)(2,1)S(1)}, u32[]{:S(2)}, u32[]{:S(2)}) %collective-permute-start.34) | collective-permute-done | bytes 262176 | tf_op jit(solution)/shard_map/ppermute | solution.py:33
  88.2 3.8 %shard_map.57 = (f32[128,512]{1,0:T(8,128)}, bf16[128,1024]{1,0:T(8,128)(2,1)}) custom-call(s32[3]{0:T(128)S(1)} %pad_add_fusion.at, bf16[4,64,512]{2,1,0:T(8,128)(2,1)S(1)} %pad_maximum_fusion.1.mine_ref, bf16[4,64,512]{2,1,0:T(8,128)(2,1)S(1)} %collective-permute-done.34.other_ref, bf16[4,512,256]{2,1,0:T(8,128)(2,1)S(1)} %get-tuple-element.36.refs_0_, ...), custom_call_target="tpu_custom_call" | custom-call | tf_op jit(solution)/shard_map/pallas_call | solution.py:58
  (32 shorter events, 0.4 us)
Async XLA Ops:
  0.6 45.9 %copy-start = (f32[128,512]{1,0:T(8,128)S(1)}, f32[128,512]{1,0:T(8,128)}, u32[]{:S(2)}) copy-start(f32[128,512]{1,0:T(8,128)} %param.5) | copy-start | bytes 786436
  0.6 3.5 %collective-permute-start = (bf16[512,512]{1,0:T(8,128)(2,1)}, bf16[512,512]{1,0:T(8,128)(2,1)S(1)}, u32[]{:S(2)}, u32[]{:S(2)}) collective-permute-start(bf16[512,512]{1,0:T(8,128)(2,1)} %left_ref.3), channel_id=1, source_target_pairs={{0,1},{1,0},{2,3},{3,2},{4,5},{5,4},{6,7},{7,6},{8,9},{9,8},{10,11... | collective-permute-start | bytes 1572872 | tf_op jit(solution)/shard_map/ppermute | solution.py:33
  1.2 2.9 %copy-start.1 = (bf16[512,512]{1,0:T(8,128)(2,1)S(1)}, bf16[512,512]{1,0:T(8,128)(2,1)}, u32[]{:S(2)}) copy-start(bf16[512,512]{1,0:T(8,128)(2,1)} %left_ref.3) | copy-start | bytes 1572868
  2.5 1.6 %collective-permute-start.2 = (bf16[512,256]{1,0:T(8,128)(2,1)S(1)}, bf16[512,256]{1,0:T(8,128)(2,1)S(1)}, u32[]{:S(2)}, u32[]{:S(2)}) collective-permute-start(bf16[512,256]{1,0:T(8,128)(2,1)S(1)} %get-tuple-element.38), channel_id=1, source_target_pairs={{0,1},{1,0},{2,3},{3,2},{4,5},{5,4},{6,7},{7,6},{8,9},{9,8},{10,11... | collective-permute-start | bytes 786440 | tf_op jit(solution)/shard_map/ppermute | solution.py:33
  2.6 4.6 %collective-permute-start.1 = (bf16[512,256]{1,0:T(8,128)(2,1)S(1)}, bf16[512,256]{1,0:T(8,128)(2,1)S(1)}, u32[]{:S(2)}, u32[]{:S(2)}) collective-permute-start(bf16[512,256]{1,0:T(8,128)(2,1)S(1)} %get-tuple-element.39), channel_id=1, source_target_pairs={{0,1},{1,0},{2,3},{3,2},{4,5},{5,4},{6,7},{7,6},{8,9},{9,8},{10,11... | collective-permute-start | bytes 786440 | tf_op jit(solution)/shard_map/ppermute | solution.py:33
  4.5 9.5 %collective-permute-start.3 = (bf16[512,256]{1,0:T(8,128)(2,1)S(1)}, bf16[512,256]{1,0:T(8,128)(2,1)S(1)}, u32[]{:S(2)}, u32[]{:S(2)}) collective-permute-start(bf16[512,256]{1,0:T(8,128)(2,1)S(1)} %shard_map.51), channel_id=1, source_target_pairs={{0,2},{1,3},{2,0},{3,1},{4,6},{5,7},{6,4},{7,5},{8,10},{9,11},{10,... | collective-permute-start | bytes 786440 | tf_op jit(solution)/shard_map/ppermute | solution.py:33
  14.1 1.6 %collective-permute-start.4 = (bf16[512,256]{1,0:T(8,128)(2,1)S(1)}, bf16[512,256]{1,0:T(8,128)(2,1)S(1)}, u32[]{:S(2)}, u32[]{:S(2)}) collective-permute-start(bf16[512,256]{1,0:T(8,128)(2,1)S(1)} %add_convert_fusion.here_ref.refs_0_), channel_id=1, source_target_pairs={{0,1},{1,0},{2,3},{3,2},{4,5},{5,4},{6,7},{7,6},{8,9},{9,8},{10,11... | collective-permute-start | bytes 786440 | tf_op jit(solution)/shard_map/ppermute | solution.py:33
  16.6 4.1 %collective-permute-start.5 = (bf16[160,128]{1,0:T(8,128)(2,1)S(1)}, bf16[160,128]{1,0:T(8,128)(2,1)S(1)}, u32[]{:S(2)}, u32[]{:S(2)}) collective-permute-start(bf16[160,128]{1,0:T(8,128)(2,1)S(1)} %get-tuple-element.21), channel_id=1, source_target_pairs={{0,4},{1,5},{2,6},{3,7},{4,0},{5,1},{6,2},{7,3},{8,12},{9,13},{10,... | collective-permute-start | bytes 122888 | tf_op jit(solution)/shard_map/ppermute | solution.py:33
  18.5 4.4 %collective-permute-start.6 = (bf16[160,128]{1,0:T(8,128)(2,1)S(1)}, bf16[160,128]{1,0:T(8,128)(2,1)S(1)}, u32[]{:S(2)}, u32[]{:S(2)}) collective-permute-start(bf16[160,128]{1,0:T(8,128)(2,1)S(1)} %get-tuple-element.22), channel_id=1, source_target_pairs={{0,2},{1,3},{2,0},{3,1},{4,6},{5,7},{6,4},{7,5},{8,10},{9,11},{10,... | collective-permute-start | bytes 122888 | tf_op jit(solution)/shard_map/ppermute | solution.py:33
  20.0 4.9 %collective-permute-start.7 = (bf16[160,128]{1,0:T(8,128)(2,1)S(1)}, bf16[160,128]{1,0:T(8,128)(2,1)S(1)}, u32[]{:S(2)}, u32[]{:S(2)}) collective-permute-start(bf16[160,128]{1,0:T(8,128)(2,1)S(1)} %get-tuple-element.23), channel_id=1, source_target_pairs={{0,6},{1,7},{2,4},{3,5},{4,2},{5,3},{6,0},{7,1},{8,14},{9,15},{10,... | collective-permute-start | bytes 122888 | tf_op jit(solution)/shard_map/ppermute | solution.py:33
  24.9 6.0 %collective-permute-start.10 = (bf16[160,128]{1,0:T(8,128)(2,1)S(1)}, bf16[160,128]{1,0:T(8,128)(2,1)S(1)}, u32[]{:S(2)}, u32[]{:S(2)}) collective-permute-start(bf16[160,128]{1,0:T(8,128)(2,1)S(1)} %convert_element_type.65), channel_id=1, source_target_pairs={{0,24},{1,25},{2,26},{3,27},{4,28},{5,29},{6,30},{7,31},{8,16},{9,... | collective-permute-start | bytes 122888 | tf_op jit(solution)/shard_map/ppermute | solution.py:33
  28.6 4.9 %collective-permute-start.9 = (bf16[160,128]{1,0:T(8,128)(2,1)S(1)}, bf16[160,128]{1,0:T(8,128)(2,1)S(1)}, u32[]{:S(2)}, u32[]{:S(2)}) collective-permute-start(bf16[160,128]{1,0:T(8,128)(2,1)S(1)} %convert_element_type.65), channel_id=1, source_target_pairs={{0,16},{1,17},{2,18},{3,19},{4,20},{5,21},{6,22},{7,23},{8,24},{9,... | collective-permute-start | bytes 122888 | tf_op jit(solution)/shard_map/ppermute | solution.py:33
  28.6 4.9 %collective-permute-start.8 = (bf16[160,128]{1,0:T(8,128)(2,1)S(1)}, bf16[160,128]{1,0:T(8,128)(2,1)S(1)}, u32[]{:S(2)}, u32[]{:S(2)}) collective-permute-start(bf16[160,128]{1,0:T(8,128)(2,1)S(1)} %convert_element_type.65), channel_id=1, source_target_pairs={{0,8},{1,9},{2,10},{3,11},{4,12},{5,13},{6,14},{7,15},{8,0},{9,1},... | collective-permute-start | bytes 122888 | tf_op jit(solution)/shard_map/ppermute | solution.py:33
  29.4 12.8 %collective-permute-start.15 = (bf16[512,256]{1,0:T(8,128)(2,1)S(1)}, bf16[512,256]{1,0:T(8,128)(2,1)S(1)}, u32[]{:S(2)}, u32[]{:S(2)}) collective-permute-start(bf16[512,256]{1,0:T(8,128)(2,1)S(1)} %add_convert_fusion.here_ref.refs_0_), channel_id=1, source_target_pairs={{0,4},{1,5},{2,6},{3,7},{4,0},{5,1},{6,2},{7,3},{8,12},{9,13},{10,... | collective-permute-start | bytes 786440 | tf_op jit(solution)/shard_map/ppermute | solution.py:33
  29.9 12.3 %collective-permute-start.14 = (bf16[512,256]{1,0:T(8,128)(2,1)S(1)}, bf16[512,256]{1,0:T(8,128)(2,1)S(1)}, u32[]{:S(2)}, u32[]{:S(2)}) collective-permute-start(bf16[512,256]{1,0:T(8,128)(2,1)S(1)} %add_convert_fusion.here_ref.refs_0_), channel_id=1, source_target_pairs={{0,2},{1,3},{2,0},{3,1},{4,6},{5,7},{6,4},{7,5},{8,10},{9,11},{10,... | collective-permute-start | bytes 786440 | tf_op jit(solution)/shard_map/ppermute | solution.py:33
  33.5 5.0 %collective-permute-start.13 = (bf16[160,128]{1,0:T(8,128)(2,1)S(1)}, bf16[160,128]{1,0:T(8,128)(2,1)S(1)}, u32[]{:S(2)}, u32[]{:S(2)}) collective-permute-start(bf16[160,128]{1,0:T(8,128)(2,1)S(1)} %add_convert_fusion.3), channel_id=1, source_target_pairs={{0,6},{1,7},{2,4},{3,5},{4,2},{5,3},{6,0},{7,1},{8,14},{9,15},{10,... | collective-permute-start | bytes 122888 | tf_op jit(solution)/shard_map/ppermute | solution.py:33
  34.1 4.9 %collective-permute-start.12 = (bf16[160,128]{1,0:T(8,128)(2,1)S(1)}, bf16[160,128]{1,0:T(8,128)(2,1)S(1)}, u32[]{:S(2)}, u32[]{:S(2)}) collective-permute-start(bf16[160,128]{1,0:T(8,128)(2,1)S(1)} %add_convert_fusion.3), channel_id=1, source_target_pairs={{0,2},{1,3},{2,0},{3,1},{4,6},{5,7},{6,4},{7,5},{8,10},{9,11},{10,... | collective-permute-start | bytes 122888 | tf_op jit(solution)/shard_map/ppermute | solution.py:33
  35.6 6.6 %collective-permute-start.11 = (bf16[160,128]{1,0:T(8,128)(2,1)S(1)}, bf16[160,128]{1,0:T(8,128)(2,1)S(1)}, u32[]{:S(2)}, u32[]{:S(2)}) collective-permute-start(bf16[160,128]{1,0:T(8,128)(2,1)S(1)} %add_convert_fusion.3), channel_id=1, source_target_pairs={{0,4},{1,5},{2,6},{3,7},{4,0},{5,1},{6,2},{7,3},{8,12},{9,13},{10,... | collective-permute-start | bytes 122888 | tf_op jit(solution)/shard_map/ppermute | solution.py:33
  38.5 7.8 %collective-permute-start.17 = (bf16[512,256]{1,0:T(8,128)(2,1)S(1)}, bf16[512,256]{1,0:T(8,128)(2,1)S(1)}, u32[]{:S(2)}, u32[]{:S(2)}) collective-permute-start(bf16[512,256]{1,0:T(8,128)(2,1)S(1)} %add_convert_fusion.here_ref.refs_0_), channel_id=1, source_target_pairs={{0,6},{1,7},{2,4},{3,5},{4,2},{5,3},{6,0},{7,1},{8,14},{9,15},{10,... | collective-permute-start | bytes 786440 | tf_op jit(solution)/shard_map/ppermute | solution.py:33
  42.2 1.5 %collective-permute-start.16 = (bf16[4,160,128]{2,1,0:T(8,128)(2,1)S(1)}, bf16[4,160,128]{2,1,0:T(8,128)(2,1)S(1)}, u32[]{:S(2)}, u32[]{:S(2)}) collective-permute-start(bf16[4,160,128]{2,1,0:T(8,128)(2,1)S(1)} %pad_maximum_fusion.2.mine_ref), channel_id=1, source_target_pairs={{0,1},{1,0},{2,3},{3,2},{4,5},{5,4},{6,7},{7,6},{8,9},{9,8},{10,11... | collective-permute-start | bytes 491528 | tf_op jit(solution)/shard_map/ppermute | solution.py:33
  42.3 5.5 %collective-permute-start.18 = (bf16[512,256]{1,0:T(8,128)(2,1)S(1)}, bf16[512,256]{1,0:T(8,128)(2,1)S(1)}, u32[]{:S(2)}, u32[]{:S(2)}) collective-permute-start(bf16[512,256]{1,0:T(8,128)(2,1)S(1)} %collective-permute-done.14.refs_2_), channel_id=1, source_target_pairs={{0,1},{1,0},{2,3},{3,2},{4,5},{5,4},{6,7},{7,6},{8,9},{9,8},{10,11... | collective-permute-start | bytes 786440 | tf_op jit(solution)/shard_map/ppermute | solution.py:33
  42.8 5.0 %collective-permute-start.19 = (bf16[512,256]{1,0:T(8,128)(2,1)S(1)}, bf16[512,256]{1,0:T(8,128)(2,1)S(1)}, u32[]{:S(2)}, u32[]{:S(2)}) collective-permute-start(bf16[512,256]{1,0:T(8,128)(2,1)S(1)} %collective-permute-done.15.refs_3_), channel_id=1, source_target_pairs={{0,1},{1,0},{2,3},{3,2},{4,5},{5,4},{6,7},{7,6},{8,9},{9,8},{10,11... | collective-permute-start | bytes 786440 | tf_op jit(solution)/shard_map/ppermute | solution.py:33
  46.4 1.6 %collective-permute-start.20 = (bf16[512,256]{1,0:T(8,128)(2,1)S(1)}, bf16[512,256]{1,0:T(8,128)(2,1)S(1)}, u32[]{:S(2)}, u32[]{:S(2)}) collective-permute-start(bf16[512,256]{1,0:T(8,128)(2,1)S(1)} %collective-permute-done.17.refs_2_), channel_id=1, source_target_pairs={{0,1},{1,0},{2,3},{3,2},{4,5},{5,4},{6,7},{7,6},{8,9},{9,8},{10,11... | collective-permute-start | bytes 786440 | tf_op jit(solution)/shard_map/ppermute | solution.py:33
  49.6 6.9 %collective-permute-start.23 = (bf16[64,512]{1,0:T(8,128)(2,1)S(1)}, bf16[64,512]{1,0:T(8,128)(2,1)S(1)}, u32[]{:S(2)}, u32[]{:S(2)}) collective-permute-start(bf16[64,512]{1,0:T(8,128)(2,1)S(1)} %convert_element_type.70), channel_id=1, source_target_pairs={{0,24},{1,25},{2,26},{3,27},{4,28},{5,29},{6,30},{7,31},{8,16},{9,... | collective-permute-start | bytes 196616 | tf_op jit(solution)/shard_map/ppermute | solution.py:33
  52.1 6.4 %collective-permute-start.22 = (bf16[64,512]{1,0:T(8,128)(2,1)S(1)}, bf16[64,512]{1,0:T(8,128)(2,1)S(1)}, u32[]{:S(2)}, u32[]{:S(2)}) collective-permute-start(bf16[64,512]{1,0:T(8,128)(2,1)S(1)} %convert_element_type.70), channel_id=1, source_target_pairs={{0,16},{1,17},{2,18},{3,19},{4,20},{5,21},{6,22},{7,23},{8,24},{9,... | collective-permute-start | bytes 196616 | tf_op jit(solution)/shard_map/ppermute | solution.py:33
  52.1 6.4 %collective-permute-start.21 = (bf16[64,512]{1,0:T(8,128)(2,1)S(1)}, bf16[64,512]{1,0:T(8,128)(2,1)S(1)}, u32[]{:S(2)}, u32[]{:S(2)}) collective-permute-start(bf16[64,512]{1,0:T(8,128)(2,1)S(1)} %convert_element_type.70), channel_id=1, source_target_pairs={{0,8},{1,9},{2,10},{3,11},{4,12},{5,13},{6,14},{7,15},{8,0},{9,1},... | collective-permute-start | bytes 196616 | tf_op jit(solution)/shard_map/ppermute | solution.py:33
  58.5 5.7 %collective-permute-start.26 = (bf16[64,512]{1,0:T(8,128)(2,1)S(1)}, bf16[64,512]{1,0:T(8,128)(2,1)S(1)}, u32[]{:S(2)}, u32[]{:S(2)}) collective-permute-start(bf16[64,512]{1,0:T(8,128)(2,1)S(1)} %add_convert_fusion.2), channel_id=1, source_target_pairs={{0,6},{1,7},{2,4},{3,5},{4,2},{5,3},{6,0},{7,1},{8,14},{9,15},{10,... | collective-permute-start | bytes 196616 | tf_op jit(solution)/shard_map/ppermute | solution.py:33
  59.3 4.9 %collective-permute-start.25 = (bf16[64,512]{1,0:T(8,128)(2,1)S(1)}, bf16[64,512]{1,0:T(8,128)(2,1)S(1)}, u32[]{:S(2)}, u32[]{:S(2)}) collective-permute-start(bf16[64,512]{1,0:T(8,128)(2,1)S(1)} %add_convert_fusion.2), channel_id=1, source_target_pairs={{0,2},{1,3},{2,0},{3,1},{4,6},{5,7},{6,4},{7,5},{8,10},{9,11},{10,... | collective-permute-start | bytes 196616 | tf_op jit(solution)/shard_map/ppermute | solution.py:33
  60.7 4.3 %collective-permute-start.24 = (bf16[64,512]{1,0:T(8,128)(2,1)S(1)}, bf16[64,512]{1,0:T(8,128)(2,1)S(1)}, u32[]{:S(2)}, u32[]{:S(2)}) collective-permute-start(bf16[64,512]{1,0:T(8,128)(2,1)S(1)} %add_convert_fusion.2), channel_id=1, source_target_pairs={{0,4},{1,5},{2,6},{3,7},{4,0},{5,1},{6,2},{7,3},{8,12},{9,13},{10,... | collective-permute-start | bytes 196616 | tf_op jit(solution)/shard_map/ppermute | solution.py:33
  65.0 1.6 %collective-permute-start.27 = (bf16[4,64,512]{2,1,0:T(8,128)(2,1)S(1)}, bf16[4,64,512]{2,1,0:T(8,128)(2,1)S(1)}, u32[]{:S(2)}, u32[]{:S(2)}) collective-permute-start(bf16[4,64,512]{2,1,0:T(8,128)(2,1)S(1)} %pad_maximum_fusion.mine_ref), channel_id=1, source_target_pairs={{0,1},{1,0},{2,3},{3,2},{4,5},{5,4},{6,7},{7,6},{8,9},{9,8},{10,11... | collective-permute-start | bytes 786440 | tf_op jit(solution)/shard_map/ppermute | solution.py:33
  70.6 6.8 %collective-permute-start.30 = (bf16[64,512]{1,0:T(8,128)(2,1)S(1)}, bf16[64,512]{1,0:T(8,128)(2,1)S(1)}, u32[]{:S(2)}, u32[]{:S(2)}) collective-permute-start(bf16[64,512]{1,0:T(8,128)(2,1)S(1)} %convert_element_type.75), channel_id=1, source_target_pairs={{0,24},{1,25},{2,26},{3,27},{4,28},{5,29},{6,30},{7,31},{8,16},{9,... | collective-permute-start | bytes 196616 | tf_op jit(solution)/shard_map/ppermute | solution.py:33
  73.2 6.2 %collective-permute-start.29 = (bf16[64,512]{1,0:T(8,128)(2,1)S(1)}, bf16[64,512]{1,0:T(8,128)(2,1)S(1)}, u32[]{:S(2)}, u32[]{:S(2)}) collective-permute-start(bf16[64,512]{1,0:T(8,128)(2,1)S(1)} %convert_element_type.75), channel_id=1, source_target_pairs={{0,16},{1,17},{2,18},{3,19},{4,20},{5,21},{6,22},{7,23},{8,24},{9,... | collective-permute-start | bytes 196616 | tf_op jit(solution)/shard_map/ppermute | solution.py:33
  73.2 6.2 %collective-permute-start.28 = (bf16[64,512]{1,0:T(8,128)(2,1)S(1)}, bf16[64,512]{1,0:T(8,128)(2,1)S(1)}, u32[]{:S(2)}, u32[]{:S(2)}) collective-permute-start(bf16[64,512]{1,0:T(8,128)(2,1)S(1)} %convert_element_type.75), channel_id=1, source_target_pairs={{0,8},{1,9},{2,10},{3,11},{4,12},{5,13},{6,14},{7,15},{8,0},{9,1},... | collective-permute-start | bytes 196616 | tf_op jit(solution)/shard_map/ppermute | solution.py:33
  79.4 5.8 %collective-permute-start.33 = (bf16[64,512]{1,0:T(8,128)(2,1)S(1)}, bf16[64,512]{1,0:T(8,128)(2,1)S(1)}, u32[]{:S(2)}, u32[]{:S(2)}) collective-permute-start(bf16[64,512]{1,0:T(8,128)(2,1)S(1)} %add_convert_fusion.1), channel_id=1, source_target_pairs={{0,6},{1,7},{2,4},{3,5},{4,2},{5,3},{6,0},{7,1},{8,14},{9,15},{10,... | collective-permute-start | bytes 196616 | tf_op jit(solution)/shard_map/ppermute | solution.py:33
  80.9 4.8 %collective-permute-start.32 = (bf16[64,512]{1,0:T(8,128)(2,1)S(1)}, bf16[64,512]{1,0:T(8,128)(2,1)S(1)}, u32[]{:S(2)}, u32[]{:S(2)}) collective-permute-start(bf16[64,512]{1,0:T(8,128)(2,1)S(1)} %add_convert_fusion.1), channel_id=1, source_target_pairs={{0,2},{1,3},{2,0},{3,1},{4,6},{5,7},{6,4},{7,5},{8,10},{9,11},{10,... | collective-permute-start | bytes 196616 | tf_op jit(solution)/shard_map/ppermute | solution.py:33
  82.3 4.3 %collective-permute-start.31 = (bf16[64,512]{1,0:T(8,128)(2,1)S(1)}, bf16[64,512]{1,0:T(8,128)(2,1)S(1)}, u32[]{:S(2)}, u32[]{:S(2)}) collective-permute-start(bf16[64,512]{1,0:T(8,128)(2,1)S(1)} %add_convert_fusion.1), channel_id=1, source_target_pairs={{0,4},{1,5},{2,6},{3,7},{4,0},{5,1},{6,2},{7,3},{8,12},{9,13},{10,... | collective-permute-start | bytes 196616 | tf_op jit(solution)/shard_map/ppermute | solution.py:33
  86.6 1.6 %collective-permute-start.34 = (bf16[4,64,512]{2,1,0:T(8,128)(2,1)S(1)}, bf16[4,64,512]{2,1,0:T(8,128)(2,1)S(1)}, u32[]{:S(2)}, u32[]{:S(2)}) collective-permute-start(bf16[4,64,512]{2,1,0:T(8,128)(2,1)S(1)} %pad_maximum_fusion.1.mine_ref), channel_id=1, source_target_pairs={{0,1},{1,0},{2,3},{3,2},{4,5},{5,4},{6,7},{7,6},{8,9},{9,8},{10,11... | collective-permute-start | bytes 786440 | tf_op jit(solution)/shard_map/ppermute | solution.py:33

commit v5 on v4

--- a/solution.py
+++ b/solution.py
@@ -33,20 +33,22 @@
     return lax.ppermute(x, AXES, [(i, i ^ mask) for i in range(count)])
 
 
-def sum_over(x, masks):
+def sum_over(x, masks, due=()):
     for k in range(0, len(masks), 2):
         sent = x.astype(BF)
         x = rounded(x) + flip(sent, masks[k]).astype(F32)
         if k + 1 < len(masks):
-            x = x + (
-                flip(sent, masks[k + 1]).astype(F32)
-                + flip(sent, masks[k] | masks[k + 1]).astype(F32)
-            )
-    return x
-
-
-def spread(x, across, near):
-    return jnp.stack([x, flip(x, near), flip(x, across), flip(x, across | near)])
+            both = flip(sent, masks[k] | masks[k + 1])
+            if k == 0:
+                both, *due = lax.optimization_barrier((both, *due))
+            x = x + (flip(sent, masks[k + 1]).astype(F32) + both.astype(F32))
+    return (x.astype(BF), *due)
+
+
+def spread(x, across, near, due=()):
+    both = flip(x, across | near)
+    both, *due = lax.optimization_barrier((both, *due))
+    return (jnp.stack([x, flip(x, near), flip(x, across), both]), *due)
 
 
 VMEM = pl.BlockSpec(memory_space=pltpu.VMEM)
@@ -276,17 +278,15 @@
         (at, reduced, there),
         scratch=[pltpu.VMEM((5 * block, block), F32)],
     )
+    own, reduced = lax.optimization_barrier((own, reduced))
+    at_x, at_y = flip(reduced, across), flip(reduced, near)
+    own = own + flip(bxy, across | near).astype(F32)
+    own = own + flip(bx, across).astype(F32)
     own = own + flip(by, near).astype(F32)
-    own = own + flip(bx, across).astype(F32)
-    own = own + flip(bxy, across | near).astype(F32)
-
-    reduced, own = lax.optimization_barrier((reduced, own))
-    at_x, at_y = flip(reduced, across), flip(reduced, near)
-    packed = sum_over(own, far).astype(BF)
-    packed, reduced = lax.optimization_barrier((packed, reduced))
+    own, reduced = lax.optimization_barrier((own, reduced))
     at_xy = flip(reduced, across | near)
-    packed = spread(packed, across, near)
-    packed, at_x, at_y = lax.optimization_barrier((packed, at_x, at_y))
+    packed, at_x, at_y = sum_over(own, far, (at_x, at_y))
+    packed, at_xy = spread(packed, across, near, (at_xy,))
     mate = flip(packed, low)
     whiten = run(
         functools.partial(whiten_kernel, voxels),
@@ -295,8 +295,6 @@
         scratch=[pltpu.VMEM((2, 5 * block, block), F32), pltpu.VMEM((rows, rows), F32)],
     )
 
-    whiten, at_xy = lax.optimization_barrier((whiten, at_xy))
-
     count = initial.shape[0] // 2
     weights = lax.dynamic_slice_in_dim(initial, at[2] * count, count, 0)
     outs = (
@@ -322,7 +320,7 @@
 
     for turn in range(ICA_ITERS):
         last = turn == ICA_ITERS - 1
-        stacked = spread(sum_over(newer, far).astype(BF), across, near)
+        (stacked,) = spread(*sum_over(newer, far), across, near)
         chunks = 4 if last else 8
         outs = (
             (shape((2 * count, rows), F32), shape((2 * count, data.shape[1]), BF))

time: 92.2 us -> 89.4 us (0.970)
  waiting for transfers between devices: 40.6 us -> 35.4 us
  starting transfers between devices: 33.9 us -> 36.3 us
    ppermute x35, waiting for transfers between devices: 40.6 us -> 35.4 us  [flip(): return lax.ppermute(x, AXES, [(i, i ^ mask) for i in range(count)])]
    ppermute x35, starting transfers between devices: 33.9 us -> 36.3 us  [flip(): return lax.ppermute(x, AXES, [(i, i ^ mask) for i in range(count)])]
where the time goes in v5:
time: 89.4 us; the launch traced here: 89.3 us
  starting transfers between devices  36.3 us (41%)
  waiting for transfers between devices  35.4 us (40%)
  Pallas kernels  15 us (17%)
  local copies, waits for them, and re-layouts  1.35 us (2%)
    ppermute x35, starting transfers between devices, flip(): return lax.ppermute(x, AXES, [(i, i ^ mask) for i in range(count)])  36.3 us
    ppermute x35, waiting for transfers between devices, flip(): return lax.ppermute(x, AXES, [(i, i ^ mask) for i in range(count)])  35.4 us
    pallas_call x8, Pallas kernels, run(): pl.pallas_call(kernel, out_shape=outs, in_specs=specs or [SMEM] + [VMEM]...  15 us
  transfers between devices with their start and end apart: 35, of which 23 were waited for; matrix products, arithmetic and copies ran while one was open for 2% of the time, Pallas kernels for 5%

profile of v5, /device:TPU:0, one launch (start us, length us, event | category | flops | bytes accessed | tf_op | source)
XLA Modules:
  0.0 89.3 jit_solution(7059532349152947967)
XLA Ops:
  0.6 0.5 collective-permute-start
  1.2 1.3 %constant_dynamic-slice_fusion.1 = (bf16[512,256]{1,0:T(8,128)(2,1)S(1)}, bf16[512,256]{1,0:T(8,128)(2,1)S(1)}, bf16[512,256]{1,0:T(8,128)(2,1)S(1)}, bf16[512,256]{1,0:T(8,128)(2,1)S(1)}) fusion(bf16[512,1024]{1,0:T(8,128)(2,1)} %param.3, s32[]{:T(128)S(6)} %select_n.18, s32[]{:T(128)S(6)} %select_n.16, s32[]{:T(128)S(6)} %select_n.15, s32[]{:T(128)S(6)} %select_n.17), kind=kLoop, calls=%fused_computation.9 | loop fusion | bytes 2097168 | tf_op jit(solution)/shard_map/dynamic_slice | solution.py:254
  2.5 0.1 collective-permute-start.2
  2.6 0.5 collective-permute-start.1
  3.1 1.0 %collective-permute-done.2.mate_right_ref = bf16[512,256]{1,0:T(8,128)(2,1)S(1)} collective-permute-done((bf16[512,256]{1,0:T(8,128)(2,1)S(1)}, bf16[512,256]{1,0:T(8,128)(2,1)S(1)}, u32[]{:S(2)}, u32[]{:S(2)}) %collective-permute-start.2) | collective-permute-done | bytes 262176 | tf_op jit(solution)/shard_map/ppermute | solution.py:33
  4.1 0.4 shard_map.51
  4.5 2.7 %collective-permute-start.3 = (bf16[512,256]{1,0:T(8,128)(2,1)S(1)}, bf16[512,256]{1,0:T(8,128)(2,1)S(1)}, u32[]{:S(2)}, u32[]{:S(2)}) collective-permute-start(bf16[512,256]{1,0:T(8,128)(2,1)S(1)} %shard_map.51), channel_id=1, source_target_pairs={{0,2},{1,3},{2,0},{3,1},{4,6},{5,7},{6,4},{7,5},{8,10},{9,11},{10,... | collective-permute-start | bytes 786440 | tf_op jit(solution)/shard_map/ppermute | solution.py:33
  7.3 0.4 shard_map.50
  7.7 6.4 %collective-permute-done.3 = bf16[512,256]{1,0:T(8,128)(2,1)S(1)} collective-permute-done((bf16[512,256]{1,0:T(8,128)(2,1)S(1)}, bf16[512,256]{1,0:T(8,128)(2,1)S(1)}, u32[]{:S(2)}, u32[]{:S(2)}) %collective-permute-start.3) | collective-permute-done | bytes 262176 | tf_op jit(solution)/shard_map/ppermute | solution.py:33
  14.1 0.1 add_convert_fusion.here_ref.refs_0_
  14.1 0.1 collective-permute-start.4
  14.2 0.1 pad_add_fusion.at
  14.3 1.4 %collective-permute-done.4.there_ref.refs_1_ = bf16[512,256]{1,0:T(8,128)(2,1)S(1)} collective-permute-done((bf16[512,256]{1,0:T(8,128)(2,1)S(1)}, bf16[512,256]{1,0:T(8,128)(2,1)S(1)}, u32[]{:S(2)}, u32[]{:S(2)}) %collective-permute-start.4) | collective-permute-done | bytes 262176 | tf_op jit(solution)/shard_map/ppermute | solution.py:33
  15.7 0.9 shard_map.52
  16.6 2.8 %collective-permute-start.5 = (bf16[160,128]{1,0:T(8,128)(2,1)S(1)}, bf16[160,128]{1,0:T(8,128)(2,1)S(1)}, u32[]{:S(2)}, u32[]{:S(2)}) collective-permute-start(bf16[160,128]{1,0:T(8,128)(2,1)S(1)} %get-tuple-element.22), channel_id=1, source_target_pairs={{0,6},{1,7},{2,4},{3,5},{4,2},{5,3},{6,0},{7,1},{8,14},{9,15},{10,... | collective-permute-start | bytes 122888 | tf_op jit(solution)/shard_map/ppermute | solution.py:33
  19.4 0.5 collective-permute-start.6
  19.9 0.3 collective-permute-start.7
  20.2 1.8 %collective-permute-start.12 = (bf16[512,256]{1,0:T(8,128)(2,1)S(1)}, bf16[512,256]{1,0:T(8,128)(2,1)S(1)}, u32[]{:S(2)}, u32[]{:S(2)}) collective-permute-start(bf16[512,256]{1,0:T(8,128)(2,1)S(1)} %add_convert_fusion.here_ref.refs_0_), channel_id=1, source_target_pairs={{0,4},{1,5},{2,6},{3,7},{4,0},{5,1},{6,2},{7,3},{8,12},{9,13},{10,... | collective-permute-start | bytes 786440 | tf_op jit(solution)/shard_map/ppermute | solution.py:33
  22.0 1.5 %collective-permute-start.11 = (bf16[512,256]{1,0:T(8,128)(2,1)S(1)}, bf16[512,256]{1,0:T(8,128)(2,1)S(1)}, u32[]{:S(2)}, u32[]{:S(2)}) collective-permute-start(bf16[512,256]{1,0:T(8,128)(2,1)S(1)} %add_convert_fusion.here_ref.refs_0_), channel_id=1, source_target_pairs={{0,2},{1,3},{2,0},{3,1},{4,6},{5,7},{6,4},{7,5},{8,10},{9,11},{10,... | collective-permute-start | bytes 786440 | tf_op jit(solution)/shard_map/ppermute | solution.py:33
  23.5 1.0 %collective-permute-done.7 = bf16[160,128]{1,0:T(8,128)(2,1)S(1)} collective-permute-done((bf16[160,128]{1,0:T(8,128)(2,1)S(1)}, bf16[160,128]{1,0:T(8,128)(2,1)S(1)}, u32[]{:S(2)}, u32[]{:S(2)}) %collective-permute-start.7) | collective-permute-done | bytes 40992 | tf_op jit(solution)/shard_map/ppermute | solution.py:33
  24.5 3.7 %collective-permute-start.10 = (bf16[160,128]{1,0:T(8,128)(2,1)S(1)}, bf16[160,128]{1,0:T(8,128)(2,1)S(1)}, u32[]{:S(2)}, u32[]{:S(2)}) collective-permute-start(bf16[160,128]{1,0:T(8,128)(2,1)S(1)} %convert_element_type.65), channel_id=1, source_target_pairs={{0,24},{1,25},{2,26},{3,27},{4,28},{5,29},{6,30},{7,31},{8,16},{9,... | collective-permute-start | bytes 122888 | tf_op jit(solution)/shard_map/ppermute | solution.py:33
  28.1 0.8 collective-permute-start.8
  28.9 1.5 %collective-permute-done.10 = bf16[160,128]{1,0:T(8,128)(2,1)S(1)} collective-permute-done((bf16[160,128]{1,0:T(8,128)(2,1)S(1)}, bf16[160,128]{1,0:T(8,128)(2,1)S(1)}, u32[]{:S(2)}, u32[]{:S(2)}) %collective-permute-start.10) | collective-permute-done | bytes 40992 | tf_op jit(solution)/shard_map/ppermute | solution.py:33
  30.4 1.3 %collective-permute-start.16 = (bf16[512,256]{1,0:T(8,128)(2,1)S(1)}, bf16[512,256]{1,0:T(8,128)(2,1)S(1)}, u32[]{:S(2)}, u32[]{:S(2)}) collective-permute-start(bf16[512,256]{1,0:T(8,128)(2,1)S(1)} %add_convert_fusion.here_ref.refs_0_), channel_id=1, source_target_pairs={{0,6},{1,7},{2,4},{3,5},{4,2},{5,3},{6,0},{7,1},{8,14},{9,15},{10,... | collective-permute-start | bytes 786440 | tf_op jit(solution)/shard_map/ppermute | solution.py:33
  31.7 1.3 %collective-permute-done.9 = bf16[160,128]{1,0:T(8,128)(2,1)S(1)} collective-permute-done((bf16[160,128]{1,0:T(8,128)(2,1)S(1)}, bf16[160,128]{1,0:T(8,128)(2,1)S(1)}, u32[]{:S(2)}, u32[]{:S(2)}) %collective-permute-start.9) | collective-permute-done | bytes 40992 | tf_op jit(solution)/shard_map/ppermute | solution.py:33
  33.1 1.5 %collective-permute-start.15 = (bf16[160,128]{1,0:T(8,128)(2,1)S(1)}, bf16[160,128]{1,0:T(8,128)(2,1)S(1)}, u32[]{:S(2)}, u32[]{:S(2)}) collective-permute-start(bf16[160,128]{1,0:T(8,128)(2,1)S(1)} %add_convert_fusion.3), channel_id=1, source_target_pairs={{0,6},{1,7},{2,4},{3,5},{4,2},{5,3},{6,0},{7,1},{8,14},{9,15},{10,... | collective-permute-start | bytes 122888 | tf_op jit(solution)/shard_map/ppermute | solution.py:33
  34.5 0.5 collective-permute-start.14
  35.1 1.6 %collective-permute-start.13 = (bf16[160,128]{1,0:T(8,128)(2,1)S(1)}, bf16[160,128]{1,0:T(8,128)(2,1)S(1)}, u32[]{:S(2)}, u32[]{:S(2)}) collective-permute-start(bf16[160,128]{1,0:T(8,128)(2,1)S(1)} %add_convert_fusion.3), channel_id=1, source_target_pairs={{0,4},{1,5},{2,6},{3,7},{4,0},{5,1},{6,2},{7,3},{8,12},{9,13},{10,... | collective-permute-start | bytes 122888 | tf_op jit(solution)/shard_map/ppermute | solution.py:33
  36.6 1.5 %collective-permute-done.16.refs_2_ = bf16[512,256]{1,0:T(8,128)(2,1)S(1)} collective-permute-done((bf16[512,256]{1,0:T(8,128)(2,1)S(1)}, bf16[512,256]{1,0:T(8,128)(2,1)S(1)}, u32[]{:S(2)}, u32[]{:S(2)}) %collective-permute-start.16) | collective-permute-done | bytes 262176 | tf_op jit(solution)/shard_map/ppermute | solution.py:33
  38.1 0.4 collective-permute-done.15
  38.6 0.1 collective-permute-start.20
  38.7 0.4 collective-permute-done.13
  39.1 0.1 collective-permute-start.17
  39.2 1.3 %collective-permute-done.17.other_ref = bf16[4,160,128]{2,1,0:T(8,128)(2,1)S(1)} collective-permute-done((bf16[4,160,128]{2,1,0:T(8,128)(2,1)S(1)}, bf16[4,160,128]{2,1,0:T(8,128)(2,1)S(1)}, u32[]{:S(2)}, u32[]{:S(2)}) %collective-permute-start.17) | collective-permute-done | bytes 163872 | tf_op jit(solution)/shard_map/ppermute | solution.py:33
  40.5 2.7 %shard_map.53.whiten_ref = bf16[512,512]{1,0:T(8,128)(2,1)S(1)} custom-call(s32[3]{0:T(128)S(1)} %pad_add_fusion.at, bf16[4,160,128]{2,1,0:T(8,128)(2,1)S(1)} %pad_maximum_fusion.2.mine_ref, bf16[4,160,128]{2,1,0:T(8,128)(2,1)S(1)} %collective-permute-done.17.other_ref), custom_call_target="tpu_custom_call" | custom-call | tf_op jit(solution)/shard_map/pallas_call | solution.py:60
  43.2 1.2 %shard_map.54 = (bf16[4,512,256]{2,1,0:T(8,128)(2,1)S(1)}, f32[64,512]{1,0:T(8,128)S(1)}, f32[64,1]{1,0:T(8,128)S(1)}) custom-call(bf16[512,512]{1,0:T(8,128)(2,1)S(1)} %shard_map.53.whiten_ref, bf16[512,256]{1,0:T(8,128)(2,1)S(1)} %add_convert_fusion.here_ref.refs_0_, bf16[512,256]{1,0:T(8,128)(2,1)S(1)} %collective-permute-done.4.there_ref.refs_1_, ...), custom_call_target="tpu_custom_call" | custom-call | tf_op jit(solution)/shard_map/pallas_call | solution.py:60
  44.5 1.6 %shard_map.55 = (bf16[4,512,256]{2,1,0:T(8,128)(2,1)S(1)}, f32[64,512]{1,0:T(8,128)S(1)}, f32[64,1]{1,0:T(8,128)}) custom-call(bf16[512,512]{1,0:T(8,128)(2,1)S(1)} %shard_map.53.whiten_ref, bf16[512,256]{1,0:T(8,128)(2,1)S(1)} %collective-permute-done.18.refs_0_, bf16[512,256]{1,0:T(8,128)(2,1)S(1)} %collective-permute-done.19.refs_1_, ...), custom_call_target="tpu_custom_call" | custom-call | tf_op jit(solution)/shard_map/pallas_call | solution.py:60
  46.1 3.5 %collective-permute-start.23 = (bf16[64,512]{1,0:T(8,128)(2,1)S(1)}, bf16[64,512]{1,0:T(8,128)(2,1)S(1)}, u32[]{:S(2)}, u32[]{:S(2)}) collective-permute-start(bf16[64,512]{1,0:T(8,128)(2,1)S(1)} %convert_element_type.70), channel_id=1, source_target_pairs={{0,24},{1,25},{2,26},{3,27},{4,28},{5,29},{6,30},{7,31},{8,16},{9,... | collective-permute-start | bytes 196616 | tf_op jit(solution)/shard_map/ppermute | solution.py:33
  49.6 1.0 %collective-permute-start.21 = (bf16[64,512]{1,0:T(8,128)(2,1)S(1)}, bf16[64,512]{1,0:T(8,128)(2,1)S(1)}, u32[]{:S(2)}, u32[]{:S(2)}) collective-permute-start(bf16[64,512]{1,0:T(8,128)(2,1)S(1)} %convert_element_type.70), channel_id=1, source_target_pairs={{0,8},{1,9},{2,10},{3,11},{4,12},{5,13},{6,14},{7,15},{8,0},{9,1},... | collective-permute-start | bytes 196616 | tf_op jit(solution)/shard_map/ppermute | solution.py:33
  50.6 2.4 %collective-permute-done.23 = bf16[64,512]{1,0:T(8,128)(2,1)S(1)} collective-permute-done((bf16[64,512]{1,0:T(8,128)(2,1)S(1)}, bf16[64,512]{1,0:T(8,128)(2,1)S(1)}, u32[]{:S(2)}, u32[]{:S(2)}) %collective-permute-start.23) | collective-permute-done | bytes 65568 | tf_op jit(solution)/shard_map/ppermute | solution.py:33
  52.9 2.2 %collective-permute-done.22 = bf16[64,512]{1,0:T(8,128)(2,1)S(1)} collective-permute-done((bf16[64,512]{1,0:T(8,128)(2,1)S(1)}, bf16[64,512]{1,0:T(8,128)(2,1)S(1)}, u32[]{:S(2)}, u32[]{:S(2)}) %collective-permute-start.22) | collective-permute-done | bytes 65568 | tf_op jit(solution)/shard_map/ppermute | solution.py:33
  55.1 0.1 collective-permute-done.21
  55.3 2.3 %collective-permute-start.26 = (bf16[64,512]{1,0:T(8,128)(2,1)S(1)}, bf16[64,512]{1,0:T(8,128)(2,1)S(1)}, u32[]{:S(2)}, u32[]{:S(2)}) collective-permute-start(bf16[64,512]{1,0:T(8,128)(2,1)S(1)} %add_convert_fusion.2), channel_id=1, source_target_pairs={{0,6},{1,7},{2,4},{3,5},{4,2},{5,3},{6,0},{7,1},{8,14},{9,15},{10,... | collective-permute-start | bytes 196616 | tf_op jit(solution)/shard_map/ppermute | solution.py:33
  57.7 0.5 collective-permute-start.25
  58.2 0.7 collective-permute-start.24
  58.9 2.4 %collective-permute-done.26 = bf16[64,512]{1,0:T(8,128)(2,1)S(1)} collective-permute-done((bf16[64,512]{1,0:T(8,128)(2,1)S(1)}, bf16[64,512]{1,0:T(8,128)(2,1)S(1)}, u32[]{:S(2)}, u32[]{:S(2)}) %collective-permute-start.26) | collective-permute-done | bytes 65568 | tf_op jit(solution)/shard_map/ppermute | solution.py:33
  61.3 0.7 collective-permute-done.25
  61.9 0.5 collective-permute-done.24
  62.5 0.1 collective-permute-start.27
  62.6 1.5 %collective-permute-done.27.other_ref = bf16[4,64,512]{2,1,0:T(8,128)(2,1)S(1)} collective-permute-done((bf16[4,64,512]{2,1,0:T(8,128)(2,1)S(1)}, bf16[4,64,512]{2,1,0:T(8,128)(2,1)S(1)}, u32[]{:S(2)}, u32[]{:S(2)}) %collective-permute-start.27) | collective-permute-done | bytes 262176 | tf_op jit(solution)/shard_map/ppermute | solution.py:33
  64.1 3.9 %shard_map.56 = f32[64,512]{1,0:T(8,128)S(1)} custom-call(s32[3]{0:T(128)S(1)} %pad_add_fusion.at, bf16[4,64,512]{2,1,0:T(8,128)(2,1)S(1)} %pad_maximum_fusion.mine_ref, bf16[4,64,512]{2,1,0:T(8,128)(2,1)S(1)} %collective-permute-done.27.other_ref, bf16[4,512,256]{2,1,0:T(8,128)(2,1)S(1)} %get-tuple-element.36.refs_0_, ...), custom_call_target="tpu_custom_call" | custom-call | tf_op jit(solution)/shard_map/pallas_call | solution.py:60
  68.0 2.6 %collective-permute-start.30 = (bf16[64,512]{1,0:T(8,128)(2,1)S(1)}, bf16[64,512]{1,0:T(8,128)(2,1)S(1)}, u32[]{:S(2)}, u32[]{:S(2)}) collective-permute-start(bf16[64,512]{1,0:T(8,128)(2,1)S(1)} %convert_element_type.75), channel_id=1, source_target_pairs={{0,24},{1,25},{2,26},{3,27},{4,28},{5,29},{6,30},{7,31},{8,16},{9,... | collective-permute-start | bytes 196616 | tf_op jit(solution)/shard_map/ppermute | solution.py:33
  70.6 1.9 %collective-permute-start.28 = (bf16[64,512]{1,0:T(8,128)(2,1)S(1)}, bf16[64,512]{1,0:T(8,128)(2,1)S(1)}, u32[]{:S(2)}, u32[]{:S(2)}) collective-permute-start(bf16[64,512]{1,0:T(8,128)(2,1)S(1)} %convert_element_type.75), channel_id=1, source_target_pairs={{0,8},{1,9},{2,10},{3,11},{4,12},{5,13},{6,14},{7,15},{8,0},{9,1},... | collective-permute-start | bytes 196616 | tf_op jit(solution)/shard_map/ppermute | solution.py:33
  72.5 2.3 %collective-permute-done.30 = bf16[64,512]{1,0:T(8,128)(2,1)S(1)} collective-permute-done((bf16[64,512]{1,0:T(8,128)(2,1)S(1)}, bf16[64,512]{1,0:T(8,128)(2,1)S(1)}, u32[]{:S(2)}, u32[]{:S(2)}) %collective-permute-start.30) | collective-permute-done | bytes 65568 | tf_op jit(solution)/shard_map/ppermute | solution.py:33
  74.8 2.0 %collective-permute-done.29 = bf16[64,512]{1,0:T(8,128)(2,1)S(1)} collective-permute-done((bf16[64,512]{1,0:T(8,128)(2,1)S(1)}, bf16[64,512]{1,0:T(8,128)(2,1)S(1)}, u32[]{:S(2)}, u32[]{:S(2)}) %collective-permute-start.29) | collective-permute-done | bytes 65568 | tf_op jit(solution)/shard_map/ppermute | solution.py:33
  76.9 1.8 %collective-permute-start.33 = (bf16[64,512]{1,0:T(8,128)(2,1)S(1)}, bf16[64,512]{1,0:T(8,128)(2,1)S(1)}, u32[]{:S(2)}, u32[]{:S(2)}) collective-permute-start(bf16[64,512]{1,0:T(8,128)(2,1)S(1)} %add_convert_fusion.1), channel_id=1, source_target_pairs={{0,6},{1,7},{2,4},{3,5},{4,2},{5,3},{6,0},{7,1},{8,14},{9,15},{10,... | collective-permute-start | bytes 196616 | tf_op jit(solution)/shard_map/ppermute | solution.py:33
  78.7 0.9 %collective-permute-start.32 = (bf16[64,512]{1,0:T(8,128)(2,1)S(1)}, bf16[64,512]{1,0:T(8,128)(2,1)S(1)}, u32[]{:S(2)}, u32[]{:S(2)}) collective-permute-start(bf16[64,512]{1,0:T(8,128)(2,1)S(1)} %add_convert_fusion.1), channel_id=1, source_target_pairs={{0,2},{1,3},{2,0},{3,1},{4,6},{5,7},{6,4},{7,5},{8,10},{9,11},{10,... | collective-permute-start | bytes 196616 | tf_op jit(solution)/shard_map/ppermute | solution.py:33
  79.6 0.9 collective-permute-start.31
  80.5 2.1 %collective-permute-done.33 = bf16[64,512]{1,0:T(8,128)(2,1)S(1)} collective-permute-done((bf16[64,512]{1,0:T(8,128)(2,1)S(1)}, bf16[64,512]{1,0:T(8,128)(2,1)S(1)}, u32[]{:S(2)}, u32[]{:S(2)}) %collective-permute-start.33) | collective-permute-done | bytes 65568 | tf_op jit(solution)/shard_map/ppermute | solution.py:33
  82.6 0.6 collective-permute-done.32
  83.2 0.7 collective-permute-done.31
  83.9 0.1 collective-permute-start.34
  84.0 1.5 %collective-permute-done.34.other_ref = bf16[4,64,512]{2,1,0:T(8,128)(2,1)S(1)} collective-permute-done((bf16[4,64,512]{2,1,0:T(8,128)(2,1)S(1)}, bf16[4,64,512]{2,1,0:T(8,128)(2,1)S(1)}, u32[]{:S(2)}, u32[]{:S(2)}) %collective-permute-start.34) | collective-permute-done | bytes 262176 | tf_op jit(solution)/shard_map/ppermute | solution.py:33
  85.5 3.8 %shard_map.57 = (f32[128,512]{1,0:T(8,128)}, bf16[128,1024]{1,0:T(8,128)(2,1)}) custom-call(s32[3]{0:T(128)S(1)} %pad_add_fusion.at, bf16[4,64,512]{2,1,0:T(8,128)(2,1)S(1)} %pad_maximum_fusion.1.mine_ref, bf16[4,64,512]{2,1,0:T(8,128)(2,1)S(1)} %collective-permute-done.34.other_ref, bf16[4,512,256]{2,1,0:T(8,128)(2,1)S(1)} %get-tuple-element.36.refs_0_, ...), custom_call_target="tpu_custom_call" | custom-call | tf_op jit(solution)/shard_map/pallas_call | solution.py:60
  (32 shorter events, 0.3 us)
Async XLA Ops:
  0.6 38.6 %copy-start = (f32[128,512]{1,0:T(8,128)S(1)}, f32[128,512]{1,0:T(8,128)}, u32[]{:S(2)}) copy-start(f32[128,512]{1,0:T(8,128)} %param.5) | copy-start | bytes 786436
  0.6 3.5 %collective-permute-start = (bf16[512,512]{1,0:T(8,128)(2,1)}, bf16[512,512]{1,0:T(8,128)(2,1)S(1)}, u32[]{:S(2)}, u32[]{:S(2)}) collective-permute-start(bf16[512,512]{1,0:T(8,128)(2,1)} %left_ref.3), channel_id=1, source_target_pairs={{0,1},{1,0},{2,3},{3,2},{4,5},{5,4},{6,7},{7,6},{8,9},{9,8},{10,11... | collective-permute-start | bytes 1572872 | tf_op jit(solution)/shard_map/ppermute | solution.py:33
  1.2 2.9 %copy-start.1 = (bf16[512,512]{1,0:T(8,128)(2,1)S(1)}, bf16[512,512]{1,0:T(8,128)(2,1)}, u32[]{:S(2)}) copy-start(bf16[512,512]{1,0:T(8,128)(2,1)} %left_ref.3) | copy-start | bytes 1572868
  2.5 1.6 %collective-permute-start.2 = (bf16[512,256]{1,0:T(8,128)(2,1)S(1)}, bf16[512,256]{1,0:T(8,128)(2,1)S(1)}, u32[]{:S(2)}, u32[]{:S(2)}) collective-permute-start(bf16[512,256]{1,0:T(8,128)(2,1)S(1)} %get-tuple-element.38), channel_id=1, source_target_pairs={{0,1},{1,0},{2,3},{3,2},{4,5},{5,4},{6,7},{7,6},{8,9},{9,8},{10,11... | collective-permute-start | bytes 786440 | tf_op jit(solution)/shard_map/ppermute | solution.py:33
  2.6 4.6 %collective-permute-start.1 = (bf16[512,256]{1,0:T(8,128)(2,1)S(1)}, bf16[512,256]{1,0:T(8,128)(2,1)S(1)}, u32[]{:S(2)}, u32[]{:S(2)}) collective-permute-start(bf16[512,256]{1,0:T(8,128)(2,1)S(1)} %get-tuple-element.39), channel_id=1, source_target_pairs={{0,1},{1,0},{2,3},{3,2},{4,5},{5,4},{6,7},{7,6},{8,9},{9,8},{10,11... | collective-permute-start | bytes 786440 | tf_op jit(solution)/shard_map/ppermute | solution.py:33
  4.5 9.5 %collective-permute-start.3 = (bf16[512,256]{1,0:T(8,128)(2,1)S(1)}, bf16[512,256]{1,0:T(8,128)(2,1)S(1)}, u32[]{:S(2)}, u32[]{:S(2)}) collective-permute-start(bf16[512,256]{1,0:T(8,128)(2,1)S(1)} %shard_map.51), channel_id=1, source_target_pairs={{0,2},{1,3},{2,0},{3,1},{4,6},{5,7},{6,4},{7,5},{8,10},{9,11},{10,... | collective-permute-start | bytes 786440 | tf_op jit(solution)/shard_map/ppermute | solution.py:33
  14.1 1.6 %collective-permute-start.4 = (bf16[512,256]{1,0:T(8,128)(2,1)S(1)}, bf16[512,256]{1,0:T(8,128)(2,1)S(1)}, u32[]{:S(2)}, u32[]{:S(2)}) collective-permute-start(bf16[512,256]{1,0:T(8,128)(2,1)S(1)} %add_convert_fusion.here_ref.refs_0_), channel_id=1, source_target_pairs={{0,1},{1,0},{2,3},{3,2},{4,5},{5,4},{6,7},{7,6},{8,9},{9,8},{10,11... | collective-permute-start | bytes 786440 | tf_op jit(solution)/shard_map/ppermute | solution.py:33
  16.6 6.8 %collective-permute-start.5 = (bf16[160,128]{1,0:T(8,128)(2,1)S(1)}, bf16[160,128]{1,0:T(8,128)(2,1)S(1)}, u32[]{:S(2)}, u32[]{:S(2)}) collective-permute-start(bf16[160,128]{1,0:T(8,128)(2,1)S(1)} %get-tuple-element.22), channel_id=1, source_target_pairs={{0,6},{1,7},{2,4},{3,5},{4,2},{5,3},{6,0},{7,1},{8,14},{9,15},{10,... | collective-permute-start | bytes 122888 | tf_op jit(solution)/shard_map/ppermute | solution.py:33
  19.4 4.1 %collective-permute-start.6 = (bf16[160,128]{1,0:T(8,128)(2,1)S(1)}, bf16[160,128]{1,0:T(8,128)(2,1)S(1)}, u32[]{:S(2)}, u32[]{:S(2)}) collective-permute-start(bf16[160,128]{1,0:T(8,128)(2,1)S(1)} %get-tuple-element.23), channel_id=1, source_target_pairs={{0,2},{1,3},{2,0},{3,1},{4,6},{5,7},{6,4},{7,5},{8,10},{9,11},{10,... | collective-permute-start | bytes 122888 | tf_op jit(solution)/shard_map/ppermute | solution.py:33
  19.9 4.5 %collective-permute-start.7 = (bf16[160,128]{1,0:T(8,128)(2,1)S(1)}, bf16[160,128]{1,0:T(8,128)(2,1)S(1)}, u32[]{:S(2)}, u32[]{:S(2)}) collective-permute-start(bf16[160,128]{1,0:T(8,128)(2,1)S(1)} %get-tuple-element.24), channel_id=1, source_target_pairs={{0,4},{1,5},{2,6},{3,7},{4,0},{5,1},{6,2},{7,3},{8,12},{9,13},{10,... | collective-permute-start | bytes 122888 | tf_op jit(solution)/shard_map/ppermute | solution.py:33
  20.2 11.5 %collective-permute-start.12 = (bf16[512,256]{1,0:T(8,128)(2,1)S(1)}, bf16[512,256]{1,0:T(8,128)(2,1)S(1)}, u32[]{:S(2)}, u32[]{:S(2)}) collective-permute-start(bf16[512,256]{1,0:T(8,128)(2,1)S(1)} %add_convert_fusion.here_ref.refs_0_), channel_id=1, source_target_pairs={{0,4},{1,5},{2,6},{3,7},{4,0},{5,1},{6,2},{7,3},{8,12},{9,13},{10,... | collective-permute-start | bytes 786440 | tf_op jit(solution)/shard_map/ppermute | solution.py:33
  22.0 9.8 %collective-permute-start.11 = (bf16[512,256]{1,0:T(8,128)(2,1)S(1)}, bf16[512,256]{1,0:T(8,128)(2,1)S(1)}, u32[]{:S(2)}, u32[]{:S(2)}) collective-permute-start(bf16[512,256]{1,0:T(8,128)(2,1)S(1)} %add_convert_fusion.here_ref.refs_0_), channel_id=1, source_target_pairs={{0,2},{1,3},{2,0},{3,1},{4,6},{5,7},{6,4},{7,5},{8,10},{9,11},{10,... | collective-permute-start | bytes 786440 | tf_op jit(solution)/shard_map/ppermute | solution.py:33
  24.5 6.0 %collective-permute-start.10 = (bf16[160,128]{1,0:T(8,128)(2,1)S(1)}, bf16[160,128]{1,0:T(8,128)(2,1)S(1)}, u32[]{:S(2)}, u32[]{:S(2)}) collective-permute-start(bf16[160,128]{1,0:T(8,128)(2,1)S(1)} %convert_element_type.65), channel_id=1, source_target_pairs={{0,24},{1,25},{2,26},{3,27},{4,28},{5,29},{6,30},{7,31},{8,16},{9,... | collective-permute-start | bytes 122888 | tf_op jit(solution)/shard_map/ppermute | solution.py:33
  28.1 4.9 %collective-permute-start.9 = (bf16[160,128]{1,0:T(8,128)(2,1)S(1)}, bf16[160,128]{1,0:T(8,128)(2,1)S(1)}, u32[]{:S(2)}, u32[]{:S(2)}) collective-permute-start(bf16[160,128]{1,0:T(8,128)(2,1)S(1)} %convert_element_type.65), channel_id=1, source_target_pairs={{0,16},{1,17},{2,18},{3,19},{4,20},{5,21},{6,22},{7,23},{8,24},{9,... | collective-permute-start | bytes 122888 | tf_op jit(solution)/shard_map/ppermute | solution.py:33
  28.1 4.9 %collective-permute-start.8 = (bf16[160,128]{1,0:T(8,128)(2,1)S(1)}, bf16[160,128]{1,0:T(8,128)(2,1)S(1)}, u32[]{:S(2)}, u32[]{:S(2)}) collective-permute-start(bf16[160,128]{1,0:T(8,128)(2,1)S(1)} %convert_element_type.65), channel_id=1, source_target_pairs={{0,8},{1,9},{2,10},{3,11},{4,12},{5,13},{6,14},{7,15},{8,0},{9,1},... | collective-permute-start | bytes 122888 | tf_op jit(solution)/shard_map/ppermute | solution.py:33
  30.4 7.7 %collective-permute-start.16 = (bf16[512,256]{1,0:T(8,128)(2,1)S(1)}, bf16[512,256]{1,0:T(8,128)(2,1)S(1)}, u32[]{:S(2)}, u32[]{:S(2)}) collective-permute-start(bf16[512,256]{1,0:T(8,128)(2,1)S(1)} %add_convert_fusion.here_ref.refs_0_), channel_id=1, source_target_pairs={{0,6},{1,7},{2,4},{3,5},{4,2},{5,3},{6,0},{7,1},{8,14},{9,15},{10,... | collective-permute-start | bytes 786440 | tf_op jit(solution)/shard_map/ppermute | solution.py:33
  33.1 5.5 %collective-permute-start.15 = (bf16[160,128]{1,0:T(8,128)(2,1)S(1)}, bf16[160,128]{1,0:T(8,128)(2,1)S(1)}, u32[]{:S(2)}, u32[]{:S(2)}) collective-permute-start(bf16[160,128]{1,0:T(8,128)(2,1)S(1)} %add_convert_fusion.3), channel_id=1, source_target_pairs={{0,6},{1,7},{2,4},{3,5},{4,2},{5,3},{6,0},{7,1},{8,14},{9,15},{10,... | collective-permute-start | bytes 122888 | tf_op jit(solution)/shard_map/ppermute | solution.py:33
  34.5 4.1 %collective-permute-start.14 = (bf16[160,128]{1,0:T(8,128)(2,1)S(1)}, bf16[160,128]{1,0:T(8,128)(2,1)S(1)}, u32[]{:S(2)}, u32[]{:S(2)}) collective-permute-start(bf16[160,128]{1,0:T(8,128)(2,1)S(1)} %add_convert_fusion.3), channel_id=1, source_target_pairs={{0,2},{1,3},{2,0},{3,1},{4,6},{5,7},{6,4},{7,5},{8,10},{9,11},{10,... | collective-permute-start | bytes 122888 | tf_op jit(solution)/shard_map/ppermute | solution.py:33
  35.1 4.0 %collective-permute-start.13 = (bf16[160,128]{1,0:T(8,128)(2,1)S(1)}, bf16[160,128]{1,0:T(8,128)(2,1)S(1)}, u32[]{:S(2)}, u32[]{:S(2)}) collective-permute-start(bf16[160,128]{1,0:T(8,128)(2,1)S(1)} %add_convert_fusion.3), channel_id=1, source_target_pairs={{0,4},{1,5},{2,6},{3,7},{4,0},{5,1},{6,2},{7,3},{8,12},{9,13},{10,... | collective-permute-start | bytes 122888 | tf_op jit(solution)/shard_map/ppermute | solution.py:33
  36.6 7.8 %collective-permute-start.18 = (bf16[512,256]{1,0:T(8,128)(2,1)S(1)}, bf16[512,256]{1,0:T(8,128)(2,1)S(1)}, u32[]{:S(2)}, u32[]{:S(2)}) collective-permute-start(bf16[512,256]{1,0:T(8,128)(2,1)S(1)} %collective-permute-done.11.refs_2_), channel_id=1, source_target_pairs={{0,1},{1,0},{2,3},{3,2},{4,5},{5,4},{6,7},{7,6},{8,9},{9,8},{10,11... | collective-permute-start | bytes 786440 | tf_op jit(solution)/shard_map/ppermute | solution.py:33
  38.1 6.3 %collective-permute-start.19 = (bf16[512,256]{1,0:T(8,128)(2,1)S(1)}, bf16[512,256]{1,0:T(8,128)(2,1)S(1)}, u32[]{:S(2)}, u32[]{:S(2)}) collective-permute-start(bf16[512,256]{1,0:T(8,128)(2,1)S(1)} %collective-permute-done.12.refs_3_), channel_id=1, source_target_pairs={{0,1},{1,0},{2,3},{3,2},{4,5},{5,4},{6,7},{7,6},{8,9},{9,8},{10,11... | collective-permute-start | bytes 786440 | tf_op jit(solution)/shard_map/ppermute | solution.py:33
  38.6 5.9 %collective-permute-start.20 = (bf16[512,256]{1,0:T(8,128)(2,1)S(1)}, bf16[512,256]{1,0:T(8,128)(2,1)S(1)}, u32[]{:S(2)}, u32[]{:S(2)}) collective-permute-start(bf16[512,256]{1,0:T(8,128)(2,1)S(1)} %collective-permute-done.16.refs_2_), channel_id=1, source_target_pairs={{0,1},{1,0},{2,3},{3,2},{4,5},{5,4},{6,7},{7,6},{8,9},{9,8},{10,11... | collective-permute-start | bytes 786440 | tf_op jit(solution)/shard_map/ppermute | solution.py:33
  39.1 1.5 %collective-permute-start.17 = (bf16[4,160,128]{2,1,0:T(8,128)(2,1)S(1)}, bf16[4,160,128]{2,1,0:T(8,128)(2,1)S(1)}, u32[]{:S(2)}, u32[]{:S(2)}) collective-permute-start(bf16[4,160,128]{2,1,0:T(8,128)(2,1)S(1)} %pad_maximum_fusion.2.mine_ref), channel_id=1, source_target_pairs={{0,1},{1,0},{2,3},{3,2},{4,5},{5,4},{6,7},{7,6},{8,9},{9,8},{10,11... | collective-permute-start | bytes 491528 | tf_op jit(solution)/shard_map/ppermute | solution.py:33
  46.1 6.8 %collective-permute-start.23 = (bf16[64,512]{1,0:T(8,128)(2,1)S(1)}, bf16[64,512]{1,0:T(8,128)(2,1)S(1)}, u32[]{:S(2)}, u32[]{:S(2)}) collective-permute-start(bf16[64,512]{1,0:T(8,128)(2,1)S(1)} %convert_element_type.70), channel_id=1, source_target_pairs={{0,24},{1,25},{2,26},{3,27},{4,28},{5,29},{6,30},{7,31},{8,16},{9,... | collective-permute-start | bytes 196616 | tf_op jit(solution)/shard_map/ppermute | solution.py:33
  49.6 5.5 %collective-permute-start.22 = (bf16[64,512]{1,0:T(8,128)(2,1)S(1)}, bf16[64,512]{1,0:T(8,128)(2,1)S(1)}, u32[]{:S(2)}, u32[]{:S(2)}) collective-permute-start(bf16[64,512]{1,0:T(8,128)(2,1)S(1)} %convert_element_type.70), channel_id=1, source_target_pairs={{0,16},{1,17},{2,18},{3,19},{4,20},{5,21},{6,22},{7,23},{8,24},{9,... | collective-permute-start | bytes 196616 | tf_op jit(solution)/shard_map/ppermute | solution.py:33
  49.6 5.7 %collective-permute-start.21 = (bf16[64,512]{1,0:T(8,128)(2,1)S(1)}, bf16[64,512]{1,0:T(8,128)(2,1)S(1)}, u32[]{:S(2)}, u32[]{:S(2)}) collective-permute-start(bf16[64,512]{1,0:T(8,128)(2,1)S(1)} %convert_element_type.70), channel_id=1, source_target_pairs={{0,8},{1,9},{2,10},{3,11},{4,12},{5,13},{6,14},{7,15},{8,0},{9,1},... | collective-permute-start | bytes 196616 | tf_op jit(solution)/shard_map/ppermute | solution.py:33
  55.3 5.9 %collective-permute-start.26 = (bf16[64,512]{1,0:T(8,128)(2,1)S(1)}, bf16[64,512]{1,0:T(8,128)(2,1)S(1)}, u32[]{:S(2)}, u32[]{:S(2)}) collective-permute-start(bf16[64,512]{1,0:T(8,128)(2,1)S(1)} %add_convert_fusion.2), channel_id=1, source_target_pairs={{0,6},{1,7},{2,4},{3,5},{4,2},{5,3},{6,0},{7,1},{8,14},{9,15},{10,... | collective-permute-start | bytes 196616 | tf_op jit(solution)/shard_map/ppermute | solution.py:33
  57.7 4.3 %collective-permute-start.25 = (bf16[64,512]{1,0:T(8,128)(2,1)S(1)}, bf16[64,512]{1,0:T(8,128)(2,1)S(1)}, u32[]{:S(2)}, u32[]{:S(2)}) collective-permute-start(bf16[64,512]{1,0:T(8,128)(2,1)S(1)} %add_convert_fusion.2), channel_id=1, source_target_pairs={{0,2},{1,3},{2,0},{3,1},{4,6},{5,7},{6,4},{7,5},{8,10},{9,11},{10,... | collective-permute-start | bytes 196616 | tf_op jit(solution)/shard_map/ppermute | solution.py:33
  58.2 4.3 %collective-permute-start.24 = (bf16[64,512]{1,0:T(8,128)(2,1)S(1)}, bf16[64,512]{1,0:T(8,128)(2,1)S(1)}, u32[]{:S(2)}, u32[]{:S(2)}) collective-permute-start(bf16[64,512]{1,0:T(8,128)(2,1)S(1)} %add_convert_fusion.2), channel_id=1, source_target_pairs={{0,4},{1,5},{2,6},{3,7},{4,0},{5,1},{6,2},{7,3},{8,12},{9,13},{10,... | collective-permute-start | bytes 196616 | tf_op jit(solution)/shard_map/ppermute | solution.py:33
  62.5 1.6 %collective-permute-start.27 = (bf16[4,64,512]{2,1,0:T(8,128)(2,1)S(1)}, bf16[4,64,512]{2,1,0:T(8,128)(2,1)S(1)}, u32[]{:S(2)}, u32[]{:S(2)}) collective-permute-start(bf16[4,64,512]{2,1,0:T(8,128)(2,1)S(1)} %pad_maximum_fusion.mine_ref), channel_id=1, source_target_pairs={{0,1},{1,0},{2,3},{3,2},{4,5},{5,4},{6,7},{7,6},{8,9},{9,8},{10,11... | collective-permute-start | bytes 786440 | tf_op jit(solution)/shard_map/ppermute | solution.py:33
  68.0 6.8 %collective-permute-start.30 = (bf16[64,512]{1,0:T(8,128)(2,1)S(1)}, bf16[64,512]{1,0:T(8,128)(2,1)S(1)}, u32[]{:S(2)}, u32[]{:S(2)}) collective-permute-start(bf16[64,512]{1,0:T(8,128)(2,1)S(1)} %convert_element_type.75), channel_id=1, source_target_pairs={{0,24},{1,25},{2,26},{3,27},{4,28},{5,29},{6,30},{7,31},{8,16},{9,... | collective-permute-start | bytes 196616 | tf_op jit(solution)/shard_map/ppermute | solution.py:33
  70.6 6.2 %collective-permute-start.29 = (bf16[64,512]{1,0:T(8,128)(2,1)S(1)}, bf16[64,512]{1,0:T(8,128)(2,1)S(1)}, u32[]{:S(2)}, u32[]{:S(2)}) collective-permute-start(bf16[64,512]{1,0:T(8,128)(2,1)S(1)} %convert_element_type.75), channel_id=1, source_target_pairs={{0,16},{1,17},{2,18},{3,19},{4,20},{5,21},{6,22},{7,23},{8,24},{9,... | collective-permute-start | bytes 196616 | tf_op jit(solution)/shard_map/ppermute | solution.py:33
  70.6 6.2 %collective-permute-start.28 = (bf16[64,512]{1,0:T(8,128)(2,1)S(1)}, bf16[64,512]{1,0:T(8,128)(2,1)S(1)}, u32[]{:S(2)}, u32[]{:S(2)}) collective-permute-start(bf16[64,512]{1,0:T(8,128)(2,1)S(1)} %convert_element_type.75), channel_id=1, source_target_pairs={{0,8},{1,9},{2,10},{3,11},{4,12},{5,13},{6,14},{7,15},{8,0},{9,1},... | collective-permute-start | bytes 196616 | tf_op jit(solution)/shard_map/ppermute | solution.py:33
  76.9 5.7 %collective-permute-start.33 = (bf16[64,512]{1,0:T(8,128)(2,1)S(1)}, bf16[64,512]{1,0:T(8,128)(2,1)S(1)}, u32[]{:S(2)}, u32[]{:S(2)}) collective-permute-start(bf16[64,512]{1,0:T(8,128)(2,1)S(1)} %add_convert_fusion.1), channel_id=1, source_target_pairs={{0,6},{1,7},{2,4},{3,5},{4,2},{5,3},{6,0},{7,1},{8,14},{9,15},{10,... | collective-permute-start | bytes 196616 | tf_op jit(solution)/shard_map/ppermute | solution.py:33
  78.7 4.5 %collective-permute-start.32 = (bf16[64,512]{1,0:T(8,128)(2,1)S(1)}, bf16[64,512]{1,0:T(8,128)(2,1)S(1)}, u32[]{:S(2)}, u32[]{:S(2)}) collective-permute-start(bf16[64,512]{1,0:T(8,128)(2,1)S(1)} %add_convert_fusion.1), channel_id=1, source_target_pairs={{0,2},{1,3},{2,0},{3,1},{4,6},{5,7},{6,4},{7,5},{8,10},{9,11},{10,... | collective-permute-start | bytes 196616 | tf_op jit(solution)/shard_map/ppermute | solution.py:33
  79.6 4.3 %collective-permute-start.31 = (bf16[64,512]{1,0:T(8,128)(2,1)S(1)}, bf16[64,512]{1,0:T(8,128)(2,1)S(1)}, u32[]{:S(2)}, u32[]{:S(2)}) collective-permute-start(bf16[64,512]{1,0:T(8,128)(2,1)S(1)} %add_convert_fusion.1), channel_id=1, source_target_pairs={{0,4},{1,5},{2,6},{3,7},{4,0},{5,1},{6,2},{7,3},{8,12},{9,13},{10,... | collective-permute-start | bytes 196616 | tf_op jit(solution)/shard_map/ppermute | solution.py:33
  83.9 1.6 %collective-permute-start.34 = (bf16[4,64,512]{2,1,0:T(8,128)(2,1)S(1)}, bf16[4,64,512]{2,1,0:T(8,128)(2,1)S(1)}, u32[]{:S(2)}, u32[]{:S(2)}) collective-permute-start(bf16[4,64,512]{2,1,0:T(8,128)(2,1)S(1)} %pad_maximum_fusion.1.mine_ref), channel_id=1, source_target_pairs={{0,1},{1,0},{2,3},{3,2},{4,5},{5,4},{6,7},{7,6},{8,9},{9,8},{10,11... | collective-permute-start | bytes 786440 | tf_op jit(solution)/shard_map/ppermute | solution.py:33

commit v6 on v5

--- a/solution.py
+++ b/solution.py
@@ -36,12 +36,15 @@
 def sum_over(x, masks, due=()):
     for k in range(0, len(masks), 2):
         sent = x.astype(BF)
-        x = rounded(x) + flip(sent, masks[k]).astype(F32)
+        first = flip(sent, masks[k])
+        if k == 0:
+            first, *due = lax.optimization_barrier((first, *due))
+        x = rounded(x) + first.astype(F32)
         if k + 1 < len(masks):
-            both = flip(sent, masks[k] | masks[k + 1])
-            if k == 0:
-                both, *due = lax.optimization_barrier((both, *due))
-            x = x + (flip(sent, masks[k + 1]).astype(F32) + both.astype(F32))
+            x = x + (
+                flip(sent, masks[k + 1]).astype(F32)
+                + flip(sent, masks[k] | masks[k + 1]).astype(F32)
+            )
     return (x.astype(BF), *due)
 
 
@@ -81,21 +84,22 @@
     rows = here_ref.shape[0]
     block = rows // 4
 
-    def put(k, i, j):
+    def product(i, j, count):
         total = 0.0
         for ref in (here_ref, there_ref):
-            left = ref[pl.ds(pl.multiple_of(i * block, block), block), :]
-            right = ref[pl.ds(pl.multiple_of(j * block, block), block), :]
+            left = ref[pl.ds(pl.multiple_of(i * block, block), count * block), :]
+            right = ref[pl.ds(pl.multiple_of(j * block, block), 2 * block), :]
             total += nt(left, right)
-        pack[k * block : (k + 1) * block] = total
+        return total
 
     low = at[0]
-    first, second, third = 2 * low, 2 * low + 1, 2 - 2 * low
-    put(0, first, first)
-    put(1, first, second)
-    put(2, second, second)
-    put(3, second, third)
-    put(4, low, 2 + low)
+    corner = product(2 * low, 2 * low, 2)
+    cross = product(2 + low, 0, 1)
+    pack[0 * block : 1 * block] = corner[:block, :block]
+    pack[1 * block : 2 * block] = corner[:block, block:]
+    pack[2 * block : 3 * block] = corner[block:, block:]
+    pack[3 * block : 4 * block] = cross[:, :block]
+    pack[4 * block : 5 * block] = cross[:, block:]
     piece = own_ref.shape[0]
 
     def quarter(i, j):
@@ -130,12 +134,11 @@
         return 2.0 * (value * value)
 
     for core in (0, 1):
-        a, b, c = 2 * core, 2 * core + 1, 2 - 2 * core
-        squares += put(a, a, core, 0)
-        squares += put(a, b, core, 1)
-        squares += put(b, b, core, 2)
-        squares += put(b, c, core, 3)
-        squares += put(core, 2 + core, core, 4)
+        squares += put(2 * core, 2 * core, core, 0)
+        squares += put(2 * core, 2 * core + 1, core, 1)
+        squares += put(2 * core + 1, 2 * core + 1, core, 2)
+        squares += put(2 + core, 0, core, 3)
+        squares += put(2 + core, 1, core, 4)
 
     cscale = jnp.sqrt(jnp.sum(squares, keepdims=True) + 1e-06)
     y = covar[...] * (1.0 / cscale)
@@ -168,36 +171,24 @@
     return pulled, jnp.sum(slopes, axis=1, keepdims=True)
 
 
-def apply_kernel(part, whiten_ref, *refs):
-    blocks, (weights_ref, white_ref, total_ref, slope_ref) = refs[:4], refs[-4:]
+def apply_kernel(whiten_ref, *refs):
+    blocks, (weights_ref, white_ref, newer_ref) = refs[:-3], refs[-3:]
     weights = weights_ref[...]
-    whites = [nn(whiten_ref[...], block[...]).astype(BF) for block in blocks]
-    for k, white in enumerate(whites):
-        white_ref[k] = white
+    whites = []
+    for k, block in enumerate(blocks):
+        whites.append(nn(whiten_ref[...], block[...]).astype(BF))
+        white_ref[k] = whites[k]
     total, slope = step(weights, whites)
-    if part:
-        slope += refs[5][...]
-        total += refs[4][...] - slope * weights
-    total_ref[...] = total
-    slope_ref[...] = slope
-
-
-def decor_kernel(last, at, mine_ref, other_ref, *refs):
-    whites, outs, (newer, lower, white, sem) = refs[:2], refs[2:-4], refs[-4:]
+    newer_ref[...] = total - slope * weights
+
+
+def decor_kernel(last, at, mine_ref, other_ref, white_ref, *refs):
+    outs, (newer, lower, white, sem) = refs[:-4], refs[-4:]
     count = mine_ref.shape[1]
     low, ax, ay = at[0], at[1], at[2]
     chunks = white.shape[0]
-    first = 3 if last else 4
-    copies = [
-        pltpu.make_async_copy(
-            ref.at[pl.ds(0, size)], white.at[pl.ds(start, size)], sem.at[k]
-        )
-        for k, (ref, start, size) in enumerate(
-            zip(whites, (0, first), (first, chunks - first))
-        )
-    ]
-    for copy in copies:
-        copy.start()
+    copy = pltpu.make_async_copy(white_ref.at[pl.ds(0, chunks)], white, sem)
+    copy.start()
     for k in range(4):
         i, j = ax ^ (k >> 1), ay ^ (k & 1)
         for ref, core in ((mine_ref, low), (other_ref, 1 - low)):
@@ -221,8 +212,7 @@
     raw = lower[...]
     gram = nt(lower[pl.ds(start, size), :], raw).astype(BF)
     weights = 1.5 * newer[pl.ds(start, size), :] - 0.5 * nn(gram, raw)
-    for copy in copies:
-        copy.wait()
+    copy.wait()
     if last:
         outs[0][...] = weights
         width = white.shape[2]
@@ -297,31 +287,19 @@
 
     count = initial.shape[0] // 2
     weights = lax.dynamic_slice_in_dim(initial, at[2] * count, count, 0)
-    outs = (
-        shape((4, rows, size), BF),
-        shape((count, rows), F32),
-        shape((count, 1), F32),
-    )
-    blocks = (reduced, there, at_x, at_y)
-    white_here, total, slope = run(
-        functools.partial(apply_kernel, False),
-        outs,
+    blocks = (reduced, there, at_x, flip(at_x, low))
+    blocks += (at_y, flip(at_y, low), at_xy, flip(at_xy, low))
+    white, newer = run(
+        apply_kernel,
+        (shape((len(blocks), rows, size), BF), shape((count, rows), F32)),
         (whiten, *blocks, weights),
-        specs=[VMEM] * 6,
-    )
-    blocks = (flip(at_x, low), flip(at_y, low), at_xy, flip(at_xy, low))
-    white_there, newer, _ = run(
-        functools.partial(apply_kernel, True),
-        outs,
-        (whiten, *blocks, total, slope, weights),
-        specs=[VMEM] * 8,
-    )
-    whites = (white_here, white_there)
+        specs=[VMEM] * (len(blocks) + 2),
+    )
 
     for turn in range(ICA_ITERS):
         last = turn == ICA_ITERS - 1
         (stacked,) = spread(*sum_over(newer, far), across, near)
-        chunks = 4 if last else 8
+        chunks = len(blocks) // 2 if last else len(blocks)
         outs = (
             (shape((2 * count, rows), F32), shape((2 * count, data.shape[1]), BF))
             if last
@@ -330,13 +308,13 @@
         newer = run(
             functools.partial(decor_kernel, last),
             outs,
-            (at, stacked, flip(stacked, low), *whites),
-            specs=[SMEM, VMEM, VMEM] + [HBM] * 2,
+            (at, stacked, flip(stacked, low), white),
+            specs=[SMEM, VMEM, VMEM] + [HBM],
             scratch=[
                 pltpu.VMEM((rows, rows), F32),
                 pltpu.VMEM((rows, rows), BF),
                 pltpu.VMEM((chunks, rows, size), BF),
-                pltpu.SemaphoreType.DMA((2,)),
+                pltpu.SemaphoreType.DMA,
             ],
         )
     return newer

time: 89.4 us -> 90.3 us (1.010)
  waiting for transfers between devices: 35.4 us -> 38.8 us
  starting transfers between devices: 36.3 us -> 34.5 us
    ppermute x35, waiting for transfers between devices: 35.4 us -> 38.8 us  [flip(): return lax.ppermute(x, AXES, [(i, i ^ mask) for i in range(count)])]
    ppermute x35, starting transfers between devices: 36.3 us -> 34.5 us  [flip(): return lax.ppermute(x, AXES, [(i, i ^ mask) for i in range(count)])]
    pallas_call x8 -> x7, Pallas kernels: 15 us -> 14.3 us  [run(): pl.pallas_call(kernel, out_shape=outs, in_specs=specs or [SMEM] + [VMEM]...]
  transfers between devices with their start and end apart: 35 -> 35, of which waited for: 23 -> 25; matrix products, arithmetic and copies ran while one was open for 2% -> 2% of each run, Pallas kernels for 5% -> 4%
where the time goes in v6:
time: 90.3 us; the launch traced here: 90.2 us
  waiting for transfers between devices  38.8 us (43%)
  starting transfers between devices  34.5 us (38%)
  Pallas kernels  14.3 us (16%)
  local copies, waits for them, and re-layouts  1.3 us (1%)
    ppermute x35, waiting for transfers between devices, flip(): return lax.ppermute(x, AXES, [(i, i ^ mask) for i in range(count)])  38.8 us
    ppermute x35, starting transfers between devices, flip(): return lax.ppermute(x, AXES, [(i, i ^ mask) for i in range(count)])  34.5 us
    pallas_call x7, Pallas kernels, run(): pl.pallas_call(kernel, out_shape=outs, in_specs=specs or [SMEM] + [VMEM]...  14.3 us
  transfers between devices with their start and end apart: 35, of which 25 were waited for; matrix products, arithmetic and copies ran while one was open for 2% of the time, Pallas kernels for 4%

profile of v6, /device:TPU:0, one launch (start us, length us, event | category | flops | bytes accessed | tf_op | source)
XLA Modules:
  0.0 90.2 jit_solution(6310289410711764224)
XLA Ops:
  0.7 0.5 collective-permute-start
  1.2 1.3 %constant_dynamic-slice_fusion.1 = (bf16[512,256]{1,0:T(8,128)(2,1)S(1)}, bf16[512,256]{1,0:T(8,128)(2,1)S(1)}, bf16[512,256]{1,0:T(8,128)(2,1)S(1)}, bf16[512,256]{1,0:T(8,128)(2,1)S(1)}) fusion(bf16[512,1024]{1,0:T(8,128)(2,1)} %param.3, s32[]{:T(128)S(6)} %select_n.18, s32[]{:T(128)S(6)} %select_n.16, s32[]{:T(128)S(6)} %select_n.15, s32[]{:T(128)S(6)} %select_n.17), kind=kLoop, calls=%fused_computation.9 | loop fusion | bytes 2097168 | tf_op jit(solution)/shard_map/dynamic_slice | solution.py:244
  2.4 0.2 collective-permute-start.2
  2.6 0.4 collective-permute-start.1
  3.0 1.0 %collective-permute-done.2.mate_right_ref = bf16[512,256]{1,0:T(8,128)(2,1)S(1)} collective-permute-done((bf16[512,256]{1,0:T(8,128)(2,1)S(1)}, bf16[512,256]{1,0:T(8,128)(2,1)S(1)}, u32[]{:S(2)}, u32[]{:S(2)}) %collective-permute-start.2) | collective-permute-done | bytes 262176 | tf_op jit(solution)/shard_map/ppermute | solution.py:33
  4.1 0.4 shard_map.51
  4.5 2.7 %collective-permute-start.3 = (bf16[512,256]{1,0:T(8,128)(2,1)S(1)}, bf16[512,256]{1,0:T(8,128)(2,1)S(1)}, u32[]{:S(2)}, u32[]{:S(2)}) collective-permute-start(bf16[512,256]{1,0:T(8,128)(2,1)S(1)} %shard_map.51), channel_id=1, source_target_pairs={{0,2},{1,3},{2,0},{3,1},{4,6},{5,7},{6,4},{7,5},{8,10},{9,11},{10,... | collective-permute-start | bytes 786440 | tf_op jit(solution)/shard_map/ppermute | solution.py:33
  7.2 0.4 shard_map.50
  7.6 6.4 %collective-permute-done.3 = bf16[512,256]{1,0:T(8,128)(2,1)S(1)} collective-permute-done((bf16[512,256]{1,0:T(8,128)(2,1)S(1)}, bf16[512,256]{1,0:T(8,128)(2,1)S(1)}, u32[]{:S(2)}, u32[]{:S(2)}) %collective-permute-start.3) | collective-permute-done | bytes 262176 | tf_op jit(solution)/shard_map/ppermute | solution.py:33
  14.1 0.1 collective-permute-start.4
  14.2 0.1 pad_add_fusion.at
  14.2 1.4 %collective-permute-done.4.there_ref.refs_1_ = bf16[512,256]{1,0:T(8,128)(2,1)S(1)} collective-permute-done((bf16[512,256]{1,0:T(8,128)(2,1)S(1)}, bf16[512,256]{1,0:T(8,128)(2,1)S(1)}, u32[]{:S(2)}, u32[]{:S(2)}) %collective-permute-start.4) | collective-permute-done | bytes 262176 | tf_op jit(solution)/shard_map/ppermute | solution.py:33
  15.7 0.9 shard_map.52
  16.6 2.8 %collective-permute-start.5 = (bf16[160,128]{1,0:T(8,128)(2,1)S(1)}, bf16[160,128]{1,0:T(8,128)(2,1)S(1)}, u32[]{:S(2)}, u32[]{:S(2)}) collective-permute-start(bf16[160,128]{1,0:T(8,128)(2,1)S(1)} %get-tuple-element.19), channel_id=1, source_target_pairs={{0,6},{1,7},{2,4},{3,5},{4,2},{5,3},{6,0},{7,1},{8,14},{9,15},{10,... | collective-permute-start | bytes 122888 | tf_op jit(solution)/shard_map/ppermute | solution.py:33
  19.3 0.5 collective-permute-start.6
  19.9 0.3 collective-permute-start.7
  20.1 1.8 %collective-permute-start.10 = (bf16[512,256]{1,0:T(8,128)(2,1)S(1)}, bf16[512,256]{1,0:T(8,128)(2,1)S(1)}, u32[]{:S(2)}, u32[]{:S(2)}) collective-permute-start(bf16[512,256]{1,0:T(8,128)(2,1)S(1)} %add_convert_fusion.here_ref.refs_0_), channel_id=1, source_target_pairs={{0,4},{1,5},{2,6},{3,7},{4,0},{5,1},{6,2},{7,3},{8,12},{9,13},{10,... | collective-permute-start | bytes 786440 | tf_op jit(solution)/shard_map/ppermute | solution.py:33
  21.9 1.5 %collective-permute-start.9 = (bf16[512,256]{1,0:T(8,128)(2,1)S(1)}, bf16[512,256]{1,0:T(8,128)(2,1)S(1)}, u32[]{:S(2)}, u32[]{:S(2)}) collective-permute-start(bf16[512,256]{1,0:T(8,128)(2,1)S(1)} %add_convert_fusion.here_ref.refs_0_), channel_id=1, source_target_pairs={{0,2},{1,3},{2,0},{3,1},{4,6},{5,7},{6,4},{7,5},{8,10},{9,11},{10,... | collective-permute-start | bytes 786440 | tf_op jit(solution)/shard_map/ppermute | solution.py:33
  23.4 1.0 %collective-permute-done.7 = bf16[160,128]{1,0:T(8,128)(2,1)S(1)} collective-permute-done((bf16[160,128]{1,0:T(8,128)(2,1)S(1)}, bf16[160,128]{1,0:T(8,128)(2,1)S(1)}, u32[]{:S(2)}, u32[]{:S(2)}) %collective-permute-start.7) | collective-permute-done | bytes 40992 | tf_op jit(solution)/shard_map/ppermute | solution.py:33
  24.4 1.6 %collective-permute-start.8 = (bf16[160,128]{1,0:T(8,128)(2,1)S(1)}, bf16[160,128]{1,0:T(8,128)(2,1)S(1)}, u32[]{:S(2)}, u32[]{:S(2)}) collective-permute-start(bf16[160,128]{1,0:T(8,128)(2,1)S(1)} %convert_element_type.65), channel_id=1, source_target_pairs={{0,8},{1,9},{2,10},{3,11},{4,12},{5,13},{6,14},{7,15},{8,0},{9,1},... | collective-permute-start | bytes 122888 | tf_op jit(solution)/shard_map/ppermute | solution.py:33
  26.1 2.5 %collective-permute-start.12 = (bf16[160,128]{1,0:T(8,128)(2,1)S(1)}, bf16[160,128]{1,0:T(8,128)(2,1)S(1)}, u32[]{:S(2)}, u32[]{:S(2)}) collective-permute-start(bf16[160,128]{1,0:T(8,128)(2,1)S(1)} %convert_element_type.65), channel_id=1, source_target_pairs={{0,24},{1,25},{2,26},{3,27},{4,28},{5,29},{6,30},{7,31},{8,16},{9,... | collective-permute-start | bytes 122888 | tf_op jit(solution)/shard_map/ppermute | solution.py:33
  28.5 0.1 collective-permute-start.11
  28.7 0.3 collective-permute-done.8
  28.9 1.1 %collective-permute-start.16 = (bf16[512,256]{1,0:T(8,128)(2,1)S(1)}, bf16[512,256]{1,0:T(8,128)(2,1)S(1)}, u32[]{:S(2)}, u32[]{:S(2)}) collective-permute-start(bf16[512,256]{1,0:T(8,128)(2,1)S(1)} %add_convert_fusion.here_ref.refs_0_), channel_id=1, source_target_pairs={{0,6},{1,7},{2,4},{3,5},{4,2},{5,3},{6,0},{7,1},{8,14},{9,15},{10,... | collective-permute-start | bytes 786440 | tf_op jit(solution)/shard_map/ppermute | solution.py:33
  30.0 1.8 %collective-permute-done.12 = bf16[160,128]{1,0:T(8,128)(2,1)S(1)} collective-permute-done((bf16[160,128]{1,0:T(8,128)(2,1)S(1)}, bf16[160,128]{1,0:T(8,128)(2,1)S(1)}, u32[]{:S(2)}, u32[]{:S(2)}) %collective-permute-start.12) | collective-permute-done | bytes 40992 | tf_op jit(solution)/shard_map/ppermute | solution.py:33
  31.9 2.0 %collective-permute-done.11 = bf16[160,128]{1,0:T(8,128)(2,1)S(1)} collective-permute-done((bf16[160,128]{1,0:T(8,128)(2,1)S(1)}, bf16[160,128]{1,0:T(8,128)(2,1)S(1)}, u32[]{:S(2)}, u32[]{:S(2)}) %collective-permute-start.11) | collective-permute-done | bytes 40992 | tf_op jit(solution)/shard_map/ppermute | solution.py:33
  33.9 1.4 %collective-permute-start.15 = (bf16[160,128]{1,0:T(8,128)(2,1)S(1)}, bf16[160,128]{1,0:T(8,128)(2,1)S(1)}, u32[]{:S(2)}, u32[]{:S(2)}) collective-permute-start(bf16[160,128]{1,0:T(8,128)(2,1)S(1)} %add_convert_fusion.3), channel_id=1, source_target_pairs={{0,6},{1,7},{2,4},{3,5},{4,2},{5,3},{6,0},{7,1},{8,14},{9,15},{10,... | collective-permute-start | bytes 122888 | tf_op jit(solution)/shard_map/ppermute | solution.py:33
  35.4 0.5 collective-permute-start.14
  35.9 1.6 %collective-permute-start.13 = (bf16[160,128]{1,0:T(8,128)(2,1)S(1)}, bf16[160,128]{1,0:T(8,128)(2,1)S(1)}, u32[]{:S(2)}, u32[]{:S(2)}) collective-permute-start(bf16[160,128]{1,0:T(8,128)(2,1)S(1)} %add_convert_fusion.3), channel_id=1, source_target_pairs={{0,4},{1,5},{2,6},{3,7},{4,0},{5,1},{6,2},{7,3},{8,12},{9,13},{10,... | collective-permute-start | bytes 122888 | tf_op jit(solution)/shard_map/ppermute | solution.py:33
  37.5 0.5 collective-permute-start.19
  38.0 0.9 collective-permute-done.15
  38.9 0.5 collective-permute-done.14
  39.4 0.5 collective-permute-done.13
  39.9 0.1 collective-permute-start.17
  40.0 1.3 %collective-permute-done.17.other_ref = bf16[4,160,128]{2,1,0:T(8,128)(2,1)S(1)} collective-permute-done((bf16[4,160,128]{2,1,0:T(8,128)(2,1)S(1)}, bf16[4,160,128]{2,1,0:T(8,128)(2,1)S(1)}, u32[]{:S(2)}, u32[]{:S(2)}) %collective-permute-start.17) | collective-permute-done | bytes 163872 | tf_op jit(solution)/shard_map/ppermute | solution.py:33
  41.4 2.6 %shard_map.53.whiten_ref = bf16[512,512]{1,0:T(8,128)(2,1)S(1)} custom-call(s32[3]{0:T(128)S(1)} %pad_add_fusion.at, bf16[4,160,128]{2,1,0:T(8,128)(2,1)S(1)} %pad_maximum_fusion.2.mine_ref, bf16[4,160,128]{2,1,0:T(8,128)(2,1)S(1)} %collective-permute-done.17.other_ref), custom_call_target="tpu_custom_call" | custom-call | tf_op jit(solution)/shard_map/pallas_call | solution.py:63
  44.0 2.2 %shard_map.54 = (bf16[8,512,256]{2,1,0:T(8,128)(2,1)S(1)}, f32[64,512]{1,0:T(8,128)S(1)}) custom-call(bf16[512,512]{1,0:T(8,128)(2,1)S(1)} %shard_map.53.whiten_ref, bf16[512,256]{1,0:T(8,128)(2,1)S(1)} %add_convert_fusion.here_ref.refs_0_, bf16[512,256]{1,0:T(8,128)(2,1)S(1)} %collective-permute-done.4.there_ref.refs_1_, ...), custom_call_target="tpu_custom_call" | custom-call | tf_op jit(solution)/shard_map/pallas_call | solution.py:63
  46.3 0.4 collective-permute-start.21
  46.7 1.2 %collective-permute-start.23 = (bf16[64,512]{1,0:T(8,128)(2,1)S(1)}, bf16[64,512]{1,0:T(8,128)(2,1)S(1)}, u32[]{:S(2)}, u32[]{:S(2)}) collective-permute-start(bf16[64,512]{1,0:T(8,128)(2,1)S(1)} %convert_element_type.70), channel_id=1, source_target_pairs={{0,24},{1,25},{2,26},{3,27},{4,28},{5,29},{6,30},{7,31},{8,16},{9,... | collective-permute-start | bytes 196616 | tf_op jit(solution)/shard_map/ppermute | solution.py:33
  47.9 1.9 %collective-permute-start.22 = (bf16[64,512]{1,0:T(8,128)(2,1)S(1)}, bf16[64,512]{1,0:T(8,128)(2,1)S(1)}, u32[]{:S(2)}, u32[]{:S(2)}) collective-permute-start(bf16[64,512]{1,0:T(8,128)(2,1)S(1)} %convert_element_type.70), channel_id=1, source_target_pairs={{0,16},{1,17},{2,18},{3,19},{4,20},{5,21},{6,22},{7,23},{8,24},{9,... | collective-permute-start | bytes 196616 | tf_op jit(solution)/shard_map/ppermute | solution.py:33
  49.8 0.8 collective-permute-done.21
  50.6 2.6 %collective-permute-done.23 = bf16[64,512]{1,0:T(8,128)(2,1)S(1)} collective-permute-done((bf16[64,512]{1,0:T(8,128)(2,1)S(1)}, bf16[64,512]{1,0:T(8,128)(2,1)S(1)}, u32[]{:S(2)}, u32[]{:S(2)}) %collective-permute-start.23) | collective-permute-done | bytes 65568 | tf_op jit(solution)/shard_map/ppermute | solution.py:33
  53.2 2.7 %collective-permute-done.22 = bf16[64,512]{1,0:T(8,128)(2,1)S(1)} collective-permute-done((bf16[64,512]{1,0:T(8,128)(2,1)S(1)}, bf16[64,512]{1,0:T(8,128)(2,1)S(1)}, u32[]{:S(2)}, u32[]{:S(2)}) %collective-permute-start.22) | collective-permute-done | bytes 65568 | tf_op jit(solution)/shard_map/ppermute | solution.py:33
  55.9 2.6 %collective-permute-start.26 = (bf16[64,512]{1,0:T(8,128)(2,1)S(1)}, bf16[64,512]{1,0:T(8,128)(2,1)S(1)}, u32[]{:S(2)}, u32[]{:S(2)}) collective-permute-start(bf16[64,512]{1,0:T(8,128)(2,1)S(1)} %add_convert_fusion.2), channel_id=1, source_target_pairs={{0,6},{1,7},{2,4},{3,5},{4,2},{5,3},{6,0},{7,1},{8,14},{9,15},{10,... | collective-permute-start | bytes 196616 | tf_op jit(solution)/shard_map/ppermute | solution.py:33
  58.5 0.5 collective-permute-start.25
  59.0 0.4 collective-permute-start.24
  59.5 1.8 %collective-permute-done.26 = bf16[64,512]{1,0:T(8,128)(2,1)S(1)} collective-permute-done((bf16[64,512]{1,0:T(8,128)(2,1)S(1)}, bf16[64,512]{1,0:T(8,128)(2,1)S(1)}, u32[]{:S(2)}, u32[]{:S(2)}) %collective-permute-start.26) | collective-permute-done | bytes 65568 | tf_op jit(solution)/shard_map/ppermute | solution.py:33
  61.3 1.5 %collective-permute-done.25 = bf16[64,512]{1,0:T(8,128)(2,1)S(1)} collective-permute-done((bf16[64,512]{1,0:T(8,128)(2,1)S(1)}, bf16[64,512]{1,0:T(8,128)(2,1)S(1)}, u32[]{:S(2)}, u32[]{:S(2)}) %collective-permute-start.25) | collective-permute-done | bytes 65568 | tf_op jit(solution)/shard_map/ppermute | solution.py:33
  62.8 0.5 collective-permute-done.24
  63.4 1.5 %collective-permute-done.27.other_ref = bf16[4,64,512]{2,1,0:T(8,128)(2,1)S(1)} collective-permute-done((bf16[4,64,512]{2,1,0:T(8,128)(2,1)S(1)}, bf16[4,64,512]{2,1,0:T(8,128)(2,1)S(1)}, u32[]{:S(2)}, u32[]{:S(2)}) %collective-permute-start.27) | collective-permute-done | bytes 262176 | tf_op jit(solution)/shard_map/ppermute | solution.py:33
  64.9 3.9 %shard_map.55 = f32[64,512]{1,0:T(8,128)S(1)} custom-call(s32[3]{0:T(128)S(1)} %pad_add_fusion.at, bf16[4,64,512]{2,1,0:T(8,128)(2,1)S(1)} %pad_maximum_fusion.mine_ref, bf16[4,64,512]{2,1,0:T(8,128)(2,1)S(1)} %collective-permute-done.27.other_ref, bf16[8,512,256]{2,1,0:T(8,128)(2,1)S(1)} %get-tuple-element.31.white_ref), custom_call_target="tpu_custom_call" | custom-call | tf_op jit(solution)/shard_map/pallas_call | solution.py:63
  69.0 1.6 %collective-permute-start.30 = (bf16[64,512]{1,0:T(8,128)(2,1)S(1)}, bf16[64,512]{1,0:T(8,128)(2,1)S(1)}, u32[]{:S(2)}, u32[]{:S(2)}) collective-permute-start(bf16[64,512]{1,0:T(8,128)(2,1)S(1)} %convert_element_type.75), channel_id=1, source_target_pairs={{0,24},{1,25},{2,26},{3,27},{4,28},{5,29},{6,30},{7,31},{8,16},{9,... | collective-permute-start | bytes 196616 | tf_op jit(solution)/shard_map/ppermute | solution.py:33
  70.5 1.9 %collective-permute-start.29 = (bf16[64,512]{1,0:T(8,128)(2,1)S(1)}, bf16[64,512]{1,0:T(8,128)(2,1)S(1)}, u32[]{:S(2)}, u32[]{:S(2)}) collective-permute-start(bf16[64,512]{1,0:T(8,128)(2,1)S(1)} %convert_element_type.75), channel_id=1, source_target_pairs={{0,16},{1,17},{2,18},{3,19},{4,20},{5,21},{6,22},{7,23},{8,24},{9,... | collective-permute-start | bytes 196616 | tf_op jit(solution)/shard_map/ppermute | solution.py:33
  72.4 0.8 collective-permute-done.28
  73.2 2.6 %collective-permute-done.30 = bf16[64,512]{1,0:T(8,128)(2,1)S(1)} collective-permute-done((bf16[64,512]{1,0:T(8,128)(2,1)S(1)}, bf16[64,512]{1,0:T(8,128)(2,1)S(1)}, u32[]{:S(2)}, u32[]{:S(2)}) %collective-permute-start.30) | collective-permute-done | bytes 65568 | tf_op jit(solution)/shard_map/ppermute | solution.py:33
  75.8 2.7 %collective-permute-done.29 = bf16[64,512]{1,0:T(8,128)(2,1)S(1)} collective-permute-done((bf16[64,512]{1,0:T(8,128)(2,1)S(1)}, bf16[64,512]{1,0:T(8,128)(2,1)S(1)}, u32[]{:S(2)}, u32[]{:S(2)}) %collective-permute-start.29) | collective-permute-done | bytes 65568 | tf_op jit(solution)/shard_map/ppermute | solution.py:33
  78.5 1.4 %collective-permute-start.33 = (bf16[64,512]{1,0:T(8,128)(2,1)S(1)}, bf16[64,512]{1,0:T(8,128)(2,1)S(1)}, u32[]{:S(2)}, u32[]{:S(2)}) collective-permute-start(bf16[64,512]{1,0:T(8,128)(2,1)S(1)} %add_convert_fusion.1), channel_id=1, source_target_pairs={{0,6},{1,7},{2,4},{3,5},{4,2},{5,3},{6,0},{7,1},{8,14},{9,15},{10,... | collective-permute-start | bytes 196616 | tf_op jit(solution)/shard_map/ppermute | solution.py:33
  80.0 0.5 collective-permute-start.32
  80.5 1.6 %collective-permute-start.31 = (bf16[64,512]{1,0:T(8,128)(2,1)S(1)}, bf16[64,512]{1,0:T(8,128)(2,1)S(1)}, u32[]{:S(2)}, u32[]{:S(2)}) collective-permute-start(bf16[64,512]{1,0:T(8,128)(2,1)S(1)} %add_convert_fusion.1), channel_id=1, source_target_pairs={{0,4},{1,5},{2,6},{3,7},{4,0},{5,1},{6,2},{7,3},{8,12},{9,13},{10,... | collective-permute-start | bytes 196616 | tf_op jit(solution)/shard_map/ppermute | solution.py:33
  82.1 1.7 %collective-permute-done.33 = bf16[64,512]{1,0:T(8,128)(2,1)S(1)} collective-permute-done((bf16[64,512]{1,0:T(8,128)(2,1)S(1)}, bf16[64,512]{1,0:T(8,128)(2,1)S(1)}, u32[]{:S(2)}, u32[]{:S(2)}) %collective-permute-start.33) | collective-permute-done | bytes 65568 | tf_op jit(solution)/shard_map/ppermute | solution.py:33
  83.8 0.4 collective-permute-done.32
  84.2 0.5 collective-permute-done.31
  84.9 1.5 %collective-permute-done.34.other_ref = bf16[4,64,512]{2,1,0:T(8,128)(2,1)S(1)} collective-permute-done((bf16[4,64,512]{2,1,0:T(8,128)(2,1)S(1)}, bf16[4,64,512]{2,1,0:T(8,128)(2,1)S(1)}, u32[]{:S(2)}, u32[]{:S(2)}) %collective-permute-start.34) | collective-permute-done | bytes 262176 | tf_op jit(solution)/shard_map/ppermute | solution.py:33
  86.4 3.8 %shard_map.56 = (f32[128,512]{1,0:T(8,128)}, bf16[128,1024]{1,0:T(8,128)(2,1)}) custom-call(s32[3]{0:T(128)S(1)} %pad_add_fusion.at, bf16[4,64,512]{2,1,0:T(8,128)(2,1)S(1)} %pad_maximum_fusion.1.mine_ref, bf16[4,64,512]{2,1,0:T(8,128)(2,1)S(1)} %collective-permute-done.34.other_ref, bf16[8,512,256]{2,1,0:T(8,128)(2,1)S(1)} %get-tuple-element.31.white_ref), custom_call_target="tpu_custom_call" | custom-call | tf_op jit(solution)/shard_map/pallas_call | solution.py:63
  (31 shorter events, 0.6 us)
Async XLA Ops:
  0.6 39.4 %copy-start = (f32[128,512]{1,0:T(8,128)S(1)}, f32[128,512]{1,0:T(8,128)}, u32[]{:S(2)}) copy-start(f32[128,512]{1,0:T(8,128)} %param.5) | copy-start | bytes 786436
  0.6 3.4 %copy-start.1 = (bf16[512,512]{1,0:T(8,128)(2,1)S(1)}, bf16[512,512]{1,0:T(8,128)(2,1)}, u32[]{:S(2)}) copy-start(bf16[512,512]{1,0:T(8,128)(2,1)} %left_ref.3) | copy-start | bytes 1572868
  0.7 3.4 %collective-permute-start = (bf16[512,512]{1,0:T(8,128)(2,1)}, bf16[512,512]{1,0:T(8,128)(2,1)S(1)}, u32[]{:S(2)}, u32[]{:S(2)}) collective-permute-start(bf16[512,512]{1,0:T(8,128)(2,1)} %left_ref.3), channel_id=1, source_target_pairs={{0,1},{1,0},{2,3},{3,2},{4,5},{5,4},{6,7},{7,6},{8,9},{9,8},{10,11... | collective-permute-start | bytes 1572872 | tf_op jit(solution)/shard_map/ppermute | solution.py:33
  2.4 1.6 %collective-permute-start.2 = (bf16[512,256]{1,0:T(8,128)(2,1)S(1)}, bf16[512,256]{1,0:T(8,128)(2,1)S(1)}, u32[]{:S(2)}, u32[]{:S(2)}) collective-permute-start(bf16[512,256]{1,0:T(8,128)(2,1)S(1)} %get-tuple-element.32), channel_id=1, source_target_pairs={{0,1},{1,0},{2,3},{3,2},{4,5},{5,4},{6,7},{7,6},{8,9},{9,8},{10,11... | collective-permute-start | bytes 786440 | tf_op jit(solution)/shard_map/ppermute | solution.py:33
  2.6 4.6 %collective-permute-start.1 = (bf16[512,256]{1,0:T(8,128)(2,1)S(1)}, bf16[512,256]{1,0:T(8,128)(2,1)S(1)}, u32[]{:S(2)}, u32[]{:S(2)}) collective-permute-start(bf16[512,256]{1,0:T(8,128)(2,1)S(1)} %get-tuple-element.33), channel_id=1, source_target_pairs={{0,1},{1,0},{2,3},{3,2},{4,5},{5,4},{6,7},{7,6},{8,9},{9,8},{10,11... | collective-permute-start | bytes 786440 | tf_op jit(solution)/shard_map/ppermute | solution.py:33
  4.5 9.5 %collective-permute-start.3 = (bf16[512,256]{1,0:T(8,128)(2,1)S(1)}, bf16[512,256]{1,0:T(8,128)(2,1)S(1)}, u32[]{:S(2)}, u32[]{:S(2)}) collective-permute-start(bf16[512,256]{1,0:T(8,128)(2,1)S(1)} %shard_map.51), channel_id=1, source_target_pairs={{0,2},{1,3},{2,0},{3,1},{4,6},{5,7},{6,4},{7,5},{8,10},{9,11},{10,... | collective-permute-start | bytes 786440 | tf_op jit(solution)/shard_map/ppermute | solution.py:33
  14.1 1.6 %collective-permute-start.4 = (bf16[512,256]{1,0:T(8,128)(2,1)S(1)}, bf16[512,256]{1,0:T(8,128)(2,1)S(1)}, u32[]{:S(2)}, u32[]{:S(2)}) collective-permute-start(bf16[512,256]{1,0:T(8,128)(2,1)S(1)} %add_convert_fusion.here_ref.refs_0_), channel_id=1, source_target_pairs={{0,1},{1,0},{2,3},{3,2},{4,5},{5,4},{6,7},{7,6},{8,9},{9,8},{10,11... | collective-permute-start | bytes 786440 | tf_op jit(solution)/shard_map/ppermute | solution.py:33
  16.6 6.8 %collective-permute-start.5 = (bf16[160,128]{1,0:T(8,128)(2,1)S(1)}, bf16[160,128]{1,0:T(8,128)(2,1)S(1)}, u32[]{:S(2)}, u32[]{:S(2)}) collective-permute-start(bf16[160,128]{1,0:T(8,128)(2,1)S(1)} %get-tuple-element.19), channel_id=1, source_target_pairs={{0,6},{1,7},{2,4},{3,5},{4,2},{5,3},{6,0},{7,1},{8,14},{9,15},{10,... | collective-permute-start | bytes 122888 | tf_op jit(solution)/shard_map/ppermute | solution.py:33
  19.3 4.1 %collective-permute-start.6 = (bf16[160,128]{1,0:T(8,128)(2,1)S(1)}, bf16[160,128]{1,0:T(8,128)(2,1)S(1)}, u32[]{:S(2)}, u32[]{:S(2)}) collective-permute-start(bf16[160,128]{1,0:T(8,128)(2,1)S(1)} %get-tuple-element.20), channel_id=1, source_target_pairs={{0,2},{1,3},{2,0},{3,1},{4,6},{5,7},{6,4},{7,5},{8,10},{9,11},{10,... | collective-permute-start | bytes 122888 | tf_op jit(solution)/shard_map/ppermute | solution.py:33
  19.9 4.5 %collective-permute-start.7 = (bf16[160,128]{1,0:T(8,128)(2,1)S(1)}, bf16[160,128]{1,0:T(8,128)(2,1)S(1)}, u32[]{:S(2)}, u32[]{:S(2)}) collective-permute-start(bf16[160,128]{1,0:T(8,128)(2,1)S(1)} %get-tuple-element.21), channel_id=1, source_target_pairs={{0,4},{1,5},{2,6},{3,7},{4,0},{5,1},{6,2},{7,3},{8,12},{9,13},{10,... | collective-permute-start | bytes 122888 | tf_op jit(solution)/shard_map/ppermute | solution.py:33
  20.1 9.9 %collective-permute-start.10 = (bf16[512,256]{1,0:T(8,128)(2,1)S(1)}, bf16[512,256]{1,0:T(8,128)(2,1)S(1)}, u32[]{:S(2)}, u32[]{:S(2)}) collective-permute-start(bf16[512,256]{1,0:T(8,128)(2,1)S(1)} %add_convert_fusion.here_ref.refs_0_), channel_id=1, source_target_pairs={{0,4},{1,5},{2,6},{3,7},{4,0},{5,1},{6,2},{7,3},{8,12},{9,13},{10,... | collective-permute-start | bytes 786440 | tf_op jit(solution)/shard_map/ppermute | solution.py:33
  21.9 8.1 %collective-permute-start.9 = (bf16[512,256]{1,0:T(8,128)(2,1)S(1)}, bf16[512,256]{1,0:T(8,128)(2,1)S(1)}, u32[]{:S(2)}, u32[]{:S(2)}) collective-permute-start(bf16[512,256]{1,0:T(8,128)(2,1)S(1)} %add_convert_fusion.here_ref.refs_0_), channel_id=1, source_target_pairs={{0,2},{1,3},{2,0},{3,1},{4,6},{5,7},{6,4},{7,5},{8,10},{9,11},{10,... | collective-permute-start | bytes 786440 | tf_op jit(solution)/shard_map/ppermute | solution.py:33
  24.4 4.5 %collective-permute-start.8 = (bf16[160,128]{1,0:T(8,128)(2,1)S(1)}, bf16[160,128]{1,0:T(8,128)(2,1)S(1)}, u32[]{:S(2)}, u32[]{:S(2)}) collective-permute-start(bf16[160,128]{1,0:T(8,128)(2,1)S(1)} %convert_element_type.65), channel_id=1, source_target_pairs={{0,8},{1,9},{2,10},{3,11},{4,12},{5,13},{6,14},{7,15},{8,0},{9,1},... | collective-permute-start | bytes 122888 | tf_op jit(solution)/shard_map/ppermute | solution.py:33
  26.1 5.8 %collective-permute-start.12 = (bf16[160,128]{1,0:T(8,128)(2,1)S(1)}, bf16[160,128]{1,0:T(8,128)(2,1)S(1)}, u32[]{:S(2)}, u32[]{:S(2)}) collective-permute-start(bf16[160,128]{1,0:T(8,128)(2,1)S(1)} %convert_element_type.65), channel_id=1, source_target_pairs={{0,24},{1,25},{2,26},{3,27},{4,28},{5,29},{6,30},{7,31},{8,16},{9,... | collective-permute-start | bytes 122888 | tf_op jit(solution)/shard_map/ppermute | solution.py:33
  28.5 5.3 %collective-permute-start.11 = (bf16[160,128]{1,0:T(8,128)(2,1)S(1)}, bf16[160,128]{1,0:T(8,128)(2,1)S(1)}, u32[]{:S(2)}, u32[]{:S(2)}) collective-permute-start(bf16[160,128]{1,0:T(8,128)(2,1)S(1)} %convert_element_type.65), channel_id=1, source_target_pairs={{0,16},{1,17},{2,18},{3,19},{4,20},{5,21},{6,22},{7,23},{8,24},{9,... | collective-permute-start | bytes 122888 | tf_op jit(solution)/shard_map/ppermute | solution.py:33
  28.9 8.5 %collective-permute-start.16 = (bf16[512,256]{1,0:T(8,128)(2,1)S(1)}, bf16[512,256]{1,0:T(8,128)(2,1)S(1)}, u32[]{:S(2)}, u32[]{:S(2)}) collective-permute-start(bf16[512,256]{1,0:T(8,128)(2,1)S(1)} %add_convert_fusion.here_ref.refs_0_), channel_id=1, source_target_pairs={{0,6},{1,7},{2,4},{3,5},{4,2},{5,3},{6,0},{7,1},{8,14},{9,15},{10,... | collective-permute-start | bytes 786440 | tf_op jit(solution)/shard_map/ppermute | solution.py:33
  33.9 5.0 %collective-permute-start.15 = (bf16[160,128]{1,0:T(8,128)(2,1)S(1)}, bf16[160,128]{1,0:T(8,128)(2,1)S(1)}, u32[]{:S(2)}, u32[]{:S(2)}) collective-permute-start(bf16[160,128]{1,0:T(8,128)(2,1)S(1)} %add_convert_fusion.3), channel_id=1, source_target_pairs={{0,6},{1,7},{2,4},{3,5},{4,2},{5,3},{6,0},{7,1},{8,14},{9,15},{10,... | collective-permute-start | bytes 122888 | tf_op jit(solution)/shard_map/ppermute | solution.py:33
  35.4 4.0 %collective-permute-start.14 = (bf16[160,128]{1,0:T(8,128)(2,1)S(1)}, bf16[160,128]{1,0:T(8,128)(2,1)S(1)}, u32[]{:S(2)}, u32[]{:S(2)}) collective-permute-start(bf16[160,128]{1,0:T(8,128)(2,1)S(1)} %add_convert_fusion.3), channel_id=1, source_target_pairs={{0,2},{1,3},{2,0},{3,1},{4,6},{5,7},{6,4},{7,5},{8,10},{9,11},{10,... | collective-permute-start | bytes 122888 | tf_op jit(solution)/shard_map/ppermute | solution.py:33
  35.9 4.0 %collective-permute-start.13 = (bf16[160,128]{1,0:T(8,128)(2,1)S(1)}, bf16[160,128]{1,0:T(8,128)(2,1)S(1)}, u32[]{:S(2)}, u32[]{:S(2)}) collective-permute-start(bf16[160,128]{1,0:T(8,128)(2,1)S(1)} %add_convert_fusion.3), channel_id=1, source_target_pairs={{0,4},{1,5},{2,6},{3,7},{4,0},{5,1},{6,2},{7,3},{8,12},{9,13},{10,... | collective-permute-start | bytes 122888 | tf_op jit(solution)/shard_map/ppermute | solution.py:33
  37.5 6.5 %collective-permute-start.18 = (bf16[512,256]{1,0:T(8,128)(2,1)S(1)}, bf16[512,256]{1,0:T(8,128)(2,1)S(1)}, u32[]{:S(2)}, u32[]{:S(2)}) collective-permute-start(bf16[512,256]{1,0:T(8,128)(2,1)S(1)} %collective-permute-done.9.refs_2_), channel_id=1, source_target_pairs={{0,1},{1,0},{2,3},{3,2},{4,5},{5,4},{6,7},{7,6},{8,9},{9,8},{10,11... | collective-permute-start | bytes 786440 | tf_op jit(solution)/shard_map/ppermute | solution.py:33
  37.5 6.6 %collective-permute-start.19 = (bf16[512,256]{1,0:T(8,128)(2,1)S(1)}, bf16[512,256]{1,0:T(8,128)(2,1)S(1)}, u32[]{:S(2)}, u32[]{:S(2)}) collective-permute-start(bf16[512,256]{1,0:T(8,128)(2,1)S(1)} %collective-permute-done.10.refs_4_), channel_id=1, source_target_pairs={{0,1},{1,0},{2,3},{3,2},{4,5},{5,4},{6,7},{7,6},{8,9},{9,8},{10,11... | collective-permute-start | bytes 786440 | tf_op jit(solution)/shard_map/ppermute | solution.py:33
  38.9 5.2 %collective-permute-start.20 = (bf16[512,256]{1,0:T(8,128)(2,1)S(1)}, bf16[512,256]{1,0:T(8,128)(2,1)S(1)}, u32[]{:S(2)}, u32[]{:S(2)}) collective-permute-start(bf16[512,256]{1,0:T(8,128)(2,1)S(1)} %collective-permute-done.16.refs_6_), channel_id=1, source_target_pairs={{0,1},{1,0},{2,3},{3,2},{4,5},{5,4},{6,7},{7,6},{8,9},{9,8},{10,11... | collective-permute-start | bytes 786440 | tf_op jit(solution)/shard_map/ppermute | solution.py:33
  39.9 1.5 %collective-permute-start.17 = (bf16[4,160,128]{2,1,0:T(8,128)(2,1)S(1)}, bf16[4,160,128]{2,1,0:T(8,128)(2,1)S(1)}, u32[]{:S(2)}, u32[]{:S(2)}) collective-permute-start(bf16[4,160,128]{2,1,0:T(8,128)(2,1)S(1)} %pad_maximum_fusion.2.mine_ref), channel_id=1, source_target_pairs={{0,1},{1,0},{2,3},{3,2},{4,5},{5,4},{6,7},{7,6},{8,9},{9,8},{10,11... | collective-permute-start | bytes 491528 | tf_op jit(solution)/shard_map/ppermute | solution.py:33
  46.3 4.3 %collective-permute-start.21 = (bf16[64,512]{1,0:T(8,128)(2,1)S(1)}, bf16[64,512]{1,0:T(8,128)(2,1)S(1)}, u32[]{:S(2)}, u32[]{:S(2)}) collective-permute-start(bf16[64,512]{1,0:T(8,128)(2,1)S(1)} %convert_element_type.70), channel_id=1, source_target_pairs={{0,8},{1,9},{2,10},{3,11},{4,12},{5,13},{6,14},{7,15},{8,0},{9,1},... | collective-permute-start | bytes 196616 | tf_op jit(solution)/shard_map/ppermute | solution.py:33
  46.7 6.5 %collective-permute-start.23 = (bf16[64,512]{1,0:T(8,128)(2,1)S(1)}, bf16[64,512]{1,0:T(8,128)(2,1)S(1)}, u32[]{:S(2)}, u32[]{:S(2)}) collective-permute-start(bf16[64,512]{1,0:T(8,128)(2,1)S(1)} %convert_element_type.70), channel_id=1, source_target_pairs={{0,24},{1,25},{2,26},{3,27},{4,28},{5,29},{6,30},{7,31},{8,16},{9,... | collective-permute-start | bytes 196616 | tf_op jit(solution)/shard_map/ppermute | solution.py:33
  47.9 8.0 %collective-permute-start.22 = (bf16[64,512]{1,0:T(8,128)(2,1)S(1)}, bf16[64,512]{1,0:T(8,128)(2,1)S(1)}, u32[]{:S(2)}, u32[]{:S(2)}) collective-permute-start(bf16[64,512]{1,0:T(8,128)(2,1)S(1)} %convert_element_type.70), channel_id=1, source_target_pairs={{0,16},{1,17},{2,18},{3,19},{4,20},{5,21},{6,22},{7,23},{8,24},{9,... | collective-permute-start | bytes 196616 | tf_op jit(solution)/shard_map/ppermute | solution.py:33
  55.9 5.3 %collective-permute-start.26 = (bf16[64,512]{1,0:T(8,128)(2,1)S(1)}, bf16[64,512]{1,0:T(8,128)(2,1)S(1)}, u32[]{:S(2)}, u32[]{:S(2)}) collective-permute-start(bf16[64,512]{1,0:T(8,128)(2,1)S(1)} %add_convert_fusion.2), channel_id=1, source_target_pairs={{0,6},{1,7},{2,4},{3,5},{4,2},{5,3},{6,0},{7,1},{8,14},{9,15},{10,... | collective-permute-start | bytes 196616 | tf_op jit(solution)/shard_map/ppermute | solution.py:33
  58.5 4.3 %collective-permute-start.25 = (bf16[64,512]{1,0:T(8,128)(2,1)S(1)}, bf16[64,512]{1,0:T(8,128)(2,1)S(1)}, u32[]{:S(2)}, u32[]{:S(2)}) collective-permute-start(bf16[64,512]{1,0:T(8,128)(2,1)S(1)} %add_convert_fusion.2), channel_id=1, source_target_pairs={{0,2},{1,3},{2,0},{3,1},{4,6},{5,7},{6,4},{7,5},{8,10},{9,11},{10,... | collective-permute-start | bytes 196616 | tf_op jit(solution)/shard_map/ppermute | solution.py:33
  59.0 4.3 %collective-permute-start.24 = (bf16[64,512]{1,0:T(8,128)(2,1)S(1)}, bf16[64,512]{1,0:T(8,128)(2,1)S(1)}, u32[]{:S(2)}, u32[]{:S(2)}) collective-permute-start(bf16[64,512]{1,0:T(8,128)(2,1)S(1)} %add_convert_fusion.2), channel_id=1, source_target_pairs={{0,4},{1,5},{2,6},{3,7},{4,0},{5,1},{6,2},{7,3},{8,12},{9,13},{10,... | collective-permute-start | bytes 196616 | tf_op jit(solution)/shard_map/ppermute | solution.py:33
  63.3 1.6 %collective-permute-start.27 = (bf16[4,64,512]{2,1,0:T(8,128)(2,1)S(1)}, bf16[4,64,512]{2,1,0:T(8,128)(2,1)S(1)}, u32[]{:S(2)}, u32[]{:S(2)}) collective-permute-start(bf16[4,64,512]{2,1,0:T(8,128)(2,1)S(1)} %pad_maximum_fusion.mine_ref), channel_id=1, source_target_pairs={{0,1},{1,0},{2,3},{3,2},{4,5},{5,4},{6,7},{7,6},{8,9},{9,8},{10,11... | collective-permute-start | bytes 786440 | tf_op jit(solution)/shard_map/ppermute | solution.py:33
  68.9 4.3 %collective-permute-start.28 = (bf16[64,512]{1,0:T(8,128)(2,1)S(1)}, bf16[64,512]{1,0:T(8,128)(2,1)S(1)}, u32[]{:S(2)}, u32[]{:S(2)}) collective-permute-start(bf16[64,512]{1,0:T(8,128)(2,1)S(1)} %convert_element_type.75), channel_id=1, source_target_pairs={{0,8},{1,9},{2,10},{3,11},{4,12},{5,13},{6,14},{7,15},{8,0},{9,1},... | collective-permute-start | bytes 196616 | tf_op jit(solution)/shard_map/ppermute | solution.py:33
  69.0 6.8 %collective-permute-start.30 = (bf16[64,512]{1,0:T(8,128)(2,1)S(1)}, bf16[64,512]{1,0:T(8,128)(2,1)S(1)}, u32[]{:S(2)}, u32[]{:S(2)}) collective-permute-start(bf16[64,512]{1,0:T(8,128)(2,1)S(1)} %convert_element_type.75), channel_id=1, source_target_pairs={{0,24},{1,25},{2,26},{3,27},{4,28},{5,29},{6,30},{7,31},{8,16},{9,... | collective-permute-start | bytes 196616 | tf_op jit(solution)/shard_map/ppermute | solution.py:33
  70.5 7.9 %collective-permute-start.29 = (bf16[64,512]{1,0:T(8,128)(2,1)S(1)}, bf16[64,512]{1,0:T(8,128)(2,1)S(1)}, u32[]{:S(2)}, u32[]{:S(2)}) collective-permute-start(bf16[64,512]{1,0:T(8,128)(2,1)S(1)} %convert_element_type.75), channel_id=1, source_target_pairs={{0,16},{1,17},{2,18},{3,19},{4,20},{5,21},{6,22},{7,23},{8,24},{9,... | collective-permute-start | bytes 196616 | tf_op jit(solution)/shard_map/ppermute | solution.py:33
  78.5 5.3 %collective-permute-start.33 = (bf16[64,512]{1,0:T(8,128)(2,1)S(1)}, bf16[64,512]{1,0:T(8,128)(2,1)S(1)}, u32[]{:S(2)}, u32[]{:S(2)}) collective-permute-start(bf16[64,512]{1,0:T(8,128)(2,1)S(1)} %add_convert_fusion.1), channel_id=1, source_target_pairs={{0,6},{1,7},{2,4},{3,5},{4,2},{5,3},{6,0},{7,1},{8,14},{9,15},{10,... | collective-permute-start | bytes 196616 | tf_op jit(solution)/shard_map/ppermute | solution.py:33
  80.0 4.3 %collective-permute-start.32 = (bf16[64,512]{1,0:T(8,128)(2,1)S(1)}, bf16[64,512]{1,0:T(8,128)(2,1)S(1)}, u32[]{:S(2)}, u32[]{:S(2)}) collective-permute-start(bf16[64,512]{1,0:T(8,128)(2,1)S(1)} %add_convert_fusion.1), channel_id=1, source_target_pairs={{0,2},{1,3},{2,0},{3,1},{4,6},{5,7},{6,4},{7,5},{8,10},{9,11},{10,... | collective-permute-start | bytes 196616 | tf_op jit(solution)/shard_map/ppermute | solution.py:33
  80.5 4.3 %collective-permute-start.31 = (bf16[64,512]{1,0:T(8,128)(2,1)S(1)}, bf16[64,512]{1,0:T(8,128)(2,1)S(1)}, u32[]{:S(2)}, u32[]{:S(2)}) collective-permute-start(bf16[64,512]{1,0:T(8,128)(2,1)S(1)} %add_convert_fusion.1), channel_id=1, source_target_pairs={{0,4},{1,5},{2,6},{3,7},{4,0},{5,1},{6,2},{7,3},{8,12},{9,13},{10,... | collective-permute-start | bytes 196616 | tf_op jit(solution)/shard_map/ppermute | solution.py:33
  84.8 1.6 %collective-permute-start.34 = (bf16[4,64,512]{2,1,0:T(8,128)(2,1)S(1)}, bf16[4,64,512]{2,1,0:T(8,128)(2,1)S(1)}, u32[]{:S(2)}, u32[]{:S(2)}) collective-permute-start(bf16[4,64,512]{2,1,0:T(8,128)(2,1)S(1)} %pad_maximum_fusion.1.mine_ref), channel_id=1, source_target_pairs={{0,1},{1,0},{2,3},{3,2},{4,5},{5,4},{6,7},{7,6},{8,9},{9,8},{10,11... | collective-permute-start | bytes 786440 | tf_op jit(solution)/shard_map/ppermute | solution.py:33

commit v7 on v6

--- a/solution.py
+++ b/solution.py
@@ -14,6 +14,15 @@
 MIB = 1 << 20
 
 
+def place():
+    vox, comp = lax.axis_index("vox"), lax.axis_index("comp")
+    return lax.rem(comp, 2), lax.div(comp, 2), lax.rem(vox, 2)
+
+
+def other(bit, flipped):
+    return 1 - bit if flipped else bit
+
+
 def nn(left, right):
     return jnp.dot(left, right, preferred_element_type=F32)
 
@@ -36,35 +45,35 @@
 def sum_over(x, masks, due=()):
     for k in range(0, len(masks), 2):
         sent = x.astype(BF)
-        first = flip(sent, masks[k])
-        if k == 0:
-            first, *due = lax.optimization_barrier((first, *due))
-        x = rounded(x) + first.astype(F32)
+        x = rounded(x) + flip(sent, masks[k]).astype(F32)
         if k + 1 < len(masks):
-            x = x + (
-                flip(sent, masks[k + 1]).astype(F32)
-                + flip(sent, masks[k] | masks[k + 1]).astype(F32)
-            )
+            both = flip(sent, masks[k] | masks[k + 1])
+            if k == 0:
+                both, *due = lax.optimization_barrier((both, *due))
+            x = x + (flip(sent, masks[k + 1]).astype(F32) + both.astype(F32))
     return (x.astype(BF), *due)
 
 
 def spread(x, across, near, due=()):
     both = flip(x, across | near)
     both, *due = lax.optimization_barrier((both, *due))
-    return (jnp.stack([x, flip(x, near), flip(x, across), both]), *due)
+    blocks = [x, flip(x, near), flip(x, across), both]
+    if due:
+        mates = flip(jnp.stack(blocks), 1)
+        return (blocks + [mates[k] for k in range(4)], *due)
+    return blocks + [flip(block, 1) for block in blocks]
 
 
 VMEM = pl.BlockSpec(memory_space=pltpu.VMEM)
-SMEM = pl.BlockSpec(memory_space=pltpu.SMEM)
 HBM = pl.BlockSpec(memory_space=pltpu.HBM)
 
 
-def run(kernel, outs, args, specs=None, scratch=(), limit=24):
+def run(kernel, outs, args, specs=None, out_spec=VMEM, scratch=(), limit=24):
     return pl.pallas_call(
         kernel,
         out_shape=outs,
-        in_specs=specs or [SMEM] + [VMEM] * (len(args) - 1),
-        out_specs=jax.tree.map(lambda _: VMEM, outs),
+        in_specs=specs or [VMEM] * len(args),
+        out_specs=jax.tree.map(lambda _: out_spec, outs),
         scratch_shapes=list(scratch),
         compiler_params=pltpu.CompilerParams(vmem_limit_bytes=limit * MIB),
     )(*args)
@@ -80,7 +89,7 @@
     out_ref[...] = total.astype(out_ref.dtype)
 
 
-def covar_kernel(at, here_ref, there_ref, own_ref, y_ref, x_ref, xy_ref, pack):
+def covar_kernel(here_ref, there_ref, own_ref, y_ref, x_ref, xy_ref, pack):
     rows = here_ref.shape[0]
     block = rows // 4
 
@@ -92,7 +101,7 @@
             total += nt(left, right)
         return total
 
-    low = at[0]
+    low, ax, ay = place()
     corner = product(2 * low, 2 * low, 2)
     cross = product(2 + low, 0, 1)
     pack[0 * block : 1 * block] = corner[:block, :block]
@@ -105,23 +114,22 @@
     def quarter(i, j):
         return pack[pl.ds(pl.multiple_of((2 * i + j) * piece, piece), piece), :]
 
-    ax, ay = at[1], at[2]
     own_ref[...] = quarter(ax, ay)
     y_ref[...] = quarter(ax, 1 - ay).astype(BF)
     x_ref[...] = quarter(1 - ax, ay).astype(BF)
     xy_ref[...] = quarter(1 - ax, 1 - ay).astype(BF)
 
 
-def whiten_kernel(voxels, at, mine_ref, other_ref, out_ref, packs, covar):
-    piece = mine_ref.shape[1]
-    block = mine_ref.shape[2]
+def whiten_kernel(voxels, *refs):
+    mine, mates, (out_ref, packs, covar) = refs[:4], refs[4:8], refs[8:]
+    piece, block = mine[0].shape
     rows = covar.shape[0]
-    low, ax, ay = at[0], at[1], at[2]
+    low, ax, ay = place()
     for k in range(4):
-        i, j = ax ^ (k >> 1), ay ^ (k & 1)
-        place = pl.ds(pl.multiple_of((2 * i + j) * piece, piece), piece)
-        packs[low, place, :] = mine_ref[k].astype(F32) * (1.0 / voxels)
-        packs[1 - low, place, :] = other_ref[k].astype(F32) * (1.0 / voxels)
+        spot = 2 * other(ax, k & 2) + other(ay, k & 1)
+        spot = pl.ds(pl.multiple_of(spot * piece, piece), piece)
+        packs[low, spot, :] = mine[k][...].astype(F32) * (1.0 / voxels)
+        packs[1 - low, spot, :] = mates[k][...].astype(F32) * (1.0 / voxels)
 
     squares = jnp.zeros((block, block), F32)
 
@@ -182,18 +190,20 @@
     newer_ref[...] = total - slope * weights
 
 
-def decor_kernel(last, at, mine_ref, other_ref, white_ref, *refs):
-    outs, (newer, lower, white, sem) = refs[:-4], refs[-4:]
-    count = mine_ref.shape[1]
-    low, ax, ay = at[0], at[1], at[2]
+def decor_kernel(last, *refs):
+    mine, mates, white_ref = refs[:4], refs[4:8], refs[8]
+    outs, scratch = (refs[9:11], refs[11:]) if last else (refs[9:10], refs[10:])
+    newer, lower, white, sem, *held = scratch
+    count = mine[0].shape[0]
+    low, ax, ay = place()
     chunks = white.shape[0]
     copy = pltpu.make_async_copy(white_ref.at[pl.ds(0, chunks)], white, sem)
     copy.start()
     for k in range(4):
-        i, j = ax ^ (k >> 1), ay ^ (k & 1)
-        for ref, core in ((mine_ref, low), (other_ref, 1 - low)):
-            start = pl.multiple_of((4 * i + 2 * core + j) * count, count)
-            lower[pl.ds(start, count), :] = ref[k]
+        spot = 4 * other(ax, k & 2) + other(ay, k & 1)
+        for ref, core in ((mine[k], low), (mates[k], 1 - low)):
+            start = pl.multiple_of((spot + 2 * core) * count, count)
+            lower[pl.ds(start, count), :] = ref[...]
 
     raw = lower[...]
     gram = nt(raw, raw)
@@ -214,13 +224,21 @@
     weights = 1.5 * newer[pl.ds(start, size), :] - 0.5 * nn(gram, raw)
     copy.wait()
     if last:
-        outs[0][...] = weights
+        unmixing, sources, sems = held
+        unmixing[...] = weights
+        copies = [pltpu.make_async_copy(unmixing, outs[0], sems.at[chunks])]
+        copies[0].start()
         width = white.shape[2]
         for k in range(chunks):
-            place = 2 * (ax ^ (k >> 1)) + (low ^ (k & 1))
-            outs[1][:, pl.ds(pl.multiple_of(place * width, width), width)] = nn(
-                weights.astype(BF), white[k]
-            ).astype(BF)
+            sources[k] = nn(weights.astype(BF), white[k]).astype(BF)
+            spot = 2 * other(ax, k & 2) + other(low, k & 1)
+            spot = pl.ds(pl.multiple_of(spot * width, width), width)
+            copies.append(
+                pltpu.make_async_copy(sources.at[k], outs[1].at[:, spot], sems.at[k])
+            )
+            copies[-1].start()
+        for copy in copies:
+            copy.wait()
     else:
         total, slope = step(weights, [white[k] for k in range(chunks)])
         outs[0][...] = total - slope * weights
@@ -229,12 +247,10 @@
 def shards(data, projection, initial):
     comps = lax.axis_size("comp")
     voxels = data.shape[1] * lax.axis_size("vox")
-    vox, comp = lax.axis_index("vox"), lax.axis_index("comp")
-    index = vox * comps + comp
     all_bits = (lax.axis_size("vox") * comps).bit_length() - 1
     low, across, near = 1, 2, comps
     far = [1 << k for k in range(near.bit_length(), all_bits)]
-    at = jnp.stack([comp & 1, comp >> 1, vox & 1]).astype(jnp.int32)
+    core, far_x, near_y = place()
     rows = projection.shape[0]
     size = data.shape[1] // comps
 
@@ -243,16 +259,14 @@
     def columns(x, core):
         return lax.dynamic_slice_in_dim(data, (x * 2 + core) * size, size, 1)
 
-    here, away = at[1], 1 - at[1]
-    other = [columns(x, 1 - at[0]) for x in (away, here)]
-    mine = [columns(x, at[0]) for x in (away, here)]
-    other = [flip(block, low) for block in other]
+    sides = (1 - far_x, far_x)
+    theirs = [flip(columns(x, 1 - core), low) for x in sides]
+    mine = [columns(x, core) for x in sides]
     sent, kept = (
         run(
             project_kernel,
             shape((rows, size), kind),
-            (projection, mine[k], mate, other[k]),
-            specs=[VMEM] * 4,
+            (projection, mine[k], mate, theirs[k]),
         )
         for k, kind in enumerate((BF, F32))
     )
@@ -265,7 +279,7 @@
     own, by, bx, bxy = run(
         covar_kernel,
         (shape((piece, block), F32), small, small, small),
-        (at, reduced, there),
+        (reduced, there),
         scratch=[pltpu.VMEM((5 * block, block), F32)],
     )
     own, reduced = lax.optimization_barrier((own, reduced))
@@ -277,45 +291,51 @@
     at_xy = flip(reduced, across | near)
     packed, at_x, at_y = sum_over(own, far, (at_x, at_y))
     packed, at_xy = spread(packed, across, near, (at_xy,))
-    mate = flip(packed, low)
     whiten = run(
         functools.partial(whiten_kernel, voxels),
         shape((rows, rows), BF),
-        (at, packed, mate),
+        packed,
         scratch=[pltpu.VMEM((2, 5 * block, block), F32), pltpu.VMEM((rows, rows), F32)],
     )
 
     count = initial.shape[0] // 2
-    weights = lax.dynamic_slice_in_dim(initial, at[2] * count, count, 0)
+    weights = lax.dynamic_slice_in_dim(initial, near_y * count, count, 0)
     blocks = (reduced, there, at_x, flip(at_x, low))
     blocks += (at_y, flip(at_y, low), at_xy, flip(at_xy, low))
     white, newer = run(
         apply_kernel,
         (shape((len(blocks), rows, size), BF), shape((count, rows), F32)),
         (whiten, *blocks, weights),
-        specs=[VMEM] * (len(blocks) + 2),
     )
 
     for turn in range(ICA_ITERS):
         last = turn == ICA_ITERS - 1
-        (stacked,) = spread(*sum_over(newer, far), across, near)
+        stacked = spread(*sum_over(newer, far), across, near)
         chunks = len(blocks) // 2 if last else len(blocks)
         outs = (
             (shape((2 * count, rows), F32), shape((2 * count, data.shape[1]), BF))
             if last
             else shape((count, rows), F32)
         )
+        scratch = [
+            pltpu.VMEM((rows, rows), F32),
+            pltpu.VMEM((rows, rows), BF),
+            pltpu.VMEM((chunks, rows, size), BF),
+            pltpu.SemaphoreType.DMA,
+        ]
+        if last:
+            scratch += [
+                pltpu.VMEM((2 * count, rows), F32),
+                pltpu.VMEM((chunks, 2 * count, size), BF),
+                pltpu.SemaphoreType.DMA((chunks + 1,)),
+            ]
         newer = run(
             functools.partial(decor_kernel, last),
             outs,
-            (at, stacked, flip(stacked, low), white),
-            specs=[SMEM, VMEM, VMEM] + [HBM],
-            scratch=[
-                pltpu.VMEM((rows, rows), F32),
-                pltpu.VMEM((rows, rows), BF),
-                pltpu.VMEM((chunks, rows, size), BF),
-                pltpu.SemaphoreType.DMA,
-            ],
+            (*stacked, white),
+            specs=[VMEM] * 8 + [HBM],
+            out_spec=HBM if last else VMEM,
+            scratch=scratch,
         )
     return newer
 

time: 90.3 us -> 85.8 us (0.950)
  waiting for transfers between devices: 38.8 us -> 34 us
  starting transfers between devices: 34.5 us -> 37.1 us
  Pallas kernels: 14.3 us -> 12.1 us
    ppermute x35 -> x41, waiting for transfers between devices: 38.8 us -> 34 us  [flip(): return lax.ppermute(x, AXES, [(i, i ^ mask) for i in range(count)])]
    ppermute x35 -> x41, starting transfers between devices: 34.5 us -> 37.1 us  [flip(): return lax.ppermute(x, AXES, [(i, i ^ mask) for i in range(count)])]
    pallas_call x7, Pallas kernels: 14.3 us -> 12.1 us  [run(): pl.pallas_call(kernel, out_shape=outs, in_specs=specs or [VMEM] * len(arg...]
  transfers between devices with their start and end apart: 35 -> 41, of which waited for: 25 -> 25; matrix products, arithmetic and copies ran while one was open for 2% -> 2% of each run, Pallas kernels for 4% -> 3%
where the time goes in v7:
time: 85.8 us; the launch traced here: 85.6 us
  starting transfers between devices  37.1 us (43%)
  waiting for transfers between devices  34 us (40%)
  Pallas kernels  12.1 us (14%)
  local copies, waits for them, and re-layouts  1.3 us (2%)
    ppermute x41, starting transfers between devices, flip(): return lax.ppermute(x, AXES, [(i, i ^ mask) for i in range(count)])  37.1 us
    ppermute x41, waiting for transfers between devices, flip(): return lax.ppermute(x, AXES, [(i, i ^ mask) for i in range(count)])  34 us
    pallas_call x7, Pallas kernels, run(): pl.pallas_call(kernel, out_shape=outs, in_specs=specs or [VMEM] * len(arg...  12.1 us
  transfers between devices with their start and end apart: 41, of which 25 were waited for; matrix products, arithmetic and copies ran while one was open for 2% of the time, Pallas kernels for 3%

profile of v7, /device:TPU:0, one launch (start us, length us, event | category | flops | bytes accessed | tf_op | source)
XLA Modules:
  0.0 85.6 jit_solution(13392873833787994181)
XLA Ops:
  0.7 0.5 collective-permute-start
  1.2 1.3 %constant_dynamic-slice_fusion.1 = (bf16[512,256]{1,0:T(8,128)(2,1)S(1)}, bf16[512,256]{1,0:T(8,128)(2,1)S(1)}, bf16[512,256]{1,0:T(8,128)(2,1)S(1)}, bf16[512,256]{1,0:T(8,128)(2,1)S(1)}) fusion(bf16[512,1024]{1,0:T(8,128)(2,1)} %param.3, s32[]{:T(128)S(6)} %select_n.18, s32[]{:T(128)S(6)} %select_n.16, s32[]{:T(128)S(6)} %select_n.15, s32[]{:T(128)S(6)} %select_n.17), kind=kLoop, calls=%fused_computation.11 | loop fusion | bytes 2097168 | tf_op jit(solution)/shard_map/dynamic_slice | solution.py:260
  2.4 0.2 collective-permute-start.2
  2.6 0.4 collective-permute-start.1
  3.0 1.0 %collective-permute-done.2.mate_right_ref = bf16[512,256]{1,0:T(8,128)(2,1)S(1)} collective-permute-done((bf16[512,256]{1,0:T(8,128)(2,1)S(1)}, bf16[512,256]{1,0:T(8,128)(2,1)S(1)}, u32[]{:S(2)}, u32[]{:S(2)}) %collective-permute-start.2) | collective-permute-done | bytes 262176 | tf_op jit(solution)/shard_map/ppermute | solution.py:42
  4.1 0.4 shard_map.51
  4.5 2.7 %collective-permute-start.3 = (bf16[512,256]{1,0:T(8,128)(2,1)S(1)}, bf16[512,256]{1,0:T(8,128)(2,1)S(1)}, u32[]{:S(2)}, u32[]{:S(2)}) collective-permute-start(bf16[512,256]{1,0:T(8,128)(2,1)S(1)} %shard_map.51), channel_id=1, source_target_pairs={{0,2},{1,3},{2,0},{3,1},{4,6},{5,7},{6,4},{7,5},{8,10},{9,11},{10,... | collective-permute-start | bytes 786440 | tf_op jit(solution)/shard_map/ppermute | solution.py:42
  7.2 0.4 shard_map.50
  7.6 6.4 %collective-permute-done.3 = bf16[512,256]{1,0:T(8,128)(2,1)S(1)} collective-permute-done((bf16[512,256]{1,0:T(8,128)(2,1)S(1)}, bf16[512,256]{1,0:T(8,128)(2,1)S(1)}, u32[]{:S(2)}, u32[]{:S(2)}) %collective-permute-start.3) | collective-permute-done | bytes 262176 | tf_op jit(solution)/shard_map/ppermute | solution.py:42
  14.0 0.1 add_convert_fusion.here_ref.refs_0_
  14.1 0.1 collective-permute-start.4
  14.2 1.5 %collective-permute-done.4.there_ref.refs_1_ = bf16[512,256]{1,0:T(8,128)(2,1)S(1)} collective-permute-done((bf16[512,256]{1,0:T(8,128)(2,1)S(1)}, bf16[512,256]{1,0:T(8,128)(2,1)S(1)}, u32[]{:S(2)}, u32[]{:S(2)}) %collective-permute-start.4) | collective-permute-done | bytes 262176 | tf_op jit(solution)/shard_map/ppermute | solution.py:42
  15.7 0.3 shard_map.52
  16.0 2.8 %collective-permute-start.5 = (bf16[160,128]{1,0:T(8,128)(2,1)S(1)}, bf16[160,128]{1,0:T(8,128)(2,1)S(1)}, u32[]{:S(2)}, u32[]{:S(2)}) collective-permute-start(bf16[160,128]{1,0:T(8,128)(2,1)S(1)} %get-tuple-element.19), channel_id=1, source_target_pairs={{0,6},{1,7},{2,4},{3,5},{4,2},{5,3},{6,0},{7,1},{8,14},{9,15},{10,... | collective-permute-start | bytes 122888 | tf_op jit(solution)/shard_map/ppermute | solution.py:42
  18.8 0.5 collective-permute-start.6
  19.3 0.3 collective-permute-start.7
  19.6 1.8 %collective-permute-start.12 = (bf16[512,256]{1,0:T(8,128)(2,1)S(1)}, bf16[512,256]{1,0:T(8,128)(2,1)S(1)}, u32[]{:S(2)}, u32[]{:S(2)}) collective-permute-start(bf16[512,256]{1,0:T(8,128)(2,1)S(1)} %add_convert_fusion.here_ref.refs_0_), channel_id=1, source_target_pairs={{0,4},{1,5},{2,6},{3,7},{4,0},{5,1},{6,2},{7,3},{8,12},{9,13},{10,... | collective-permute-start | bytes 786440 | tf_op jit(solution)/shard_map/ppermute | solution.py:42
  21.4 1.5 %collective-permute-start.11 = (bf16[512,256]{1,0:T(8,128)(2,1)S(1)}, bf16[512,256]{1,0:T(8,128)(2,1)S(1)}, u32[]{:S(2)}, u32[]{:S(2)}) collective-permute-start(bf16[512,256]{1,0:T(8,128)(2,1)S(1)} %add_convert_fusion.here_ref.refs_0_), channel_id=1, source_target_pairs={{0,2},{1,3},{2,0},{3,1},{4,6},{5,7},{6,4},{7,5},{8,10},{9,11},{10,... | collective-permute-start | bytes 786440 | tf_op jit(solution)/shard_map/ppermute | solution.py:42
  22.9 1.0 %collective-permute-done.7 = bf16[160,128]{1,0:T(8,128)(2,1)S(1)} collective-permute-done((bf16[160,128]{1,0:T(8,128)(2,1)S(1)}, bf16[160,128]{1,0:T(8,128)(2,1)S(1)}, u32[]{:S(2)}, u32[]{:S(2)}) %collective-permute-start.7) | collective-permute-done | bytes 40992 | tf_op jit(solution)/shard_map/ppermute | solution.py:42
  23.9 3.7 %collective-permute-start.10 = (bf16[160,128]{1,0:T(8,128)(2,1)S(1)}, bf16[160,128]{1,0:T(8,128)(2,1)S(1)}, u32[]{:S(2)}, u32[]{:S(2)}) collective-permute-start(bf16[160,128]{1,0:T(8,128)(2,1)S(1)} %convert_element_type.65), channel_id=1, source_target_pairs={{0,24},{1,25},{2,26},{3,27},{4,28},{5,29},{6,30},{7,31},{8,16},{9,... | collective-permute-start | bytes 122888 | tf_op jit(solution)/shard_map/ppermute | solution.py:42
  27.6 0.8 collective-permute-start.8
  28.3 1.5 %collective-permute-done.10 = bf16[160,128]{1,0:T(8,128)(2,1)S(1)} collective-permute-done((bf16[160,128]{1,0:T(8,128)(2,1)S(1)}, bf16[160,128]{1,0:T(8,128)(2,1)S(1)}, u32[]{:S(2)}, u32[]{:S(2)}) %collective-permute-start.10) | collective-permute-done | bytes 40992 | tf_op jit(solution)/shard_map/ppermute | solution.py:42
  29.8 1.3 %collective-permute-start.16 = (bf16[512,256]{1,0:T(8,128)(2,1)S(1)}, bf16[512,256]{1,0:T(8,128)(2,1)S(1)}, u32[]{:S(2)}, u32[]{:S(2)}) collective-permute-start(bf16[512,256]{1,0:T(8,128)(2,1)S(1)} %add_convert_fusion.here_ref.refs_0_), channel_id=1, source_target_pairs={{0,6},{1,7},{2,4},{3,5},{4,2},{5,3},{6,0},{7,1},{8,14},{9,15},{10,... | collective-permute-start | bytes 786440 | tf_op jit(solution)/shard_map/ppermute | solution.py:42
  31.1 1.3 %collective-permute-done.9 = bf16[160,128]{1,0:T(8,128)(2,1)S(1)} collective-permute-done((bf16[160,128]{1,0:T(8,128)(2,1)S(1)}, bf16[160,128]{1,0:T(8,128)(2,1)S(1)}, u32[]{:S(2)}, u32[]{:S(2)}) %collective-permute-start.9) | collective-permute-done | bytes 40992 | tf_op jit(solution)/shard_map/ppermute | solution.py:42
  32.5 1.4 %collective-permute-start.15 = (bf16[160,128]{1,0:T(8,128)(2,1)S(1)}, bf16[160,128]{1,0:T(8,128)(2,1)S(1)}, u32[]{:S(2)}, u32[]{:S(2)}) collective-permute-start(bf16[160,128]{1,0:T(8,128)(2,1)S(1)} %add_convert_fusion.3.refs_0_), channel_id=1, source_target_pairs={{0,6},{1,7},{2,4},{3,5},{4,2},{5,3},{6,0},{7,1},{8,14},{9,15},{10,... | collective-permute-start | bytes 122888 | tf_op jit(solution)/shard_map/ppermute | solution.py:42
  33.9 0.5 collective-permute-start.14
  34.5 1.6 %collective-permute-start.13 = (bf16[160,128]{1,0:T(8,128)(2,1)S(1)}, bf16[160,128]{1,0:T(8,128)(2,1)S(1)}, u32[]{:S(2)}, u32[]{:S(2)}) collective-permute-start(bf16[160,128]{1,0:T(8,128)(2,1)S(1)} %add_convert_fusion.3.refs_0_), channel_id=1, source_target_pairs={{0,4},{1,5},{2,6},{3,7},{4,0},{5,1},{6,2},{7,3},{8,12},{9,13},{10,... | collective-permute-start | bytes 122888 | tf_op jit(solution)/shard_map/ppermute | solution.py:42
  36.0 1.5 %collective-permute-done.16.refs_6_ = bf16[512,256]{1,0:T(8,128)(2,1)S(1)} collective-permute-done((bf16[512,256]{1,0:T(8,128)(2,1)S(1)}, bf16[512,256]{1,0:T(8,128)(2,1)S(1)}, u32[]{:S(2)}, u32[]{:S(2)}) %collective-permute-start.16) | collective-permute-done | bytes 262176 | tf_op jit(solution)/shard_map/ppermute | solution.py:42
  37.6 0.4 collective-permute-done.15.refs_3_
  38.0 0.5 collective-permute-done.13.refs_1_
  38.5 0.1 collective-permute-start.17
  38.6 0.5 collective-permute-start.18
  39.1 0.1 collective-permute-start.19
  39.2 0.4 collective-permute-start.20
  39.6 0.4 collective-permute-done.17
  40.0 2.1 %shard_map.53.whiten_ref = bf16[512,512]{1,0:T(8,128)(2,1)S(1)} custom-call(bf16[160,128]{1,0:T(8,128)(2,1)S(1)} %add_convert_fusion.3.refs_0_, bf16[160,128]{1,0:T(8,128)(2,1)S(1)} %collective-permute-done.13.refs_1_, bf16[160,128]{1,0:T(8,128)(2,1)S(1)} %collective-permute-done.14.refs_2_, bf16[160,128]{1,0:T(8,128)(2,1)S(1)} %collective-permute-done.15.refs_3_, ...), custom_call_target="tpu_custom_call" | custom-call | tf_op jit(solution)/shard_map/pallas_call | solution.py:72
  42.1 2.2 %shard_map.54 = (bf16[8,512,256]{2,1,0:T(8,128)(2,1)S(1)}, f32[64,512]{1,0:T(8,128)S(1)}) custom-call(bf16[512,512]{1,0:T(8,128)(2,1)S(1)} %shard_map.53.whiten_ref, bf16[512,256]{1,0:T(8,128)(2,1)S(1)} %add_convert_fusion.here_ref.refs_0_, bf16[512,256]{1,0:T(8,128)(2,1)S(1)} %collective-permute-done.4.there_ref.refs_1_, ...), custom_call_target="tpu_custom_call" | custom-call | tf_op jit(solution)/shard_map/pallas_call | solution.py:72
  44.4 3.5 %collective-permute-start.23 = (bf16[64,512]{1,0:T(8,128)(2,1)S(1)}, bf16[64,512]{1,0:T(8,128)(2,1)S(1)}, u32[]{:S(2)}, u32[]{:S(2)}) collective-permute-start(bf16[64,512]{1,0:T(8,128)(2,1)S(1)} %convert_element_type.70), channel_id=1, source_target_pairs={{0,24},{1,25},{2,26},{3,27},{4,28},{5,29},{6,30},{7,31},{8,16},{9,... | collective-permute-start | bytes 196616 | tf_op jit(solution)/shard_map/ppermute | solution.py:42
  47.9 1.0 %collective-permute-start.21 = (bf16[64,512]{1,0:T(8,128)(2,1)S(1)}, bf16[64,512]{1,0:T(8,128)(2,1)S(1)}, u32[]{:S(2)}, u32[]{:S(2)}) collective-permute-start(bf16[64,512]{1,0:T(8,128)(2,1)S(1)} %convert_element_type.70), channel_id=1, source_target_pairs={{0,8},{1,9},{2,10},{3,11},{4,12},{5,13},{6,14},{7,15},{8,0},{9,1},... | collective-permute-start | bytes 196616 | tf_op jit(solution)/shard_map/ppermute | solution.py:42
  48.8 2.4 %collective-permute-done.23 = bf16[64,512]{1,0:T(8,128)(2,1)S(1)} collective-permute-done((bf16[64,512]{1,0:T(8,128)(2,1)S(1)}, bf16[64,512]{1,0:T(8,128)(2,1)S(1)}, u32[]{:S(2)}, u32[]{:S(2)}) %collective-permute-start.23) | collective-permute-done | bytes 65568 | tf_op jit(solution)/shard_map/ppermute | solution.py:42
  51.2 2.2 %collective-permute-done.22 = bf16[64,512]{1,0:T(8,128)(2,1)S(1)} collective-permute-done((bf16[64,512]{1,0:T(8,128)(2,1)S(1)}, bf16[64,512]{1,0:T(8,128)(2,1)S(1)}, u32[]{:S(2)}, u32[]{:S(2)}) %collective-permute-start.22) | collective-permute-done | bytes 65568 | tf_op jit(solution)/shard_map/ppermute | solution.py:42
  53.4 0.1 collective-permute-done.21
  53.6 2.3 %collective-permute-start.26 = (bf16[64,512]{1,0:T(8,128)(2,1)S(1)}, bf16[64,512]{1,0:T(8,128)(2,1)S(1)}, u32[]{:S(2)}, u32[]{:S(2)}) collective-permute-start(bf16[64,512]{1,0:T(8,128)(2,1)S(1)} %add_convert_fusion.2.refs_0_), channel_id=1, source_target_pairs={{0,6},{1,7},{2,4},{3,5},{4,2},{5,3},{6,0},{7,1},{8,14},{9,15},{10,... | collective-permute-start | bytes 196616 | tf_op jit(solution)/shard_map/ppermute | solution.py:42
  55.9 0.5 collective-permute-start.25
  56.5 0.7 collective-permute-start.24
  57.2 2.4 %collective-permute-done.26.refs_3_ = bf16[64,512]{1,0:T(8,128)(2,1)S(1)} collective-permute-done((bf16[64,512]{1,0:T(8,128)(2,1)S(1)}, bf16[64,512]{1,0:T(8,128)(2,1)S(1)}, u32[]{:S(2)}, u32[]{:S(2)}) %collective-permute-start.26) | collective-permute-done | bytes 65568 | tf_op jit(solution)/shard_map/ppermute | solution.py:42
  59.5 0.7 collective-permute-done.25.refs_2_
  60.2 0.5 collective-permute-done.24.refs_1_
  60.8 0.7 collective-permute-done.29.refs_6_
  61.4 0.5 collective-permute-done.28.refs_5_
  62.0 3.4 %shard_map.55 = f32[64,512]{1,0:T(8,128)S(1)} custom-call(bf16[64,512]{1,0:T(8,128)(2,1)S(1)} %add_convert_fusion.2.refs_0_, bf16[64,512]{1,0:T(8,128)(2,1)S(1)} %collective-permute-done.24.refs_1_, bf16[64,512]{1,0:T(8,128)(2,1)S(1)} %collective-permute-done.25.refs_2_, bf16[64,512]{1,0:T(8,128)(2,1)S(1)} %collective-permute-done.26.refs_3_, ...), custom_call_target="tpu_custom_call" | custom-call | tf_op jit(solution)/shard_map/pallas_call | solution.py:72
  65.4 2.6 %collective-permute-start.33 = (bf16[64,512]{1,0:T(8,128)(2,1)S(1)}, bf16[64,512]{1,0:T(8,128)(2,1)S(1)}, u32[]{:S(2)}, u32[]{:S(2)}) collective-permute-start(bf16[64,512]{1,0:T(8,128)(2,1)S(1)} %convert_element_type.75), channel_id=1, source_target_pairs={{0,24},{1,25},{2,26},{3,27},{4,28},{5,29},{6,30},{7,31},{8,16},{9,... | collective-permute-start | bytes 196616 | tf_op jit(solution)/shard_map/ppermute | solution.py:42
  68.0 1.9 %collective-permute-start.31 = (bf16[64,512]{1,0:T(8,128)(2,1)S(1)}, bf16[64,512]{1,0:T(8,128)(2,1)S(1)}, u32[]{:S(2)}, u32[]{:S(2)}) collective-permute-start(bf16[64,512]{1,0:T(8,128)(2,1)S(1)} %convert_element_type.75), channel_id=1, source_target_pairs={{0,8},{1,9},{2,10},{3,11},{4,12},{5,13},{6,14},{7,15},{8,0},{9,1},... | collective-permute-start | bytes 196616 | tf_op jit(solution)/shard_map/ppermute | solution.py:42
  69.8 2.4 %collective-permute-done.33 = bf16[64,512]{1,0:T(8,128)(2,1)S(1)} collective-permute-done((bf16[64,512]{1,0:T(8,128)(2,1)S(1)}, bf16[64,512]{1,0:T(8,128)(2,1)S(1)}, u32[]{:S(2)}, u32[]{:S(2)}) %collective-permute-start.33) | collective-permute-done | bytes 65568 | tf_op jit(solution)/shard_map/ppermute | solution.py:42
  72.2 2.0 %collective-permute-done.32 = bf16[64,512]{1,0:T(8,128)(2,1)S(1)} collective-permute-done((bf16[64,512]{1,0:T(8,128)(2,1)S(1)}, bf16[64,512]{1,0:T(8,128)(2,1)S(1)}, u32[]{:S(2)}, u32[]{:S(2)}) %collective-permute-start.32) | collective-permute-done | bytes 65568 | tf_op jit(solution)/shard_map/ppermute | solution.py:42
  74.2 1.8 %collective-permute-start.36 = (bf16[64,512]{1,0:T(8,128)(2,1)S(1)}, bf16[64,512]{1,0:T(8,128)(2,1)S(1)}, u32[]{:S(2)}, u32[]{:S(2)}) collective-permute-start(bf16[64,512]{1,0:T(8,128)(2,1)S(1)} %add_convert_fusion.1.refs_0_), channel_id=1, source_target_pairs={{0,6},{1,7},{2,4},{3,5},{4,2},{5,3},{6,0},{7,1},{8,14},{9,15},{10,... | collective-permute-start | bytes 196616 | tf_op jit(solution)/shard_map/ppermute | solution.py:42
  76.0 0.9 %collective-permute-start.35 = (bf16[64,512]{1,0:T(8,128)(2,1)S(1)}, bf16[64,512]{1,0:T(8,128)(2,1)S(1)}, u32[]{:S(2)}, u32[]{:S(2)}) collective-permute-start(bf16[64,512]{1,0:T(8,128)(2,1)S(1)} %add_convert_fusion.1.refs_0_), channel_id=1, source_target_pairs={{0,2},{1,3},{2,0},{3,1},{4,6},{5,7},{6,4},{7,5},{8,10},{9,11},{10,... | collective-permute-start | bytes 196616 | tf_op jit(solution)/shard_map/ppermute | solution.py:42
  76.9 0.9 %collective-permute-start.34 = (bf16[64,512]{1,0:T(8,128)(2,1)S(1)}, bf16[64,512]{1,0:T(8,128)(2,1)S(1)}, u32[]{:S(2)}, u32[]{:S(2)}) collective-permute-start(bf16[64,512]{1,0:T(8,128)(2,1)S(1)} %add_convert_fusion.1.refs_0_), channel_id=1, source_target_pairs={{0,4},{1,5},{2,6},{3,7},{4,0},{5,1},{6,2},{7,3},{8,12},{9,13},{10,... | collective-permute-start | bytes 196616 | tf_op jit(solution)/shard_map/ppermute | solution.py:42
  77.8 2.1 %collective-permute-done.36.refs_3_ = bf16[64,512]{1,0:T(8,128)(2,1)S(1)} collective-permute-done((bf16[64,512]{1,0:T(8,128)(2,1)S(1)}, bf16[64,512]{1,0:T(8,128)(2,1)S(1)}, u32[]{:S(2)}, u32[]{:S(2)}) %collective-permute-start.36) | collective-permute-done | bytes 65568 | tf_op jit(solution)/shard_map/ppermute | solution.py:42
  79.9 0.6 collective-permute-done.35.refs_2_
  80.5 0.6 collective-permute-done.34.refs_1_
  81.2 0.6 collective-permute-done.39.refs_6_
  81.8 0.6 collective-permute-done.38.refs_5_
  82.4 3.2 %shard_map.56 = (f32[128,512]{1,0:T(8,128)}, bf16[128,1024]{1,0:T(8,128)(2,1)}) custom-call(bf16[64,512]{1,0:T(8,128)(2,1)S(1)} %add_convert_fusion.1.refs_0_, bf16[64,512]{1,0:T(8,128)(2,1)S(1)} %collective-permute-done.34.refs_1_, bf16[64,512]{1,0:T(8,128)(2,1)S(1)} %collective-permute-done.35.refs_2_, ...), custom_call_target="tpu_custom_call" | custom-call | tf_op jit(solution)/shard_map/pallas_call | solution.py:72
  (41 shorter events, 0.3 us)
Async XLA Ops:
  0.6 39.0 %copy-start = (f32[128,512]{1,0:T(8,128)S(1)}, f32[128,512]{1,0:T(8,128)}, u32[]{:S(2)}) copy-start(f32[128,512]{1,0:T(8,128)} %param.5) | copy-start | bytes 786436
  0.6 3.4 %copy-start.1 = (bf16[512,512]{1,0:T(8,128)(2,1)S(1)}, bf16[512,512]{1,0:T(8,128)(2,1)}, u32[]{:S(2)}) copy-start(bf16[512,512]{1,0:T(8,128)(2,1)} %left_ref.3) | copy-start | bytes 1572868
  0.7 3.4 %collective-permute-start = (bf16[512,512]{1,0:T(8,128)(2,1)}, bf16[512,512]{1,0:T(8,128)(2,1)S(1)}, u32[]{:S(2)}, u32[]{:S(2)}) collective-permute-start(bf16[512,512]{1,0:T(8,128)(2,1)} %left_ref.3), channel_id=1, source_target_pairs={{0,1},{1,0},{2,3},{3,2},{4,5},{5,4},{6,7},{7,6},{8,9},{9,8},{10,11... | collective-permute-start | bytes 1572872 | tf_op jit(solution)/shard_map/ppermute | solution.py:42
  2.4 1.6 %collective-permute-start.2 = (bf16[512,256]{1,0:T(8,128)(2,1)S(1)}, bf16[512,256]{1,0:T(8,128)(2,1)S(1)}, u32[]{:S(2)}, u32[]{:S(2)}) collective-permute-start(bf16[512,256]{1,0:T(8,128)(2,1)S(1)} %get-tuple-element.32), channel_id=1, source_target_pairs={{0,1},{1,0},{2,3},{3,2},{4,5},{5,4},{6,7},{7,6},{8,9},{9,8},{10,11... | collective-permute-start | bytes 786440 | tf_op jit(solution)/shard_map/ppermute | solution.py:42
  2.6 4.6 %collective-permute-start.1 = (bf16[512,256]{1,0:T(8,128)(2,1)S(1)}, bf16[512,256]{1,0:T(8,128)(2,1)S(1)}, u32[]{:S(2)}, u32[]{:S(2)}) collective-permute-start(bf16[512,256]{1,0:T(8,128)(2,1)S(1)} %get-tuple-element.33), channel_id=1, source_target_pairs={{0,1},{1,0},{2,3},{3,2},{4,5},{5,4},{6,7},{7,6},{8,9},{9,8},{10,11... | collective-permute-start | bytes 786440 | tf_op jit(solution)/shard_map/ppermute | solution.py:42
  4.5 9.5 %collective-permute-start.3 = (bf16[512,256]{1,0:T(8,128)(2,1)S(1)}, bf16[512,256]{1,0:T(8,128)(2,1)S(1)}, u32[]{:S(2)}, u32[]{:S(2)}) collective-permute-start(bf16[512,256]{1,0:T(8,128)(2,1)S(1)} %shard_map.51), channel_id=1, source_target_pairs={{0,2},{1,3},{2,0},{3,1},{4,6},{5,7},{6,4},{7,5},{8,10},{9,11},{10,... | collective-permute-start | bytes 786440 | tf_op jit(solution)/shard_map/ppermute | solution.py:42
  14.1 1.6 %collective-permute-start.4 = (bf16[512,256]{1,0:T(8,128)(2,1)S(1)}, bf16[512,256]{1,0:T(8,128)(2,1)S(1)}, u32[]{:S(2)}, u32[]{:S(2)}) collective-permute-start(bf16[512,256]{1,0:T(8,128)(2,1)S(1)} %add_convert_fusion.here_ref.refs_0_), channel_id=1, source_target_pairs={{0,1},{1,0},{2,3},{3,2},{4,5},{5,4},{6,7},{7,6},{8,9},{9,8},{10,11... | collective-permute-start | bytes 786440 | tf_op jit(solution)/shard_map/ppermute | solution.py:42
  16.0 6.8 %collective-permute-start.5 = (bf16[160,128]{1,0:T(8,128)(2,1)S(1)}, bf16[160,128]{1,0:T(8,128)(2,1)S(1)}, u32[]{:S(2)}, u32[]{:S(2)}) collective-permute-start(bf16[160,128]{1,0:T(8,128)(2,1)S(1)} %get-tuple-element.19), channel_id=1, source_target_pairs={{0,6},{1,7},{2,4},{3,5},{4,2},{5,3},{6,0},{7,1},{8,14},{9,15},{10,... | collective-permute-start | bytes 122888 | tf_op jit(solution)/shard_map/ppermute | solution.py:42
  18.8 4.1 %collective-permute-start.6 = (bf16[160,128]{1,0:T(8,128)(2,1)S(1)}, bf16[160,128]{1,0:T(8,128)(2,1)S(1)}, u32[]{:S(2)}, u32[]{:S(2)}) collective-permute-start(bf16[160,128]{1,0:T(8,128)(2,1)S(1)} %get-tuple-element.20), channel_id=1, source_target_pairs={{0,2},{1,3},{2,0},{3,1},{4,6},{5,7},{6,4},{7,5},{8,10},{9,11},{10,... | collective-permute-start | bytes 122888 | tf_op jit(solution)/shard_map/ppermute | solution.py:42
  19.3 4.5 %collective-permute-start.7 = (bf16[160,128]{1,0:T(8,128)(2,1)S(1)}, bf16[160,128]{1,0:T(8,128)(2,1)S(1)}, u32[]{:S(2)}, u32[]{:S(2)}) collective-permute-start(bf16[160,128]{1,0:T(8,128)(2,1)S(1)} %get-tuple-element.21), channel_id=1, source_target_pairs={{0,4},{1,5},{2,6},{3,7},{4,0},{5,1},{6,2},{7,3},{8,12},{9,13},{10,... | collective-permute-start | bytes 122888 | tf_op jit(solution)/shard_map/ppermute | solution.py:42
  19.6 11.5 %collective-permute-start.12 = (bf16[512,256]{1,0:T(8,128)(2,1)S(1)}, bf16[512,256]{1,0:T(8,128)(2,1)S(1)}, u32[]{:S(2)}, u32[]{:S(2)}) collective-permute-start(bf16[512,256]{1,0:T(8,128)(2,1)S(1)} %add_convert_fusion.here_ref.refs_0_), channel_id=1, source_target_pairs={{0,4},{1,5},{2,6},{3,7},{4,0},{5,1},{6,2},{7,3},{8,12},{9,13},{10,... | collective-permute-start | bytes 786440 | tf_op jit(solution)/shard_map/ppermute | solution.py:42
  21.4 9.8 %collective-permute-start.11 = (bf16[512,256]{1,0:T(8,128)(2,1)S(1)}, bf16[512,256]{1,0:T(8,128)(2,1)S(1)}, u32[]{:S(2)}, u32[]{:S(2)}) collective-permute-start(bf16[512,256]{1,0:T(8,128)(2,1)S(1)} %add_convert_fusion.here_ref.refs_0_), channel_id=1, source_target_pairs={{0,2},{1,3},{2,0},{3,1},{4,6},{5,7},{6,4},{7,5},{8,10},{9,11},{10,... | collective-permute-start | bytes 786440 | tf_op jit(solution)/shard_map/ppermute | solution.py:42
  23.9 6.0 %collective-permute-start.10 = (bf16[160,128]{1,0:T(8,128)(2,1)S(1)}, bf16[160,128]{1,0:T(8,128)(2,1)S(1)}, u32[]{:S(2)}, u32[]{:S(2)}) collective-permute-start(bf16[160,128]{1,0:T(8,128)(2,1)S(1)} %convert_element_type.65), channel_id=1, source_target_pairs={{0,24},{1,25},{2,26},{3,27},{4,28},{5,29},{6,30},{7,31},{8,16},{9,... | collective-permute-start | bytes 122888 | tf_op jit(solution)/shard_map/ppermute | solution.py:42
  27.5 4.9 %collective-permute-start.9 = (bf16[160,128]{1,0:T(8,128)(2,1)S(1)}, bf16[160,128]{1,0:T(8,128)(2,1)S(1)}, u32[]{:S(2)}, u32[]{:S(2)}) collective-permute-start(bf16[160,128]{1,0:T(8,128)(2,1)S(1)} %convert_element_type.65), channel_id=1, source_target_pairs={{0,16},{1,17},{2,18},{3,19},{4,20},{5,21},{6,22},{7,23},{8,24},{9,... | collective-permute-start | bytes 122888 | tf_op jit(solution)/shard_map/ppermute | solution.py:42
  27.6 4.9 %collective-permute-start.8 = (bf16[160,128]{1,0:T(8,128)(2,1)S(1)}, bf16[160,128]{1,0:T(8,128)(2,1)S(1)}, u32[]{:S(2)}, u32[]{:S(2)}) collective-permute-start(bf16[160,128]{1,0:T(8,128)(2,1)S(1)} %convert_element_type.65), channel_id=1, source_target_pairs={{0,8},{1,9},{2,10},{3,11},{4,12},{5,13},{6,14},{7,15},{8,0},{9,1},... | collective-permute-start | bytes 122888 | tf_op jit(solution)/shard_map/ppermute | solution.py:42
  29.8 7.7 %collective-permute-start.16 = (bf16[512,256]{1,0:T(8,128)(2,1)S(1)}, bf16[512,256]{1,0:T(8,128)(2,1)S(1)}, u32[]{:S(2)}, u32[]{:S(2)}) collective-permute-start(bf16[512,256]{1,0:T(8,128)(2,1)S(1)} %add_convert_fusion.here_ref.refs_0_), channel_id=1, source_target_pairs={{0,6},{1,7},{2,4},{3,5},{4,2},{5,3},{6,0},{7,1},{8,14},{9,15},{10,... | collective-permute-start | bytes 786440 | tf_op jit(solution)/shard_map/ppermute | solution.py:42
  32.5 5.5 %collective-permute-start.15 = (bf16[160,128]{1,0:T(8,128)(2,1)S(1)}, bf16[160,128]{1,0:T(8,128)(2,1)S(1)}, u32[]{:S(2)}, u32[]{:S(2)}) collective-permute-start(bf16[160,128]{1,0:T(8,128)(2,1)S(1)} %add_convert_fusion.3.refs_0_), channel_id=1, source_target_pairs={{0,6},{1,7},{2,4},{3,5},{4,2},{5,3},{6,0},{7,1},{8,14},{9,15},{10,... | collective-permute-start | bytes 122888 | tf_op jit(solution)/shard_map/ppermute | solution.py:42
  33.9 4.1 %collective-permute-start.14 = (bf16[160,128]{1,0:T(8,128)(2,1)S(1)}, bf16[160,128]{1,0:T(8,128)(2,1)S(1)}, u32[]{:S(2)}, u32[]{:S(2)}) collective-permute-start(bf16[160,128]{1,0:T(8,128)(2,1)S(1)} %add_convert_fusion.3.refs_0_), channel_id=1, source_target_pairs={{0,2},{1,3},{2,0},{3,1},{4,6},{5,7},{6,4},{7,5},{8,10},{9,11},{10,... | collective-permute-start | bytes 122888 | tf_op jit(solution)/shard_map/ppermute | solution.py:42
  34.5 4.0 %collective-permute-start.13 = (bf16[160,128]{1,0:T(8,128)(2,1)S(1)}, bf16[160,128]{1,0:T(8,128)(2,1)S(1)}, u32[]{:S(2)}, u32[]{:S(2)}) collective-permute-start(bf16[160,128]{1,0:T(8,128)(2,1)S(1)} %add_convert_fusion.3.refs_0_), channel_id=1, source_target_pairs={{0,4},{1,5},{2,6},{3,7},{4,0},{5,1},{6,2},{7,3},{8,12},{9,13},{10,... | collective-permute-start | bytes 122888 | tf_op jit(solution)/shard_map/ppermute | solution.py:42
  38.5 1.5 %collective-permute-start.17 = (bf16[4,160,128]{2,1,0:T(8,128)(2,1)S(1)}, bf16[4,160,128]{2,1,0:T(8,128)(2,1)S(1)}, u32[]{:S(2)}, u32[]{:S(2)}) collective-permute-start(bf16[4,160,128]{2,1,0:T(8,128)(2,1)S(1)} %pad_maximum_fusion), channel_id=1, source_target_pairs={{0,1},{1,0},{2,3},{3,2},{4,5},{5,4},{6,7},{7,6},{8,9},{9,8},{10,11... | collective-permute-start | bytes 491528 | tf_op jit(solution)/shard_map/ppermute | solution.py:42
  38.6 3.5 %collective-permute-start.18 = (bf16[512,256]{1,0:T(8,128)(2,1)S(1)}, bf16[512,256]{1,0:T(8,128)(2,1)S(1)}, u32[]{:S(2)}, u32[]{:S(2)}) collective-permute-start(bf16[512,256]{1,0:T(8,128)(2,1)S(1)} %collective-permute-done.11.refs_2_), channel_id=1, source_target_pairs={{0,1},{1,0},{2,3},{3,2},{4,5},{5,4},{6,7},{7,6},{8,9},{9,8},{10,11... | collective-permute-start | bytes 786440 | tf_op jit(solution)/shard_map/ppermute | solution.py:42
  39.1 3.0 %collective-permute-start.19 = (bf16[512,256]{1,0:T(8,128)(2,1)S(1)}, bf16[512,256]{1,0:T(8,128)(2,1)S(1)}, u32[]{:S(2)}, u32[]{:S(2)}) collective-permute-start(bf16[512,256]{1,0:T(8,128)(2,1)S(1)} %collective-permute-done.12.refs_4_), channel_id=1, source_target_pairs={{0,1},{1,0},{2,3},{3,2},{4,5},{5,4},{6,7},{7,6},{8,9},{9,8},{10,11... | collective-permute-start | bytes 786440 | tf_op jit(solution)/shard_map/ppermute | solution.py:42
  39.2 2.9 %collective-permute-start.20 = (bf16[512,256]{1,0:T(8,128)(2,1)S(1)}, bf16[512,256]{1,0:T(8,128)(2,1)S(1)}, u32[]{:S(2)}, u32[]{:S(2)}) collective-permute-start(bf16[512,256]{1,0:T(8,128)(2,1)S(1)} %collective-permute-done.16.refs_6_), channel_id=1, source_target_pairs={{0,1},{1,0},{2,3},{3,2},{4,5},{5,4},{6,7},{7,6},{8,9},{9,8},{10,11... | collective-permute-start | bytes 786440 | tf_op jit(solution)/shard_map/ppermute | solution.py:42
  44.4 6.8 %collective-permute-start.23 = (bf16[64,512]{1,0:T(8,128)(2,1)S(1)}, bf16[64,512]{1,0:T(8,128)(2,1)S(1)}, u32[]{:S(2)}, u32[]{:S(2)}) collective-permute-start(bf16[64,512]{1,0:T(8,128)(2,1)S(1)} %convert_element_type.70), channel_id=1, source_target_pairs={{0,24},{1,25},{2,26},{3,27},{4,28},{5,29},{6,30},{7,31},{8,16},{9,... | collective-permute-start | bytes 196616 | tf_op jit(solution)/shard_map/ppermute | solution.py:42
  47.9 5.5 %collective-permute-start.22 = (bf16[64,512]{1,0:T(8,128)(2,1)S(1)}, bf16[64,512]{1,0:T(8,128)(2,1)S(1)}, u32[]{:S(2)}, u32[]{:S(2)}) collective-permute-start(bf16[64,512]{1,0:T(8,128)(2,1)S(1)} %convert_element_type.70), channel_id=1, source_target_pairs={{0,16},{1,17},{2,18},{3,19},{4,20},{5,21},{6,22},{7,23},{8,24},{9,... | collective-permute-start | bytes 196616 | tf_op jit(solution)/shard_map/ppermute | solution.py:42
  47.9 5.7 %collective-permute-start.21 = (bf16[64,512]{1,0:T(8,128)(2,1)S(1)}, bf16[64,512]{1,0:T(8,128)(2,1)S(1)}, u32[]{:S(2)}, u32[]{:S(2)}) collective-permute-start(bf16[64,512]{1,0:T(8,128)(2,1)S(1)} %convert_element_type.70), channel_id=1, source_target_pairs={{0,8},{1,9},{2,10},{3,11},{4,12},{5,13},{6,14},{7,15},{8,0},{9,1},... | collective-permute-start | bytes 196616 | tf_op jit(solution)/shard_map/ppermute | solution.py:42
  53.6 5.9 %collective-permute-start.26 = (bf16[64,512]{1,0:T(8,128)(2,1)S(1)}, bf16[64,512]{1,0:T(8,128)(2,1)S(1)}, u32[]{:S(2)}, u32[]{:S(2)}) collective-permute-start(bf16[64,512]{1,0:T(8,128)(2,1)S(1)} %add_convert_fusion.2.refs_0_), channel_id=1, source_target_pairs={{0,6},{1,7},{2,4},{3,5},{4,2},{5,3},{6,0},{7,1},{8,14},{9,15},{10,... | collective-permute-start | bytes 196616 | tf_op jit(solution)/shard_map/ppermute | solution.py:42
  55.9 4.3 %collective-permute-start.25 = (bf16[64,512]{1,0:T(8,128)(2,1)S(1)}, bf16[64,512]{1,0:T(8,128)(2,1)S(1)}, u32[]{:S(2)}, u32[]{:S(2)}) collective-permute-start(bf16[64,512]{1,0:T(8,128)(2,1)S(1)} %add_convert_fusion.2.refs_0_), channel_id=1, source_target_pairs={{0,2},{1,3},{2,0},{3,1},{4,6},{5,7},{6,4},{7,5},{8,10},{9,11},{10,... | collective-permute-start | bytes 196616 | tf_op jit(solution)/shard_map/ppermute | solution.py:42
  56.5 4.3 %collective-permute-start.24 = (bf16[64,512]{1,0:T(8,128)(2,1)S(1)}, bf16[64,512]{1,0:T(8,128)(2,1)S(1)}, u32[]{:S(2)}, u32[]{:S(2)}) collective-permute-start(bf16[64,512]{1,0:T(8,128)(2,1)S(1)} %add_convert_fusion.2.refs_0_), channel_id=1, source_target_pairs={{0,4},{1,5},{2,6},{3,7},{4,0},{5,1},{6,2},{7,3},{8,12},{9,13},{10,... | collective-permute-start | bytes 196616 | tf_op jit(solution)/shard_map/ppermute | solution.py:42
  57.2 3.6 %collective-permute-start.27 = (bf16[64,512]{1,0:T(8,128)(2,1)S(1)}, bf16[64,512]{1,0:T(8,128)(2,1)S(1)}, u32[]{:S(2)}, u32[]{:S(2)}) collective-permute-start(bf16[64,512]{1,0:T(8,128)(2,1)S(1)} %add_convert_fusion.2.refs_0_), channel_id=1, source_target_pairs={{0,1},{1,0},{2,3},{3,2},{4,5},{5,4},{6,7},{7,6},{8,9},{9,8},{10,11... | collective-permute-start | bytes 196616 | tf_op jit(solution)/shard_map/ppermute | solution.py:42
  59.5 1.3 %collective-permute-start.30 = (bf16[64,512]{1,0:T(8,128)(2,1)S(1)}, bf16[64,512]{1,0:T(8,128)(2,1)S(1)}, u32[]{:S(2)}, u32[]{:S(2)}) collective-permute-start(bf16[64,512]{1,0:T(8,128)(2,1)S(1)} %collective-permute-done.26.refs_3_), channel_id=1, source_target_pairs={{0,1},{1,0},{2,3},{3,2},{4,5},{5,4},{6,7},{7,6},{8,9},{9,8},{10,11... | collective-permute-start | bytes 196616 | tf_op jit(solution)/shard_map/ppermute | solution.py:42
  60.2 1.3 %collective-permute-start.29 = (bf16[64,512]{1,0:T(8,128)(2,1)S(1)}, bf16[64,512]{1,0:T(8,128)(2,1)S(1)}, u32[]{:S(2)}, u32[]{:S(2)}) collective-permute-start(bf16[64,512]{1,0:T(8,128)(2,1)S(1)} %collective-permute-done.25.refs_2_), channel_id=1, source_target_pairs={{0,1},{1,0},{2,3},{3,2},{4,5},{5,4},{6,7},{7,6},{8,9},{9,8},{10,11... | collective-permute-start | bytes 196616 | tf_op jit(solution)/shard_map/ppermute | solution.py:42
  60.7 1.3 %collective-permute-start.28 = (bf16[64,512]{1,0:T(8,128)(2,1)S(1)}, bf16[64,512]{1,0:T(8,128)(2,1)S(1)}, u32[]{:S(2)}, u32[]{:S(2)}) collective-permute-start(bf16[64,512]{1,0:T(8,128)(2,1)S(1)} %collective-permute-done.24.refs_1_), channel_id=1, source_target_pairs={{0,1},{1,0},{2,3},{3,2},{4,5},{5,4},{6,7},{7,6},{8,9},{9,8},{10,11... | collective-permute-start | bytes 196616 | tf_op jit(solution)/shard_map/ppermute | solution.py:42
  65.4 6.8 %collective-permute-start.33 = (bf16[64,512]{1,0:T(8,128)(2,1)S(1)}, bf16[64,512]{1,0:T(8,128)(2,1)S(1)}, u32[]{:S(2)}, u32[]{:S(2)}) collective-permute-start(bf16[64,512]{1,0:T(8,128)(2,1)S(1)} %convert_element_type.75), channel_id=1, source_target_pairs={{0,24},{1,25},{2,26},{3,27},{4,28},{5,29},{6,30},{7,31},{8,16},{9,... | collective-permute-start | bytes 196616 | tf_op jit(solution)/shard_map/ppermute | solution.py:42
  68.0 6.2 %collective-permute-start.32 = (bf16[64,512]{1,0:T(8,128)(2,1)S(1)}, bf16[64,512]{1,0:T(8,128)(2,1)S(1)}, u32[]{:S(2)}, u32[]{:S(2)}) collective-permute-start(bf16[64,512]{1,0:T(8,128)(2,1)S(1)} %convert_element_type.75), channel_id=1, source_target_pairs={{0,16},{1,17},{2,18},{3,19},{4,20},{5,21},{6,22},{7,23},{8,24},{9,... | collective-permute-start | bytes 196616 | tf_op jit(solution)/shard_map/ppermute | solution.py:42
  68.0 6.2 %collective-permute-start.31 = (bf16[64,512]{1,0:T(8,128)(2,1)S(1)}, bf16[64,512]{1,0:T(8,128)(2,1)S(1)}, u32[]{:S(2)}, u32[]{:S(2)}) collective-permute-start(bf16[64,512]{1,0:T(8,128)(2,1)S(1)} %convert_element_type.75), channel_id=1, source_target_pairs={{0,8},{1,9},{2,10},{3,11},{4,12},{5,13},{6,14},{7,15},{8,0},{9,1},... | collective-permute-start | bytes 196616 | tf_op jit(solution)/shard_map/ppermute | solution.py:42
  74.2 5.7 %collective-permute-start.36 = (bf16[64,512]{1,0:T(8,128)(2,1)S(1)}, bf16[64,512]{1,0:T(8,128)(2,1)S(1)}, u32[]{:S(2)}, u32[]{:S(2)}) collective-permute-start(bf16[64,512]{1,0:T(8,128)(2,1)S(1)} %add_convert_fusion.1.refs_0_), channel_id=1, source_target_pairs={{0,6},{1,7},{2,4},{3,5},{4,2},{5,3},{6,0},{7,1},{8,14},{9,15},{10,... | collective-permute-start | bytes 196616 | tf_op jit(solution)/shard_map/ppermute | solution.py:42
  76.0 4.5 %collective-permute-start.35 = (bf16[64,512]{1,0:T(8,128)(2,1)S(1)}, bf16[64,512]{1,0:T(8,128)(2,1)S(1)}, u32[]{:S(2)}, u32[]{:S(2)}) collective-permute-start(bf16[64,512]{1,0:T(8,128)(2,1)S(1)} %add_convert_fusion.1.refs_0_), channel_id=1, source_target_pairs={{0,2},{1,3},{2,0},{3,1},{4,6},{5,7},{6,4},{7,5},{8,10},{9,11},{10,... | collective-permute-start | bytes 196616 | tf_op jit(solution)/shard_map/ppermute | solution.py:42
  76.9 4.3 %collective-permute-start.34 = (bf16[64,512]{1,0:T(8,128)(2,1)S(1)}, bf16[64,512]{1,0:T(8,128)(2,1)S(1)}, u32[]{:S(2)}, u32[]{:S(2)}) collective-permute-start(bf16[64,512]{1,0:T(8,128)(2,1)S(1)} %add_convert_fusion.1.refs_0_), channel_id=1, source_target_pairs={{0,4},{1,5},{2,6},{3,7},{4,0},{5,1},{6,2},{7,3},{8,12},{9,13},{10,... | collective-permute-start | bytes 196616 | tf_op jit(solution)/shard_map/ppermute | solution.py:42
  77.8 3.4 %collective-permute-start.37 = (bf16[64,512]{1,0:T(8,128)(2,1)S(1)}, bf16[64,512]{1,0:T(8,128)(2,1)S(1)}, u32[]{:S(2)}, u32[]{:S(2)}) collective-permute-start(bf16[64,512]{1,0:T(8,128)(2,1)S(1)} %add_convert_fusion.1.refs_0_), channel_id=1, source_target_pairs={{0,1},{1,0},{2,3},{3,2},{4,5},{5,4},{6,7},{7,6},{8,9},{9,8},{10,11... | collective-permute-start | bytes 196616 | tf_op jit(solution)/shard_map/ppermute | solution.py:42
  79.9 1.3 %collective-permute-start.40 = (bf16[64,512]{1,0:T(8,128)(2,1)S(1)}, bf16[64,512]{1,0:T(8,128)(2,1)S(1)}, u32[]{:S(2)}, u32[]{:S(2)}) collective-permute-start(bf16[64,512]{1,0:T(8,128)(2,1)S(1)} %collective-permute-done.36.refs_3_), channel_id=1, source_target_pairs={{0,1},{1,0},{2,3},{3,2},{4,5},{5,4},{6,7},{7,6},{8,9},{9,8},{10,11... | collective-permute-start | bytes 196616 | tf_op jit(solution)/shard_map/ppermute | solution.py:42
  80.5 1.3 %collective-permute-start.39 = (bf16[64,512]{1,0:T(8,128)(2,1)S(1)}, bf16[64,512]{1,0:T(8,128)(2,1)S(1)}, u32[]{:S(2)}, u32[]{:S(2)}) collective-permute-start(bf16[64,512]{1,0:T(8,128)(2,1)S(1)} %collective-permute-done.35.refs_2_), channel_id=1, source_target_pairs={{0,1},{1,0},{2,3},{3,2},{4,5},{5,4},{6,7},{7,6},{8,9},{9,8},{10,11... | collective-permute-start | bytes 196616 | tf_op jit(solution)/shard_map/ppermute | solution.py:42
  81.2 1.3 %collective-permute-start.38 = (bf16[64,512]{1,0:T(8,128)(2,1)S(1)}, bf16[64,512]{1,0:T(8,128)(2,1)S(1)}, u32[]{:S(2)}, u32[]{:S(2)}) collective-permute-start(bf16[64,512]{1,0:T(8,128)(2,1)S(1)} %collective-permute-done.34.refs_1_), channel_id=1, source_target_pairs={{0,1},{1,0},{2,3},{3,2},{4,5},{5,4},{6,7},{7,6},{8,9},{9,8},{10,11... | collective-permute-start | bytes 196616 | tf_op jit(solution)/shard_map/ppermute | solution.py:42

commit v8 on v7

--- a/solution.py
+++ b/solution.py
@@ -10,6 +10,7 @@
 ICA_ITERS = 2
 AXES = ("vox", "comp")
 BF = jnp.bfloat16
+HALF = jnp.float16
 F32 = jnp.float32
 MIB = 1 << 20
 
@@ -33,8 +34,9 @@
     )
 
 
-def rounded(x):
-    return lax.reduce_precision(x, 8, 7)
+def rounded(x, kind):
+    info = jnp.finfo(kind)
+    return lax.reduce_precision(x, info.nexp, info.nmant)
 
 
 def flip(x, mask):
@@ -42,16 +44,16 @@
     return lax.ppermute(x, AXES, [(i, i ^ mask) for i in range(count)])
 
 
-def sum_over(x, masks, due=()):
+def sum_over(x, masks, kind, due=()):
     for k in range(0, len(masks), 2):
-        sent = x.astype(BF)
-        x = rounded(x) + flip(sent, masks[k]).astype(F32)
+        sent = x.astype(kind)
+        x = rounded(x, kind) + flip(sent, masks[k]).astype(F32)
         if k + 1 < len(masks):
             both = flip(sent, masks[k] | masks[k + 1])
             if k == 0:
                 both, *due = lax.optimization_barrier((both, *due))
             x = x + (flip(sent, masks[k + 1]).astype(F32) + both.astype(F32))
-    return (x.astype(BF), *due)
+    return (x.astype(kind), *due)
 
 
 def spread(x, across, near, due=()):
@@ -81,6 +83,16 @@
 
 def shape(dims, dtype):
     return jax.ShapeDtypeStruct(dims, dtype)
+
+
+def sent_kernel(left_ref, right_ref, mate_left_ref, mate_right_ref, out_ref):
+    total = nn(left_ref[...], right_ref[...])
+    total += nn(mate_left_ref[...], mate_right_ref[...])
+    rows = total.shape[0]
+    most = jnp.max(jnp.abs(total), axis=0, keepdims=True)
+    power = jnp.floor(jnp.log2(jnp.maximum(most, 1e-30))) - 14.0
+    out_ref[:rows] = total * jnp.exp2(-power)
+    out_ref[rows:] = jnp.broadcast_to(power, (out_ref.shape[0] - rows, total.shape[1]))
 
 
 def project_kernel(left_ref, right_ref, mate_left_ref, mate_right_ref, out_ref):
@@ -179,7 +191,7 @@
     return pulled, jnp.sum(slopes, axis=1, keepdims=True)
 
 
-def apply_kernel(whiten_ref, *refs):
+def apply_kernel(scale, whiten_ref, *refs):
     blocks, (weights_ref, white_ref, newer_ref) = refs[:-3], refs[-3:]
     weights = weights_ref[...]
     whites = []
@@ -187,10 +199,10 @@
         whites.append(nn(whiten_ref[...], block[...]).astype(BF))
         white_ref[k] = whites[k]
     total, slope = step(weights, whites)
-    newer_ref[...] = total - slope * weights
-
-
-def decor_kernel(last, *refs):
+    newer_ref[...] = (total - slope * weights) * scale
+
+
+def decor_kernel(last, scale, *refs):
     mine, mates, white_ref = refs[:4], refs[4:8], refs[8]
     outs, scratch = (refs[9:11], refs[11:]) if last else (refs[9:10], refs[10:])
     newer, lower, white, sem, *held = scratch
@@ -203,12 +215,13 @@
         spot = 4 * other(ax, k & 2) + other(ay, k & 1)
         for ref, core in ((mine[k], low), (mates[k], 1 - low)):
             start = pl.multiple_of((spot + 2 * core) * count, count)
-            lower[pl.ds(start, count), :] = ref[...]
+            newer[pl.ds(start, count), :] = ref[...]
+            lower[pl.ds(start, count), :] = ref[...].astype(BF)
 
     raw = lower[...]
     gram = nt(raw, raw)
     gscale = jnp.sqrt(jnp.sum(gram * gram, keepdims=True) + 1e-06)
-    value = 1.5 * raw.astype(F32) - (0.5 / gscale) * nn(gram.astype(BF), raw)
+    value = 1.5 * newer[...] - (0.5 / gscale) * nn(gram.astype(BF), raw)
     value = value * lax.rsqrt(gscale)
     raw = value.astype(BF)
     gram = nt(raw, raw).astype(BF)
@@ -241,7 +254,7 @@
             copy.wait()
     else:
         total, slope = step(weights, [white[k] for k in range(chunks)])
-        outs[0][...] = total - slope * weights
+        outs[0][...] = (total - slope * weights) * scale
 
 
 def shards(data, projection, initial):
@@ -263,14 +276,13 @@
     theirs = [flip(columns(x, 1 - core), low) for x in sides]
     mine = [columns(x, core) for x in sides]
     sent, kept = (
-        run(
-            project_kernel,
-            shape((rows, size), kind),
-            (projection, mine[k], mate, theirs[k]),
+        run(kernel, shape((count, size), F32), (projection, mine[k], mate, theirs[k]))
+        for k, (kernel, count) in enumerate(
+            ((sent_kernel, rows + 16), (project_kernel, rows))
         )
-        for k, kind in enumerate((BF, F32))
-    )
-    reduced = (kept + flip(sent, across).astype(F32)).astype(BF)
+    )
+    sent = flip(sent.astype(HALF), across).astype(F32)
+    reduced = (kept + sent[:rows] * jnp.exp2(sent[rows : rows + 1])).astype(BF)
 
     block = rows // 4
     piece = 5 * block // 4
@@ -289,7 +301,7 @@
     own = own + flip(by, near).astype(F32)
     own, reduced = lax.optimization_barrier((own, reduced))
     at_xy = flip(reduced, across | near)
-    packed, at_x, at_y = sum_over(own, far, (at_x, at_y))
+    packed, at_x, at_y = sum_over(own, far, BF, (at_x, at_y))
     packed, at_xy = spread(packed, across, near, (at_xy,))
     whiten = run(
         functools.partial(whiten_kernel, voxels),
@@ -300,17 +312,19 @@
 
     count = initial.shape[0] // 2
     weights = lax.dynamic_slice_in_dim(initial, near_y * count, count, 0)
+    scale = 8192.0 / voxels
     blocks = (reduced, there, at_x, flip(at_x, low))
     blocks += (at_y, flip(at_y, low), at_xy, flip(at_xy, low))
     white, newer = run(
-        apply_kernel,
+        functools.partial(apply_kernel, scale),
         (shape((len(blocks), rows, size), BF), shape((count, rows), F32)),
         (whiten, *blocks, weights),
     )
 
     for turn in range(ICA_ITERS):
         last = turn == ICA_ITERS - 1
-        stacked = spread(*sum_over(newer, far), across, near)
+        stacked = spread(*sum_over(newer, far, HALF), across, near)
+        stacked = [part.astype(F32) * (1.0 / scale) for part in stacked]
         chunks = len(blocks) // 2 if last else len(blocks)
         outs = (
             (shape((2 * count, rows), F32), shape((2 * count, data.shape[1]), BF))
@@ -330,7 +344,7 @@
                 pltpu.SemaphoreType.DMA((chunks + 1,)),
             ]
         newer = run(
-            functools.partial(decor_kernel, last),
+            functools.partial(decor_kernel, last, scale),
             outs,
             (*stacked, white),
             specs=[VMEM] * 8 + [HBM],

time: 85.8 us -> 86.4 us (level)
  transfers between devices with their start and end apart: 41 -> 41, of which waited for: 25 -> 26; matrix products, arithmetic and copies ran while one was open for 2% -> 2% of each run, Pallas kernels for 3% -> 3%
where the time goes in v8:
time: 86.4 us; the launch traced here: 86.2 us
  starting transfers between devices  36.8 us (43%)
  waiting for transfers between devices  34.3 us (40%)
  Pallas kernels  12.3 us (14%)
  local copies, waits for them, and re-layouts  1.3 us (2%)
  between operations  0.97 us (1%)
    ppermute x41, starting transfers between devices, flip(): return lax.ppermute(x, AXES, [(i, i ^ mask) for i in range(count)])  36.8 us
    ppermute x41, waiting for transfers between devices, flip(): return lax.ppermute(x, AXES, [(i, i ^ mask) for i in range(count)])  34.3 us
    pallas_call x7, Pallas kernels, run(): pl.pallas_call(kernel, out_shape=outs, in_specs=specs or [VMEM] * len(arg...  12.3 us
  transfers between devices with their start and end apart: 41, of which 26 were waited for; matrix products, arithmetic and copies ran while one was open for 2% of the time, Pallas kernels for 3%

profile of v8, /device:TPU:0, one launch (start us, length us, event | category | flops | bytes accessed | tf_op | source)
XLA Modules:
  0.0 86.2 jit_solution(9756976815689312400)
XLA Ops:
  0.7 0.5 collective-permute-start
  1.2 1.3 %constant_dynamic-slice_fusion.1 = (bf16[512,256]{1,0:T(8,128)(2,1)S(1)}, bf16[512,256]{1,0:T(8,128)(2,1)S(1)}, bf16[512,256]{1,0:T(8,128)(2,1)S(1)}, bf16[512,256]{1,0:T(8,128)(2,1)S(1)}) fusion(bf16[512,1024]{1,0:T(8,128)(2,1)} %param.3, s32[]{:T(128)S(6)} %select_n.18, s32[]{:T(128)S(6)} %select_n.16, s32[]{:T(128)S(6)} %select_n.15, s32[]{:T(128)S(6)} %select_n.17), kind=kLoop, calls=%fused_computation.13 | loop fusion | bytes 2097168 | tf_op jit(solution)/shard_map/dynamic_slice | solution.py:273
  2.4 0.2 collective-permute-start.2
  2.6 1.4 %collective-permute-done.2.mate_right_ref = bf16[512,256]{1,0:T(8,128)(2,1)S(1)} collective-permute-done((bf16[512,256]{1,0:T(8,128)(2,1)S(1)}, bf16[512,256]{1,0:T(8,128)(2,1)S(1)}, u32[]{:S(2)}, u32[]{:S(2)}) %collective-permute-start.2) | collective-permute-done | bytes 262176 | tf_op jit(solution)/shard_map/ppermute | solution.py:44
  4.1 0.5 shard_map.51
  4.6 2.7 %collective-permute-start.3 = (f16[528,256]{1,0:T(8,128)(2,1)S(1)}, f16[528,256]{1,0:T(8,128)(2,1)S(1)}, u32[]{:S(2)}, u32[]{:S(2)}) collective-permute-start(f16[528,256]{1,0:T(8,128)(2,1)S(1)} %convert_element_type.111), channel_id=1, source_target_pairs={{0,2},{1,3},{2,0},{3,1},{4,6},{5,7},{6,4},{7,5},{8,10},{9,11},{10,... | collective-permute-start | bytes 811016 | tf_op jit(solution)/shard_map/ppermute | solution.py:44
  7.3 0.1 collective-permute-start.1
  7.4 1.5 %collective-permute-done.1.mate_right_ref = bf16[512,256]{1,0:T(8,128)(2,1)S(1)} collective-permute-done((bf16[512,256]{1,0:T(8,128)(2,1)S(1)}, bf16[512,256]{1,0:T(8,128)(2,1)S(1)}, u32[]{:S(2)}, u32[]{:S(2)}) %collective-permute-start.1) | collective-permute-done | bytes 262176 | tf_op jit(solution)/shard_map/ppermute | solution.py:44
  8.8 0.4 shard_map.50
  9.3 5.0 %collective-permute-done.3 = f16[528,256]{1,0:T(8,128)(2,1)S(1)} collective-permute-done((f16[528,256]{1,0:T(8,128)(2,1)S(1)}, f16[528,256]{1,0:T(8,128)(2,1)S(1)}, u32[]{:S(2)}, u32[]{:S(2)}) %collective-permute-start.3) | collective-permute-done | bytes 270368 | tf_op jit(solution)/shard_map/ppermute | solution.py:44
  14.5 1.5 %collective-permute-done.4.there_ref.refs_1_ = bf16[512,256]{1,0:T(8,128)(2,1)S(1)} collective-permute-done((bf16[512,256]{1,0:T(8,128)(2,1)S(1)}, bf16[512,256]{1,0:T(8,128)(2,1)S(1)}, u32[]{:S(2)}, u32[]{:S(2)}) %collective-permute-start.4) | collective-permute-done | bytes 262176 | tf_op jit(solution)/shard_map/ppermute | solution.py:44
  16.1 0.4 shard_map.52
  16.4 2.8 %collective-permute-start.5 = (bf16[160,128]{1,0:T(8,128)(2,1)S(1)}, bf16[160,128]{1,0:T(8,128)(2,1)S(1)}, u32[]{:S(2)}, u32[]{:S(2)}) collective-permute-start(bf16[160,128]{1,0:T(8,128)(2,1)S(1)} %get-tuple-element.19), channel_id=1, source_target_pairs={{0,6},{1,7},{2,4},{3,5},{4,2},{5,3},{6,0},{7,1},{8,14},{9,15},{10,... | collective-permute-start | bytes 122888 | tf_op jit(solution)/shard_map/ppermute | solution.py:44
  19.2 0.5 collective-permute-start.6
  19.7 0.3 collective-permute-start.7
  20.0 1.8 %collective-permute-start.12 = (bf16[512,256]{1,0:T(8,128)(2,1)S(1)}, bf16[512,256]{1,0:T(8,128)(2,1)S(1)}, u32[]{:S(2)}, u32[]{:S(2)}) collective-permute-start(bf16[512,256]{1,0:T(8,128)(2,1)S(1)} %fusion.1.here_ref.refs_0_), channel_id=1, source_target_pairs={{0,4},{1,5},{2,6},{3,7},{4,0},{5,1},{6,2},{7,3},{8,12},{9,13},{10,... | collective-permute-start | bytes 786440 | tf_op jit(solution)/shard_map/ppermute | solution.py:44
  21.7 1.5 %collective-permute-start.11 = (bf16[512,256]{1,0:T(8,128)(2,1)S(1)}, bf16[512,256]{1,0:T(8,128)(2,1)S(1)}, u32[]{:S(2)}, u32[]{:S(2)}) collective-permute-start(bf16[512,256]{1,0:T(8,128)(2,1)S(1)} %fusion.1.here_ref.refs_0_), channel_id=1, source_target_pairs={{0,2},{1,3},{2,0},{3,1},{4,6},{5,7},{6,4},{7,5},{8,10},{9,11},{10,... | collective-permute-start | bytes 786440 | tf_op jit(solution)/shard_map/ppermute | solution.py:44
  23.2 1.0 %collective-permute-done.7 = bf16[160,128]{1,0:T(8,128)(2,1)S(1)} collective-permute-done((bf16[160,128]{1,0:T(8,128)(2,1)S(1)}, bf16[160,128]{1,0:T(8,128)(2,1)S(1)}, u32[]{:S(2)}, u32[]{:S(2)}) %collective-permute-start.7) | collective-permute-done | bytes 40992 | tf_op jit(solution)/shard_map/ppermute | solution.py:44
  24.2 3.7 %collective-permute-start.10 = (bf16[160,128]{1,0:T(8,128)(2,1)S(1)}, bf16[160,128]{1,0:T(8,128)(2,1)S(1)}, u32[]{:S(2)}, u32[]{:S(2)}) collective-permute-start(bf16[160,128]{1,0:T(8,128)(2,1)S(1)} %convert_element_type.117), channel_id=1, source_target_pairs={{0,24},{1,25},{2,26},{3,27},{4,28},{5,29},{6,30},{7,31},{8,16},{9,... | collective-permute-start | bytes 122888 | tf_op jit(solution)/shard_map/ppermute | solution.py:44
  27.9 0.8 collective-permute-start.8
  28.7 1.5 %collective-permute-done.10 = bf16[160,128]{1,0:T(8,128)(2,1)S(1)} collective-permute-done((bf16[160,128]{1,0:T(8,128)(2,1)S(1)}, bf16[160,128]{1,0:T(8,128)(2,1)S(1)}, u32[]{:S(2)}, u32[]{:S(2)}) %collective-permute-start.10) | collective-permute-done | bytes 40992 | tf_op jit(solution)/shard_map/ppermute | solution.py:44
  30.2 1.3 %collective-permute-start.16 = (bf16[512,256]{1,0:T(8,128)(2,1)S(1)}, bf16[512,256]{1,0:T(8,128)(2,1)S(1)}, u32[]{:S(2)}, u32[]{:S(2)}) collective-permute-start(bf16[512,256]{1,0:T(8,128)(2,1)S(1)} %fusion.1.here_ref.refs_0_), channel_id=1, source_target_pairs={{0,6},{1,7},{2,4},{3,5},{4,2},{5,3},{6,0},{7,1},{8,14},{9,15},{10,... | collective-permute-start | bytes 786440 | tf_op jit(solution)/shard_map/ppermute | solution.py:44
  31.5 1.3 %collective-permute-done.9 = bf16[160,128]{1,0:T(8,128)(2,1)S(1)} collective-permute-done((bf16[160,128]{1,0:T(8,128)(2,1)S(1)}, bf16[160,128]{1,0:T(8,128)(2,1)S(1)}, u32[]{:S(2)}, u32[]{:S(2)}) %collective-permute-start.9) | collective-permute-done | bytes 40992 | tf_op jit(solution)/shard_map/ppermute | solution.py:44
  32.8 1.4 %collective-permute-start.15 = (bf16[160,128]{1,0:T(8,128)(2,1)S(1)}, bf16[160,128]{1,0:T(8,128)(2,1)S(1)}, u32[]{:S(2)}, u32[]{:S(2)}) collective-permute-start(bf16[160,128]{1,0:T(8,128)(2,1)S(1)} %add_convert_fusion.2.refs_0_), channel_id=1, source_target_pairs={{0,6},{1,7},{2,4},{3,5},{4,2},{5,3},{6,0},{7,1},{8,14},{9,15},{10,... | collective-permute-start | bytes 122888 | tf_op jit(solution)/shard_map/ppermute | solution.py:44
  34.3 0.5 collective-permute-start.14
  34.8 1.6 %collective-permute-start.13 = (bf16[160,128]{1,0:T(8,128)(2,1)S(1)}, bf16[160,128]{1,0:T(8,128)(2,1)S(1)}, u32[]{:S(2)}, u32[]{:S(2)}) collective-permute-start(bf16[160,128]{1,0:T(8,128)(2,1)S(1)} %add_convert_fusion.2.refs_0_), channel_id=1, source_target_pairs={{0,4},{1,5},{2,6},{3,7},{4,0},{5,1},{6,2},{7,3},{8,12},{9,13},{10,... | collective-permute-start | bytes 122888 | tf_op jit(solution)/shard_map/ppermute | solution.py:44
  36.4 1.5 %collective-permute-done.16.refs_6_ = bf16[512,256]{1,0:T(8,128)(2,1)S(1)} collective-permute-done((bf16[512,256]{1,0:T(8,128)(2,1)S(1)}, bf16[512,256]{1,0:T(8,128)(2,1)S(1)}, u32[]{:S(2)}, u32[]{:S(2)}) %collective-permute-start.16) | collective-permute-done | bytes 262176 | tf_op jit(solution)/shard_map/ppermute | solution.py:44
  37.9 0.4 collective-permute-done.15.refs_3_
  38.3 0.5 collective-permute-done.13.refs_1_
  39.0 0.5 collective-permute-start.18
  39.4 0.1 collective-permute-start.19
  39.5 0.4 collective-permute-start.20
  40.0 0.4 collective-permute-done.17
  40.3 2.1 %shard_map.53.whiten_ref = bf16[512,512]{1,0:T(8,128)(2,1)S(1)} custom-call(bf16[160,128]{1,0:T(8,128)(2,1)S(1)} %add_convert_fusion.2.refs_0_, bf16[160,128]{1,0:T(8,128)(2,1)S(1)} %collective-permute-done.13.refs_1_, bf16[160,128]{1,0:T(8,128)(2,1)S(1)} %collective-permute-done.14.refs_2_, bf16[160,128]{1,0:T(8,128)(2,1)S(1)} %collective-permute-done.15.refs_3_, ...), custom_call_target="tpu_custom_call" | custom-call | tf_op jit(solution)/shard_map/pallas_call | solution.py:74
  42.5 2.2 %shard_map.54 = (bf16[8,512,256]{2,1,0:T(8,128)(2,1)S(1)}, f32[64,512]{1,0:T(8,128)S(1)}) custom-call(bf16[512,512]{1,0:T(8,128)(2,1)S(1)} %shard_map.53.whiten_ref, bf16[512,256]{1,0:T(8,128)(2,1)S(1)} %fusion.1.here_ref.refs_0_, bf16[512,256]{1,0:T(8,128)(2,1)S(1)} %collective-permute-done.4.there_ref.refs_1_, ...), custom_call_target="tpu_custom_call" | custom-call | tf_op jit(solution)/shard_map/pallas_call | solution.py:74
  44.7 3.5 %collective-permute-start.23 = (f16[64,512]{1,0:T(8,128)(2,1)S(1)}, f16[64,512]{1,0:T(8,128)(2,1)S(1)}, u32[]{:S(2)}, u32[]{:S(2)}) collective-permute-start(f16[64,512]{1,0:T(8,128)(2,1)S(1)} %convert_element_type.122), channel_id=1, source_target_pairs={{0,24},{1,25},{2,26},{3,27},{4,28},{5,29},{6,30},{7,31},{8,16},{9,... | collective-permute-start | bytes 196616 | tf_op jit(solution)/shard_map/ppermute | solution.py:44
  48.2 1.0 %collective-permute-start.21 = (f16[64,512]{1,0:T(8,128)(2,1)S(1)}, f16[64,512]{1,0:T(8,128)(2,1)S(1)}, u32[]{:S(2)}, u32[]{:S(2)}) collective-permute-start(f16[64,512]{1,0:T(8,128)(2,1)S(1)} %convert_element_type.122), channel_id=1, source_target_pairs={{0,8},{1,9},{2,10},{3,11},{4,12},{5,13},{6,14},{7,15},{8,0},{9,1},... | collective-permute-start | bytes 196616 | tf_op jit(solution)/shard_map/ppermute | solution.py:44
  49.2 2.4 %collective-permute-done.23 = f16[64,512]{1,0:T(8,128)(2,1)S(1)} collective-permute-done((f16[64,512]{1,0:T(8,128)(2,1)S(1)}, f16[64,512]{1,0:T(8,128)(2,1)S(1)}, u32[]{:S(2)}, u32[]{:S(2)}) %collective-permute-start.23) | collective-permute-done | bytes 65568 | tf_op jit(solution)/shard_map/ppermute | solution.py:44
  51.5 2.2 %collective-permute-done.22 = f16[64,512]{1,0:T(8,128)(2,1)S(1)} collective-permute-done((f16[64,512]{1,0:T(8,128)(2,1)S(1)}, f16[64,512]{1,0:T(8,128)(2,1)S(1)}, u32[]{:S(2)}, u32[]{:S(2)}) %collective-permute-start.22) | collective-permute-done | bytes 65568 | tf_op jit(solution)/shard_map/ppermute | solution.py:44
  53.8 0.1 collective-permute-done.21
  53.9 0.1 fusion.4
  54.0 2.3 %collective-permute-start.26 = (f16[64,512]{1,0:T(8,128)(2,1)S(1)}, f16[64,512]{1,0:T(8,128)(2,1)S(1)}, u32[]{:S(2)}, u32[]{:S(2)}) collective-permute-start(f16[64,512]{1,0:T(8,128)(2,1)S(1)} %get-tuple-element.35), channel_id=1, source_target_pairs={{0,6},{1,7},{2,4},{3,5},{4,2},{5,3},{6,0},{7,1},{8,14},{9,15},{10,... | collective-permute-start | bytes 196616 | tf_op jit(solution)/shard_map/ppermute | solution.py:44
  56.3 0.5 collective-permute-start.25
  56.9 0.7 collective-permute-start.24
  57.6 2.4 %collective-permute-done.26 = f16[64,512]{1,0:T(8,128)(2,1)S(1)} collective-permute-done((f16[64,512]{1,0:T(8,128)(2,1)S(1)}, f16[64,512]{1,0:T(8,128)(2,1)S(1)}, u32[]{:S(2)}, u32[]{:S(2)}) %collective-permute-start.26) | collective-permute-done | bytes 65568 | tf_op jit(solution)/shard_map/ppermute | solution.py:44
  59.9 0.7 collective-permute-done.25
  60.6 0.5 collective-permute-done.24
  61.3 0.6 collective-permute-done.29
  61.9 0.5 collective-permute-done.28
  62.4 3.4 %shard_map.55 = f32[64,512]{1,0:T(8,128)S(1)} custom-call(f32[64,512]{1,0:T(8,128)S(1)} %get-tuple-element.34.refs_0_, f32[64,512]{1,0:T(8,128)S(1)} %convert_element_type.128.refs_1_, f32[64,512]{1,0:T(8,128)S(1)} %convert_element_type.129.refs_2_, f32[64,512]{1,0:T(8,128)S(1)} %convert_element_type.130.refs_3_, ...), custom_call_target="tpu_custom_call" | custom-call | tf_op jit(solution)/shard_map/pallas_call | solution.py:74
  65.8 2.6 %collective-permute-start.33 = (f16[64,512]{1,0:T(8,128)(2,1)S(1)}, f16[64,512]{1,0:T(8,128)(2,1)S(1)}, u32[]{:S(2)}, u32[]{:S(2)}) collective-permute-start(f16[64,512]{1,0:T(8,128)(2,1)S(1)} %convert_element_type.135), channel_id=1, source_target_pairs={{0,24},{1,25},{2,26},{3,27},{4,28},{5,29},{6,30},{7,31},{8,16},{9,... | collective-permute-start | bytes 196616 | tf_op jit(solution)/shard_map/ppermute | solution.py:44
  68.4 1.8 %collective-permute-start.31 = (f16[64,512]{1,0:T(8,128)(2,1)S(1)}, f16[64,512]{1,0:T(8,128)(2,1)S(1)}, u32[]{:S(2)}, u32[]{:S(2)}) collective-permute-start(f16[64,512]{1,0:T(8,128)(2,1)S(1)} %convert_element_type.135), channel_id=1, source_target_pairs={{0,8},{1,9},{2,10},{3,11},{4,12},{5,13},{6,14},{7,15},{8,0},{9,1},... | collective-permute-start | bytes 196616 | tf_op jit(solution)/shard_map/ppermute | solution.py:44
  70.3 2.4 %collective-permute-done.33 = f16[64,512]{1,0:T(8,128)(2,1)S(1)} collective-permute-done((f16[64,512]{1,0:T(8,128)(2,1)S(1)}, f16[64,512]{1,0:T(8,128)(2,1)S(1)}, u32[]{:S(2)}, u32[]{:S(2)}) %collective-permute-start.33) | collective-permute-done | bytes 65568 | tf_op jit(solution)/shard_map/ppermute | solution.py:44
  72.6 2.0 %collective-permute-done.32 = f16[64,512]{1,0:T(8,128)(2,1)S(1)} collective-permute-done((f16[64,512]{1,0:T(8,128)(2,1)S(1)}, f16[64,512]{1,0:T(8,128)(2,1)S(1)}, u32[]{:S(2)}, u32[]{:S(2)}) %collective-permute-start.32) | collective-permute-done | bytes 65568 | tf_op jit(solution)/shard_map/ppermute | solution.py:44
  74.7 0.1 fusion.3
  74.8 1.7 %collective-permute-start.36 = (f16[64,512]{1,0:T(8,128)(2,1)S(1)}, f16[64,512]{1,0:T(8,128)(2,1)S(1)}, u32[]{:S(2)}, u32[]{:S(2)}) collective-permute-start(f16[64,512]{1,0:T(8,128)(2,1)S(1)} %get-tuple-element.33), channel_id=1, source_target_pairs={{0,6},{1,7},{2,4},{3,5},{4,2},{5,3},{6,0},{7,1},{8,14},{9,15},{10,... | collective-permute-start | bytes 196616 | tf_op jit(solution)/shard_map/ppermute | solution.py:44
  76.5 0.9 %collective-permute-start.35 = (f16[64,512]{1,0:T(8,128)(2,1)S(1)}, f16[64,512]{1,0:T(8,128)(2,1)S(1)}, u32[]{:S(2)}, u32[]{:S(2)}) collective-permute-start(f16[64,512]{1,0:T(8,128)(2,1)S(1)} %get-tuple-element.33), channel_id=1, source_target_pairs={{0,2},{1,3},{2,0},{3,1},{4,6},{5,7},{6,4},{7,5},{8,10},{9,11},{10,... | collective-permute-start | bytes 196616 | tf_op jit(solution)/shard_map/ppermute | solution.py:44
  77.4 0.9 %collective-permute-start.34 = (f16[64,512]{1,0:T(8,128)(2,1)S(1)}, f16[64,512]{1,0:T(8,128)(2,1)S(1)}, u32[]{:S(2)}, u32[]{:S(2)}) collective-permute-start(f16[64,512]{1,0:T(8,128)(2,1)S(1)} %get-tuple-element.33), channel_id=1, source_target_pairs={{0,4},{1,5},{2,6},{3,7},{4,0},{5,1},{6,2},{7,3},{8,12},{9,13},{10,... | collective-permute-start | bytes 196616 | tf_op jit(solution)/shard_map/ppermute | solution.py:44
  78.3 2.1 %collective-permute-done.36 = f16[64,512]{1,0:T(8,128)(2,1)S(1)} collective-permute-done((f16[64,512]{1,0:T(8,128)(2,1)S(1)}, f16[64,512]{1,0:T(8,128)(2,1)S(1)}, u32[]{:S(2)}, u32[]{:S(2)}) %collective-permute-start.36) | collective-permute-done | bytes 65568 | tf_op jit(solution)/shard_map/ppermute | solution.py:44
  80.5 0.6 collective-permute-done.35
  81.1 0.6 collective-permute-done.34
  81.8 0.5 collective-permute-done.39
  82.3 0.6 collective-permute-done.38
  83.0 3.3 %shard_map.56 = (f32[128,512]{1,0:T(8,128)}, bf16[128,1024]{1,0:T(8,128)(2,1)}) custom-call(f32[64,512]{1,0:T(8,128)S(1)} %get-tuple-element.32.refs_0_, f32[64,512]{1,0:T(8,128)S(1)} %convert_element_type.141.refs_1_, f32[64,512]{1,0:T(8,128)S(1)} %convert_element_type.142.refs_2_, f32[64,512]{1,0:T(8,128)S(1)} %convert_element_type.143.refs_3_, ...), custom_call_target="tpu_custom_call" | custom-call | tf_op jit(solution)/shard_map/pallas_call | solution.py:74
  (58 shorter events, 0.7 us)
Async XLA Ops:
  0.6 39.3 %copy-start = (f32[128,512]{1,0:T(8,128)S(1)}, f32[128,512]{1,0:T(8,128)}, u32[]{:S(2)}) copy-start(f32[128,512]{1,0:T(8,128)} %param.5) | copy-start | bytes 786436
  0.6 3.4 %copy-start.1 = (bf16[512,512]{1,0:T(8,128)(2,1)S(1)}, bf16[512,512]{1,0:T(8,128)(2,1)}, u32[]{:S(2)}) copy-start(bf16[512,512]{1,0:T(8,128)(2,1)} %left_ref.3) | copy-start | bytes 1572868
  0.7 3.4 %collective-permute-start = (bf16[512,512]{1,0:T(8,128)(2,1)}, bf16[512,512]{1,0:T(8,128)(2,1)S(1)}, u32[]{:S(2)}, u32[]{:S(2)}) collective-permute-start(bf16[512,512]{1,0:T(8,128)(2,1)} %left_ref.3), channel_id=1, source_target_pairs={{0,1},{1,0},{2,3},{3,2},{4,5},{5,4},{6,7},{7,6},{8,9},{9,8},{10,11... | collective-permute-start | bytes 1572872 | tf_op jit(solution)/shard_map/ppermute | solution.py:44
  2.4 1.6 %collective-permute-start.2 = (bf16[512,256]{1,0:T(8,128)(2,1)S(1)}, bf16[512,256]{1,0:T(8,128)(2,1)S(1)}, u32[]{:S(2)}, u32[]{:S(2)}) collective-permute-start(bf16[512,256]{1,0:T(8,128)(2,1)S(1)} %get-tuple-element.36), channel_id=1, source_target_pairs={{0,1},{1,0},{2,3},{3,2},{4,5},{5,4},{6,7},{7,6},{8,9},{9,8},{10,11... | collective-permute-start | bytes 786440 | tf_op jit(solution)/shard_map/ppermute | solution.py:44
  4.6 9.7 %collective-permute-start.3 = (f16[528,256]{1,0:T(8,128)(2,1)S(1)}, f16[528,256]{1,0:T(8,128)(2,1)S(1)}, u32[]{:S(2)}, u32[]{:S(2)}) collective-permute-start(f16[528,256]{1,0:T(8,128)(2,1)S(1)} %convert_element_type.111), channel_id=1, source_target_pairs={{0,2},{1,3},{2,0},{3,1},{4,6},{5,7},{6,4},{7,5},{8,10},{9,11},{10,... | collective-permute-start | bytes 811016 | tf_op jit(solution)/shard_map/ppermute | solution.py:44
  7.3 1.5 %collective-permute-start.1 = (bf16[512,256]{1,0:T(8,128)(2,1)S(1)}, bf16[512,256]{1,0:T(8,128)(2,1)S(1)}, u32[]{:S(2)}, u32[]{:S(2)}) collective-permute-start(bf16[512,256]{1,0:T(8,128)(2,1)S(1)} %get-tuple-element.37), channel_id=1, source_target_pairs={{0,1},{1,0},{2,3},{3,2},{4,5},{5,4},{6,7},{7,6},{8,9},{9,8},{10,11... | collective-permute-start | bytes 786440 | tf_op jit(solution)/shard_map/ppermute | solution.py:44
  14.5 1.6 %collective-permute-start.4 = (bf16[512,256]{1,0:T(8,128)(2,1)S(1)}, bf16[512,256]{1,0:T(8,128)(2,1)S(1)}, u32[]{:S(2)}, u32[]{:S(2)}) collective-permute-start(bf16[512,256]{1,0:T(8,128)(2,1)S(1)} %fusion.1.here_ref.refs_0_), channel_id=1, source_target_pairs={{0,1},{1,0},{2,3},{3,2},{4,5},{5,4},{6,7},{7,6},{8,9},{9,8},{10,11... | collective-permute-start | bytes 786440 | tf_op jit(solution)/shard_map/ppermute | solution.py:44
  16.4 6.8 %collective-permute-start.5 = (bf16[160,128]{1,0:T(8,128)(2,1)S(1)}, bf16[160,128]{1,0:T(8,128)(2,1)S(1)}, u32[]{:S(2)}, u32[]{:S(2)}) collective-permute-start(bf16[160,128]{1,0:T(8,128)(2,1)S(1)} %get-tuple-element.19), channel_id=1, source_target_pairs={{0,6},{1,7},{2,4},{3,5},{4,2},{5,3},{6,0},{7,1},{8,14},{9,15},{10,... | collective-permute-start | bytes 122888 | tf_op jit(solution)/shard_map/ppermute | solution.py:44
  19.2 4.1 %collective-permute-start.6 = (bf16[160,128]{1,0:T(8,128)(2,1)S(1)}, bf16[160,128]{1,0:T(8,128)(2,1)S(1)}, u32[]{:S(2)}, u32[]{:S(2)}) collective-permute-start(bf16[160,128]{1,0:T(8,128)(2,1)S(1)} %get-tuple-element.20), channel_id=1, source_target_pairs={{0,2},{1,3},{2,0},{3,1},{4,6},{5,7},{6,4},{7,5},{8,10},{9,11},{10,... | collective-permute-start | bytes 122888 | tf_op jit(solution)/shard_map/ppermute | solution.py:44
  19.7 4.5 %collective-permute-start.7 = (bf16[160,128]{1,0:T(8,128)(2,1)S(1)}, bf16[160,128]{1,0:T(8,128)(2,1)S(1)}, u32[]{:S(2)}, u32[]{:S(2)}) collective-permute-start(bf16[160,128]{1,0:T(8,128)(2,1)S(1)} %get-tuple-element.21), channel_id=1, source_target_pairs={{0,4},{1,5},{2,6},{3,7},{4,0},{5,1},{6,2},{7,3},{8,12},{9,13},{10,... | collective-permute-start | bytes 122888 | tf_op jit(solution)/shard_map/ppermute | solution.py:44
  20.0 11.5 %collective-permute-start.12 = (bf16[512,256]{1,0:T(8,128)(2,1)S(1)}, bf16[512,256]{1,0:T(8,128)(2,1)S(1)}, u32[]{:S(2)}, u32[]{:S(2)}) collective-permute-start(bf16[512,256]{1,0:T(8,128)(2,1)S(1)} %fusion.1.here_ref.refs_0_), channel_id=1, source_target_pairs={{0,4},{1,5},{2,6},{3,7},{4,0},{5,1},{6,2},{7,3},{8,12},{9,13},{10,... | collective-permute-start | bytes 786440 | tf_op jit(solution)/shard_map/ppermute | solution.py:44
  21.7 9.8 %collective-permute-start.11 = (bf16[512,256]{1,0:T(8,128)(2,1)S(1)}, bf16[512,256]{1,0:T(8,128)(2,1)S(1)}, u32[]{:S(2)}, u32[]{:S(2)}) collective-permute-start(bf16[512,256]{1,0:T(8,128)(2,1)S(1)} %fusion.1.here_ref.refs_0_), channel_id=1, source_target_pairs={{0,2},{1,3},{2,0},{3,1},{4,6},{5,7},{6,4},{7,5},{8,10},{9,11},{10,... | collective-permute-start | bytes 786440 | tf_op jit(solution)/shard_map/ppermute | solution.py:44
  24.2 5.9 %collective-permute-start.10 = (bf16[160,128]{1,0:T(8,128)(2,1)S(1)}, bf16[160,128]{1,0:T(8,128)(2,1)S(1)}, u32[]{:S(2)}, u32[]{:S(2)}) collective-permute-start(bf16[160,128]{1,0:T(8,128)(2,1)S(1)} %convert_element_type.117), channel_id=1, source_target_pairs={{0,24},{1,25},{2,26},{3,27},{4,28},{5,29},{6,30},{7,31},{8,16},{9,... | collective-permute-start | bytes 122888 | tf_op jit(solution)/shard_map/ppermute | solution.py:44
  27.9 4.9 %collective-permute-start.9 = (bf16[160,128]{1,0:T(8,128)(2,1)S(1)}, bf16[160,128]{1,0:T(8,128)(2,1)S(1)}, u32[]{:S(2)}, u32[]{:S(2)}) collective-permute-start(bf16[160,128]{1,0:T(8,128)(2,1)S(1)} %convert_element_type.117), channel_id=1, source_target_pairs={{0,16},{1,17},{2,18},{3,19},{4,20},{5,21},{6,22},{7,23},{8,24},{9,... | collective-permute-start | bytes 122888 | tf_op jit(solution)/shard_map/ppermute | solution.py:44
  27.9 4.9 %collective-permute-start.8 = (bf16[160,128]{1,0:T(8,128)(2,1)S(1)}, bf16[160,128]{1,0:T(8,128)(2,1)S(1)}, u32[]{:S(2)}, u32[]{:S(2)}) collective-permute-start(bf16[160,128]{1,0:T(8,128)(2,1)S(1)} %convert_element_type.117), channel_id=1, source_target_pairs={{0,8},{1,9},{2,10},{3,11},{4,12},{5,13},{6,14},{7,15},{8,0},{9,1},... | collective-permute-start | bytes 122888 | tf_op jit(solution)/shard_map/ppermute | solution.py:44
  30.2 7.7 %collective-permute-start.16 = (bf16[512,256]{1,0:T(8,128)(2,1)S(1)}, bf16[512,256]{1,0:T(8,128)(2,1)S(1)}, u32[]{:S(2)}, u32[]{:S(2)}) collective-permute-start(bf16[512,256]{1,0:T(8,128)(2,1)S(1)} %fusion.1.here_ref.refs_0_), channel_id=1, source_target_pairs={{0,6},{1,7},{2,4},{3,5},{4,2},{5,3},{6,0},{7,1},{8,14},{9,15},{10,... | collective-permute-start | bytes 786440 | tf_op jit(solution)/shard_map/ppermute | solution.py:44
  32.8 5.5 %collective-permute-start.15 = (bf16[160,128]{1,0:T(8,128)(2,1)S(1)}, bf16[160,128]{1,0:T(8,128)(2,1)S(1)}, u32[]{:S(2)}, u32[]{:S(2)}) collective-permute-start(bf16[160,128]{1,0:T(8,128)(2,1)S(1)} %add_convert_fusion.2.refs_0_), channel_id=1, source_target_pairs={{0,6},{1,7},{2,4},{3,5},{4,2},{5,3},{6,0},{7,1},{8,14},{9,15},{10,... | collective-permute-start | bytes 122888 | tf_op jit(solution)/shard_map/ppermute | solution.py:44
  34.3 4.1 %collective-permute-start.14 = (bf16[160,128]{1,0:T(8,128)(2,1)S(1)}, bf16[160,128]{1,0:T(8,128)(2,1)S(1)}, u32[]{:S(2)}, u32[]{:S(2)}) collective-permute-start(bf16[160,128]{1,0:T(8,128)(2,1)S(1)} %add_convert_fusion.2.refs_0_), channel_id=1, source_target_pairs={{0,2},{1,3},{2,0},{3,1},{4,6},{5,7},{6,4},{7,5},{8,10},{9,11},{10,... | collective-permute-start | bytes 122888 | tf_op jit(solution)/shard_map/ppermute | solution.py:44
  34.8 4.0 %collective-permute-start.13 = (bf16[160,128]{1,0:T(8,128)(2,1)S(1)}, bf16[160,128]{1,0:T(8,128)(2,1)S(1)}, u32[]{:S(2)}, u32[]{:S(2)}) collective-permute-start(bf16[160,128]{1,0:T(8,128)(2,1)S(1)} %add_convert_fusion.2.refs_0_), channel_id=1, source_target_pairs={{0,4},{1,5},{2,6},{3,7},{4,0},{5,1},{6,2},{7,3},{8,12},{9,13},{10,... | collective-permute-start | bytes 122888 | tf_op jit(solution)/shard_map/ppermute | solution.py:44
  38.9 1.5 %collective-permute-start.17 = (bf16[4,160,128]{2,1,0:T(8,128)(2,1)S(1)}, bf16[4,160,128]{2,1,0:T(8,128)(2,1)S(1)}, u32[]{:S(2)}, u32[]{:S(2)}) collective-permute-start(bf16[4,160,128]{2,1,0:T(8,128)(2,1)S(1)} %pad_maximum_fusion), channel_id=1, source_target_pairs={{0,1},{1,0},{2,3},{3,2},{4,5},{5,4},{6,7},{7,6},{8,9},{9,8},{10,11... | collective-permute-start | bytes 491528 | tf_op jit(solution)/shard_map/ppermute | solution.py:44
  39.0 3.5 %collective-permute-start.18 = (bf16[512,256]{1,0:T(8,128)(2,1)S(1)}, bf16[512,256]{1,0:T(8,128)(2,1)S(1)}, u32[]{:S(2)}, u32[]{:S(2)}) collective-permute-start(bf16[512,256]{1,0:T(8,128)(2,1)S(1)} %collective-permute-done.11.refs_2_), channel_id=1, source_target_pairs={{0,1},{1,0},{2,3},{3,2},{4,5},{5,4},{6,7},{7,6},{8,9},{9,8},{10,11... | collective-permute-start | bytes 786440 | tf_op jit(solution)/shard_map/ppermute | solution.py:44
  39.4 3.0 %collective-permute-start.19 = (bf16[512,256]{1,0:T(8,128)(2,1)S(1)}, bf16[512,256]{1,0:T(8,128)(2,1)S(1)}, u32[]{:S(2)}, u32[]{:S(2)}) collective-permute-start(bf16[512,256]{1,0:T(8,128)(2,1)S(1)} %collective-permute-done.12.refs_4_), channel_id=1, source_target_pairs={{0,1},{1,0},{2,3},{3,2},{4,5},{5,4},{6,7},{7,6},{8,9},{9,8},{10,11... | collective-permute-start | bytes 786440 | tf_op jit(solution)/shard_map/ppermute | solution.py:44
  39.5 2.9 %collective-permute-start.20 = (bf16[512,256]{1,0:T(8,128)(2,1)S(1)}, bf16[512,256]{1,0:T(8,128)(2,1)S(1)}, u32[]{:S(2)}, u32[]{:S(2)}) collective-permute-start(bf16[512,256]{1,0:T(8,128)(2,1)S(1)} %collective-permute-done.16.refs_6_), channel_id=1, source_target_pairs={{0,1},{1,0},{2,3},{3,2},{4,5},{5,4},{6,7},{7,6},{8,9},{9,8},{10,11... | collective-permute-start | bytes 786440 | tf_op jit(solution)/shard_map/ppermute | solution.py:44
  44.7 6.8 %collective-permute-start.23 = (f16[64,512]{1,0:T(8,128)(2,1)S(1)}, f16[64,512]{1,0:T(8,128)(2,1)S(1)}, u32[]{:S(2)}, u32[]{:S(2)}) collective-permute-start(f16[64,512]{1,0:T(8,128)(2,1)S(1)} %convert_element_type.122), channel_id=1, source_target_pairs={{0,24},{1,25},{2,26},{3,27},{4,28},{5,29},{6,30},{7,31},{8,16},{9,... | collective-permute-start | bytes 196616 | tf_op jit(solution)/shard_map/ppermute | solution.py:44
  48.2 5.6 %collective-permute-start.22 = (f16[64,512]{1,0:T(8,128)(2,1)S(1)}, f16[64,512]{1,0:T(8,128)(2,1)S(1)}, u32[]{:S(2)}, u32[]{:S(2)}) collective-permute-start(f16[64,512]{1,0:T(8,128)(2,1)S(1)} %convert_element_type.122), channel_id=1, source_target_pairs={{0,16},{1,17},{2,18},{3,19},{4,20},{5,21},{6,22},{7,23},{8,24},{9,... | collective-permute-start | bytes 196616 | tf_op jit(solution)/shard_map/ppermute | solution.py:44
  48.2 5.7 %collective-permute-start.21 = (f16[64,512]{1,0:T(8,128)(2,1)S(1)}, f16[64,512]{1,0:T(8,128)(2,1)S(1)}, u32[]{:S(2)}, u32[]{:S(2)}) collective-permute-start(f16[64,512]{1,0:T(8,128)(2,1)S(1)} %convert_element_type.122), channel_id=1, source_target_pairs={{0,8},{1,9},{2,10},{3,11},{4,12},{5,13},{6,14},{7,15},{8,0},{9,1},... | collective-permute-start | bytes 196616 | tf_op jit(solution)/shard_map/ppermute | solution.py:44
  54.0 5.9 %collective-permute-start.26 = (f16[64,512]{1,0:T(8,128)(2,1)S(1)}, f16[64,512]{1,0:T(8,128)(2,1)S(1)}, u32[]{:S(2)}, u32[]{:S(2)}) collective-permute-start(f16[64,512]{1,0:T(8,128)(2,1)S(1)} %get-tuple-element.35), channel_id=1, source_target_pairs={{0,6},{1,7},{2,4},{3,5},{4,2},{5,3},{6,0},{7,1},{8,14},{9,15},{10,... | collective-permute-start | bytes 196616 | tf_op jit(solution)/shard_map/ppermute | solution.py:44
  56.3 4.3 %collective-permute-start.25 = (f16[64,512]{1,0:T(8,128)(2,1)S(1)}, f16[64,512]{1,0:T(8,128)(2,1)S(1)}, u32[]{:S(2)}, u32[]{:S(2)}) collective-permute-start(f16[64,512]{1,0:T(8,128)(2,1)S(1)} %get-tuple-element.35), channel_id=1, source_target_pairs={{0,2},{1,3},{2,0},{3,1},{4,6},{5,7},{6,4},{7,5},{8,10},{9,11},{10,... | collective-permute-start | bytes 196616 | tf_op jit(solution)/shard_map/ppermute | solution.py:44
  56.9 4.3 %collective-permute-start.24 = (f16[64,512]{1,0:T(8,128)(2,1)S(1)}, f16[64,512]{1,0:T(8,128)(2,1)S(1)}, u32[]{:S(2)}, u32[]{:S(2)}) collective-permute-start(f16[64,512]{1,0:T(8,128)(2,1)S(1)} %get-tuple-element.35), channel_id=1, source_target_pairs={{0,4},{1,5},{2,6},{3,7},{4,0},{5,1},{6,2},{7,3},{8,12},{9,13},{10,... | collective-permute-start | bytes 196616 | tf_op jit(solution)/shard_map/ppermute | solution.py:44
  57.6 3.6 %collective-permute-start.27 = (f16[64,512]{1,0:T(8,128)(2,1)S(1)}, f16[64,512]{1,0:T(8,128)(2,1)S(1)}, u32[]{:S(2)}, u32[]{:S(2)}) collective-permute-start(f16[64,512]{1,0:T(8,128)(2,1)S(1)} %get-tuple-element.35), channel_id=1, source_target_pairs={{0,1},{1,0},{2,3},{3,2},{4,5},{5,4},{6,7},{7,6},{8,9},{9,8},{10,11... | collective-permute-start | bytes 196616 | tf_op jit(solution)/shard_map/ppermute | solution.py:44
  59.9 1.3 %collective-permute-start.30 = (f16[64,512]{1,0:T(8,128)(2,1)S(1)}, f16[64,512]{1,0:T(8,128)(2,1)S(1)}, u32[]{:S(2)}, u32[]{:S(2)}) collective-permute-start(f16[64,512]{1,0:T(8,128)(2,1)S(1)} %collective-permute-done.26), channel_id=1, source_target_pairs={{0,1},{1,0},{2,3},{3,2},{4,5},{5,4},{6,7},{7,6},{8,9},{9,8},{10,11... | collective-permute-start | bytes 196616 | tf_op jit(solution)/shard_map/ppermute | solution.py:44
  60.6 1.3 %collective-permute-start.29 = (f16[64,512]{1,0:T(8,128)(2,1)S(1)}, f16[64,512]{1,0:T(8,128)(2,1)S(1)}, u32[]{:S(2)}, u32[]{:S(2)}) collective-permute-start(f16[64,512]{1,0:T(8,128)(2,1)S(1)} %collective-permute-done.25), channel_id=1, source_target_pairs={{0,1},{1,0},{2,3},{3,2},{4,5},{5,4},{6,7},{7,6},{8,9},{9,8},{10,11... | collective-permute-start | bytes 196616 | tf_op jit(solution)/shard_map/ppermute | solution.py:44
  61.1 1.3 %collective-permute-start.28 = (f16[64,512]{1,0:T(8,128)(2,1)S(1)}, f16[64,512]{1,0:T(8,128)(2,1)S(1)}, u32[]{:S(2)}, u32[]{:S(2)}) collective-permute-start(f16[64,512]{1,0:T(8,128)(2,1)S(1)} %collective-permute-done.24), channel_id=1, source_target_pairs={{0,1},{1,0},{2,3},{3,2},{4,5},{5,4},{6,7},{7,6},{8,9},{9,8},{10,11... | collective-permute-start | bytes 196616 | tf_op jit(solution)/shard_map/ppermute | solution.py:44
  65.8 6.8 %collective-permute-start.33 = (f16[64,512]{1,0:T(8,128)(2,1)S(1)}, f16[64,512]{1,0:T(8,128)(2,1)S(1)}, u32[]{:S(2)}, u32[]{:S(2)}) collective-permute-start(f16[64,512]{1,0:T(8,128)(2,1)S(1)} %convert_element_type.135), channel_id=1, source_target_pairs={{0,24},{1,25},{2,26},{3,27},{4,28},{5,29},{6,30},{7,31},{8,16},{9,... | collective-permute-start | bytes 196616 | tf_op jit(solution)/shard_map/ppermute | solution.py:44
  68.4 6.2 %collective-permute-start.32 = (f16[64,512]{1,0:T(8,128)(2,1)S(1)}, f16[64,512]{1,0:T(8,128)(2,1)S(1)}, u32[]{:S(2)}, u32[]{:S(2)}) collective-permute-start(f16[64,512]{1,0:T(8,128)(2,1)S(1)} %convert_element_type.135), channel_id=1, source_target_pairs={{0,16},{1,17},{2,18},{3,19},{4,20},{5,21},{6,22},{7,23},{8,24},{9,... | collective-permute-start | bytes 196616 | tf_op jit(solution)/shard_map/ppermute | solution.py:44
  68.4 6.2 %collective-permute-start.31 = (f16[64,512]{1,0:T(8,128)(2,1)S(1)}, f16[64,512]{1,0:T(8,128)(2,1)S(1)}, u32[]{:S(2)}, u32[]{:S(2)}) collective-permute-start(f16[64,512]{1,0:T(8,128)(2,1)S(1)} %convert_element_type.135), channel_id=1, source_target_pairs={{0,8},{1,9},{2,10},{3,11},{4,12},{5,13},{6,14},{7,15},{8,0},{9,1},... | collective-permute-start | bytes 196616 | tf_op jit(solution)/shard_map/ppermute | solution.py:44
  74.8 5.7 %collective-permute-start.36 = (f16[64,512]{1,0:T(8,128)(2,1)S(1)}, f16[64,512]{1,0:T(8,128)(2,1)S(1)}, u32[]{:S(2)}, u32[]{:S(2)}) collective-permute-start(f16[64,512]{1,0:T(8,128)(2,1)S(1)} %get-tuple-element.33), channel_id=1, source_target_pairs={{0,6},{1,7},{2,4},{3,5},{4,2},{5,3},{6,0},{7,1},{8,14},{9,15},{10,... | collective-permute-start | bytes 196616 | tf_op jit(solution)/shard_map/ppermute | solution.py:44
  76.5 4.5 %collective-permute-start.35 = (f16[64,512]{1,0:T(8,128)(2,1)S(1)}, f16[64,512]{1,0:T(8,128)(2,1)S(1)}, u32[]{:S(2)}, u32[]{:S(2)}) collective-permute-start(f16[64,512]{1,0:T(8,128)(2,1)S(1)} %get-tuple-element.33), channel_id=1, source_target_pairs={{0,2},{1,3},{2,0},{3,1},{4,6},{5,7},{6,4},{7,5},{8,10},{9,11},{10,... | collective-permute-start | bytes 196616 | tf_op jit(solution)/shard_map/ppermute | solution.py:44
  77.4 4.3 %collective-permute-start.34 = (f16[64,512]{1,0:T(8,128)(2,1)S(1)}, f16[64,512]{1,0:T(8,128)(2,1)S(1)}, u32[]{:S(2)}, u32[]{:S(2)}) collective-permute-start(f16[64,512]{1,0:T(8,128)(2,1)S(1)} %get-tuple-element.33), channel_id=1, source_target_pairs={{0,4},{1,5},{2,6},{3,7},{4,0},{5,1},{6,2},{7,3},{8,12},{9,13},{10,... | collective-permute-start | bytes 196616 | tf_op jit(solution)/shard_map/ppermute | solution.py:44
  78.3 3.4 %collective-permute-start.37 = (f16[64,512]{1,0:T(8,128)(2,1)S(1)}, f16[64,512]{1,0:T(8,128)(2,1)S(1)}, u32[]{:S(2)}, u32[]{:S(2)}) collective-permute-start(f16[64,512]{1,0:T(8,128)(2,1)S(1)} %get-tuple-element.33), channel_id=1, source_target_pairs={{0,1},{1,0},{2,3},{3,2},{4,5},{5,4},{6,7},{7,6},{8,9},{9,8},{10,11... | collective-permute-start | bytes 196616 | tf_op jit(solution)/shard_map/ppermute | solution.py:44
  80.4 1.3 %collective-permute-start.40 = (f16[64,512]{1,0:T(8,128)(2,1)S(1)}, f16[64,512]{1,0:T(8,128)(2,1)S(1)}, u32[]{:S(2)}, u32[]{:S(2)}) collective-permute-start(f16[64,512]{1,0:T(8,128)(2,1)S(1)} %collective-permute-done.36), channel_id=1, source_target_pairs={{0,1},{1,0},{2,3},{3,2},{4,5},{5,4},{6,7},{7,6},{8,9},{9,8},{10,11... | collective-permute-start | bytes 196616 | tf_op jit(solution)/shard_map/ppermute | solution.py:44
  81.1 1.3 %collective-permute-start.39 = (f16[64,512]{1,0:T(8,128)(2,1)S(1)}, f16[64,512]{1,0:T(8,128)(2,1)S(1)}, u32[]{:S(2)}, u32[]{:S(2)}) collective-permute-start(f16[64,512]{1,0:T(8,128)(2,1)S(1)} %collective-permute-done.35), channel_id=1, source_target_pairs={{0,1},{1,0},{2,3},{3,2},{4,5},{5,4},{6,7},{7,6},{8,9},{9,8},{10,11... | collective-permute-start | bytes 196616 | tf_op jit(solution)/shard_map/ppermute | solution.py:44
  81.7 1.3 %collective-permute-start.38 = (f16[64,512]{1,0:T(8,128)(2,1)S(1)}, f16[64,512]{1,0:T(8,128)(2,1)S(1)}, u32[]{:S(2)}, u32[]{:S(2)}) collective-permute-start(f16[64,512]{1,0:T(8,128)(2,1)S(1)} %collective-permute-done.34), channel_id=1, source_target_pairs={{0,1},{1,0},{2,3},{3,2},{4,5},{5,4},{6,7},{7,6},{8,9},{9,8},{10,11... | collective-permute-start | bytes 196616 | tf_op jit(solution)/shard_map/ppermute | solution.py:44

commit v9 on v8

--- a/solution.py
+++ b/solution.py
@@ -70,14 +70,17 @@
 HBM = pl.BlockSpec(memory_space=pltpu.HBM)
 
 
-def run(kernel, outs, args, specs=None, out_spec=VMEM, scratch=(), limit=24):
+def run(kernel, outs, args, specs=None, out_spec=VMEM, scratch=(), cost=0):
     return pl.pallas_call(
         kernel,
         out_shape=outs,
         in_specs=specs or [VMEM] * len(args),
         out_specs=jax.tree.map(lambda _: out_spec, outs),
         scratch_shapes=list(scratch),
-        compiler_params=pltpu.CompilerParams(vmem_limit_bytes=limit * MIB),
+        compiler_params=pltpu.CompilerParams(vmem_limit_bytes=24 * MIB),
+        cost_estimate=pl.CostEstimate(flops=cost, bytes_accessed=cost // 256, transcendentals=0)
+        if cost
+        else None,
     )(*args)
 
 
@@ -133,7 +136,8 @@
 
 
 def whiten_kernel(voxels, *refs):
-    mine, mates, (out_ref, packs, covar) = refs[:4], refs[4:8], refs[8:]
+    mine, mates = refs[:4], refs[4:8]
+    weights_ref, out_ref, mixed_ref, packs, covar = refs[8:]
     piece, block = mine[0].shape
     rows = covar.shape[0]
     low, ax, ay = place()
@@ -177,7 +181,9 @@
     z3 = 3.375 * eye + 1.5 * rest - 0.5 * (
         5.0625 * left + nn(left.astype(BF), right.astype(BF))
     )
-    out_ref[...] = (z3 * lax.rsqrt(cscale)).astype(BF)
+    whiten = (z3 * lax.rsqrt(cscale)).astype(BF)
+    out_ref[...] = whiten
+    mixed_ref[...] = nn(weights_ref[...].astype(BF), whiten).astype(BF)
 
 
 def step(weights, blocks):
@@ -191,26 +197,30 @@
     return pulled, jnp.sum(slopes, axis=1, keepdims=True)
 
 
-def apply_kernel(scale, whiten_ref, *refs):
-    blocks, (weights_ref, white_ref, newer_ref) = refs[:-3], refs[-3:]
-    weights = weights_ref[...]
-    whites = []
-    for k, block in enumerate(blocks):
-        whites.append(nn(whiten_ref[...], block[...]).astype(BF))
-        white_ref[k] = whites[k]
-    total, slope = step(weights, whites)
-    newer_ref[...] = (total - slope * weights) * scale
+def apply_kernel(scale, mixed_ref, whiten_ref, weights_ref, *refs):
+    blocks, newer_ref = [ref[...] for ref in refs[:-1]], refs[-1]
+    bents = [jnp.tanh(nn(mixed_ref[...], block)) for block in blocks]
+    total, slopes = 0.0, 0.0
+    for bent, block in zip(bents, blocks):
+        total += nt(bent.astype(BF), block)
+        slopes += 1.0 - bent * bent
+    pulled = nt(total.astype(BF), whiten_ref[...])
+    slope = jnp.sum(slopes, axis=1, keepdims=True)
+    newer_ref[...] = (pulled - slope * weights_ref[...]) * scale
+
+
+def white_kernel(whiten_ref, *refs):
+    for k, block in enumerate(refs[:-1]):
+        refs[-1][k] = nn(whiten_ref[...], block[...]).astype(BF)
 
 
 def decor_kernel(last, scale, *refs):
     mine, mates, white_ref = refs[:4], refs[4:8], refs[8]
     outs, scratch = (refs[9:11], refs[11:]) if last else (refs[9:10], refs[10:])
-    newer, lower, white, sem, *held = scratch
+    newer, lower, *held = scratch
     count = mine[0].shape[0]
     low, ax, ay = place()
-    chunks = white.shape[0]
-    copy = pltpu.make_async_copy(white_ref.at[pl.ds(0, chunks)], white, sem)
-    copy.start()
+    chunks = white_ref.shape[0] // 2 if last else white_ref.shape[0]
     for k in range(4):
         spot = 4 * other(ax, k & 2) + other(ay, k & 1)
         for ref, core in ((mine[k], low), (mates[k], 1 - low)):
@@ -235,15 +245,14 @@
     raw = lower[...]
     gram = nt(lower[pl.ds(start, size), :], raw).astype(BF)
     weights = 1.5 * newer[pl.ds(start, size), :] - 0.5 * nn(gram, raw)
-    copy.wait()
     if last:
         unmixing, sources, sems = held
         unmixing[...] = weights
         copies = [pltpu.make_async_copy(unmixing, outs[0], sems.at[chunks])]
         copies[0].start()
-        width = white.shape[2]
+        width = white_ref.shape[2]
         for k in range(chunks):
-            sources[k] = nn(weights.astype(BF), white[k]).astype(BF)
+            sources[k] = nn(weights.astype(BF), white_ref[k]).astype(BF)
             spot = 2 * other(ax, k & 2) + other(low, k & 1)
             spot = pl.ds(pl.multiple_of(spot * width, width), width)
             copies.append(
@@ -253,7 +262,7 @@
         for copy in copies:
             copy.wait()
     else:
-        total, slope = step(weights, [white[k] for k in range(chunks)])
+        total, slope = step(weights, [white_ref[k] for k in range(chunks)])
         outs[0][...] = (total - slope * weights) * scale
 
 
@@ -303,27 +312,38 @@
     at_xy = flip(reduced, across | near)
     packed, at_x, at_y = sum_over(own, far, BF, (at_x, at_y))
     packed, at_xy = spread(packed, across, near, (at_xy,))
-    whiten = run(
-        functools.partial(whiten_kernel, voxels),
-        shape((rows, rows), BF),
-        packed,
-        scratch=[pltpu.VMEM((2, 5 * block, block), F32), pltpu.VMEM((rows, rows), F32)],
-    )
-
     count = initial.shape[0] // 2
     weights = lax.dynamic_slice_in_dim(initial, near_y * count, count, 0)
+    whiten, mixed = run(
+        functools.partial(whiten_kernel, voxels),
+        (shape((rows, rows), BF), shape((count, rows), BF)),
+        (*packed, weights),
+        scratch=[pltpu.VMEM((2, 5 * block, block), F32), pltpu.VMEM((rows, rows), F32)],
+    )
+
     scale = 8192.0 / voxels
     blocks = (reduced, there, at_x, flip(at_x, low))
     blocks += (at_y, flip(at_y, low), at_xy, flip(at_xy, low))
-    white, newer = run(
+    newer = run(
         functools.partial(apply_kernel, scale),
-        (shape((len(blocks), rows, size), BF), shape((count, rows), F32)),
-        (whiten, *blocks, weights),
-    )
+        shape((count, rows), F32),
+        (mixed, whiten, weights, *blocks),
+    )
+    newer, whiten = lax.optimization_barrier((newer, whiten))
 
     for turn in range(ICA_ITERS):
         last = turn == ICA_ITERS - 1
-        stacked = spread(*sum_over(newer, far, HALF), across, near)
+        if not turn:
+            white = run(
+                white_kernel,
+                shape((len(blocks), rows, size), BF),
+                (whiten, *blocks),
+                cost=2 * len(blocks) * rows * rows * size,
+            )
+        (summed, *held) = sum_over(newer, far, HALF, () if turn else (white,))
+        if held:
+            (white,) = held
+        stacked = spread(summed, across, near)
         stacked = [part.astype(F32) * (1.0 / scale) for part in stacked]
         chunks = len(blocks) // 2 if last else len(blocks)
         outs = (
@@ -334,8 +354,6 @@
         scratch = [
             pltpu.VMEM((rows, rows), F32),
             pltpu.VMEM((rows, rows), BF),
-            pltpu.VMEM((chunks, rows, size), BF),
-            pltpu.SemaphoreType.DMA,
         ]
         if last:
             scratch += [
@@ -347,7 +365,6 @@
             functools.partial(decor_kernel, last, scale),
             outs,
             (*stacked, white),
-            specs=[VMEM] * 8 + [HBM],
             out_spec=HBM if last else VMEM,
             scratch=scratch,
         )

time: 86.4 us -> 85.3 us (0.987)
  waiting for transfers between devices: 34.3 us -> 33 us
    ppermute x41, waiting for transfers between devices: 34.3 us -> 33 us  [flip(): return lax.ppermute(x, AXES, [(i, i ^ mask) for i in range(count)])]
    pallas_call x7 -> x8, Pallas kernels: 12.3 us -> 12.5 us  [run(): pl.pallas_call(kernel, out_shape=outs, in_specs=specs or [VMEM] * len(arg...]
  transfers between devices with their start and end apart: 41 -> 41, of which waited for: 26 -> 26; matrix products, arithmetic and copies ran while one was open for 2% -> 2% of each run, Pallas kernels for 3% -> 5%
where the time goes in v9:
time: 85.3 us; the launch traced here: 85.1 us
  starting transfers between devices  36.8 us (43%)
  waiting for transfers between devices  33 us (39%)
  Pallas kernels  12.5 us (15%)
  local copies, waits for them, and re-layouts  1.3 us (2%)
  between operations  0.97 us (1%)
    ppermute x41, starting transfers between devices, flip(): return lax.ppermute(x, AXES, [(i, i ^ mask) for i in range(count)])  36.8 us
    ppermute x41, waiting for transfers between devices, flip(): return lax.ppermute(x, AXES, [(i, i ^ mask) for i in range(count)])  33 us
    pallas_call x8, Pallas kernels, run(): pl.pallas_call(kernel, out_shape=outs, in_specs=specs or [VMEM] * len(arg...  12.5 us
  transfers between devices with their start and end apart: 41, of which 26 were waited for; matrix products, arithmetic and copies ran while one was open for 2% of the time, Pallas kernels for 5%

profile of v9, /device:TPU:0, one launch (start us, length us, event | category | flops | bytes accessed | tf_op | source)
XLA Modules:
  0.0 85.1 jit_solution(14595027050297628772)
XLA Ops:
  0.7 0.5 collective-permute-start
  1.2 1.3 %constant_dynamic-slice_fusion.1 = (bf16[512,256]{1,0:T(8,128)(2,1)S(1)}, bf16[512,256]{1,0:T(8,128)(2,1)S(1)}, bf16[512,256]{1,0:T(8,128)(2,1)S(1)}, bf16[512,256]{1,0:T(8,128)(2,1)S(1)}) fusion(bf16[512,1024]{1,0:T(8,128)(2,1)} %param.3, s32[]{:T(128)S(6)} %select_n.18, s32[]{:T(128)S(6)} %select_n.16, s32[]{:T(128)S(6)} %select_n.15, s32[]{:T(128)S(6)} %select_n.17), kind=kLoop, calls=%fused_computation.13 | loop fusion | bytes 2097168 | tf_op jit(solution)/shard_map/dynamic_slice | solution.py:282
  2.4 0.2 collective-permute-start.2
  2.6 1.4 %collective-permute-done.2.mate_right_ref = bf16[512,256]{1,0:T(8,128)(2,1)S(1)} collective-permute-done((bf16[512,256]{1,0:T(8,128)(2,1)S(1)}, bf16[512,256]{1,0:T(8,128)(2,1)S(1)}, u32[]{:S(2)}, u32[]{:S(2)}) %collective-permute-start.2) | collective-permute-done | bytes 262176 | tf_op jit(solution)/shard_map/ppermute | solution.py:44
  4.1 0.5 shard_map.51
  4.6 2.7 %collective-permute-start.3 = (f16[528,256]{1,0:T(8,128)(2,1)S(1)}, f16[528,256]{1,0:T(8,128)(2,1)S(1)}, u32[]{:S(2)}, u32[]{:S(2)}) collective-permute-start(f16[528,256]{1,0:T(8,128)(2,1)S(1)} %convert_element_type.111), channel_id=1, source_target_pairs={{0,2},{1,3},{2,0},{3,1},{4,6},{5,7},{6,4},{7,5},{8,10},{9,11},{10,... | collective-permute-start | bytes 811016 | tf_op jit(solution)/shard_map/ppermute | solution.py:44
  7.4 1.5 %collective-permute-done.1.mate_right_ref = bf16[512,256]{1,0:T(8,128)(2,1)S(1)} collective-permute-done((bf16[512,256]{1,0:T(8,128)(2,1)S(1)}, bf16[512,256]{1,0:T(8,128)(2,1)S(1)}, u32[]{:S(2)}, u32[]{:S(2)}) %collective-permute-start.1) | collective-permute-done | bytes 262176 | tf_op jit(solution)/shard_map/ppermute | solution.py:44
  8.8 0.4 shard_map.50
  9.3 5.0 %collective-permute-done.3 = f16[528,256]{1,0:T(8,128)(2,1)S(1)} collective-permute-done((f16[528,256]{1,0:T(8,128)(2,1)S(1)}, f16[528,256]{1,0:T(8,128)(2,1)S(1)}, u32[]{:S(2)}, u32[]{:S(2)}) %collective-permute-start.3) | collective-permute-done | bytes 270368 | tf_op jit(solution)/shard_map/ppermute | solution.py:44
  14.5 1.5 %collective-permute-done.4.there_ref.refs_1_ = bf16[512,256]{1,0:T(8,128)(2,1)S(1)} collective-permute-done((bf16[512,256]{1,0:T(8,128)(2,1)S(1)}, bf16[512,256]{1,0:T(8,128)(2,1)S(1)}, u32[]{:S(2)}, u32[]{:S(2)}) %collective-permute-start.4) | collective-permute-done | bytes 262176 | tf_op jit(solution)/shard_map/ppermute | solution.py:44
  16.1 0.4 shard_map.52
  16.4 2.8 %collective-permute-start.5 = (bf16[160,128]{1,0:T(8,128)(2,1)S(1)}, bf16[160,128]{1,0:T(8,128)(2,1)S(1)}, u32[]{:S(2)}, u32[]{:S(2)}) collective-permute-start(bf16[160,128]{1,0:T(8,128)(2,1)S(1)} %get-tuple-element.23), channel_id=1, source_target_pairs={{0,6},{1,7},{2,4},{3,5},{4,2},{5,3},{6,0},{7,1},{8,14},{9,15},{10,... | collective-permute-start | bytes 122888 | tf_op jit(solution)/shard_map/ppermute | solution.py:44
  19.2 0.5 collective-permute-start.6
  19.7 0.3 collective-permute-start.7
  20.0 1.8 %collective-permute-start.12 = (bf16[512,256]{1,0:T(8,128)(2,1)S(1)}, bf16[512,256]{1,0:T(8,128)(2,1)S(1)}, u32[]{:S(2)}, u32[]{:S(2)}) collective-permute-start(bf16[512,256]{1,0:T(8,128)(2,1)S(1)} %fusion.1.here_ref.refs_0_), channel_id=1, source_target_pairs={{0,4},{1,5},{2,6},{3,7},{4,0},{5,1},{6,2},{7,3},{8,12},{9,13},{10,... | collective-permute-start | bytes 786440 | tf_op jit(solution)/shard_map/ppermute | solution.py:44
  21.7 1.5 %collective-permute-start.11 = (bf16[512,256]{1,0:T(8,128)(2,1)S(1)}, bf16[512,256]{1,0:T(8,128)(2,1)S(1)}, u32[]{:S(2)}, u32[]{:S(2)}) collective-permute-start(bf16[512,256]{1,0:T(8,128)(2,1)S(1)} %fusion.1.here_ref.refs_0_), channel_id=1, source_target_pairs={{0,2},{1,3},{2,0},{3,1},{4,6},{5,7},{6,4},{7,5},{8,10},{9,11},{10,... | collective-permute-start | bytes 786440 | tf_op jit(solution)/shard_map/ppermute | solution.py:44
  23.2 1.0 %collective-permute-done.7 = bf16[160,128]{1,0:T(8,128)(2,1)S(1)} collective-permute-done((bf16[160,128]{1,0:T(8,128)(2,1)S(1)}, bf16[160,128]{1,0:T(8,128)(2,1)S(1)}, u32[]{:S(2)}, u32[]{:S(2)}) %collective-permute-start.7) | collective-permute-done | bytes 40992 | tf_op jit(solution)/shard_map/ppermute | solution.py:44
  24.2 3.7 %collective-permute-start.10 = (bf16[160,128]{1,0:T(8,128)(2,1)S(1)}, bf16[160,128]{1,0:T(8,128)(2,1)S(1)}, u32[]{:S(2)}, u32[]{:S(2)}) collective-permute-start(bf16[160,128]{1,0:T(8,128)(2,1)S(1)} %convert_element_type.117), channel_id=1, source_target_pairs={{0,24},{1,25},{2,26},{3,27},{4,28},{5,29},{6,30},{7,31},{8,16},{9,... | collective-permute-start | bytes 122888 | tf_op jit(solution)/shard_map/ppermute | solution.py:44
  27.9 0.8 collective-permute-start.8
  28.7 1.5 %collective-permute-done.10 = bf16[160,128]{1,0:T(8,128)(2,1)S(1)} collective-permute-done((bf16[160,128]{1,0:T(8,128)(2,1)S(1)}, bf16[160,128]{1,0:T(8,128)(2,1)S(1)}, u32[]{:S(2)}, u32[]{:S(2)}) %collective-permute-start.10) | collective-permute-done | bytes 40992 | tf_op jit(solution)/shard_map/ppermute | solution.py:44
  30.2 1.3 %collective-permute-start.16 = (bf16[512,256]{1,0:T(8,128)(2,1)S(1)}, bf16[512,256]{1,0:T(8,128)(2,1)S(1)}, u32[]{:S(2)}, u32[]{:S(2)}) collective-permute-start(bf16[512,256]{1,0:T(8,128)(2,1)S(1)} %fusion.1.here_ref.refs_0_), channel_id=1, source_target_pairs={{0,6},{1,7},{2,4},{3,5},{4,2},{5,3},{6,0},{7,1},{8,14},{9,15},{10,... | collective-permute-start | bytes 786440 | tf_op jit(solution)/shard_map/ppermute | solution.py:44
  31.5 1.3 %collective-permute-done.9 = bf16[160,128]{1,0:T(8,128)(2,1)S(1)} collective-permute-done((bf16[160,128]{1,0:T(8,128)(2,1)S(1)}, bf16[160,128]{1,0:T(8,128)(2,1)S(1)}, u32[]{:S(2)}, u32[]{:S(2)}) %collective-permute-start.9) | collective-permute-done | bytes 40992 | tf_op jit(solution)/shard_map/ppermute | solution.py:44
  32.9 1.4 %collective-permute-start.15 = (bf16[160,128]{1,0:T(8,128)(2,1)S(1)}, bf16[160,128]{1,0:T(8,128)(2,1)S(1)}, u32[]{:S(2)}, u32[]{:S(2)}) collective-permute-start(bf16[160,128]{1,0:T(8,128)(2,1)S(1)} %add_convert_fusion.2.refs_0_), channel_id=1, source_target_pairs={{0,6},{1,7},{2,4},{3,5},{4,2},{5,3},{6,0},{7,1},{8,14},{9,15},{10,... | collective-permute-start | bytes 122888 | tf_op jit(solution)/shard_map/ppermute | solution.py:44
  34.3 0.5 collective-permute-start.14
  34.8 1.6 %collective-permute-start.13 = (bf16[160,128]{1,0:T(8,128)(2,1)S(1)}, bf16[160,128]{1,0:T(8,128)(2,1)S(1)}, u32[]{:S(2)}, u32[]{:S(2)}) collective-permute-start(bf16[160,128]{1,0:T(8,128)(2,1)S(1)} %add_convert_fusion.2.refs_0_), channel_id=1, source_target_pairs={{0,4},{1,5},{2,6},{3,7},{4,0},{5,1},{6,2},{7,3},{8,12},{9,13},{10,... | collective-permute-start | bytes 122888 | tf_op jit(solution)/shard_map/ppermute | solution.py:44
  36.4 1.5 %collective-permute-done.16.refs_6_ = bf16[512,256]{1,0:T(8,128)(2,1)S(1)} collective-permute-done((bf16[512,256]{1,0:T(8,128)(2,1)S(1)}, bf16[512,256]{1,0:T(8,128)(2,1)S(1)}, u32[]{:S(2)}, u32[]{:S(2)}) %collective-permute-start.16) | collective-permute-done | bytes 262176 | tf_op jit(solution)/shard_map/ppermute | solution.py:44
  37.9 0.4 collective-permute-done.15.refs_3_
  38.3 0.5 collective-permute-done.13.refs_1_
  39.0 0.5 collective-permute-start.18
  39.4 0.1 collective-permute-start.19
  39.5 0.4 collective-permute-start.20
  40.0 0.4 collective-permute-done.17
  40.3 2.3 %shard_map.53 = (bf16[512,512]{1,0:T(8,128)(2,1)S(1)}, bf16[64,512]{1,0:T(8,128)(2,1)S(1)}) custom-call(bf16[160,128]{1,0:T(8,128)(2,1)S(1)} %add_convert_fusion.2.refs_0_, bf16[160,128]{1,0:T(8,128)(2,1)S(1)} %collective-permute-done.13.refs_1_, bf16[160,128]{1,0:T(8,128)(2,1)S(1)} %collective-permute-done.14.refs_2_, ...), custom_call_target="tpu_custom_call" | custom-call | tf_op jit(solution)/shard_map/pallas_call | solution.py:74
  42.7 1.3 %shard_map.54 = f32[64,512]{1,0:T(8,128)S(1)} custom-call(bf16[64,512]{1,0:T(8,128)(2,1)S(1)} %get-tuple-element.31.mixed_ref, bf16[512,512]{1,0:T(8,128)(2,1)S(1)} %get-tuple-element.37.whiten_ref, f32[64,512]{1,0:T(8,128)S(1)} %constant_dynamic-slice_fusion.refs_8_.weights_ref, bf16[512,256]{1,0:T(8,128)(2,1)S(1)} %fusion.1.here_ref.refs_0_, ...), custom_call_target="tpu_custom_call" | custom-call | tf_op jit(solution)/shard_map/pallas_call | solution.py:74
  44.0 3.5 %collective-permute-start.23 = (f16[64,512]{1,0:T(8,128)(2,1)S(1)}, f16[64,512]{1,0:T(8,128)(2,1)S(1)}, u32[]{:S(2)}, u32[]{:S(2)}) collective-permute-start(f16[64,512]{1,0:T(8,128)(2,1)S(1)} %convert_element_type.122), channel_id=1, source_target_pairs={{0,24},{1,25},{2,26},{3,27},{4,28},{5,29},{6,30},{7,31},{8,16},{9,... | collective-permute-start | bytes 196616 | tf_op jit(solution)/shard_map/ppermute | solution.py:44
  47.5 1.0 %collective-permute-start.21 = (f16[64,512]{1,0:T(8,128)(2,1)S(1)}, f16[64,512]{1,0:T(8,128)(2,1)S(1)}, u32[]{:S(2)}, u32[]{:S(2)}) collective-permute-start(f16[64,512]{1,0:T(8,128)(2,1)S(1)} %convert_element_type.122), channel_id=1, source_target_pairs={{0,8},{1,9},{2,10},{3,11},{4,12},{5,13},{6,14},{7,15},{8,0},{9,1},... | collective-permute-start | bytes 196616 | tf_op jit(solution)/shard_map/ppermute | solution.py:44
  48.5 1.3 %shard_map.55.refs_8_ = bf16[8,512,256]{2,1,0:T(8,128)(2,1)S(1)} custom-call(bf16[512,512]{1,0:T(8,128)(2,1)S(1)} %get-tuple-element.37.whiten_ref, bf16[512,256]{1,0:T(8,128)(2,1)S(1)} %fusion.1.here_ref.refs_0_, bf16[512,256]{1,0:T(8,128)(2,1)S(1)} %collective-permute-done.4.there_ref.refs_1_, bf16[512,256]{1,0:T(8,128)(2,1)S(1)} %collective-permute-done.11.refs_2_, ...), custom_call_target="tpu_custom_call" | custom-call | flops 1073741824 | bytes 4194304 | tf_op jit(solution)/shard_map/pallas_call | solution.py:74
  49.7 1.1 %collective-permute-done.23 = f16[64,512]{1,0:T(8,128)(2,1)S(1)} collective-permute-done((f16[64,512]{1,0:T(8,128)(2,1)S(1)}, f16[64,512]{1,0:T(8,128)(2,1)S(1)}, u32[]{:S(2)}, u32[]{:S(2)}) %collective-permute-start.23) | collective-permute-done | bytes 65568 | tf_op jit(solution)/shard_map/ppermute | solution.py:44
  50.8 2.2 %collective-permute-done.22 = f16[64,512]{1,0:T(8,128)(2,1)S(1)} collective-permute-done((f16[64,512]{1,0:T(8,128)(2,1)S(1)}, f16[64,512]{1,0:T(8,128)(2,1)S(1)}, u32[]{:S(2)}, u32[]{:S(2)}) %collective-permute-start.22) | collective-permute-done | bytes 65568 | tf_op jit(solution)/shard_map/ppermute | solution.py:44
  53.1 0.1 collective-permute-done.21
  53.2 0.1 fusion.4
  53.3 2.3 %collective-permute-start.26 = (f16[64,512]{1,0:T(8,128)(2,1)S(1)}, f16[64,512]{1,0:T(8,128)(2,1)S(1)}, u32[]{:S(2)}, u32[]{:S(2)}) collective-permute-start(f16[64,512]{1,0:T(8,128)(2,1)S(1)} %get-tuple-element.43), channel_id=1, source_target_pairs={{0,6},{1,7},{2,4},{3,5},{4,2},{5,3},{6,0},{7,1},{8,14},{9,15},{10,... | collective-permute-start | bytes 196616 | tf_op jit(solution)/shard_map/ppermute | solution.py:44
  55.6 0.5 collective-permute-start.25
  56.1 0.7 collective-permute-start.24
  56.8 2.4 %collective-permute-done.26 = f16[64,512]{1,0:T(8,128)(2,1)S(1)} collective-permute-done((f16[64,512]{1,0:T(8,128)(2,1)S(1)}, f16[64,512]{1,0:T(8,128)(2,1)S(1)}, u32[]{:S(2)}, u32[]{:S(2)}) %collective-permute-start.26) | collective-permute-done | bytes 65568 | tf_op jit(solution)/shard_map/ppermute | solution.py:44
  59.2 0.7 collective-permute-done.25
  59.9 0.5 collective-permute-done.24
  60.5 0.6 collective-permute-done.29
  61.1 0.5 collective-permute-done.28
  61.7 3.2 %shard_map.56 = f32[64,512]{1,0:T(8,128)S(1)} custom-call(f32[64,512]{1,0:T(8,128)S(1)} %get-tuple-element.42.refs_0_, f32[64,512]{1,0:T(8,128)S(1)} %convert_element_type.128.refs_1_, f32[64,512]{1,0:T(8,128)S(1)} %convert_element_type.129.refs_2_, f32[64,512]{1,0:T(8,128)S(1)} %convert_element_type.130.refs_3_, ...), custom_call_target="tpu_custom_call" | custom-call | tf_op jit(solution)/shard_map/pallas_call | solution.py:74
  64.9 2.6 %collective-permute-start.33 = (f16[64,512]{1,0:T(8,128)(2,1)S(1)}, f16[64,512]{1,0:T(8,128)(2,1)S(1)}, u32[]{:S(2)}, u32[]{:S(2)}) collective-permute-start(f16[64,512]{1,0:T(8,128)(2,1)S(1)} %convert_element_type.135), channel_id=1, source_target_pairs={{0,24},{1,25},{2,26},{3,27},{4,28},{5,29},{6,30},{7,31},{8,16},{9,... | collective-permute-start | bytes 196616 | tf_op jit(solution)/shard_map/ppermute | solution.py:44
  67.5 1.9 %collective-permute-start.31 = (f16[64,512]{1,0:T(8,128)(2,1)S(1)}, f16[64,512]{1,0:T(8,128)(2,1)S(1)}, u32[]{:S(2)}, u32[]{:S(2)}) collective-permute-start(f16[64,512]{1,0:T(8,128)(2,1)S(1)} %convert_element_type.135), channel_id=1, source_target_pairs={{0,8},{1,9},{2,10},{3,11},{4,12},{5,13},{6,14},{7,15},{8,0},{9,1},... | collective-permute-start | bytes 196616 | tf_op jit(solution)/shard_map/ppermute | solution.py:44
  69.4 2.4 %collective-permute-done.33 = f16[64,512]{1,0:T(8,128)(2,1)S(1)} collective-permute-done((f16[64,512]{1,0:T(8,128)(2,1)S(1)}, f16[64,512]{1,0:T(8,128)(2,1)S(1)}, u32[]{:S(2)}, u32[]{:S(2)}) %collective-permute-start.33) | collective-permute-done | bytes 65568 | tf_op jit(solution)/shard_map/ppermute | solution.py:44
  71.7 2.0 %collective-permute-done.32 = f16[64,512]{1,0:T(8,128)(2,1)S(1)} collective-permute-done((f16[64,512]{1,0:T(8,128)(2,1)S(1)}, f16[64,512]{1,0:T(8,128)(2,1)S(1)}, u32[]{:S(2)}, u32[]{:S(2)}) %collective-permute-start.32) | collective-permute-done | bytes 65568 | tf_op jit(solution)/shard_map/ppermute | solution.py:44
  73.7 0.1 fusion.3
  73.9 1.7 %collective-permute-start.36 = (f16[64,512]{1,0:T(8,128)(2,1)S(1)}, f16[64,512]{1,0:T(8,128)(2,1)S(1)}, u32[]{:S(2)}, u32[]{:S(2)}) collective-permute-start(f16[64,512]{1,0:T(8,128)(2,1)S(1)} %get-tuple-element.41), channel_id=1, source_target_pairs={{0,6},{1,7},{2,4},{3,5},{4,2},{5,3},{6,0},{7,1},{8,14},{9,15},{10,... | collective-permute-start | bytes 196616 | tf_op jit(solution)/shard_map/ppermute | solution.py:44
  75.6 0.9 %collective-permute-start.35 = (f16[64,512]{1,0:T(8,128)(2,1)S(1)}, f16[64,512]{1,0:T(8,128)(2,1)S(1)}, u32[]{:S(2)}, u32[]{:S(2)}) collective-permute-start(f16[64,512]{1,0:T(8,128)(2,1)S(1)} %get-tuple-element.41), channel_id=1, source_target_pairs={{0,2},{1,3},{2,0},{3,1},{4,6},{5,7},{6,4},{7,5},{8,10},{9,11},{10,... | collective-permute-start | bytes 196616 | tf_op jit(solution)/shard_map/ppermute | solution.py:44
  76.5 0.9 %collective-permute-start.34 = (f16[64,512]{1,0:T(8,128)(2,1)S(1)}, f16[64,512]{1,0:T(8,128)(2,1)S(1)}, u32[]{:S(2)}, u32[]{:S(2)}) collective-permute-start(f16[64,512]{1,0:T(8,128)(2,1)S(1)} %get-tuple-element.41), channel_id=1, source_target_pairs={{0,4},{1,5},{2,6},{3,7},{4,0},{5,1},{6,2},{7,3},{8,12},{9,13},{10,... | collective-permute-start | bytes 196616 | tf_op jit(solution)/shard_map/ppermute | solution.py:44
  77.4 2.1 %collective-permute-done.36 = f16[64,512]{1,0:T(8,128)(2,1)S(1)} collective-permute-done((f16[64,512]{1,0:T(8,128)(2,1)S(1)}, f16[64,512]{1,0:T(8,128)(2,1)S(1)}, u32[]{:S(2)}, u32[]{:S(2)}) %collective-permute-start.36) | collective-permute-done | bytes 65568 | tf_op jit(solution)/shard_map/ppermute | solution.py:44
  79.5 0.6 collective-permute-done.35
  80.1 0.6 collective-permute-done.34
  80.9 0.5 collective-permute-done.39
  81.4 0.6 collective-permute-done.38
  82.0 3.1 %shard_map.57 = (f32[128,512]{1,0:T(8,128)}, bf16[128,1024]{1,0:T(8,128)(2,1)}) custom-call(f32[64,512]{1,0:T(8,128)S(1)} %get-tuple-element.40.refs_0_, f32[64,512]{1,0:T(8,128)S(1)} %convert_element_type.141.refs_1_, f32[64,512]{1,0:T(8,128)S(1)} %convert_element_type.142.refs_2_, f32[64,512]{1,0:T(8,128)S(1)} %convert_element_type.143.refs_3_, ...), custom_call_target="tpu_custom_call" | custom-call | tf_op jit(solution)/shard_map/pallas_call | solution.py:74
  (59 shorter events, 0.7 us)
Async XLA Ops:
  0.6 39.3 %copy-start = (f32[128,512]{1,0:T(8,128)S(1)}, f32[128,512]{1,0:T(8,128)}, u32[]{:S(2)}) copy-start(f32[128,512]{1,0:T(8,128)} %param.5) | copy-start | bytes 786436
  0.6 3.4 %copy-start.1 = (bf16[512,512]{1,0:T(8,128)(2,1)S(1)}, bf16[512,512]{1,0:T(8,128)(2,1)}, u32[]{:S(2)}) copy-start(bf16[512,512]{1,0:T(8,128)(2,1)} %left_ref.3) | copy-start | bytes 1572868
  0.7 3.4 %collective-permute-start = (bf16[512,512]{1,0:T(8,128)(2,1)}, bf16[512,512]{1,0:T(8,128)(2,1)S(1)}, u32[]{:S(2)}, u32[]{:S(2)}) collective-permute-start(bf16[512,512]{1,0:T(8,128)(2,1)} %left_ref.3), channel_id=1, source_target_pairs={{0,1},{1,0},{2,3},{3,2},{4,5},{5,4},{6,7},{7,6},{8,9},{9,8},{10,11... | collective-permute-start | bytes 1572872 | tf_op jit(solution)/shard_map/ppermute | solution.py:44
  2.4 1.6 %collective-permute-start.2 = (bf16[512,256]{1,0:T(8,128)(2,1)S(1)}, bf16[512,256]{1,0:T(8,128)(2,1)S(1)}, u32[]{:S(2)}, u32[]{:S(2)}) collective-permute-start(bf16[512,256]{1,0:T(8,128)(2,1)S(1)} %get-tuple-element.44), channel_id=1, source_target_pairs={{0,1},{1,0},{2,3},{3,2},{4,5},{5,4},{6,7},{7,6},{8,9},{9,8},{10,11... | collective-permute-start | bytes 786440 | tf_op jit(solution)/shard_map/ppermute | solution.py:44
  4.6 9.7 %collective-permute-start.3 = (f16[528,256]{1,0:T(8,128)(2,1)S(1)}, f16[528,256]{1,0:T(8,128)(2,1)S(1)}, u32[]{:S(2)}, u32[]{:S(2)}) collective-permute-start(f16[528,256]{1,0:T(8,128)(2,1)S(1)} %convert_element_type.111), channel_id=1, source_target_pairs={{0,2},{1,3},{2,0},{3,1},{4,6},{5,7},{6,4},{7,5},{8,10},{9,11},{10,... | collective-permute-start | bytes 811016 | tf_op jit(solution)/shard_map/ppermute | solution.py:44
  7.3 1.5 %collective-permute-start.1 = (bf16[512,256]{1,0:T(8,128)(2,1)S(1)}, bf16[512,256]{1,0:T(8,128)(2,1)S(1)}, u32[]{:S(2)}, u32[]{:S(2)}) collective-permute-start(bf16[512,256]{1,0:T(8,128)(2,1)S(1)} %get-tuple-element.45), channel_id=1, source_target_pairs={{0,1},{1,0},{2,3},{3,2},{4,5},{5,4},{6,7},{7,6},{8,9},{9,8},{10,11... | collective-permute-start | bytes 786440 | tf_op jit(solution)/shard_map/ppermute | solution.py:44
  14.5 1.6 %collective-permute-start.4 = (bf16[512,256]{1,0:T(8,128)(2,1)S(1)}, bf16[512,256]{1,0:T(8,128)(2,1)S(1)}, u32[]{:S(2)}, u32[]{:S(2)}) collective-permute-start(bf16[512,256]{1,0:T(8,128)(2,1)S(1)} %fusion.1.here_ref.refs_0_), channel_id=1, source_target_pairs={{0,1},{1,0},{2,3},{3,2},{4,5},{5,4},{6,7},{7,6},{8,9},{9,8},{10,11... | collective-permute-start | bytes 786440 | tf_op jit(solution)/shard_map/ppermute | solution.py:44
  16.4 6.8 %collective-permute-start.5 = (bf16[160,128]{1,0:T(8,128)(2,1)S(1)}, bf16[160,128]{1,0:T(8,128)(2,1)S(1)}, u32[]{:S(2)}, u32[]{:S(2)}) collective-permute-start(bf16[160,128]{1,0:T(8,128)(2,1)S(1)} %get-tuple-element.23), channel_id=1, source_target_pairs={{0,6},{1,7},{2,4},{3,5},{4,2},{5,3},{6,0},{7,1},{8,14},{9,15},{10,... | collective-permute-start | bytes 122888 | tf_op jit(solution)/shard_map/ppermute | solution.py:44
  19.2 4.1 %collective-permute-start.6 = (bf16[160,128]{1,0:T(8,128)(2,1)S(1)}, bf16[160,128]{1,0:T(8,128)(2,1)S(1)}, u32[]{:S(2)}, u32[]{:S(2)}) collective-permute-start(bf16[160,128]{1,0:T(8,128)(2,1)S(1)} %get-tuple-element.24), channel_id=1, source_target_pairs={{0,2},{1,3},{2,0},{3,1},{4,6},{5,7},{6,4},{7,5},{8,10},{9,11},{10,... | collective-permute-start | bytes 122888 | tf_op jit(solution)/shard_map/ppermute | solution.py:44
  19.7 4.5 %collective-permute-start.7 = (bf16[160,128]{1,0:T(8,128)(2,1)S(1)}, bf16[160,128]{1,0:T(8,128)(2,1)S(1)}, u32[]{:S(2)}, u32[]{:S(2)}) collective-permute-start(bf16[160,128]{1,0:T(8,128)(2,1)S(1)} %get-tuple-element.25), channel_id=1, source_target_pairs={{0,4},{1,5},{2,6},{3,7},{4,0},{5,1},{6,2},{7,3},{8,12},{9,13},{10,... | collective-permute-start | bytes 122888 | tf_op jit(solution)/shard_map/ppermute | solution.py:44
  20.0 11.5 %collective-permute-start.12 = (bf16[512,256]{1,0:T(8,128)(2,1)S(1)}, bf16[512,256]{1,0:T(8,128)(2,1)S(1)}, u32[]{:S(2)}, u32[]{:S(2)}) collective-permute-start(bf16[512,256]{1,0:T(8,128)(2,1)S(1)} %fusion.1.here_ref.refs_0_), channel_id=1, source_target_pairs={{0,4},{1,5},{2,6},{3,7},{4,0},{5,1},{6,2},{7,3},{8,12},{9,13},{10,... | collective-permute-start | bytes 786440 | tf_op jit(solution)/shard_map/ppermute | solution.py:44
  21.7 9.8 %collective-permute-start.11 = (bf16[512,256]{1,0:T(8,128)(2,1)S(1)}, bf16[512,256]{1,0:T(8,128)(2,1)S(1)}, u32[]{:S(2)}, u32[]{:S(2)}) collective-permute-start(bf16[512,256]{1,0:T(8,128)(2,1)S(1)} %fusion.1.here_ref.refs_0_), channel_id=1, source_target_pairs={{0,2},{1,3},{2,0},{3,1},{4,6},{5,7},{6,4},{7,5},{8,10},{9,11},{10,... | collective-permute-start | bytes 786440 | tf_op jit(solution)/shard_map/ppermute | solution.py:44
  24.2 5.9 %collective-permute-start.10 = (bf16[160,128]{1,0:T(8,128)(2,1)S(1)}, bf16[160,128]{1,0:T(8,128)(2,1)S(1)}, u32[]{:S(2)}, u32[]{:S(2)}) collective-permute-start(bf16[160,128]{1,0:T(8,128)(2,1)S(1)} %convert_element_type.117), channel_id=1, source_target_pairs={{0,24},{1,25},{2,26},{3,27},{4,28},{5,29},{6,30},{7,31},{8,16},{9,... | collective-permute-start | bytes 122888 | tf_op jit(solution)/shard_map/ppermute | solution.py:44
  27.9 4.9 %collective-permute-start.9 = (bf16[160,128]{1,0:T(8,128)(2,1)S(1)}, bf16[160,128]{1,0:T(8,128)(2,1)S(1)}, u32[]{:S(2)}, u32[]{:S(2)}) collective-permute-start(bf16[160,128]{1,0:T(8,128)(2,1)S(1)} %convert_element_type.117), channel_id=1, source_target_pairs={{0,16},{1,17},{2,18},{3,19},{4,20},{5,21},{6,22},{7,23},{8,24},{9,... | collective-permute-start | bytes 122888 | tf_op jit(solution)/shard_map/ppermute | solution.py:44
  27.9 4.9 %collective-permute-start.8 = (bf16[160,128]{1,0:T(8,128)(2,1)S(1)}, bf16[160,128]{1,0:T(8,128)(2,1)S(1)}, u32[]{:S(2)}, u32[]{:S(2)}) collective-permute-start(bf16[160,128]{1,0:T(8,128)(2,1)S(1)} %convert_element_type.117), channel_id=1, source_target_pairs={{0,8},{1,9},{2,10},{3,11},{4,12},{5,13},{6,14},{7,15},{8,0},{9,1},... | collective-permute-start | bytes 122888 | tf_op jit(solution)/shard_map/ppermute | solution.py:44
  30.2 7.7 %collective-permute-start.16 = (bf16[512,256]{1,0:T(8,128)(2,1)S(1)}, bf16[512,256]{1,0:T(8,128)(2,1)S(1)}, u32[]{:S(2)}, u32[]{:S(2)}) collective-permute-start(bf16[512,256]{1,0:T(8,128)(2,1)S(1)} %fusion.1.here_ref.refs_0_), channel_id=1, source_target_pairs={{0,6},{1,7},{2,4},{3,5},{4,2},{5,3},{6,0},{7,1},{8,14},{9,15},{10,... | collective-permute-start | bytes 786440 | tf_op jit(solution)/shard_map/ppermute | solution.py:44
  32.9 5.5 %collective-permute-start.15 = (bf16[160,128]{1,0:T(8,128)(2,1)S(1)}, bf16[160,128]{1,0:T(8,128)(2,1)S(1)}, u32[]{:S(2)}, u32[]{:S(2)}) collective-permute-start(bf16[160,128]{1,0:T(8,128)(2,1)S(1)} %add_convert_fusion.2.refs_0_), channel_id=1, source_target_pairs={{0,6},{1,7},{2,4},{3,5},{4,2},{5,3},{6,0},{7,1},{8,14},{9,15},{10,... | collective-permute-start | bytes 122888 | tf_op jit(solution)/shard_map/ppermute | solution.py:44
  34.3 4.0 %collective-permute-start.14 = (bf16[160,128]{1,0:T(8,128)(2,1)S(1)}, bf16[160,128]{1,0:T(8,128)(2,1)S(1)}, u32[]{:S(2)}, u32[]{:S(2)}) collective-permute-start(bf16[160,128]{1,0:T(8,128)(2,1)S(1)} %add_convert_fusion.2.refs_0_), channel_id=1, source_target_pairs={{0,2},{1,3},{2,0},{3,1},{4,6},{5,7},{6,4},{7,5},{8,10},{9,11},{10,... | collective-permute-start | bytes 122888 | tf_op jit(solution)/shard_map/ppermute | solution.py:44
  34.8 4.0 %collective-permute-start.13 = (bf16[160,128]{1,0:T(8,128)(2,1)S(1)}, bf16[160,128]{1,0:T(8,128)(2,1)S(1)}, u32[]{:S(2)}, u32[]{:S(2)}) collective-permute-start(bf16[160,128]{1,0:T(8,128)(2,1)S(1)} %add_convert_fusion.2.refs_0_), channel_id=1, source_target_pairs={{0,4},{1,5},{2,6},{3,7},{4,0},{5,1},{6,2},{7,3},{8,12},{9,13},{10,... | collective-permute-start | bytes 122888 | tf_op jit(solution)/shard_map/ppermute | solution.py:44
  38.9 1.5 %collective-permute-start.17 = (bf16[4,160,128]{2,1,0:T(8,128)(2,1)S(1)}, bf16[4,160,128]{2,1,0:T(8,128)(2,1)S(1)}, u32[]{:S(2)}, u32[]{:S(2)}) collective-permute-start(bf16[4,160,128]{2,1,0:T(8,128)(2,1)S(1)} %pad_maximum_fusion), channel_id=1, source_target_pairs={{0,1},{1,0},{2,3},{3,2},{4,5},{5,4},{6,7},{7,6},{8,9},{9,8},{10,11... | collective-permute-start | bytes 491528 | tf_op jit(solution)/shard_map/ppermute | solution.py:44
  39.0 3.7 %collective-permute-start.18 = (bf16[512,256]{1,0:T(8,128)(2,1)S(1)}, bf16[512,256]{1,0:T(8,128)(2,1)S(1)}, u32[]{:S(2)}, u32[]{:S(2)}) collective-permute-start(bf16[512,256]{1,0:T(8,128)(2,1)S(1)} %collective-permute-done.11.refs_2_), channel_id=1, source_target_pairs={{0,1},{1,0},{2,3},{3,2},{4,5},{5,4},{6,7},{7,6},{8,9},{9,8},{10,11... | collective-permute-start | bytes 786440 | tf_op jit(solution)/shard_map/ppermute | solution.py:44
  39.4 3.2 %collective-permute-start.19 = (bf16[512,256]{1,0:T(8,128)(2,1)S(1)}, bf16[512,256]{1,0:T(8,128)(2,1)S(1)}, u32[]{:S(2)}, u32[]{:S(2)}) collective-permute-start(bf16[512,256]{1,0:T(8,128)(2,1)S(1)} %collective-permute-done.12.refs_4_), channel_id=1, source_target_pairs={{0,1},{1,0},{2,3},{3,2},{4,5},{5,4},{6,7},{7,6},{8,9},{9,8},{10,11... | collective-permute-start | bytes 786440 | tf_op jit(solution)/shard_map/ppermute | solution.py:44
  39.5 3.1 %collective-permute-start.20 = (bf16[512,256]{1,0:T(8,128)(2,1)S(1)}, bf16[512,256]{1,0:T(8,128)(2,1)S(1)}, u32[]{:S(2)}, u32[]{:S(2)}) collective-permute-start(bf16[512,256]{1,0:T(8,128)(2,1)S(1)} %collective-permute-done.16.refs_6_), channel_id=1, source_target_pairs={{0,1},{1,0},{2,3},{3,2},{4,5},{5,4},{6,7},{7,6},{8,9},{9,8},{10,11... | collective-permute-start | bytes 786440 | tf_op jit(solution)/shard_map/ppermute | solution.py:44
  44.0 6.8 %collective-permute-start.23 = (f16[64,512]{1,0:T(8,128)(2,1)S(1)}, f16[64,512]{1,0:T(8,128)(2,1)S(1)}, u32[]{:S(2)}, u32[]{:S(2)}) collective-permute-start(f16[64,512]{1,0:T(8,128)(2,1)S(1)} %convert_element_type.122), channel_id=1, source_target_pairs={{0,24},{1,25},{2,26},{3,27},{4,28},{5,29},{6,30},{7,31},{8,16},{9,... | collective-permute-start | bytes 196616 | tf_op jit(solution)/shard_map/ppermute | solution.py:44
  47.5 5.6 %collective-permute-start.22 = (f16[64,512]{1,0:T(8,128)(2,1)S(1)}, f16[64,512]{1,0:T(8,128)(2,1)S(1)}, u32[]{:S(2)}, u32[]{:S(2)}) collective-permute-start(f16[64,512]{1,0:T(8,128)(2,1)S(1)} %convert_element_type.122), channel_id=1, source_target_pairs={{0,16},{1,17},{2,18},{3,19},{4,20},{5,21},{6,22},{7,23},{8,24},{9,... | collective-permute-start | bytes 196616 | tf_op jit(solution)/shard_map/ppermute | solution.py:44
  47.5 5.7 %collective-permute-start.21 = (f16[64,512]{1,0:T(8,128)(2,1)S(1)}, f16[64,512]{1,0:T(8,128)(2,1)S(1)}, u32[]{:S(2)}, u32[]{:S(2)}) collective-permute-start(f16[64,512]{1,0:T(8,128)(2,1)S(1)} %convert_element_type.122), channel_id=1, source_target_pairs={{0,8},{1,9},{2,10},{3,11},{4,12},{5,13},{6,14},{7,15},{8,0},{9,1},... | collective-permute-start | bytes 196616 | tf_op jit(solution)/shard_map/ppermute | solution.py:44
  53.3 5.9 %collective-permute-start.26 = (f16[64,512]{1,0:T(8,128)(2,1)S(1)}, f16[64,512]{1,0:T(8,128)(2,1)S(1)}, u32[]{:S(2)}, u32[]{:S(2)}) collective-permute-start(f16[64,512]{1,0:T(8,128)(2,1)S(1)} %get-tuple-element.43), channel_id=1, source_target_pairs={{0,6},{1,7},{2,4},{3,5},{4,2},{5,3},{6,0},{7,1},{8,14},{9,15},{10,... | collective-permute-start | bytes 196616 | tf_op jit(solution)/shard_map/ppermute | solution.py:44
  55.6 4.3 %collective-permute-start.25 = (f16[64,512]{1,0:T(8,128)(2,1)S(1)}, f16[64,512]{1,0:T(8,128)(2,1)S(1)}, u32[]{:S(2)}, u32[]{:S(2)}) collective-permute-start(f16[64,512]{1,0:T(8,128)(2,1)S(1)} %get-tuple-element.43), channel_id=1, source_target_pairs={{0,2},{1,3},{2,0},{3,1},{4,6},{5,7},{6,4},{7,5},{8,10},{9,11},{10,... | collective-permute-start | bytes 196616 | tf_op jit(solution)/shard_map/ppermute | solution.py:44
  56.1 4.3 %collective-permute-start.24 = (f16[64,512]{1,0:T(8,128)(2,1)S(1)}, f16[64,512]{1,0:T(8,128)(2,1)S(1)}, u32[]{:S(2)}, u32[]{:S(2)}) collective-permute-start(f16[64,512]{1,0:T(8,128)(2,1)S(1)} %get-tuple-element.43), channel_id=1, source_target_pairs={{0,4},{1,5},{2,6},{3,7},{4,0},{5,1},{6,2},{7,3},{8,12},{9,13},{10,... | collective-permute-start | bytes 196616 | tf_op jit(solution)/shard_map/ppermute | solution.py:44
  56.8 3.6 %collective-permute-start.27 = (f16[64,512]{1,0:T(8,128)(2,1)S(1)}, f16[64,512]{1,0:T(8,128)(2,1)S(1)}, u32[]{:S(2)}, u32[]{:S(2)}) collective-permute-start(f16[64,512]{1,0:T(8,128)(2,1)S(1)} %get-tuple-element.43), channel_id=1, source_target_pairs={{0,1},{1,0},{2,3},{3,2},{4,5},{5,4},{6,7},{7,6},{8,9},{9,8},{10,11... | collective-permute-start | bytes 196616 | tf_op jit(solution)/shard_map/ppermute | solution.py:44
  59.2 1.3 %collective-permute-start.30 = (f16[64,512]{1,0:T(8,128)(2,1)S(1)}, f16[64,512]{1,0:T(8,128)(2,1)S(1)}, u32[]{:S(2)}, u32[]{:S(2)}) collective-permute-start(f16[64,512]{1,0:T(8,128)(2,1)S(1)} %collective-permute-done.26), channel_id=1, source_target_pairs={{0,1},{1,0},{2,3},{3,2},{4,5},{5,4},{6,7},{7,6},{8,9},{9,8},{10,11... | collective-permute-start | bytes 196616 | tf_op jit(solution)/shard_map/ppermute | solution.py:44
  59.9 1.3 %collective-permute-start.29 = (f16[64,512]{1,0:T(8,128)(2,1)S(1)}, f16[64,512]{1,0:T(8,128)(2,1)S(1)}, u32[]{:S(2)}, u32[]{:S(2)}) collective-permute-start(f16[64,512]{1,0:T(8,128)(2,1)S(1)} %collective-permute-done.25), channel_id=1, source_target_pairs={{0,1},{1,0},{2,3},{3,2},{4,5},{5,4},{6,7},{7,6},{8,9},{9,8},{10,11... | collective-permute-start | bytes 196616 | tf_op jit(solution)/shard_map/ppermute | solution.py:44
  60.4 1.3 %collective-permute-start.28 = (f16[64,512]{1,0:T(8,128)(2,1)S(1)}, f16[64,512]{1,0:T(8,128)(2,1)S(1)}, u32[]{:S(2)}, u32[]{:S(2)}) collective-permute-start(f16[64,512]{1,0:T(8,128)(2,1)S(1)} %collective-permute-done.24), channel_id=1, source_target_pairs={{0,1},{1,0},{2,3},{3,2},{4,5},{5,4},{6,7},{7,6},{8,9},{9,8},{10,11... | collective-permute-start | bytes 196616 | tf_op jit(solution)/shard_map/ppermute | solution.py:44
  64.9 6.8 %collective-permute-start.33 = (f16[64,512]{1,0:T(8,128)(2,1)S(1)}, f16[64,512]{1,0:T(8,128)(2,1)S(1)}, u32[]{:S(2)}, u32[]{:S(2)}) collective-permute-start(f16[64,512]{1,0:T(8,128)(2,1)S(1)} %convert_element_type.135), channel_id=1, source_target_pairs={{0,24},{1,25},{2,26},{3,27},{4,28},{5,29},{6,30},{7,31},{8,16},{9,... | collective-permute-start | bytes 196616 | tf_op jit(solution)/shard_map/ppermute | solution.py:44
  67.5 6.2 %collective-permute-start.32 = (f16[64,512]{1,0:T(8,128)(2,1)S(1)}, f16[64,512]{1,0:T(8,128)(2,1)S(1)}, u32[]{:S(2)}, u32[]{:S(2)}) collective-permute-start(f16[64,512]{1,0:T(8,128)(2,1)S(1)} %convert_element_type.135), channel_id=1, source_target_pairs={{0,16},{1,17},{2,18},{3,19},{4,20},{5,21},{6,22},{7,23},{8,24},{9,... | collective-permute-start | bytes 196616 | tf_op jit(solution)/shard_map/ppermute | solution.py:44
  67.5 6.2 %collective-permute-start.31 = (f16[64,512]{1,0:T(8,128)(2,1)S(1)}, f16[64,512]{1,0:T(8,128)(2,1)S(1)}, u32[]{:S(2)}, u32[]{:S(2)}) collective-permute-start(f16[64,512]{1,0:T(8,128)(2,1)S(1)} %convert_element_type.135), channel_id=1, source_target_pairs={{0,8},{1,9},{2,10},{3,11},{4,12},{5,13},{6,14},{7,15},{8,0},{9,1},... | collective-permute-start | bytes 196616 | tf_op jit(solution)/shard_map/ppermute | solution.py:44
  73.9 5.7 %collective-permute-start.36 = (f16[64,512]{1,0:T(8,128)(2,1)S(1)}, f16[64,512]{1,0:T(8,128)(2,1)S(1)}, u32[]{:S(2)}, u32[]{:S(2)}) collective-permute-start(f16[64,512]{1,0:T(8,128)(2,1)S(1)} %get-tuple-element.41), channel_id=1, source_target_pairs={{0,6},{1,7},{2,4},{3,5},{4,2},{5,3},{6,0},{7,1},{8,14},{9,15},{10,... | collective-permute-start | bytes 196616 | tf_op jit(solution)/shard_map/ppermute | solution.py:44
  75.6 4.5 %collective-permute-start.35 = (f16[64,512]{1,0:T(8,128)(2,1)S(1)}, f16[64,512]{1,0:T(8,128)(2,1)S(1)}, u32[]{:S(2)}, u32[]{:S(2)}) collective-permute-start(f16[64,512]{1,0:T(8,128)(2,1)S(1)} %get-tuple-element.41), channel_id=1, source_target_pairs={{0,2},{1,3},{2,0},{3,1},{4,6},{5,7},{6,4},{7,5},{8,10},{9,11},{10,... | collective-permute-start | bytes 196616 | tf_op jit(solution)/shard_map/ppermute | solution.py:44
  76.5 4.3 %collective-permute-start.34 = (f16[64,512]{1,0:T(8,128)(2,1)S(1)}, f16[64,512]{1,0:T(8,128)(2,1)S(1)}, u32[]{:S(2)}, u32[]{:S(2)}) collective-permute-start(f16[64,512]{1,0:T(8,128)(2,1)S(1)} %get-tuple-element.41), channel_id=1, source_target_pairs={{0,4},{1,5},{2,6},{3,7},{4,0},{5,1},{6,2},{7,3},{8,12},{9,13},{10,... | collective-permute-start | bytes 196616 | tf_op jit(solution)/shard_map/ppermute | solution.py:44
  77.4 3.4 %collective-permute-start.37 = (f16[64,512]{1,0:T(8,128)(2,1)S(1)}, f16[64,512]{1,0:T(8,128)(2,1)S(1)}, u32[]{:S(2)}, u32[]{:S(2)}) collective-permute-start(f16[64,512]{1,0:T(8,128)(2,1)S(1)} %get-tuple-element.41), channel_id=1, source_target_pairs={{0,1},{1,0},{2,3},{3,2},{4,5},{5,4},{6,7},{7,6},{8,9},{9,8},{10,11... | collective-permute-start | bytes 196616 | tf_op jit(solution)/shard_map/ppermute | solution.py:44
  79.5 1.3 %collective-permute-start.40 = (f16[64,512]{1,0:T(8,128)(2,1)S(1)}, f16[64,512]{1,0:T(8,128)(2,1)S(1)}, u32[]{:S(2)}, u32[]{:S(2)}) collective-permute-start(f16[64,512]{1,0:T(8,128)(2,1)S(1)} %collective-permute-done.36), channel_id=1, source_target_pairs={{0,1},{1,0},{2,3},{3,2},{4,5},{5,4},{6,7},{7,6},{8,9},{9,8},{10,11... | collective-permute-start | bytes 196616 | tf_op jit(solution)/shard_map/ppermute | solution.py:44
  80.1 1.3 %collective-permute-start.39 = (f16[64,512]{1,0:T(8,128)(2,1)S(1)}, f16[64,512]{1,0:T(8,128)(2,1)S(1)}, u32[]{:S(2)}, u32[]{:S(2)}) collective-permute-start(f16[64,512]{1,0:T(8,128)(2,1)S(1)} %collective-permute-done.35), channel_id=1, source_target_pairs={{0,1},{1,0},{2,3},{3,2},{4,5},{5,4},{6,7},{7,6},{8,9},{9,8},{10,11... | collective-permute-start | bytes 196616 | tf_op jit(solution)/shard_map/ppermute | solution.py:44
  80.8 1.3 %collective-permute-start.38 = (f16[64,512]{1,0:T(8,128)(2,1)S(1)}, f16[64,512]{1,0:T(8,128)(2,1)S(1)}, u32[]{:S(2)}, u32[]{:S(2)}) collective-permute-start(f16[64,512]{1,0:T(8,128)(2,1)S(1)} %collective-permute-done.34), channel_id=1, source_target_pairs={{0,1},{1,0},{2,3},{3,2},{4,5},{5,4},{6,7},{7,6},{8,9},{9,8},{10,11... | collective-permute-start | bytes 196616 | tf_op jit(solution)/shard_map/ppermute | solution.py:44

commit v10 on v9

--- a/solution.py
+++ b/solution.py
@@ -142,7 +142,7 @@
     rows = covar.shape[0]
     low, ax, ay = place()
     for k in range(4):
-        spot = 2 * other(ax, k & 2) + other(ay, k & 1)
+        spot = 2 * other(ax, k & 1) + other(ay, k & 2)
         spot = pl.ds(pl.multiple_of(spot * piece, piece), piece)
         packs[low, spot, :] = mine[k][...].astype(F32) * (1.0 / voxels)
         packs[1 - low, spot, :] = mates[k][...].astype(F32) * (1.0 / voxels)
@@ -186,15 +186,14 @@
     mixed_ref[...] = nn(weights_ref[...].astype(BF), whiten).astype(BF)
 
 
-def step(weights, blocks):
+def step(weights, white_ref, turned_ref):
     low = weights.astype(BF)
-    bents = [jnp.tanh(nn(low, block)) for block in blocks]
-    pulled = nt(bents[0].astype(BF), blocks[0])
-    slopes = 1.0 - bents[0] * bents[0]
-    for bent, block in zip(bents[1:], blocks[1:]):
-        pulled += nt(bent.astype(BF), block)
+    total, slopes = 0.0, 0.0
+    bents = [jnp.tanh(nn(low, white_ref[k])) for k in range(white_ref.shape[0])]
+    for k, bent in enumerate(bents):
+        total += nn(bent.astype(BF), turned_ref[k])
         slopes += 1.0 - bent * bent
-    return pulled, jnp.sum(slopes, axis=1, keepdims=True)
+    return total, jnp.sum(slopes, axis=1, keepdims=True)
 
 
 def apply_kernel(scale, mixed_ref, whiten_ref, weights_ref, *refs):
@@ -210,19 +209,22 @@
 
 
 def white_kernel(whiten_ref, *refs):
-    for k, block in enumerate(refs[:-1]):
-        refs[-1][k] = nn(whiten_ref[...], block[...]).astype(BF)
+    blocks, (white_ref, turned_ref) = refs[:-2], refs[-2:]
+    for k, block in enumerate(blocks):
+        white = nn(whiten_ref[...], block[...])
+        white_ref[k] = white.astype(BF)
+        turned_ref[k] = white.astype(BF).T
 
 
 def decor_kernel(last, scale, *refs):
-    mine, mates, white_ref = refs[:4], refs[4:8], refs[8]
-    outs, scratch = (refs[9:11], refs[11:]) if last else (refs[9:10], refs[10:])
+    mine, mates, white_ref, turned_ref = refs[:4], refs[4:8], refs[8], refs[9]
+    outs, scratch = (refs[10:12], refs[12:]) if last else (refs[10:11], refs[11:])
     newer, lower, *held = scratch
     count = mine[0].shape[0]
     low, ax, ay = place()
     chunks = white_ref.shape[0] // 2 if last else white_ref.shape[0]
     for k in range(4):
-        spot = 4 * other(ax, k & 2) + other(ay, k & 1)
+        spot = 4 * other(ax, k in (1, 2)) + other(ay, k in (1, 3))
         for ref, core in ((mine[k], low), (mates[k], 1 - low)):
             start = pl.multiple_of((spot + 2 * core) * count, count)
             newer[pl.ds(start, count), :] = ref[...]
@@ -262,7 +264,7 @@
         for copy in copies:
             copy.wait()
     else:
-        total, slope = step(weights, [white_ref[k] for k in range(chunks)])
+        total, slope = step(weights, white_ref, turned_ref)
         outs[0][...] = (total - slope * weights) * scale
 
 
@@ -272,6 +274,7 @@
     all_bits = (lax.axis_size("vox") * comps).bit_length() - 1
     low, across, near = 1, 2, comps
     far = [1 << k for k in range(near.bit_length(), all_bits)]
+    far = far[1::-1] + far[2:]
     core, far_x, near_y = place()
     rows = projection.shape[0]
     size = data.shape[1] // comps
@@ -310,8 +313,8 @@
     own = own + flip(by, near).astype(F32)
     own, reduced = lax.optimization_barrier((own, reduced))
     at_xy = flip(reduced, across | near)
-    packed, at_x, at_y = sum_over(own, far, BF, (at_x, at_y))
-    packed, at_xy = spread(packed, across, near, (at_xy,))
+    packed, at_y, at_x = sum_over(own, far, BF, (at_y, at_x))
+    packed, at_xy = spread(packed, near, across, (at_xy,))
     count = initial.shape[0] // 2
     weights = lax.dynamic_slice_in_dim(initial, near_y * count, count, 0)
     whiten, mixed = run(
@@ -334,16 +337,20 @@
     for turn in range(ICA_ITERS):
         last = turn == ICA_ITERS - 1
         if not turn:
-            white = run(
+            whites = run(
                 white_kernel,
-                shape((len(blocks), rows, size), BF),
+                (
+                    shape((len(blocks), rows, size), BF),
+                    shape((len(blocks), size, rows), BF),
+                ),
                 (whiten, *blocks),
                 cost=2 * len(blocks) * rows * rows * size,
             )
-        (summed, *held) = sum_over(newer, far, HALF, () if turn else (white,))
+        (summed, *held) = sum_over(newer, far, HALF, () if turn else whites[:1])
         if held:
-            (white,) = held
+            whites = (*held, whites[1])
         stacked = spread(summed, across, near)
+        stacked = [stacked[k] for k in (0, 3, 2, 1, 4, 7, 6, 5)]
         stacked = [part.astype(F32) * (1.0 / scale) for part in stacked]
         chunks = len(blocks) // 2 if last else len(blocks)
         outs = (
@@ -364,7 +371,7 @@
         newer = run(
             functools.partial(decor_kernel, last, scale),
             outs,
-            (*stacked, white),
+            (*stacked, *whites),
             out_spec=HBM if last else VMEM,
             scratch=scratch,
         )

time: 85.3 us -> 85 us (level)
  transfers between devices with their start and end apart: 41 -> 41, of which waited for: 26 -> 25; matrix products, arithmetic and copies ran while one was open for 2% -> 2% of each run, Pallas kernels for 5% -> 5%
where the time goes in v10:
time: 85 us; the launch traced here: 84.9 us
  starting transfers between devices  36.8 us (43%)
  waiting for transfers between devices  32.9 us (39%)
  Pallas kernels  12.3 us (14%)
  local copies, waits for them, and re-layouts  1.3 us (2%)
  between operations  0.98 us (1%)
    ppermute x41, starting transfers between devices, flip(): return lax.ppermute(x, AXES, [(i, i ^ mask) for i in range(count)])  36.8 us
    ppermute x41, waiting for transfers between devices, flip(): return lax.ppermute(x, AXES, [(i, i ^ mask) for i in range(count)])  32.9 us
    pallas_call x8, Pallas kernels, run(): pl.pallas_call(kernel, out_shape=outs, in_specs=specs or [VMEM] * len(arg...  12.3 us
  transfers between devices with their start and end apart: 41, of which 25 were waited for; matrix products, arithmetic and copies ran while one was open for 2% of the time, Pallas kernels for 5%

profile of v10, /device:TPU:0, one launch (start us, length us, event | category | flops | bytes accessed | tf_op | source)
XLA Modules:
  0.0 84.9 jit_solution(13289262892709795829)
XLA Ops:
  0.7 0.5 collective-permute-start
  1.2 1.3 %constant_dynamic-slice_fusion.1 = (bf16[512,256]{1,0:T(8,128)(2,1)S(1)}, bf16[512,256]{1,0:T(8,128)(2,1)S(1)}, bf16[512,256]{1,0:T(8,128)(2,1)S(1)}, bf16[512,256]{1,0:T(8,128)(2,1)S(1)}) fusion(bf16[512,1024]{1,0:T(8,128)(2,1)} %param.3, s32[]{:T(128)S(6)} %select_n.18, s32[]{:T(128)S(6)} %select_n.16, s32[]{:T(128)S(6)} %select_n.15, s32[]{:T(128)S(6)} %select_n.17), kind=kLoop, calls=%fused_computation.13 | loop fusion | bytes 2097168 | tf_op jit(solution)/shard_map/dynamic_slice | solution.py:285
  2.4 0.2 collective-permute-start.2
  2.6 1.4 %collective-permute-done.2.mate_right_ref = bf16[512,256]{1,0:T(8,128)(2,1)S(1)} collective-permute-done((bf16[512,256]{1,0:T(8,128)(2,1)S(1)}, bf16[512,256]{1,0:T(8,128)(2,1)S(1)}, u32[]{:S(2)}, u32[]{:S(2)}) %collective-permute-start.2) | collective-permute-done | bytes 262176 | tf_op jit(solution)/shard_map/ppermute | solution.py:44
  4.1 0.5 shard_map.51
  4.6 2.7 %collective-permute-start.3 = (f16[528,256]{1,0:T(8,128)(2,1)S(1)}, f16[528,256]{1,0:T(8,128)(2,1)S(1)}, u32[]{:S(2)}, u32[]{:S(2)}) collective-permute-start(f16[528,256]{1,0:T(8,128)(2,1)S(1)} %convert_element_type.111), channel_id=1, source_target_pairs={{0,2},{1,3},{2,0},{3,1},{4,6},{5,7},{6,4},{7,5},{8,10},{9,11},{10,... | collective-permute-start | bytes 811016 | tf_op jit(solution)/shard_map/ppermute | solution.py:44
  7.3 0.1 collective-permute-start.1
  7.4 1.5 %collective-permute-done.1.mate_right_ref = bf16[512,256]{1,0:T(8,128)(2,1)S(1)} collective-permute-done((bf16[512,256]{1,0:T(8,128)(2,1)S(1)}, bf16[512,256]{1,0:T(8,128)(2,1)S(1)}, u32[]{:S(2)}, u32[]{:S(2)}) %collective-permute-start.1) | collective-permute-done | bytes 262176 | tf_op jit(solution)/shard_map/ppermute | solution.py:44
  8.8 0.4 shard_map.50
  9.3 5.0 %collective-permute-done.3 = f16[528,256]{1,0:T(8,128)(2,1)S(1)} collective-permute-done((f16[528,256]{1,0:T(8,128)(2,1)S(1)}, f16[528,256]{1,0:T(8,128)(2,1)S(1)}, u32[]{:S(2)}, u32[]{:S(2)}) %collective-permute-start.3) | collective-permute-done | bytes 270368 | tf_op jit(solution)/shard_map/ppermute | solution.py:44
  14.5 1.5 %collective-permute-done.4.there_ref.refs_1_ = bf16[512,256]{1,0:T(8,128)(2,1)S(1)} collective-permute-done((bf16[512,256]{1,0:T(8,128)(2,1)S(1)}, bf16[512,256]{1,0:T(8,128)(2,1)S(1)}, u32[]{:S(2)}, u32[]{:S(2)}) %collective-permute-start.4) | collective-permute-done | bytes 262176 | tf_op jit(solution)/shard_map/ppermute | solution.py:44
  16.1 0.4 shard_map.52
  16.4 2.8 %collective-permute-start.5 = (bf16[160,128]{1,0:T(8,128)(2,1)S(1)}, bf16[160,128]{1,0:T(8,128)(2,1)S(1)}, u32[]{:S(2)}, u32[]{:S(2)}) collective-permute-start(bf16[160,128]{1,0:T(8,128)(2,1)S(1)} %get-tuple-element.25), channel_id=1, source_target_pairs={{0,6},{1,7},{2,4},{3,5},{4,2},{5,3},{6,0},{7,1},{8,14},{9,15},{10,... | collective-permute-start | bytes 122888 | tf_op jit(solution)/shard_map/ppermute | solution.py:44
  19.2 0.5 collective-permute-start.6
  19.7 0.3 collective-permute-start.7
  20.0 1.8 %collective-permute-start.11 = (bf16[512,256]{1,0:T(8,128)(2,1)S(1)}, bf16[512,256]{1,0:T(8,128)(2,1)S(1)}, u32[]{:S(2)}, u32[]{:S(2)}) collective-permute-start(bf16[512,256]{1,0:T(8,128)(2,1)S(1)} %fusion.1.here_ref.refs_0_), channel_id=1, source_target_pairs={{0,4},{1,5},{2,6},{3,7},{4,0},{5,1},{6,2},{7,3},{8,12},{9,13},{10,... | collective-permute-start | bytes 786440 | tf_op jit(solution)/shard_map/ppermute | solution.py:44
  21.7 1.5 %collective-permute-start.12 = (bf16[512,256]{1,0:T(8,128)(2,1)S(1)}, bf16[512,256]{1,0:T(8,128)(2,1)S(1)}, u32[]{:S(2)}, u32[]{:S(2)}) collective-permute-start(bf16[512,256]{1,0:T(8,128)(2,1)S(1)} %fusion.1.here_ref.refs_0_), channel_id=1, source_target_pairs={{0,2},{1,3},{2,0},{3,1},{4,6},{5,7},{6,4},{7,5},{8,10},{9,11},{10,... | collective-permute-start | bytes 786440 | tf_op jit(solution)/shard_map/ppermute | solution.py:44
  23.2 1.0 %collective-permute-done.7 = bf16[160,128]{1,0:T(8,128)(2,1)S(1)} collective-permute-done((bf16[160,128]{1,0:T(8,128)(2,1)S(1)}, bf16[160,128]{1,0:T(8,128)(2,1)S(1)}, u32[]{:S(2)}, u32[]{:S(2)}) %collective-permute-start.7) | collective-permute-done | bytes 40992 | tf_op jit(solution)/shard_map/ppermute | solution.py:44
  24.2 3.7 %collective-permute-start.10 = (bf16[160,128]{1,0:T(8,128)(2,1)S(1)}, bf16[160,128]{1,0:T(8,128)(2,1)S(1)}, u32[]{:S(2)}, u32[]{:S(2)}) collective-permute-start(bf16[160,128]{1,0:T(8,128)(2,1)S(1)} %convert_element_type.117), channel_id=1, source_target_pairs={{0,24},{1,25},{2,26},{3,27},{4,28},{5,29},{6,30},{7,31},{8,16},{9,... | collective-permute-start | bytes 122888 | tf_op jit(solution)/shard_map/ppermute | solution.py:44
  27.9 0.8 collective-permute-start.9
  28.7 1.5 %collective-permute-done.10 = bf16[160,128]{1,0:T(8,128)(2,1)S(1)} collective-permute-done((bf16[160,128]{1,0:T(8,128)(2,1)S(1)}, bf16[160,128]{1,0:T(8,128)(2,1)S(1)}, u32[]{:S(2)}, u32[]{:S(2)}) %collective-permute-start.10) | collective-permute-done | bytes 40992 | tf_op jit(solution)/shard_map/ppermute | solution.py:44
  30.2 1.3 %collective-permute-start.16 = (bf16[512,256]{1,0:T(8,128)(2,1)S(1)}, bf16[512,256]{1,0:T(8,128)(2,1)S(1)}, u32[]{:S(2)}, u32[]{:S(2)}) collective-permute-start(bf16[512,256]{1,0:T(8,128)(2,1)S(1)} %fusion.1.here_ref.refs_0_), channel_id=1, source_target_pairs={{0,6},{1,7},{2,4},{3,5},{4,2},{5,3},{6,0},{7,1},{8,14},{9,15},{10,... | collective-permute-start | bytes 786440 | tf_op jit(solution)/shard_map/ppermute | solution.py:44
  31.5 1.3 %collective-permute-done.8 = bf16[160,128]{1,0:T(8,128)(2,1)S(1)} collective-permute-done((bf16[160,128]{1,0:T(8,128)(2,1)S(1)}, bf16[160,128]{1,0:T(8,128)(2,1)S(1)}, u32[]{:S(2)}, u32[]{:S(2)}) %collective-permute-start.8) | collective-permute-done | bytes 40992 | tf_op jit(solution)/shard_map/ppermute | solution.py:44
  32.8 1.4 %collective-permute-start.15 = (bf16[160,128]{1,0:T(8,128)(2,1)S(1)}, bf16[160,128]{1,0:T(8,128)(2,1)S(1)}, u32[]{:S(2)}, u32[]{:S(2)}) collective-permute-start(bf16[160,128]{1,0:T(8,128)(2,1)S(1)} %add_convert_fusion.2.refs_0_), channel_id=1, source_target_pairs={{0,6},{1,7},{2,4},{3,5},{4,2},{5,3},{6,0},{7,1},{8,14},{9,15},{10,... | collective-permute-start | bytes 122888 | tf_op jit(solution)/shard_map/ppermute | solution.py:44
  34.3 0.5 collective-permute-start.13
  34.8 1.6 %collective-permute-start.14 = (bf16[160,128]{1,0:T(8,128)(2,1)S(1)}, bf16[160,128]{1,0:T(8,128)(2,1)S(1)}, u32[]{:S(2)}, u32[]{:S(2)}) collective-permute-start(bf16[160,128]{1,0:T(8,128)(2,1)S(1)} %add_convert_fusion.2.refs_0_), channel_id=1, source_target_pairs={{0,4},{1,5},{2,6},{3,7},{4,0},{5,1},{6,2},{7,3},{8,12},{9,13},{10,... | collective-permute-start | bytes 122888 | tf_op jit(solution)/shard_map/ppermute | solution.py:44
  36.4 1.9 %collective-permute-done.15.refs_3_ = bf16[160,128]{1,0:T(8,128)(2,1)S(1)} collective-permute-done((bf16[160,128]{1,0:T(8,128)(2,1)S(1)}, bf16[160,128]{1,0:T(8,128)(2,1)S(1)}, u32[]{:S(2)}, u32[]{:S(2)}) %collective-permute-start.15) | collective-permute-done | bytes 40992 | tf_op jit(solution)/shard_map/ppermute | solution.py:44
  38.4 0.5 collective-permute-done.14.refs_2_
  39.0 0.5 collective-permute-start.18
  39.4 0.1 collective-permute-start.19
  39.5 0.4 collective-permute-start.20
  40.0 0.4 collective-permute-done.17
  40.3 2.3 %shard_map.53 = (bf16[512,512]{1,0:T(8,128)(2,1)S(1)}, bf16[64,512]{1,0:T(8,128)(2,1)S(1)}) custom-call(bf16[160,128]{1,0:T(8,128)(2,1)S(1)} %add_convert_fusion.2.refs_0_, bf16[160,128]{1,0:T(8,128)(2,1)S(1)} %collective-permute-done.13.refs_1_, bf16[160,128]{1,0:T(8,128)(2,1)S(1)} %collective-permute-done.14.refs_2_, ...), custom_call_target="tpu_custom_call" | custom-call | tf_op jit(solution)/shard_map/pallas_call | solution.py:74
  42.7 1.3 %shard_map.54 = f32[64,512]{1,0:T(8,128)S(1)} custom-call(bf16[64,512]{1,0:T(8,128)(2,1)S(1)} %get-tuple-element.33.mixed_ref, bf16[512,512]{1,0:T(8,128)(2,1)S(1)} %get-tuple-element.39.whiten_ref, f32[64,512]{1,0:T(8,128)S(1)} %constant_dynamic-slice_fusion.refs_8_.weights_ref, bf16[512,256]{1,0:T(8,128)(2,1)S(1)} %fusion.1.here_ref.refs_0_, ...), custom_call_target="tpu_custom_call" | custom-call | tf_op jit(solution)/shard_map/pallas_call | solution.py:74
  44.0 3.5 %collective-permute-start.23 = (f16[64,512]{1,0:T(8,128)(2,1)S(1)}, f16[64,512]{1,0:T(8,128)(2,1)S(1)}, u32[]{:S(2)}, u32[]{:S(2)}) collective-permute-start(f16[64,512]{1,0:T(8,128)(2,1)S(1)} %convert_element_type.122), channel_id=1, source_target_pairs={{0,24},{1,25},{2,26},{3,27},{4,28},{5,29},{6,30},{7,31},{8,16},{9,... | collective-permute-start | bytes 196616 | tf_op jit(solution)/shard_map/ppermute | solution.py:44
  47.5 1.0 %collective-permute-start.22 = (f16[64,512]{1,0:T(8,128)(2,1)S(1)}, f16[64,512]{1,0:T(8,128)(2,1)S(1)}, u32[]{:S(2)}, u32[]{:S(2)}) collective-permute-start(f16[64,512]{1,0:T(8,128)(2,1)S(1)} %convert_element_type.122), channel_id=1, source_target_pairs={{0,8},{1,9},{2,10},{3,11},{4,12},{5,13},{6,14},{7,15},{8,0},{9,1},... | collective-permute-start | bytes 196616 | tf_op jit(solution)/shard_map/ppermute | solution.py:44
  48.5 1.3 %shard_map.55 = (bf16[8,512,256]{2,1,0:T(8,128)(2,1)S(1)}, bf16[8,256,512]{2,1,0:T(8,128)(2,1)S(1)}) custom-call(bf16[512,512]{1,0:T(8,128)(2,1)S(1)} %get-tuple-element.39.whiten_ref, bf16[512,256]{1,0:T(8,128)(2,1)S(1)} %fusion.1.here_ref.refs_0_, bf16[512,256]{1,0:T(8,128)(2,1)S(1)} %collective-permute-done.4.there_ref.refs_1_, ...), custom_call_target="tpu_custom_call" | custom-call | flops 1073741824 | bytes 4194304 | tf_op jit(solution)/shard_map/pallas_call | solution.py:74
  49.8 1.0 %collective-permute-done.23 = f16[64,512]{1,0:T(8,128)(2,1)S(1)} collective-permute-done((f16[64,512]{1,0:T(8,128)(2,1)S(1)}, f16[64,512]{1,0:T(8,128)(2,1)S(1)}, u32[]{:S(2)}, u32[]{:S(2)}) %collective-permute-start.23) | collective-permute-done | bytes 65568 | tf_op jit(solution)/shard_map/ppermute | solution.py:44
  50.8 2.2 %collective-permute-done.21 = f16[64,512]{1,0:T(8,128)(2,1)S(1)} collective-permute-done((f16[64,512]{1,0:T(8,128)(2,1)S(1)}, f16[64,512]{1,0:T(8,128)(2,1)S(1)}, u32[]{:S(2)}, u32[]{:S(2)}) %collective-permute-start.21) | collective-permute-done | bytes 65568 | tf_op jit(solution)/shard_map/ppermute | solution.py:44
  53.1 0.1 collective-permute-done.22
  53.2 0.1 fusion.4
  53.3 2.3 %collective-permute-start.24 = (f16[64,512]{1,0:T(8,128)(2,1)S(1)}, f16[64,512]{1,0:T(8,128)(2,1)S(1)}, u32[]{:S(2)}, u32[]{:S(2)}) collective-permute-start(f16[64,512]{1,0:T(8,128)(2,1)S(1)} %get-tuple-element.47), channel_id=1, source_target_pairs={{0,6},{1,7},{2,4},{3,5},{4,2},{5,3},{6,0},{7,1},{8,14},{9,15},{10,... | collective-permute-start | bytes 196616 | tf_op jit(solution)/shard_map/ppermute | solution.py:44
  55.6 0.5 collective-permute-start.25
  56.1 0.7 collective-permute-start.26
  56.8 2.4 %collective-permute-done.24 = f16[64,512]{1,0:T(8,128)(2,1)S(1)} collective-permute-done((f16[64,512]{1,0:T(8,128)(2,1)S(1)}, f16[64,512]{1,0:T(8,128)(2,1)S(1)}, u32[]{:S(2)}, u32[]{:S(2)}) %collective-permute-start.24) | collective-permute-done | bytes 65568 | tf_op jit(solution)/shard_map/ppermute | solution.py:44
  59.2 0.7 collective-permute-done.25
  59.9 0.5 collective-permute-done.26
  60.5 0.6 collective-permute-done.29
  61.1 0.5 collective-permute-done.30
  61.7 2.9 %shard_map.56 = f32[64,512]{1,0:T(8,128)S(1)} custom-call(f32[64,512]{1,0:T(8,128)S(1)} %get-tuple-element.46.refs_0_, f32[64,512]{1,0:T(8,128)S(1)} %convert_element_type.128.refs_1_, f32[64,512]{1,0:T(8,128)S(1)} %convert_element_type.129.refs_2_, f32[64,512]{1,0:T(8,128)S(1)} %convert_element_type.130.refs_3_, ...), custom_call_target="tpu_custom_call" | custom-call | tf_op jit(solution)/shard_map/pallas_call | solution.py:74
  64.6 2.6 %collective-permute-start.33 = (f16[64,512]{1,0:T(8,128)(2,1)S(1)}, f16[64,512]{1,0:T(8,128)(2,1)S(1)}, u32[]{:S(2)}, u32[]{:S(2)}) collective-permute-start(f16[64,512]{1,0:T(8,128)(2,1)S(1)} %convert_element_type.135), channel_id=1, source_target_pairs={{0,24},{1,25},{2,26},{3,27},{4,28},{5,29},{6,30},{7,31},{8,16},{9,... | collective-permute-start | bytes 196616 | tf_op jit(solution)/shard_map/ppermute | solution.py:44
  67.2 1.9 %collective-permute-start.32 = (f16[64,512]{1,0:T(8,128)(2,1)S(1)}, f16[64,512]{1,0:T(8,128)(2,1)S(1)}, u32[]{:S(2)}, u32[]{:S(2)}) collective-permute-start(f16[64,512]{1,0:T(8,128)(2,1)S(1)} %convert_element_type.135), channel_id=1, source_target_pairs={{0,8},{1,9},{2,10},{3,11},{4,12},{5,13},{6,14},{7,15},{8,0},{9,1},... | collective-permute-start | bytes 196616 | tf_op jit(solution)/shard_map/ppermute | solution.py:44
  69.1 2.4 %collective-permute-done.33 = f16[64,512]{1,0:T(8,128)(2,1)S(1)} collective-permute-done((f16[64,512]{1,0:T(8,128)(2,1)S(1)}, f16[64,512]{1,0:T(8,128)(2,1)S(1)}, u32[]{:S(2)}, u32[]{:S(2)}) %collective-permute-start.33) | collective-permute-done | bytes 65568 | tf_op jit(solution)/shard_map/ppermute | solution.py:44
  71.5 2.0 %collective-permute-done.31 = f16[64,512]{1,0:T(8,128)(2,1)S(1)} collective-permute-done((f16[64,512]{1,0:T(8,128)(2,1)S(1)}, f16[64,512]{1,0:T(8,128)(2,1)S(1)}, u32[]{:S(2)}, u32[]{:S(2)}) %collective-permute-start.31) | collective-permute-done | bytes 65568 | tf_op jit(solution)/shard_map/ppermute | solution.py:44
  73.5 0.1 fusion.3
  73.6 1.7 %collective-permute-start.34 = (f16[64,512]{1,0:T(8,128)(2,1)S(1)}, f16[64,512]{1,0:T(8,128)(2,1)S(1)}, u32[]{:S(2)}, u32[]{:S(2)}) collective-permute-start(f16[64,512]{1,0:T(8,128)(2,1)S(1)} %get-tuple-element.45), channel_id=1, source_target_pairs={{0,6},{1,7},{2,4},{3,5},{4,2},{5,3},{6,0},{7,1},{8,14},{9,15},{10,... | collective-permute-start | bytes 196616 | tf_op jit(solution)/shard_map/ppermute | solution.py:44
  75.3 0.9 %collective-permute-start.35 = (f16[64,512]{1,0:T(8,128)(2,1)S(1)}, f16[64,512]{1,0:T(8,128)(2,1)S(1)}, u32[]{:S(2)}, u32[]{:S(2)}) collective-permute-start(f16[64,512]{1,0:T(8,128)(2,1)S(1)} %get-tuple-element.45), channel_id=1, source_target_pairs={{0,2},{1,3},{2,0},{3,1},{4,6},{5,7},{6,4},{7,5},{8,10},{9,11},{10,... | collective-permute-start | bytes 196616 | tf_op jit(solution)/shard_map/ppermute | solution.py:44
  76.2 0.9 %collective-permute-start.36 = (f16[64,512]{1,0:T(8,128)(2,1)S(1)}, f16[64,512]{1,0:T(8,128)(2,1)S(1)}, u32[]{:S(2)}, u32[]{:S(2)}) collective-permute-start(f16[64,512]{1,0:T(8,128)(2,1)S(1)} %get-tuple-element.45), channel_id=1, source_target_pairs={{0,4},{1,5},{2,6},{3,7},{4,0},{5,1},{6,2},{7,3},{8,12},{9,13},{10,... | collective-permute-start | bytes 196616 | tf_op jit(solution)/shard_map/ppermute | solution.py:44
  77.1 2.1 %collective-permute-done.34 = f16[64,512]{1,0:T(8,128)(2,1)S(1)} collective-permute-done((f16[64,512]{1,0:T(8,128)(2,1)S(1)}, f16[64,512]{1,0:T(8,128)(2,1)S(1)}, u32[]{:S(2)}, u32[]{:S(2)}) %collective-permute-start.34) | collective-permute-done | bytes 65568 | tf_op jit(solution)/shard_map/ppermute | solution.py:44
  79.3 0.6 collective-permute-done.35
  79.8 0.6 collective-permute-done.36
  80.6 0.5 collective-permute-done.39
  81.1 0.6 collective-permute-done.40
  81.8 3.1 %shard_map.57 = (f32[128,512]{1,0:T(8,128)}, bf16[128,1024]{1,0:T(8,128)(2,1)}) custom-call(f32[64,512]{1,0:T(8,128)S(1)} %get-tuple-element.44.refs_0_, f32[64,512]{1,0:T(8,128)S(1)} %convert_element_type.141.refs_1_, f32[64,512]{1,0:T(8,128)S(1)} %convert_element_type.142.refs_2_, f32[64,512]{1,0:T(8,128)S(1)} %convert_element_type.143.refs_3_, ...), custom_call_target="tpu_custom_call" | custom-call | tf_op jit(solution)/shard_map/pallas_call | solution.py:74
  (59 shorter events, 0.7 us)
Async XLA Ops:
  0.6 39.3 %copy-start = (f32[128,512]{1,0:T(8,128)S(1)}, f32[128,512]{1,0:T(8,128)}, u32[]{:S(2)}) copy-start(f32[128,512]{1,0:T(8,128)} %param.5) | copy-start | bytes 786436
  0.6 3.4 %copy-start.1 = (bf16[512,512]{1,0:T(8,128)(2,1)S(1)}, bf16[512,512]{1,0:T(8,128)(2,1)}, u32[]{:S(2)}) copy-start(bf16[512,512]{1,0:T(8,128)(2,1)} %left_ref.3) | copy-start | bytes 1572868
  0.7 3.4 %collective-permute-start = (bf16[512,512]{1,0:T(8,128)(2,1)}, bf16[512,512]{1,0:T(8,128)(2,1)S(1)}, u32[]{:S(2)}, u32[]{:S(2)}) collective-permute-start(bf16[512,512]{1,0:T(8,128)(2,1)} %left_ref.3), channel_id=1, source_target_pairs={{0,1},{1,0},{2,3},{3,2},{4,5},{5,4},{6,7},{7,6},{8,9},{9,8},{10,11... | collective-permute-start | bytes 1572872 | tf_op jit(solution)/shard_map/ppermute | solution.py:44
  2.4 1.6 %collective-permute-start.2 = (bf16[512,256]{1,0:T(8,128)(2,1)S(1)}, bf16[512,256]{1,0:T(8,128)(2,1)S(1)}, u32[]{:S(2)}, u32[]{:S(2)}) collective-permute-start(bf16[512,256]{1,0:T(8,128)(2,1)S(1)} %get-tuple-element.48), channel_id=1, source_target_pairs={{0,1},{1,0},{2,3},{3,2},{4,5},{5,4},{6,7},{7,6},{8,9},{9,8},{10,11... | collective-permute-start | bytes 786440 | tf_op jit(solution)/shard_map/ppermute | solution.py:44
  4.6 9.7 %collective-permute-start.3 = (f16[528,256]{1,0:T(8,128)(2,1)S(1)}, f16[528,256]{1,0:T(8,128)(2,1)S(1)}, u32[]{:S(2)}, u32[]{:S(2)}) collective-permute-start(f16[528,256]{1,0:T(8,128)(2,1)S(1)} %convert_element_type.111), channel_id=1, source_target_pairs={{0,2},{1,3},{2,0},{3,1},{4,6},{5,7},{6,4},{7,5},{8,10},{9,11},{10,... | collective-permute-start | bytes 811016 | tf_op jit(solution)/shard_map/ppermute | solution.py:44
  7.3 1.5 %collective-permute-start.1 = (bf16[512,256]{1,0:T(8,128)(2,1)S(1)}, bf16[512,256]{1,0:T(8,128)(2,1)S(1)}, u32[]{:S(2)}, u32[]{:S(2)}) collective-permute-start(bf16[512,256]{1,0:T(8,128)(2,1)S(1)} %get-tuple-element.49), channel_id=1, source_target_pairs={{0,1},{1,0},{2,3},{3,2},{4,5},{5,4},{6,7},{7,6},{8,9},{9,8},{10,11... | collective-permute-start | bytes 786440 | tf_op jit(solution)/shard_map/ppermute | solution.py:44
  14.5 1.6 %collective-permute-start.4 = (bf16[512,256]{1,0:T(8,128)(2,1)S(1)}, bf16[512,256]{1,0:T(8,128)(2,1)S(1)}, u32[]{:S(2)}, u32[]{:S(2)}) collective-permute-start(bf16[512,256]{1,0:T(8,128)(2,1)S(1)} %fusion.1.here_ref.refs_0_), channel_id=1, source_target_pairs={{0,1},{1,0},{2,3},{3,2},{4,5},{5,4},{6,7},{7,6},{8,9},{9,8},{10,11... | collective-permute-start | bytes 786440 | tf_op jit(solution)/shard_map/ppermute | solution.py:44
  16.4 6.8 %collective-permute-start.5 = (bf16[160,128]{1,0:T(8,128)(2,1)S(1)}, bf16[160,128]{1,0:T(8,128)(2,1)S(1)}, u32[]{:S(2)}, u32[]{:S(2)}) collective-permute-start(bf16[160,128]{1,0:T(8,128)(2,1)S(1)} %get-tuple-element.25), channel_id=1, source_target_pairs={{0,6},{1,7},{2,4},{3,5},{4,2},{5,3},{6,0},{7,1},{8,14},{9,15},{10,... | collective-permute-start | bytes 122888 | tf_op jit(solution)/shard_map/ppermute | solution.py:44
  19.2 4.1 %collective-permute-start.6 = (bf16[160,128]{1,0:T(8,128)(2,1)S(1)}, bf16[160,128]{1,0:T(8,128)(2,1)S(1)}, u32[]{:S(2)}, u32[]{:S(2)}) collective-permute-start(bf16[160,128]{1,0:T(8,128)(2,1)S(1)} %get-tuple-element.26), channel_id=1, source_target_pairs={{0,2},{1,3},{2,0},{3,1},{4,6},{5,7},{6,4},{7,5},{8,10},{9,11},{10,... | collective-permute-start | bytes 122888 | tf_op jit(solution)/shard_map/ppermute | solution.py:44
  19.7 4.5 %collective-permute-start.7 = (bf16[160,128]{1,0:T(8,128)(2,1)S(1)}, bf16[160,128]{1,0:T(8,128)(2,1)S(1)}, u32[]{:S(2)}, u32[]{:S(2)}) collective-permute-start(bf16[160,128]{1,0:T(8,128)(2,1)S(1)} %get-tuple-element.27), channel_id=1, source_target_pairs={{0,4},{1,5},{2,6},{3,7},{4,0},{5,1},{6,2},{7,3},{8,12},{9,13},{10,... | collective-permute-start | bytes 122888 | tf_op jit(solution)/shard_map/ppermute | solution.py:44
  20.0 11.5 %collective-permute-start.11 = (bf16[512,256]{1,0:T(8,128)(2,1)S(1)}, bf16[512,256]{1,0:T(8,128)(2,1)S(1)}, u32[]{:S(2)}, u32[]{:S(2)}) collective-permute-start(bf16[512,256]{1,0:T(8,128)(2,1)S(1)} %fusion.1.here_ref.refs_0_), channel_id=1, source_target_pairs={{0,4},{1,5},{2,6},{3,7},{4,0},{5,1},{6,2},{7,3},{8,12},{9,13},{10,... | collective-permute-start | bytes 786440 | tf_op jit(solution)/shard_map/ppermute | solution.py:44
  21.7 9.8 %collective-permute-start.12 = (bf16[512,256]{1,0:T(8,128)(2,1)S(1)}, bf16[512,256]{1,0:T(8,128)(2,1)S(1)}, u32[]{:S(2)}, u32[]{:S(2)}) collective-permute-start(bf16[512,256]{1,0:T(8,128)(2,1)S(1)} %fusion.1.here_ref.refs_0_), channel_id=1, source_target_pairs={{0,2},{1,3},{2,0},{3,1},{4,6},{5,7},{6,4},{7,5},{8,10},{9,11},{10,... | collective-permute-start | bytes 786440 | tf_op jit(solution)/shard_map/ppermute | solution.py:44
  24.2 5.9 %collective-permute-start.10 = (bf16[160,128]{1,0:T(8,128)(2,1)S(1)}, bf16[160,128]{1,0:T(8,128)(2,1)S(1)}, u32[]{:S(2)}, u32[]{:S(2)}) collective-permute-start(bf16[160,128]{1,0:T(8,128)(2,1)S(1)} %convert_element_type.117), channel_id=1, source_target_pairs={{0,24},{1,25},{2,26},{3,27},{4,28},{5,29},{6,30},{7,31},{8,16},{9,... | collective-permute-start | bytes 122888 | tf_op jit(solution)/shard_map/ppermute | solution.py:44
  27.9 4.9 %collective-permute-start.8 = (bf16[160,128]{1,0:T(8,128)(2,1)S(1)}, bf16[160,128]{1,0:T(8,128)(2,1)S(1)}, u32[]{:S(2)}, u32[]{:S(2)}) collective-permute-start(bf16[160,128]{1,0:T(8,128)(2,1)S(1)} %convert_element_type.117), channel_id=1, source_target_pairs={{0,16},{1,17},{2,18},{3,19},{4,20},{5,21},{6,22},{7,23},{8,24},{9,... | collective-permute-start | bytes 122888 | tf_op jit(solution)/shard_map/ppermute | solution.py:44
  27.9 4.9 %collective-permute-start.9 = (bf16[160,128]{1,0:T(8,128)(2,1)S(1)}, bf16[160,128]{1,0:T(8,128)(2,1)S(1)}, u32[]{:S(2)}, u32[]{:S(2)}) collective-permute-start(bf16[160,128]{1,0:T(8,128)(2,1)S(1)} %convert_element_type.117), channel_id=1, source_target_pairs={{0,8},{1,9},{2,10},{3,11},{4,12},{5,13},{6,14},{7,15},{8,0},{9,1},... | collective-permute-start | bytes 122888 | tf_op jit(solution)/shard_map/ppermute | solution.py:44
  30.2 8.2 %collective-permute-start.16 = (bf16[512,256]{1,0:T(8,128)(2,1)S(1)}, bf16[512,256]{1,0:T(8,128)(2,1)S(1)}, u32[]{:S(2)}, u32[]{:S(2)}) collective-permute-start(bf16[512,256]{1,0:T(8,128)(2,1)S(1)} %fusion.1.here_ref.refs_0_), channel_id=1, source_target_pairs={{0,6},{1,7},{2,4},{3,5},{4,2},{5,3},{6,0},{7,1},{8,14},{9,15},{10,... | collective-permute-start | bytes 786440 | tf_op jit(solution)/shard_map/ppermute | solution.py:44
  32.8 5.5 %collective-permute-start.15 = (bf16[160,128]{1,0:T(8,128)(2,1)S(1)}, bf16[160,128]{1,0:T(8,128)(2,1)S(1)}, u32[]{:S(2)}, u32[]{:S(2)}) collective-permute-start(bf16[160,128]{1,0:T(8,128)(2,1)S(1)} %add_convert_fusion.2.refs_0_), channel_id=1, source_target_pairs={{0,6},{1,7},{2,4},{3,5},{4,2},{5,3},{6,0},{7,1},{8,14},{9,15},{10,... | collective-permute-start | bytes 122888 | tf_op jit(solution)/shard_map/ppermute | solution.py:44
  34.3 4.1 %collective-permute-start.13 = (bf16[160,128]{1,0:T(8,128)(2,1)S(1)}, bf16[160,128]{1,0:T(8,128)(2,1)S(1)}, u32[]{:S(2)}, u32[]{:S(2)}) collective-permute-start(bf16[160,128]{1,0:T(8,128)(2,1)S(1)} %add_convert_fusion.2.refs_0_), channel_id=1, source_target_pairs={{0,2},{1,3},{2,0},{3,1},{4,6},{5,7},{6,4},{7,5},{8,10},{9,11},{10,... | collective-permute-start | bytes 122888 | tf_op jit(solution)/shard_map/ppermute | solution.py:44
  34.8 4.0 %collective-permute-start.14 = (bf16[160,128]{1,0:T(8,128)(2,1)S(1)}, bf16[160,128]{1,0:T(8,128)(2,1)S(1)}, u32[]{:S(2)}, u32[]{:S(2)}) collective-permute-start(bf16[160,128]{1,0:T(8,128)(2,1)S(1)} %add_convert_fusion.2.refs_0_), channel_id=1, source_target_pairs={{0,4},{1,5},{2,6},{3,7},{4,0},{5,1},{6,2},{7,3},{8,12},{9,13},{10,... | collective-permute-start | bytes 122888 | tf_op jit(solution)/shard_map/ppermute | solution.py:44
  38.9 1.5 %collective-permute-start.17 = (bf16[4,160,128]{2,1,0:T(8,128)(2,1)S(1)}, bf16[4,160,128]{2,1,0:T(8,128)(2,1)S(1)}, u32[]{:S(2)}, u32[]{:S(2)}) collective-permute-start(bf16[4,160,128]{2,1,0:T(8,128)(2,1)S(1)} %pad_maximum_fusion), channel_id=1, source_target_pairs={{0,1},{1,0},{2,3},{3,2},{4,5},{5,4},{6,7},{7,6},{8,9},{9,8},{10,11... | collective-permute-start | bytes 491528 | tf_op jit(solution)/shard_map/ppermute | solution.py:44
  39.0 3.7 %collective-permute-start.18 = (bf16[512,256]{1,0:T(8,128)(2,1)S(1)}, bf16[512,256]{1,0:T(8,128)(2,1)S(1)}, u32[]{:S(2)}, u32[]{:S(2)}) collective-permute-start(bf16[512,256]{1,0:T(8,128)(2,1)S(1)} %collective-permute-done.12.refs_2_), channel_id=1, source_target_pairs={{0,1},{1,0},{2,3},{3,2},{4,5},{5,4},{6,7},{7,6},{8,9},{9,8},{10,11... | collective-permute-start | bytes 786440 | tf_op jit(solution)/shard_map/ppermute | solution.py:44
  39.4 3.2 %collective-permute-start.19 = (bf16[512,256]{1,0:T(8,128)(2,1)S(1)}, bf16[512,256]{1,0:T(8,128)(2,1)S(1)}, u32[]{:S(2)}, u32[]{:S(2)}) collective-permute-start(bf16[512,256]{1,0:T(8,128)(2,1)S(1)} %collective-permute-done.11.refs_4_), channel_id=1, source_target_pairs={{0,1},{1,0},{2,3},{3,2},{4,5},{5,4},{6,7},{7,6},{8,9},{9,8},{10,11... | collective-permute-start | bytes 786440 | tf_op jit(solution)/shard_map/ppermute | solution.py:44
  39.5 3.1 %collective-permute-start.20 = (bf16[512,256]{1,0:T(8,128)(2,1)S(1)}, bf16[512,256]{1,0:T(8,128)(2,1)S(1)}, u32[]{:S(2)}, u32[]{:S(2)}) collective-permute-start(bf16[512,256]{1,0:T(8,128)(2,1)S(1)} %collective-permute-done.16.refs_6_), channel_id=1, source_target_pairs={{0,1},{1,0},{2,3},{3,2},{4,5},{5,4},{6,7},{7,6},{8,9},{9,8},{10,11... | collective-permute-start | bytes 786440 | tf_op jit(solution)/shard_map/ppermute | solution.py:44
  44.0 6.8 %collective-permute-start.23 = (f16[64,512]{1,0:T(8,128)(2,1)S(1)}, f16[64,512]{1,0:T(8,128)(2,1)S(1)}, u32[]{:S(2)}, u32[]{:S(2)}) collective-permute-start(f16[64,512]{1,0:T(8,128)(2,1)S(1)} %convert_element_type.122), channel_id=1, source_target_pairs={{0,24},{1,25},{2,26},{3,27},{4,28},{5,29},{6,30},{7,31},{8,16},{9,... | collective-permute-start | bytes 196616 | tf_op jit(solution)/shard_map/ppermute | solution.py:44
  47.5 5.6 %collective-permute-start.21 = (f16[64,512]{1,0:T(8,128)(2,1)S(1)}, f16[64,512]{1,0:T(8,128)(2,1)S(1)}, u32[]{:S(2)}, u32[]{:S(2)}) collective-permute-start(f16[64,512]{1,0:T(8,128)(2,1)S(1)} %convert_element_type.122), channel_id=1, source_target_pairs={{0,16},{1,17},{2,18},{3,19},{4,20},{5,21},{6,22},{7,23},{8,24},{9,... | collective-permute-start | bytes 196616 | tf_op jit(solution)/shard_map/ppermute | solution.py:44
  47.5 5.7 %collective-permute-start.22 = (f16[64,512]{1,0:T(8,128)(2,1)S(1)}, f16[64,512]{1,0:T(8,128)(2,1)S(1)}, u32[]{:S(2)}, u32[]{:S(2)}) collective-permute-start(f16[64,512]{1,0:T(8,128)(2,1)S(1)} %convert_element_type.122), channel_id=1, source_target_pairs={{0,8},{1,9},{2,10},{3,11},{4,12},{5,13},{6,14},{7,15},{8,0},{9,1},... | collective-permute-start | bytes 196616 | tf_op jit(solution)/shard_map/ppermute | solution.py:44
  53.3 5.9 %collective-permute-start.24 = (f16[64,512]{1,0:T(8,128)(2,1)S(1)}, f16[64,512]{1,0:T(8,128)(2,1)S(1)}, u32[]{:S(2)}, u32[]{:S(2)}) collective-permute-start(f16[64,512]{1,0:T(8,128)(2,1)S(1)} %get-tuple-element.47), channel_id=1, source_target_pairs={{0,6},{1,7},{2,4},{3,5},{4,2},{5,3},{6,0},{7,1},{8,14},{9,15},{10,... | collective-permute-start | bytes 196616 | tf_op jit(solution)/shard_map/ppermute | solution.py:44
  55.6 4.3 %collective-permute-start.25 = (f16[64,512]{1,0:T(8,128)(2,1)S(1)}, f16[64,512]{1,0:T(8,128)(2,1)S(1)}, u32[]{:S(2)}, u32[]{:S(2)}) collective-permute-start(f16[64,512]{1,0:T(8,128)(2,1)S(1)} %get-tuple-element.47), channel_id=1, source_target_pairs={{0,2},{1,3},{2,0},{3,1},{4,6},{5,7},{6,4},{7,5},{8,10},{9,11},{10,... | collective-permute-start | bytes 196616 | tf_op jit(solution)/shard_map/ppermute | solution.py:44
  56.1 4.3 %collective-permute-start.26 = (f16[64,512]{1,0:T(8,128)(2,1)S(1)}, f16[64,512]{1,0:T(8,128)(2,1)S(1)}, u32[]{:S(2)}, u32[]{:S(2)}) collective-permute-start(f16[64,512]{1,0:T(8,128)(2,1)S(1)} %get-tuple-element.47), channel_id=1, source_target_pairs={{0,4},{1,5},{2,6},{3,7},{4,0},{5,1},{6,2},{7,3},{8,12},{9,13},{10,... | collective-permute-start | bytes 196616 | tf_op jit(solution)/shard_map/ppermute | solution.py:44
  56.8 3.6 %collective-permute-start.27 = (f16[64,512]{1,0:T(8,128)(2,1)S(1)}, f16[64,512]{1,0:T(8,128)(2,1)S(1)}, u32[]{:S(2)}, u32[]{:S(2)}) collective-permute-start(f16[64,512]{1,0:T(8,128)(2,1)S(1)} %get-tuple-element.47), channel_id=1, source_target_pairs={{0,1},{1,0},{2,3},{3,2},{4,5},{5,4},{6,7},{7,6},{8,9},{9,8},{10,11... | collective-permute-start | bytes 196616 | tf_op jit(solution)/shard_map/ppermute | solution.py:44
  59.2 1.3 %collective-permute-start.28 = (f16[64,512]{1,0:T(8,128)(2,1)S(1)}, f16[64,512]{1,0:T(8,128)(2,1)S(1)}, u32[]{:S(2)}, u32[]{:S(2)}) collective-permute-start(f16[64,512]{1,0:T(8,128)(2,1)S(1)} %collective-permute-done.24), channel_id=1, source_target_pairs={{0,1},{1,0},{2,3},{3,2},{4,5},{5,4},{6,7},{7,6},{8,9},{9,8},{10,11... | collective-permute-start | bytes 196616 | tf_op jit(solution)/shard_map/ppermute | solution.py:44
  59.9 1.3 %collective-permute-start.29 = (f16[64,512]{1,0:T(8,128)(2,1)S(1)}, f16[64,512]{1,0:T(8,128)(2,1)S(1)}, u32[]{:S(2)}, u32[]{:S(2)}) collective-permute-start(f16[64,512]{1,0:T(8,128)(2,1)S(1)} %collective-permute-done.25), channel_id=1, source_target_pairs={{0,1},{1,0},{2,3},{3,2},{4,5},{5,4},{6,7},{7,6},{8,9},{9,8},{10,11... | collective-permute-start | bytes 196616 | tf_op jit(solution)/shard_map/ppermute | solution.py:44
  60.4 1.3 %collective-permute-start.30 = (f16[64,512]{1,0:T(8,128)(2,1)S(1)}, f16[64,512]{1,0:T(8,128)(2,1)S(1)}, u32[]{:S(2)}, u32[]{:S(2)}) collective-permute-start(f16[64,512]{1,0:T(8,128)(2,1)S(1)} %collective-permute-done.26), channel_id=1, source_target_pairs={{0,1},{1,0},{2,3},{3,2},{4,5},{5,4},{6,7},{7,6},{8,9},{9,8},{10,11... | collective-permute-start | bytes 196616 | tf_op jit(solution)/shard_map/ppermute | solution.py:44
  64.6 6.8 %collective-permute-start.33 = (f16[64,512]{1,0:T(8,128)(2,1)S(1)}, f16[64,512]{1,0:T(8,128)(2,1)S(1)}, u32[]{:S(2)}, u32[]{:S(2)}) collective-permute-start(f16[64,512]{1,0:T(8,128)(2,1)S(1)} %convert_element_type.135), channel_id=1, source_target_pairs={{0,24},{1,25},{2,26},{3,27},{4,28},{5,29},{6,30},{7,31},{8,16},{9,... | collective-permute-start | bytes 196616 | tf_op jit(solution)/shard_map/ppermute | solution.py:44
  67.2 6.2 %collective-permute-start.31 = (f16[64,512]{1,0:T(8,128)(2,1)S(1)}, f16[64,512]{1,0:T(8,128)(2,1)S(1)}, u32[]{:S(2)}, u32[]{:S(2)}) collective-permute-start(f16[64,512]{1,0:T(8,128)(2,1)S(1)} %convert_element_type.135), channel_id=1, source_target_pairs={{0,16},{1,17},{2,18},{3,19},{4,20},{5,21},{6,22},{7,23},{8,24},{9,... | collective-permute-start | bytes 196616 | tf_op jit(solution)/shard_map/ppermute | solution.py:44
  67.2 6.2 %collective-permute-start.32 = (f16[64,512]{1,0:T(8,128)(2,1)S(1)}, f16[64,512]{1,0:T(8,128)(2,1)S(1)}, u32[]{:S(2)}, u32[]{:S(2)}) collective-permute-start(f16[64,512]{1,0:T(8,128)(2,1)S(1)} %convert_element_type.135), channel_id=1, source_target_pairs={{0,8},{1,9},{2,10},{3,11},{4,12},{5,13},{6,14},{7,15},{8,0},{9,1},... | collective-permute-start | bytes 196616 | tf_op jit(solution)/shard_map/ppermute | solution.py:44
  73.6 5.7 %collective-permute-start.34 = (f16[64,512]{1,0:T(8,128)(2,1)S(1)}, f16[64,512]{1,0:T(8,128)(2,1)S(1)}, u32[]{:S(2)}, u32[]{:S(2)}) collective-permute-start(f16[64,512]{1,0:T(8,128)(2,1)S(1)} %get-tuple-element.45), channel_id=1, source_target_pairs={{0,6},{1,7},{2,4},{3,5},{4,2},{5,3},{6,0},{7,1},{8,14},{9,15},{10,... | collective-permute-start | bytes 196616 | tf_op jit(solution)/shard_map/ppermute | solution.py:44
  75.3 4.5 %collective-permute-start.35 = (f16[64,512]{1,0:T(8,128)(2,1)S(1)}, f16[64,512]{1,0:T(8,128)(2,1)S(1)}, u32[]{:S(2)}, u32[]{:S(2)}) collective-permute-start(f16[64,512]{1,0:T(8,128)(2,1)S(1)} %get-tuple-element.45), channel_id=1, source_target_pairs={{0,2},{1,3},{2,0},{3,1},{4,6},{5,7},{6,4},{7,5},{8,10},{9,11},{10,... | collective-permute-start | bytes 196616 | tf_op jit(solution)/shard_map/ppermute | solution.py:44
  76.2 4.3 %collective-permute-start.36 = (f16[64,512]{1,0:T(8,128)(2,1)S(1)}, f16[64,512]{1,0:T(8,128)(2,1)S(1)}, u32[]{:S(2)}, u32[]{:S(2)}) collective-permute-start(f16[64,512]{1,0:T(8,128)(2,1)S(1)} %get-tuple-element.45), channel_id=1, source_target_pairs={{0,4},{1,5},{2,6},{3,7},{4,0},{5,1},{6,2},{7,3},{8,12},{9,13},{10,... | collective-permute-start | bytes 196616 | tf_op jit(solution)/shard_map/ppermute | solution.py:44
  77.1 3.4 %collective-permute-start.37 = (f16[64,512]{1,0:T(8,128)(2,1)S(1)}, f16[64,512]{1,0:T(8,128)(2,1)S(1)}, u32[]{:S(2)}, u32[]{:S(2)}) collective-permute-start(f16[64,512]{1,0:T(8,128)(2,1)S(1)} %get-tuple-element.45), channel_id=1, source_target_pairs={{0,1},{1,0},{2,3},{3,2},{4,5},{5,4},{6,7},{7,6},{8,9},{9,8},{10,11... | collective-permute-start | bytes 196616 | tf_op jit(solution)/shard_map/ppermute | solution.py:44
  79.3 1.3 %collective-permute-start.38 = (f16[64,512]{1,0:T(8,128)(2,1)S(1)}, f16[64,512]{1,0:T(8,128)(2,1)S(1)}, u32[]{:S(2)}, u32[]{:S(2)}) collective-permute-start(f16[64,512]{1,0:T(8,128)(2,1)S(1)} %collective-permute-done.34), channel_id=1, source_target_pairs={{0,1},{1,0},{2,3},{3,2},{4,5},{5,4},{6,7},{7,6},{8,9},{9,8},{10,11... | collective-permute-start | bytes 196616 | tf_op jit(solution)/shard_map/ppermute | solution.py:44
  79.8 1.3 %collective-permute-start.39 = (f16[64,512]{1,0:T(8,128)(2,1)S(1)}, f16[64,512]{1,0:T(8,128)(2,1)S(1)}, u32[]{:S(2)}, u32[]{:S(2)}) collective-permute-start(f16[64,512]{1,0:T(8,128)(2,1)S(1)} %collective-permute-done.35), channel_id=1, source_target_pairs={{0,1},{1,0},{2,3},{3,2},{4,5},{5,4},{6,7},{7,6},{8,9},{9,8},{10,11... | collective-permute-start | bytes 196616 | tf_op jit(solution)/shard_map/ppermute | solution.py:44
  80.5 1.3 %collective-permute-start.40 = (f16[64,512]{1,0:T(8,128)(2,1)S(1)}, f16[64,512]{1,0:T(8,128)(2,1)S(1)}, u32[]{:S(2)}, u32[]{:S(2)}) collective-permute-start(f16[64,512]{1,0:T(8,128)(2,1)S(1)} %collective-permute-done.36), channel_id=1, source_target_pairs={{0,1},{1,0},{2,3},{3,2},{4,5},{5,4},{6,7},{7,6},{8,9},{9,8},{10,11... | collective-permute-start | bytes 196616 | tf_op jit(solution)/shard_map/ppermute | solution.py:44

commit v11 on v10

--- a/solution.py
+++ b/solution.py
@@ -171,18 +171,31 @@
         == lax.broadcasted_iota(jnp.int32, (rows, rows), 1)
     ).astype(F32)
     yb = y.astype(BF)
-    square = nn(yb, yb)
-    squared = square.astype(BF)
-    rest = -2.4375 * y + 1.6875 * square
-    rest += nn(squared, (0.0625 * square - 0.5625 * y).astype(BF))
-    restb = rest.astype(BF)
-    left = 2.25 * y + nn(yb, restb)
-    right = 4.5 * rest + nn(restb, restb)
-    z3 = 3.375 * eye + 1.5 * rest - 0.5 * (
-        5.0625 * left + nn(left.astype(BF), right.astype(BF))
-    )
-    whiten = (z3 * lax.rsqrt(cscale)).astype(BF)
-    out_ref[...] = whiten
+    parts = [slice(k, k + rows // 2) for k in (0, rows // 2)]
+
+    def product(left, right):
+        return [nn(part, right) for part in left]
+
+    def whole(halves):
+        return jnp.concatenate([half.astype(BF) for half in halves])
+
+    ys, ybs = [y[part] for part in parts], [yb[part] for part in parts]
+    squares = product(ybs, yb)
+    inner = whole([0.0625 * s - 0.5625 * part for s, part in zip(squares, ys)])
+    thirds = product([s.astype(BF) for s in squares], inner)
+    rest = [
+        -2.4375 * part + 1.6875 * s + third
+        for part, s, third in zip(ys, squares, thirds)
+    ]
+    restb = whole(rest)
+    rights = product([half.astype(BF) for half in rest], restb)
+    right = whole([4.5 * half + more for half, more in zip(rest, rights)])
+    lefts = [2.25 * part + more for part, more in zip(ys, product(ybs, restb))]
+    lasts = product([left.astype(BF) for left in lefts], right)
+    for part, half, left, more in zip(parts, rest, lefts, lasts):
+        z3 = 3.375 * eye[part] + 1.5 * half - 0.5 * (5.0625 * left + more)
+        out_ref[part] = (z3 * lax.rsqrt(cscale)).astype(BF)
+    whiten = out_ref[...]
     mixed_ref[...] = nn(weights_ref[...].astype(BF), whiten).astype(BF)
 
 
@@ -231,14 +244,23 @@
             lower[pl.ds(start, count), :] = ref[...].astype(BF)
 
     raw = lower[...]
-    gram = nt(raw, raw)
-    gscale = jnp.sqrt(jnp.sum(gram * gram, keepdims=True) + 1e-06)
-    value = 1.5 * newer[...] - (0.5 / gscale) * nn(gram.astype(BF), raw)
-    value = value * lax.rsqrt(gscale)
-    raw = value.astype(BF)
-    gram = nt(raw, raw).astype(BF)
-    newer[...] = 1.5 * value - 0.5 * nn(gram, raw)
-    lower[...] = newer[...].astype(BF)
+    rows = raw.shape[0]
+    half = rows // 2
+    halves = (slice(0, half), slice(half, rows))
+    grams = [nt(raw[part], raw) for part in halves]
+    squares = sum(jnp.sum(gram * gram, keepdims=True) for gram in grams)
+    gscale = jnp.sqrt(squares + 1e-06)
+    factor, root = 0.5 / gscale, lax.rsqrt(gscale)
+    values = [
+        (1.5 * newer[part] - factor * nn(gram.astype(BF), raw)) * root
+        for part, gram in zip(halves, grams)
+    ]
+    raw = jnp.concatenate([value.astype(BF) for value in values])
+    for part, value in zip(halves, values):
+        gram = nt(raw[part], raw).astype(BF)
+        value = 1.5 * value - 0.5 * nn(gram, raw)
+        newer[part] = value
+        lower[part] = value.astype(BF)
     start = pl.multiple_of((4 * ax + 2 * low) * count, count)
     size = 2 * count
     if not last:

time: 85 us -> 84.9 us (level)
  no operation moved by 1% of the time
where the time goes in v11:
time: 84.9 us; the launch traced here: 84.8 us
  starting transfers between devices  36.8 us (43%)
  waiting for transfers between devices  32.9 us (39%)
  Pallas kernels  12.2 us (14%)
  local copies, waits for them, and re-layouts  1.3 us (2%)
  between operations  0.98 us (1%)
    ppermute x41, starting transfers between devices, flip(): return lax.ppermute(x, AXES, [(i, i ^ mask) for i in range(count)])  36.8 us
    ppermute x41, waiting for transfers between devices, flip(): return lax.ppermute(x, AXES, [(i, i ^ mask) for i in range(count)])  32.9 us
    pallas_call x8, Pallas kernels, run(): pl.pallas_call(kernel, out_shape=outs, in_specs=specs or [VMEM] * len(arg...  12.2 us
  transfers between devices with their start and end apart: 41, of which 25 were waited for; matrix products, arithmetic and copies ran while one was open for 2% of the time, Pallas kernels for 5%

profile of v11, /device:TPU:0, one launch (start us, length us, event | category | flops | bytes accessed | tf_op | source)
XLA Modules:
  0.0 84.8 jit_solution(12859445931667372513)
XLA Ops:
  0.7 0.5 collective-permute-start
  1.2 1.3 %constant_dynamic-slice_fusion.1 = (bf16[512,256]{1,0:T(8,128)(2,1)S(1)}, bf16[512,256]{1,0:T(8,128)(2,1)S(1)}, bf16[512,256]{1,0:T(8,128)(2,1)S(1)}, bf16[512,256]{1,0:T(8,128)(2,1)S(1)}) fusion(bf16[512,1024]{1,0:T(8,128)(2,1)} %param.3, s32[]{:T(128)S(6)} %select_n.18, s32[]{:T(128)S(6)} %select_n.16, s32[]{:T(128)S(6)} %select_n.15, s32[]{:T(128)S(6)} %select_n.17), kind=kLoop, calls=%fused_computation.13 | loop fusion | bytes 2097168 | tf_op jit(solution)/shard_map/dynamic_slice | solution.py:307
  2.4 0.2 collective-permute-start.2
  2.6 1.4 %collective-permute-done.2.mate_right_ref = bf16[512,256]{1,0:T(8,128)(2,1)S(1)} collective-permute-done((bf16[512,256]{1,0:T(8,128)(2,1)S(1)}, bf16[512,256]{1,0:T(8,128)(2,1)S(1)}, u32[]{:S(2)}, u32[]{:S(2)}) %collective-permute-start.2) | collective-permute-done | bytes 262176 | tf_op jit(solution)/shard_map/ppermute | solution.py:44
  4.1 0.5 shard_map.51
  4.6 2.7 %collective-permute-start.3 = (f16[528,256]{1,0:T(8,128)(2,1)S(1)}, f16[528,256]{1,0:T(8,128)(2,1)S(1)}, u32[]{:S(2)}, u32[]{:S(2)}) collective-permute-start(f16[528,256]{1,0:T(8,128)(2,1)S(1)} %convert_element_type.111), channel_id=1, source_target_pairs={{0,2},{1,3},{2,0},{3,1},{4,6},{5,7},{6,4},{7,5},{8,10},{9,11},{10,... | collective-permute-start | bytes 811016 | tf_op jit(solution)/shard_map/ppermute | solution.py:44
  7.3 0.1 collective-permute-start.1
  7.4 1.5 %collective-permute-done.1.mate_right_ref = bf16[512,256]{1,0:T(8,128)(2,1)S(1)} collective-permute-done((bf16[512,256]{1,0:T(8,128)(2,1)S(1)}, bf16[512,256]{1,0:T(8,128)(2,1)S(1)}, u32[]{:S(2)}, u32[]{:S(2)}) %collective-permute-start.1) | collective-permute-done | bytes 262176 | tf_op jit(solution)/shard_map/ppermute | solution.py:44
  8.8 0.4 shard_map.50
  9.3 5.0 %collective-permute-done.3 = f16[528,256]{1,0:T(8,128)(2,1)S(1)} collective-permute-done((f16[528,256]{1,0:T(8,128)(2,1)S(1)}, f16[528,256]{1,0:T(8,128)(2,1)S(1)}, u32[]{:S(2)}, u32[]{:S(2)}) %collective-permute-start.3) | collective-permute-done | bytes 270368 | tf_op jit(solution)/shard_map/ppermute | solution.py:44
  14.5 1.5 %collective-permute-done.4.there_ref.refs_1_ = bf16[512,256]{1,0:T(8,128)(2,1)S(1)} collective-permute-done((bf16[512,256]{1,0:T(8,128)(2,1)S(1)}, bf16[512,256]{1,0:T(8,128)(2,1)S(1)}, u32[]{:S(2)}, u32[]{:S(2)}) %collective-permute-start.4) | collective-permute-done | bytes 262176 | tf_op jit(solution)/shard_map/ppermute | solution.py:44
  16.1 0.4 shard_map.52
  16.4 2.8 %collective-permute-start.5 = (bf16[160,128]{1,0:T(8,128)(2,1)S(1)}, bf16[160,128]{1,0:T(8,128)(2,1)S(1)}, u32[]{:S(2)}, u32[]{:S(2)}) collective-permute-start(bf16[160,128]{1,0:T(8,128)(2,1)S(1)} %get-tuple-element.25), channel_id=1, source_target_pairs={{0,6},{1,7},{2,4},{3,5},{4,2},{5,3},{6,0},{7,1},{8,14},{9,15},{10,... | collective-permute-start | bytes 122888 | tf_op jit(solution)/shard_map/ppermute | solution.py:44
  19.2 0.5 collective-permute-start.6
  19.7 0.3 collective-permute-start.7
  20.0 1.8 %collective-permute-start.11 = (bf16[512,256]{1,0:T(8,128)(2,1)S(1)}, bf16[512,256]{1,0:T(8,128)(2,1)S(1)}, u32[]{:S(2)}, u32[]{:S(2)}) collective-permute-start(bf16[512,256]{1,0:T(8,128)(2,1)S(1)} %fusion.1.here_ref.refs_0_), channel_id=1, source_target_pairs={{0,4},{1,5},{2,6},{3,7},{4,0},{5,1},{6,2},{7,3},{8,12},{9,13},{10,... | collective-permute-start | bytes 786440 | tf_op jit(solution)/shard_map/ppermute | solution.py:44
  21.7 1.5 %collective-permute-start.12 = (bf16[512,256]{1,0:T(8,128)(2,1)S(1)}, bf16[512,256]{1,0:T(8,128)(2,1)S(1)}, u32[]{:S(2)}, u32[]{:S(2)}) collective-permute-start(bf16[512,256]{1,0:T(8,128)(2,1)S(1)} %fusion.1.here_ref.refs_0_), channel_id=1, source_target_pairs={{0,2},{1,3},{2,0},{3,1},{4,6},{5,7},{6,4},{7,5},{8,10},{9,11},{10,... | collective-permute-start | bytes 786440 | tf_op jit(solution)/shard_map/ppermute | solution.py:44
  23.2 1.0 %collective-permute-done.7 = bf16[160,128]{1,0:T(8,128)(2,1)S(1)} collective-permute-done((bf16[160,128]{1,0:T(8,128)(2,1)S(1)}, bf16[160,128]{1,0:T(8,128)(2,1)S(1)}, u32[]{:S(2)}, u32[]{:S(2)}) %collective-permute-start.7) | collective-permute-done | bytes 40992 | tf_op jit(solution)/shard_map/ppermute | solution.py:44
  24.2 3.7 %collective-permute-start.10 = (bf16[160,128]{1,0:T(8,128)(2,1)S(1)}, bf16[160,128]{1,0:T(8,128)(2,1)S(1)}, u32[]{:S(2)}, u32[]{:S(2)}) collective-permute-start(bf16[160,128]{1,0:T(8,128)(2,1)S(1)} %convert_element_type.117), channel_id=1, source_target_pairs={{0,24},{1,25},{2,26},{3,27},{4,28},{5,29},{6,30},{7,31},{8,16},{9,... | collective-permute-start | bytes 122888 | tf_op jit(solution)/shard_map/ppermute | solution.py:44
  27.9 0.8 collective-permute-start.9
  28.7 1.5 %collective-permute-done.10 = bf16[160,128]{1,0:T(8,128)(2,1)S(1)} collective-permute-done((bf16[160,128]{1,0:T(8,128)(2,1)S(1)}, bf16[160,128]{1,0:T(8,128)(2,1)S(1)}, u32[]{:S(2)}, u32[]{:S(2)}) %collective-permute-start.10) | collective-permute-done | bytes 40992 | tf_op jit(solution)/shard_map/ppermute | solution.py:44
  30.2 1.3 %collective-permute-start.16 = (bf16[512,256]{1,0:T(8,128)(2,1)S(1)}, bf16[512,256]{1,0:T(8,128)(2,1)S(1)}, u32[]{:S(2)}, u32[]{:S(2)}) collective-permute-start(bf16[512,256]{1,0:T(8,128)(2,1)S(1)} %fusion.1.here_ref.refs_0_), channel_id=1, source_target_pairs={{0,6},{1,7},{2,4},{3,5},{4,2},{5,3},{6,0},{7,1},{8,14},{9,15},{10,... | collective-permute-start | bytes 786440 | tf_op jit(solution)/shard_map/ppermute | solution.py:44
  31.5 1.3 %collective-permute-done.8 = bf16[160,128]{1,0:T(8,128)(2,1)S(1)} collective-permute-done((bf16[160,128]{1,0:T(8,128)(2,1)S(1)}, bf16[160,128]{1,0:T(8,128)(2,1)S(1)}, u32[]{:S(2)}, u32[]{:S(2)}) %collective-permute-start.8) | collective-permute-done | bytes 40992 | tf_op jit(solution)/shard_map/ppermute | solution.py:44
  32.8 1.4 %collective-permute-start.15 = (bf16[160,128]{1,0:T(8,128)(2,1)S(1)}, bf16[160,128]{1,0:T(8,128)(2,1)S(1)}, u32[]{:S(2)}, u32[]{:S(2)}) collective-permute-start(bf16[160,128]{1,0:T(8,128)(2,1)S(1)} %add_convert_fusion.2.refs_0_), channel_id=1, source_target_pairs={{0,6},{1,7},{2,4},{3,5},{4,2},{5,3},{6,0},{7,1},{8,14},{9,15},{10,... | collective-permute-start | bytes 122888 | tf_op jit(solution)/shard_map/ppermute | solution.py:44
  34.3 0.5 collective-permute-start.13
  34.8 1.6 %collective-permute-start.14 = (bf16[160,128]{1,0:T(8,128)(2,1)S(1)}, bf16[160,128]{1,0:T(8,128)(2,1)S(1)}, u32[]{:S(2)}, u32[]{:S(2)}) collective-permute-start(bf16[160,128]{1,0:T(8,128)(2,1)S(1)} %add_convert_fusion.2.refs_0_), channel_id=1, source_target_pairs={{0,4},{1,5},{2,6},{3,7},{4,0},{5,1},{6,2},{7,3},{8,12},{9,13},{10,... | collective-permute-start | bytes 122888 | tf_op jit(solution)/shard_map/ppermute | solution.py:44
  36.4 1.9 %collective-permute-done.15.refs_3_ = bf16[160,128]{1,0:T(8,128)(2,1)S(1)} collective-permute-done((bf16[160,128]{1,0:T(8,128)(2,1)S(1)}, bf16[160,128]{1,0:T(8,128)(2,1)S(1)}, u32[]{:S(2)}, u32[]{:S(2)}) %collective-permute-start.15) | collective-permute-done | bytes 40992 | tf_op jit(solution)/shard_map/ppermute | solution.py:44
  38.4 0.5 collective-permute-done.14.refs_2_
  39.0 0.5 collective-permute-start.18
  39.4 0.1 collective-permute-start.19
  39.5 0.4 collective-permute-start.20
  40.0 0.4 collective-permute-done.17
  40.3 2.2 %shard_map.53 = (bf16[512,512]{1,0:T(8,128)(2,1)S(1)}, bf16[64,512]{1,0:T(8,128)(2,1)S(1)}) custom-call(bf16[160,128]{1,0:T(8,128)(2,1)S(1)} %add_convert_fusion.2.refs_0_, bf16[160,128]{1,0:T(8,128)(2,1)S(1)} %collective-permute-done.13.refs_1_, bf16[160,128]{1,0:T(8,128)(2,1)S(1)} %collective-permute-done.14.refs_2_, ...), custom_call_target="tpu_custom_call" | custom-call | tf_op jit(solution)/shard_map/pallas_call | solution.py:74
  42.6 1.3 %shard_map.54 = f32[64,512]{1,0:T(8,128)S(1)} custom-call(bf16[64,512]{1,0:T(8,128)(2,1)S(1)} %get-tuple-element.33.mixed_ref, bf16[512,512]{1,0:T(8,128)(2,1)S(1)} %get-tuple-element.39.whiten_ref, f32[64,512]{1,0:T(8,128)S(1)} %constant_dynamic-slice_fusion.refs_8_.weights_ref, bf16[512,256]{1,0:T(8,128)(2,1)S(1)} %fusion.1.here_ref.refs_0_, ...), custom_call_target="tpu_custom_call" | custom-call | tf_op jit(solution)/shard_map/pallas_call | solution.py:74
  43.9 3.5 %collective-permute-start.23 = (f16[64,512]{1,0:T(8,128)(2,1)S(1)}, f16[64,512]{1,0:T(8,128)(2,1)S(1)}, u32[]{:S(2)}, u32[]{:S(2)}) collective-permute-start(f16[64,512]{1,0:T(8,128)(2,1)S(1)} %convert_element_type.122), channel_id=1, source_target_pairs={{0,24},{1,25},{2,26},{3,27},{4,28},{5,29},{6,30},{7,31},{8,16},{9,... | collective-permute-start | bytes 196616 | tf_op jit(solution)/shard_map/ppermute | solution.py:44
  47.4 1.0 %collective-permute-start.22 = (f16[64,512]{1,0:T(8,128)(2,1)S(1)}, f16[64,512]{1,0:T(8,128)(2,1)S(1)}, u32[]{:S(2)}, u32[]{:S(2)}) collective-permute-start(f16[64,512]{1,0:T(8,128)(2,1)S(1)} %convert_element_type.122), channel_id=1, source_target_pairs={{0,8},{1,9},{2,10},{3,11},{4,12},{5,13},{6,14},{7,15},{8,0},{9,1},... | collective-permute-start | bytes 196616 | tf_op jit(solution)/shard_map/ppermute | solution.py:44
  48.4 1.3 %shard_map.55 = (bf16[8,512,256]{2,1,0:T(8,128)(2,1)S(1)}, bf16[8,256,512]{2,1,0:T(8,128)(2,1)S(1)}) custom-call(bf16[512,512]{1,0:T(8,128)(2,1)S(1)} %get-tuple-element.39.whiten_ref, bf16[512,256]{1,0:T(8,128)(2,1)S(1)} %fusion.1.here_ref.refs_0_, bf16[512,256]{1,0:T(8,128)(2,1)S(1)} %collective-permute-done.4.there_ref.refs_1_, ...), custom_call_target="tpu_custom_call" | custom-call | flops 1073741824 | bytes 4194304 | tf_op jit(solution)/shard_map/pallas_call | solution.py:74
  49.7 1.0 %collective-permute-done.23 = f16[64,512]{1,0:T(8,128)(2,1)S(1)} collective-permute-done((f16[64,512]{1,0:T(8,128)(2,1)S(1)}, f16[64,512]{1,0:T(8,128)(2,1)S(1)}, u32[]{:S(2)}, u32[]{:S(2)}) %collective-permute-start.23) | collective-permute-done | bytes 65568 | tf_op jit(solution)/shard_map/ppermute | solution.py:44
  50.7 2.2 %collective-permute-done.21 = f16[64,512]{1,0:T(8,128)(2,1)S(1)} collective-permute-done((f16[64,512]{1,0:T(8,128)(2,1)S(1)}, f16[64,512]{1,0:T(8,128)(2,1)S(1)}, u32[]{:S(2)}, u32[]{:S(2)}) %collective-permute-start.21) | collective-permute-done | bytes 65568 | tf_op jit(solution)/shard_map/ppermute | solution.py:44
  53.0 0.1 collective-permute-done.22
  53.1 0.1 fusion.4
  53.2 2.3 %collective-permute-start.24 = (f16[64,512]{1,0:T(8,128)(2,1)S(1)}, f16[64,512]{1,0:T(8,128)(2,1)S(1)}, u32[]{:S(2)}, u32[]{:S(2)}) collective-permute-start(f16[64,512]{1,0:T(8,128)(2,1)S(1)} %get-tuple-element.47), channel_id=1, source_target_pairs={{0,6},{1,7},{2,4},{3,5},{4,2},{5,3},{6,0},{7,1},{8,14},{9,15},{10,... | collective-permute-start | bytes 196616 | tf_op jit(solution)/shard_map/ppermute | solution.py:44
  55.5 0.5 collective-permute-start.25
  56.1 0.7 collective-permute-start.26
  56.8 2.4 %collective-permute-done.24 = f16[64,512]{1,0:T(8,128)(2,1)S(1)} collective-permute-done((f16[64,512]{1,0:T(8,128)(2,1)S(1)}, f16[64,512]{1,0:T(8,128)(2,1)S(1)}, u32[]{:S(2)}, u32[]{:S(2)}) %collective-permute-start.24) | collective-permute-done | bytes 65568 | tf_op jit(solution)/shard_map/ppermute | solution.py:44
  59.1 0.7 collective-permute-done.25
  59.8 0.5 collective-permute-done.26
  60.5 0.6 collective-permute-done.29
  61.1 0.5 collective-permute-done.30
  61.6 2.9 %shard_map.56 = f32[64,512]{1,0:T(8,128)S(1)} custom-call(f32[64,512]{1,0:T(8,128)S(1)} %get-tuple-element.46.refs_0_, f32[64,512]{1,0:T(8,128)S(1)} %convert_element_type.128.refs_1_, f32[64,512]{1,0:T(8,128)S(1)} %convert_element_type.129.refs_2_, f32[64,512]{1,0:T(8,128)S(1)} %convert_element_type.130.refs_3_, ...), custom_call_target="tpu_custom_call" | custom-call | tf_op jit(solution)/shard_map/pallas_call | solution.py:74
  64.6 2.6 %collective-permute-start.33 = (f16[64,512]{1,0:T(8,128)(2,1)S(1)}, f16[64,512]{1,0:T(8,128)(2,1)S(1)}, u32[]{:S(2)}, u32[]{:S(2)}) collective-permute-start(f16[64,512]{1,0:T(8,128)(2,1)S(1)} %convert_element_type.135), channel_id=1, source_target_pairs={{0,24},{1,25},{2,26},{3,27},{4,28},{5,29},{6,30},{7,31},{8,16},{9,... | collective-permute-start | bytes 196616 | tf_op jit(solution)/shard_map/ppermute | solution.py:44
  67.2 1.9 %collective-permute-start.32 = (f16[64,512]{1,0:T(8,128)(2,1)S(1)}, f16[64,512]{1,0:T(8,128)(2,1)S(1)}, u32[]{:S(2)}, u32[]{:S(2)}) collective-permute-start(f16[64,512]{1,0:T(8,128)(2,1)S(1)} %convert_element_type.135), channel_id=1, source_target_pairs={{0,8},{1,9},{2,10},{3,11},{4,12},{5,13},{6,14},{7,15},{8,0},{9,1},... | collective-permute-start | bytes 196616 | tf_op jit(solution)/shard_map/ppermute | solution.py:44
  69.0 2.4 %collective-permute-done.33 = f16[64,512]{1,0:T(8,128)(2,1)S(1)} collective-permute-done((f16[64,512]{1,0:T(8,128)(2,1)S(1)}, f16[64,512]{1,0:T(8,128)(2,1)S(1)}, u32[]{:S(2)}, u32[]{:S(2)}) %collective-permute-start.33) | collective-permute-done | bytes 65568 | tf_op jit(solution)/shard_map/ppermute | solution.py:44
  71.4 2.0 %collective-permute-done.31 = f16[64,512]{1,0:T(8,128)(2,1)S(1)} collective-permute-done((f16[64,512]{1,0:T(8,128)(2,1)S(1)}, f16[64,512]{1,0:T(8,128)(2,1)S(1)}, u32[]{:S(2)}, u32[]{:S(2)}) %collective-permute-start.31) | collective-permute-done | bytes 65568 | tf_op jit(solution)/shard_map/ppermute | solution.py:44
  73.4 0.1 fusion.3
  73.5 1.7 %collective-permute-start.34 = (f16[64,512]{1,0:T(8,128)(2,1)S(1)}, f16[64,512]{1,0:T(8,128)(2,1)S(1)}, u32[]{:S(2)}, u32[]{:S(2)}) collective-permute-start(f16[64,512]{1,0:T(8,128)(2,1)S(1)} %get-tuple-element.45), channel_id=1, source_target_pairs={{0,6},{1,7},{2,4},{3,5},{4,2},{5,3},{6,0},{7,1},{8,14},{9,15},{10,... | collective-permute-start | bytes 196616 | tf_op jit(solution)/shard_map/ppermute | solution.py:44
  75.2 0.9 %collective-permute-start.35 = (f16[64,512]{1,0:T(8,128)(2,1)S(1)}, f16[64,512]{1,0:T(8,128)(2,1)S(1)}, u32[]{:S(2)}, u32[]{:S(2)}) collective-permute-start(f16[64,512]{1,0:T(8,128)(2,1)S(1)} %get-tuple-element.45), channel_id=1, source_target_pairs={{0,2},{1,3},{2,0},{3,1},{4,6},{5,7},{6,4},{7,5},{8,10},{9,11},{10,... | collective-permute-start | bytes 196616 | tf_op jit(solution)/shard_map/ppermute | solution.py:44
  76.2 0.9 %collective-permute-start.36 = (f16[64,512]{1,0:T(8,128)(2,1)S(1)}, f16[64,512]{1,0:T(8,128)(2,1)S(1)}, u32[]{:S(2)}, u32[]{:S(2)}) collective-permute-start(f16[64,512]{1,0:T(8,128)(2,1)S(1)} %get-tuple-element.45), channel_id=1, source_target_pairs={{0,4},{1,5},{2,6},{3,7},{4,0},{5,1},{6,2},{7,3},{8,12},{9,13},{10,... | collective-permute-start | bytes 196616 | tf_op jit(solution)/shard_map/ppermute | solution.py:44
  77.1 2.1 %collective-permute-done.34 = f16[64,512]{1,0:T(8,128)(2,1)S(1)} collective-permute-done((f16[64,512]{1,0:T(8,128)(2,1)S(1)}, f16[64,512]{1,0:T(8,128)(2,1)S(1)}, u32[]{:S(2)}, u32[]{:S(2)}) %collective-permute-start.34) | collective-permute-done | bytes 65568 | tf_op jit(solution)/shard_map/ppermute | solution.py:44
  79.2 0.6 collective-permute-done.35
  79.8 0.6 collective-permute-done.36
  80.5 0.5 collective-permute-done.39
  81.0 0.6 collective-permute-done.40
  81.7 3.1 %shard_map.57 = (f32[128,512]{1,0:T(8,128)}, bf16[128,1024]{1,0:T(8,128)(2,1)}) custom-call(f32[64,512]{1,0:T(8,128)S(1)} %get-tuple-element.44.refs_0_, f32[64,512]{1,0:T(8,128)S(1)} %convert_element_type.141.refs_1_, f32[64,512]{1,0:T(8,128)S(1)} %convert_element_type.142.refs_2_, f32[64,512]{1,0:T(8,128)S(1)} %convert_element_type.143.refs_3_, ...), custom_call_target="tpu_custom_call" | custom-call | tf_op jit(solution)/shard_map/pallas_call | solution.py:74
  (59 shorter events, 0.7 us)
Async XLA Ops:
  0.6 39.3 %copy-start = (f32[128,512]{1,0:T(8,128)S(1)}, f32[128,512]{1,0:T(8,128)}, u32[]{:S(2)}) copy-start(f32[128,512]{1,0:T(8,128)} %param.5) | copy-start | bytes 786436
  0.6 3.4 %copy-start.1 = (bf16[512,512]{1,0:T(8,128)(2,1)S(1)}, bf16[512,512]{1,0:T(8,128)(2,1)}, u32[]{:S(2)}) copy-start(bf16[512,512]{1,0:T(8,128)(2,1)} %left_ref.3) | copy-start | bytes 1572868
  0.7 3.4 %collective-permute-start = (bf16[512,512]{1,0:T(8,128)(2,1)}, bf16[512,512]{1,0:T(8,128)(2,1)S(1)}, u32[]{:S(2)}, u32[]{:S(2)}) collective-permute-start(bf16[512,512]{1,0:T(8,128)(2,1)} %left_ref.3), channel_id=1, source_target_pairs={{0,1},{1,0},{2,3},{3,2},{4,5},{5,4},{6,7},{7,6},{8,9},{9,8},{10,11... | collective-permute-start | bytes 1572872 | tf_op jit(solution)/shard_map/ppermute | solution.py:44
  2.4 1.6 %collective-permute-start.2 = (bf16[512,256]{1,0:T(8,128)(2,1)S(1)}, bf16[512,256]{1,0:T(8,128)(2,1)S(1)}, u32[]{:S(2)}, u32[]{:S(2)}) collective-permute-start(bf16[512,256]{1,0:T(8,128)(2,1)S(1)} %get-tuple-element.48), channel_id=1, source_target_pairs={{0,1},{1,0},{2,3},{3,2},{4,5},{5,4},{6,7},{7,6},{8,9},{9,8},{10,11... | collective-permute-start | bytes 786440 | tf_op jit(solution)/shard_map/ppermute | solution.py:44
  4.6 9.7 %collective-permute-start.3 = (f16[528,256]{1,0:T(8,128)(2,1)S(1)}, f16[528,256]{1,0:T(8,128)(2,1)S(1)}, u32[]{:S(2)}, u32[]{:S(2)}) collective-permute-start(f16[528,256]{1,0:T(8,128)(2,1)S(1)} %convert_element_type.111), channel_id=1, source_target_pairs={{0,2},{1,3},{2,0},{3,1},{4,6},{5,7},{6,4},{7,5},{8,10},{9,11},{10,... | collective-permute-start | bytes 811016 | tf_op jit(solution)/shard_map/ppermute | solution.py:44
  7.3 1.5 %collective-permute-start.1 = (bf16[512,256]{1,0:T(8,128)(2,1)S(1)}, bf16[512,256]{1,0:T(8,128)(2,1)S(1)}, u32[]{:S(2)}, u32[]{:S(2)}) collective-permute-start(bf16[512,256]{1,0:T(8,128)(2,1)S(1)} %get-tuple-element.49), channel_id=1, source_target_pairs={{0,1},{1,0},{2,3},{3,2},{4,5},{5,4},{6,7},{7,6},{8,9},{9,8},{10,11... | collective-permute-start | bytes 786440 | tf_op jit(solution)/shard_map/ppermute | solution.py:44
  14.5 1.6 %collective-permute-start.4 = (bf16[512,256]{1,0:T(8,128)(2,1)S(1)}, bf16[512,256]{1,0:T(8,128)(2,1)S(1)}, u32[]{:S(2)}, u32[]{:S(2)}) collective-permute-start(bf16[512,256]{1,0:T(8,128)(2,1)S(1)} %fusion.1.here_ref.refs_0_), channel_id=1, source_target_pairs={{0,1},{1,0},{2,3},{3,2},{4,5},{5,4},{6,7},{7,6},{8,9},{9,8},{10,11... | collective-permute-start | bytes 786440 | tf_op jit(solution)/shard_map/ppermute | solution.py:44
  16.4 6.8 %collective-permute-start.5 = (bf16[160,128]{1,0:T(8,128)(2,1)S(1)}, bf16[160,128]{1,0:T(8,128)(2,1)S(1)}, u32[]{:S(2)}, u32[]{:S(2)}) collective-permute-start(bf16[160,128]{1,0:T(8,128)(2,1)S(1)} %get-tuple-element.25), channel_id=1, source_target_pairs={{0,6},{1,7},{2,4},{3,5},{4,2},{5,3},{6,0},{7,1},{8,14},{9,15},{10,... | collective-permute-start | bytes 122888 | tf_op jit(solution)/shard_map/ppermute | solution.py:44
  19.2 4.1 %collective-permute-start.6 = (bf16[160,128]{1,0:T(8,128)(2,1)S(1)}, bf16[160,128]{1,0:T(8,128)(2,1)S(1)}, u32[]{:S(2)}, u32[]{:S(2)}) collective-permute-start(bf16[160,128]{1,0:T(8,128)(2,1)S(1)} %get-tuple-element.26), channel_id=1, source_target_pairs={{0,2},{1,3},{2,0},{3,1},{4,6},{5,7},{6,4},{7,5},{8,10},{9,11},{10,... | collective-permute-start | bytes 122888 | tf_op jit(solution)/shard_map/ppermute | solution.py:44
  19.7 4.5 %collective-permute-start.7 = (bf16[160,128]{1,0:T(8,128)(2,1)S(1)}, bf16[160,128]{1,0:T(8,128)(2,1)S(1)}, u32[]{:S(2)}, u32[]{:S(2)}) collective-permute-start(bf16[160,128]{1,0:T(8,128)(2,1)S(1)} %get-tuple-element.27), channel_id=1, source_target_pairs={{0,4},{1,5},{2,6},{3,7},{4,0},{5,1},{6,2},{7,3},{8,12},{9,13},{10,... | collective-permute-start | bytes 122888 | tf_op jit(solution)/shard_map/ppermute | solution.py:44
  20.0 11.5 %collective-permute-start.11 = (bf16[512,256]{1,0:T(8,128)(2,1)S(1)}, bf16[512,256]{1,0:T(8,128)(2,1)S(1)}, u32[]{:S(2)}, u32[]{:S(2)}) collective-permute-start(bf16[512,256]{1,0:T(8,128)(2,1)S(1)} %fusion.1.here_ref.refs_0_), channel_id=1, source_target_pairs={{0,4},{1,5},{2,6},{3,7},{4,0},{5,1},{6,2},{7,3},{8,12},{9,13},{10,... | collective-permute-start | bytes 786440 | tf_op jit(solution)/shard_map/ppermute | solution.py:44
  21.7 9.8 %collective-permute-start.12 = (bf16[512,256]{1,0:T(8,128)(2,1)S(1)}, bf16[512,256]{1,0:T(8,128)(2,1)S(1)}, u32[]{:S(2)}, u32[]{:S(2)}) collective-permute-start(bf16[512,256]{1,0:T(8,128)(2,1)S(1)} %fusion.1.here_ref.refs_0_), channel_id=1, source_target_pairs={{0,2},{1,3},{2,0},{3,1},{4,6},{5,7},{6,4},{7,5},{8,10},{9,11},{10,... | collective-permute-start | bytes 786440 | tf_op jit(solution)/shard_map/ppermute | solution.py:44
  24.2 5.9 %collective-permute-start.10 = (bf16[160,128]{1,0:T(8,128)(2,1)S(1)}, bf16[160,128]{1,0:T(8,128)(2,1)S(1)}, u32[]{:S(2)}, u32[]{:S(2)}) collective-permute-start(bf16[160,128]{1,0:T(8,128)(2,1)S(1)} %convert_element_type.117), channel_id=1, source_target_pairs={{0,24},{1,25},{2,26},{3,27},{4,28},{5,29},{6,30},{7,31},{8,16},{9,... | collective-permute-start | bytes 122888 | tf_op jit(solution)/shard_map/ppermute | solution.py:44
  27.9 4.9 %collective-permute-start.8 = (bf16[160,128]{1,0:T(8,128)(2,1)S(1)}, bf16[160,128]{1,0:T(8,128)(2,1)S(1)}, u32[]{:S(2)}, u32[]{:S(2)}) collective-permute-start(bf16[160,128]{1,0:T(8,128)(2,1)S(1)} %convert_element_type.117), channel_id=1, source_target_pairs={{0,16},{1,17},{2,18},{3,19},{4,20},{5,21},{6,22},{7,23},{8,24},{9,... | collective-permute-start | bytes 122888 | tf_op jit(solution)/shard_map/ppermute | solution.py:44
  27.9 4.9 %collective-permute-start.9 = (bf16[160,128]{1,0:T(8,128)(2,1)S(1)}, bf16[160,128]{1,0:T(8,128)(2,1)S(1)}, u32[]{:S(2)}, u32[]{:S(2)}) collective-permute-start(bf16[160,128]{1,0:T(8,128)(2,1)S(1)} %convert_element_type.117), channel_id=1, source_target_pairs={{0,8},{1,9},{2,10},{3,11},{4,12},{5,13},{6,14},{7,15},{8,0},{9,1},... | collective-permute-start | bytes 122888 | tf_op jit(solution)/shard_map/ppermute | solution.py:44
  30.2 8.2 %collective-permute-start.16 = (bf16[512,256]{1,0:T(8,128)(2,1)S(1)}, bf16[512,256]{1,0:T(8,128)(2,1)S(1)}, u32[]{:S(2)}, u32[]{:S(2)}) collective-permute-start(bf16[512,256]{1,0:T(8,128)(2,1)S(1)} %fusion.1.here_ref.refs_0_), channel_id=1, source_target_pairs={{0,6},{1,7},{2,4},{3,5},{4,2},{5,3},{6,0},{7,1},{8,14},{9,15},{10,... | collective-permute-start | bytes 786440 | tf_op jit(solution)/shard_map/ppermute | solution.py:44
  32.8 5.5 %collective-permute-start.15 = (bf16[160,128]{1,0:T(8,128)(2,1)S(1)}, bf16[160,128]{1,0:T(8,128)(2,1)S(1)}, u32[]{:S(2)}, u32[]{:S(2)}) collective-permute-start(bf16[160,128]{1,0:T(8,128)(2,1)S(1)} %add_convert_fusion.2.refs_0_), channel_id=1, source_target_pairs={{0,6},{1,7},{2,4},{3,5},{4,2},{5,3},{6,0},{7,1},{8,14},{9,15},{10,... | collective-permute-start | bytes 122888 | tf_op jit(solution)/shard_map/ppermute | solution.py:44
  34.3 4.1 %collective-permute-start.13 = (bf16[160,128]{1,0:T(8,128)(2,1)S(1)}, bf16[160,128]{1,0:T(8,128)(2,1)S(1)}, u32[]{:S(2)}, u32[]{:S(2)}) collective-permute-start(bf16[160,128]{1,0:T(8,128)(2,1)S(1)} %add_convert_fusion.2.refs_0_), channel_id=1, source_target_pairs={{0,2},{1,3},{2,0},{3,1},{4,6},{5,7},{6,4},{7,5},{8,10},{9,11},{10,... | collective-permute-start | bytes 122888 | tf_op jit(solution)/shard_map/ppermute | solution.py:44
  34.8 4.0 %collective-permute-start.14 = (bf16[160,128]{1,0:T(8,128)(2,1)S(1)}, bf16[160,128]{1,0:T(8,128)(2,1)S(1)}, u32[]{:S(2)}, u32[]{:S(2)}) collective-permute-start(bf16[160,128]{1,0:T(8,128)(2,1)S(1)} %add_convert_fusion.2.refs_0_), channel_id=1, source_target_pairs={{0,4},{1,5},{2,6},{3,7},{4,0},{5,1},{6,2},{7,3},{8,12},{9,13},{10,... | collective-permute-start | bytes 122888 | tf_op jit(solution)/shard_map/ppermute | solution.py:44
  38.9 1.5 %collective-permute-start.17 = (bf16[4,160,128]{2,1,0:T(8,128)(2,1)S(1)}, bf16[4,160,128]{2,1,0:T(8,128)(2,1)S(1)}, u32[]{:S(2)}, u32[]{:S(2)}) collective-permute-start(bf16[4,160,128]{2,1,0:T(8,128)(2,1)S(1)} %pad_maximum_fusion), channel_id=1, source_target_pairs={{0,1},{1,0},{2,3},{3,2},{4,5},{5,4},{6,7},{7,6},{8,9},{9,8},{10,11... | collective-permute-start | bytes 491528 | tf_op jit(solution)/shard_map/ppermute | solution.py:44
  39.0 3.6 %collective-permute-start.18 = (bf16[512,256]{1,0:T(8,128)(2,1)S(1)}, bf16[512,256]{1,0:T(8,128)(2,1)S(1)}, u32[]{:S(2)}, u32[]{:S(2)}) collective-permute-start(bf16[512,256]{1,0:T(8,128)(2,1)S(1)} %collective-permute-done.12.refs_2_), channel_id=1, source_target_pairs={{0,1},{1,0},{2,3},{3,2},{4,5},{5,4},{6,7},{7,6},{8,9},{9,8},{10,11... | collective-permute-start | bytes 786440 | tf_op jit(solution)/shard_map/ppermute | solution.py:44
  39.4 3.1 %collective-permute-start.19 = (bf16[512,256]{1,0:T(8,128)(2,1)S(1)}, bf16[512,256]{1,0:T(8,128)(2,1)S(1)}, u32[]{:S(2)}, u32[]{:S(2)}) collective-permute-start(bf16[512,256]{1,0:T(8,128)(2,1)S(1)} %collective-permute-done.11.refs_4_), channel_id=1, source_target_pairs={{0,1},{1,0},{2,3},{3,2},{4,5},{5,4},{6,7},{7,6},{8,9},{9,8},{10,11... | collective-permute-start | bytes 786440 | tf_op jit(solution)/shard_map/ppermute | solution.py:44
  39.5 3.0 %collective-permute-start.20 = (bf16[512,256]{1,0:T(8,128)(2,1)S(1)}, bf16[512,256]{1,0:T(8,128)(2,1)S(1)}, u32[]{:S(2)}, u32[]{:S(2)}) collective-permute-start(bf16[512,256]{1,0:T(8,128)(2,1)S(1)} %collective-permute-done.16.refs_6_), channel_id=1, source_target_pairs={{0,1},{1,0},{2,3},{3,2},{4,5},{5,4},{6,7},{7,6},{8,9},{9,8},{10,11... | collective-permute-start | bytes 786440 | tf_op jit(solution)/shard_map/ppermute | solution.py:44
  43.9 6.8 %collective-permute-start.23 = (f16[64,512]{1,0:T(8,128)(2,1)S(1)}, f16[64,512]{1,0:T(8,128)(2,1)S(1)}, u32[]{:S(2)}, u32[]{:S(2)}) collective-permute-start(f16[64,512]{1,0:T(8,128)(2,1)S(1)} %convert_element_type.122), channel_id=1, source_target_pairs={{0,24},{1,25},{2,26},{3,27},{4,28},{5,29},{6,30},{7,31},{8,16},{9,... | collective-permute-start | bytes 196616 | tf_op jit(solution)/shard_map/ppermute | solution.py:44
  47.4 5.6 %collective-permute-start.21 = (f16[64,512]{1,0:T(8,128)(2,1)S(1)}, f16[64,512]{1,0:T(8,128)(2,1)S(1)}, u32[]{:S(2)}, u32[]{:S(2)}) collective-permute-start(f16[64,512]{1,0:T(8,128)(2,1)S(1)} %convert_element_type.122), channel_id=1, source_target_pairs={{0,16},{1,17},{2,18},{3,19},{4,20},{5,21},{6,22},{7,23},{8,24},{9,... | collective-permute-start | bytes 196616 | tf_op jit(solution)/shard_map/ppermute | solution.py:44
  47.4 5.7 %collective-permute-start.22 = (f16[64,512]{1,0:T(8,128)(2,1)S(1)}, f16[64,512]{1,0:T(8,128)(2,1)S(1)}, u32[]{:S(2)}, u32[]{:S(2)}) collective-permute-start(f16[64,512]{1,0:T(8,128)(2,1)S(1)} %convert_element_type.122), channel_id=1, source_target_pairs={{0,8},{1,9},{2,10},{3,11},{4,12},{5,13},{6,14},{7,15},{8,0},{9,1},... | collective-permute-start | bytes 196616 | tf_op jit(solution)/shard_map/ppermute | solution.py:44
  53.2 5.9 %collective-permute-start.24 = (f16[64,512]{1,0:T(8,128)(2,1)S(1)}, f16[64,512]{1,0:T(8,128)(2,1)S(1)}, u32[]{:S(2)}, u32[]{:S(2)}) collective-permute-start(f16[64,512]{1,0:T(8,128)(2,1)S(1)} %get-tuple-element.47), channel_id=1, source_target_pairs={{0,6},{1,7},{2,4},{3,5},{4,2},{5,3},{6,0},{7,1},{8,14},{9,15},{10,... | collective-permute-start | bytes 196616 | tf_op jit(solution)/shard_map/ppermute | solution.py:44
  55.5 4.3 %collective-permute-start.25 = (f16[64,512]{1,0:T(8,128)(2,1)S(1)}, f16[64,512]{1,0:T(8,128)(2,1)S(1)}, u32[]{:S(2)}, u32[]{:S(2)}) collective-permute-start(f16[64,512]{1,0:T(8,128)(2,1)S(1)} %get-tuple-element.47), channel_id=1, source_target_pairs={{0,2},{1,3},{2,0},{3,1},{4,6},{5,7},{6,4},{7,5},{8,10},{9,11},{10,... | collective-permute-start | bytes 196616 | tf_op jit(solution)/shard_map/ppermute | solution.py:44
  56.1 4.3 %collective-permute-start.26 = (f16[64,512]{1,0:T(8,128)(2,1)S(1)}, f16[64,512]{1,0:T(8,128)(2,1)S(1)}, u32[]{:S(2)}, u32[]{:S(2)}) collective-permute-start(f16[64,512]{1,0:T(8,128)(2,1)S(1)} %get-tuple-element.47), channel_id=1, source_target_pairs={{0,4},{1,5},{2,6},{3,7},{4,0},{5,1},{6,2},{7,3},{8,12},{9,13},{10,... | collective-permute-start | bytes 196616 | tf_op jit(solution)/shard_map/ppermute | solution.py:44
  56.8 3.6 %collective-permute-start.27 = (f16[64,512]{1,0:T(8,128)(2,1)S(1)}, f16[64,512]{1,0:T(8,128)(2,1)S(1)}, u32[]{:S(2)}, u32[]{:S(2)}) collective-permute-start(f16[64,512]{1,0:T(8,128)(2,1)S(1)} %get-tuple-element.47), channel_id=1, source_target_pairs={{0,1},{1,0},{2,3},{3,2},{4,5},{5,4},{6,7},{7,6},{8,9},{9,8},{10,11... | collective-permute-start | bytes 196616 | tf_op jit(solution)/shard_map/ppermute | solution.py:44
  59.1 1.3 %collective-permute-start.28 = (f16[64,512]{1,0:T(8,128)(2,1)S(1)}, f16[64,512]{1,0:T(8,128)(2,1)S(1)}, u32[]{:S(2)}, u32[]{:S(2)}) collective-permute-start(f16[64,512]{1,0:T(8,128)(2,1)S(1)} %collective-permute-done.24), channel_id=1, source_target_pairs={{0,1},{1,0},{2,3},{3,2},{4,5},{5,4},{6,7},{7,6},{8,9},{9,8},{10,11... | collective-permute-start | bytes 196616 | tf_op jit(solution)/shard_map/ppermute | solution.py:44
  59.8 1.3 %collective-permute-start.29 = (f16[64,512]{1,0:T(8,128)(2,1)S(1)}, f16[64,512]{1,0:T(8,128)(2,1)S(1)}, u32[]{:S(2)}, u32[]{:S(2)}) collective-permute-start(f16[64,512]{1,0:T(8,128)(2,1)S(1)} %collective-permute-done.25), channel_id=1, source_target_pairs={{0,1},{1,0},{2,3},{3,2},{4,5},{5,4},{6,7},{7,6},{8,9},{9,8},{10,11... | collective-permute-start | bytes 196616 | tf_op jit(solution)/shard_map/ppermute | solution.py:44
  60.3 1.3 %collective-permute-start.30 = (f16[64,512]{1,0:T(8,128)(2,1)S(1)}, f16[64,512]{1,0:T(8,128)(2,1)S(1)}, u32[]{:S(2)}, u32[]{:S(2)}) collective-permute-start(f16[64,512]{1,0:T(8,128)(2,1)S(1)} %collective-permute-done.26), channel_id=1, source_target_pairs={{0,1},{1,0},{2,3},{3,2},{4,5},{5,4},{6,7},{7,6},{8,9},{9,8},{10,11... | collective-permute-start | bytes 196616 | tf_op jit(solution)/shard_map/ppermute | solution.py:44
  64.6 6.8 %collective-permute-start.33 = (f16[64,512]{1,0:T(8,128)(2,1)S(1)}, f16[64,512]{1,0:T(8,128)(2,1)S(1)}, u32[]{:S(2)}, u32[]{:S(2)}) collective-permute-start(f16[64,512]{1,0:T(8,128)(2,1)S(1)} %convert_element_type.135), channel_id=1, source_target_pairs={{0,24},{1,25},{2,26},{3,27},{4,28},{5,29},{6,30},{7,31},{8,16},{9,... | collective-permute-start | bytes 196616 | tf_op jit(solution)/shard_map/ppermute | solution.py:44
  67.2 6.2 %collective-permute-start.31 = (f16[64,512]{1,0:T(8,128)(2,1)S(1)}, f16[64,512]{1,0:T(8,128)(2,1)S(1)}, u32[]{:S(2)}, u32[]{:S(2)}) collective-permute-start(f16[64,512]{1,0:T(8,128)(2,1)S(1)} %convert_element_type.135), channel_id=1, source_target_pairs={{0,16},{1,17},{2,18},{3,19},{4,20},{5,21},{6,22},{7,23},{8,24},{9,... | collective-permute-start | bytes 196616 | tf_op jit(solution)/shard_map/ppermute | solution.py:44
  67.2 6.2 %collective-permute-start.32 = (f16[64,512]{1,0:T(8,128)(2,1)S(1)}, f16[64,512]{1,0:T(8,128)(2,1)S(1)}, u32[]{:S(2)}, u32[]{:S(2)}) collective-permute-start(f16[64,512]{1,0:T(8,128)(2,1)S(1)} %convert_element_type.135), channel_id=1, source_target_pairs={{0,8},{1,9},{2,10},{3,11},{4,12},{5,13},{6,14},{7,15},{8,0},{9,1},... | collective-permute-start | bytes 196616 | tf_op jit(solution)/shard_map/ppermute | solution.py:44
  73.5 5.7 %collective-permute-start.34 = (f16[64,512]{1,0:T(8,128)(2,1)S(1)}, f16[64,512]{1,0:T(8,128)(2,1)S(1)}, u32[]{:S(2)}, u32[]{:S(2)}) collective-permute-start(f16[64,512]{1,0:T(8,128)(2,1)S(1)} %get-tuple-element.45), channel_id=1, source_target_pairs={{0,6},{1,7},{2,4},{3,5},{4,2},{5,3},{6,0},{7,1},{8,14},{9,15},{10,... | collective-permute-start | bytes 196616 | tf_op jit(solution)/shard_map/ppermute | solution.py:44
  75.2 4.5 %collective-permute-start.35 = (f16[64,512]{1,0:T(8,128)(2,1)S(1)}, f16[64,512]{1,0:T(8,128)(2,1)S(1)}, u32[]{:S(2)}, u32[]{:S(2)}) collective-permute-start(f16[64,512]{1,0:T(8,128)(2,1)S(1)} %get-tuple-element.45), channel_id=1, source_target_pairs={{0,2},{1,3},{2,0},{3,1},{4,6},{5,7},{6,4},{7,5},{8,10},{9,11},{10,... | collective-permute-start | bytes 196616 | tf_op jit(solution)/shard_map/ppermute | solution.py:44
  76.2 4.3 %collective-permute-start.36 = (f16[64,512]{1,0:T(8,128)(2,1)S(1)}, f16[64,512]{1,0:T(8,128)(2,1)S(1)}, u32[]{:S(2)}, u32[]{:S(2)}) collective-permute-start(f16[64,512]{1,0:T(8,128)(2,1)S(1)} %get-tuple-element.45), channel_id=1, source_target_pairs={{0,4},{1,5},{2,6},{3,7},{4,0},{5,1},{6,2},{7,3},{8,12},{9,13},{10,... | collective-permute-start | bytes 196616 | tf_op jit(solution)/shard_map/ppermute | solution.py:44
  77.1 3.4 %collective-permute-start.37 = (f16[64,512]{1,0:T(8,128)(2,1)S(1)}, f16[64,512]{1,0:T(8,128)(2,1)S(1)}, u32[]{:S(2)}, u32[]{:S(2)}) collective-permute-start(f16[64,512]{1,0:T(8,128)(2,1)S(1)} %get-tuple-element.45), channel_id=1, source_target_pairs={{0,1},{1,0},{2,3},{3,2},{4,5},{5,4},{6,7},{7,6},{8,9},{9,8},{10,11... | collective-permute-start | bytes 196616 | tf_op jit(solution)/shard_map/ppermute | solution.py:44
  79.2 1.3 %collective-permute-start.38 = (f16[64,512]{1,0:T(8,128)(2,1)S(1)}, f16[64,512]{1,0:T(8,128)(2,1)S(1)}, u32[]{:S(2)}, u32[]{:S(2)}) collective-permute-start(f16[64,512]{1,0:T(8,128)(2,1)S(1)} %collective-permute-done.34), channel_id=1, source_target_pairs={{0,1},{1,0},{2,3},{3,2},{4,5},{5,4},{6,7},{7,6},{8,9},{9,8},{10,11... | collective-permute-start | bytes 196616 | tf_op jit(solution)/shard_map/ppermute | solution.py:44
  79.8 1.3 %collective-permute-start.39 = (f16[64,512]{1,0:T(8,128)(2,1)S(1)}, f16[64,512]{1,0:T(8,128)(2,1)S(1)}, u32[]{:S(2)}, u32[]{:S(2)}) collective-permute-start(f16[64,512]{1,0:T(8,128)(2,1)S(1)} %collective-permute-done.35), channel_id=1, source_target_pairs={{0,1},{1,0},{2,3},{3,2},{4,5},{5,4},{6,7},{7,6},{8,9},{9,8},{10,11... | collective-permute-start | bytes 196616 | tf_op jit(solution)/shard_map/ppermute | solution.py:44
  80.4 1.3 %collective-permute-start.40 = (f16[64,512]{1,0:T(8,128)(2,1)S(1)}, f16[64,512]{1,0:T(8,128)(2,1)S(1)}, u32[]{:S(2)}, u32[]{:S(2)}) collective-permute-start(f16[64,512]{1,0:T(8,128)(2,1)S(1)} %collective-permute-done.36), channel_id=1, source_target_pairs={{0,1},{1,0},{2,3},{3,2},{4,5},{5,4},{6,7},{7,6},{8,9},{9,8},{10,11... | collective-permute-start | bytes 196616 | tf_op jit(solution)/shard_map/ppermute | solution.py:44

commit v12 on v11

--- a/solution.py
+++ b/solution.py
@@ -34,11 +34,6 @@
     )
 
 
-def rounded(x, kind):
-    info = jnp.finfo(kind)
-    return lax.reduce_precision(x, info.nexp, info.nmant)
-
-
 def flip(x, mask):
     count = lax.axis_size("vox") * lax.axis_size("comp")
     return lax.ppermute(x, AXES, [(i, i ^ mask) for i in range(count)])
@@ -46,8 +41,8 @@
 
 def sum_over(x, masks, kind, due=()):
     for k in range(0, len(masks), 2):
-        sent = x.astype(kind)
-        x = rounded(x, kind) + flip(sent, masks[k]).astype(F32)
+        sent = lax.optimization_barrier(x.astype(kind))
+        x = sent.astype(F32) + flip(sent, masks[k]).astype(F32)
         if k + 1 < len(masks):
             both = flip(sent, masks[k] | masks[k + 1])
             if k == 0:
@@ -368,7 +363,7 @@
                 (whiten, *blocks),
                 cost=2 * len(blocks) * rows * rows * size,
             )
-        (summed, *held) = sum_over(newer, far, HALF, () if turn else whites[:1])
+        (summed, *held) = sum_over(newer, far[1::-1] + far[2:], HALF, () if turn else whites[:1])
         if held:
             whites = (*held, whites[1])
         stacked = spread(summed, across, near)

time: 84.9 us -> 86.1 us (1.014)
  waiting for transfers between devices: 32.9 us -> 34.9 us
    ppermute x41, waiting for transfers between devices: 32.9 us -> 34.9 us  [flip(): return lax.ppermute(x, AXES, [(i, i ^ mask) for i in range(count)])]
  transfers between devices with their start and end apart: 41 -> 41, of which waited for: 25 -> 24; matrix products, arithmetic and copies ran while one was open for 2% -> 2% of each run, Pallas kernels for 5% -> 5%
where the time goes in v12:
time: 86.1 us; the launch traced here: 85.9 us
  starting transfers between devices  36.1 us (42%)
  waiting for transfers between devices  34.9 us (41%)
  Pallas kernels  12.2 us (14%)
  local copies, waits for them, and re-layouts  1.3 us (2%)
  between operations  0.97 us (1%)
    ppermute x41, starting transfers between devices, flip(): return lax.ppermute(x, AXES, [(i, i ^ mask) for i in range(count)])  36.1 us
    ppermute x41, waiting for transfers between devices, flip(): return lax.ppermute(x, AXES, [(i, i ^ mask) for i in range(count)])  34.9 us
    pallas_call x8, Pallas kernels, run(): pl.pallas_call(kernel, out_shape=outs, in_specs=specs or [VMEM] * len(arg...  12.2 us
  transfers between devices with their start and end apart: 41, of which 24 were waited for; matrix products, arithmetic and copies ran while one was open for 2% of the time, Pallas kernels for 5%

profile of v12, /device:TPU:0, one launch (start us, length us, event | category | flops | bytes accessed | tf_op | source)
XLA Modules:
  0.0 85.9 jit_solution(11817905017692492866)
XLA Ops:
  0.7 0.5 collective-permute-start
  1.2 1.3 %constant_dynamic-slice_fusion.1 = (bf16[512,256]{1,0:T(8,128)(2,1)S(1)}, bf16[512,256]{1,0:T(8,128)(2,1)S(1)}, bf16[512,256]{1,0:T(8,128)(2,1)S(1)}, bf16[512,256]{1,0:T(8,128)(2,1)S(1)}) fusion(bf16[512,1024]{1,0:T(8,128)(2,1)} %param.3, s32[]{:T(128)S(6)} %select_n.18, s32[]{:T(128)S(6)} %select_n.16, s32[]{:T(128)S(6)} %select_n.15, s32[]{:T(128)S(6)} %select_n.17), kind=kLoop, calls=%fused_computation.13 | loop fusion | bytes 2097168 | tf_op jit(solution)/shard_map/dynamic_slice | solution.py:302
  2.4 0.2 collective-permute-start.2
  2.6 1.4 %collective-permute-done.2.mate_right_ref = bf16[512,256]{1,0:T(8,128)(2,1)S(1)} collective-permute-done((bf16[512,256]{1,0:T(8,128)(2,1)S(1)}, bf16[512,256]{1,0:T(8,128)(2,1)S(1)}, u32[]{:S(2)}, u32[]{:S(2)}) %collective-permute-start.2) | collective-permute-done | bytes 262176 | tf_op jit(solution)/shard_map/ppermute | solution.py:39
  4.1 0.5 shard_map.51
  4.6 2.7 %collective-permute-start.3 = (f16[528,256]{1,0:T(8,128)(2,1)S(1)}, f16[528,256]{1,0:T(8,128)(2,1)S(1)}, u32[]{:S(2)}, u32[]{:S(2)}) collective-permute-start(f16[528,256]{1,0:T(8,128)(2,1)S(1)} %convert_element_type.120), channel_id=1, source_target_pairs={{0,2},{1,3},{2,0},{3,1},{4,6},{5,7},{6,4},{7,5},{8,10},{9,11},{10,... | collective-permute-start | bytes 811016 | tf_op jit(solution)/shard_map/ppermute | solution.py:39
  7.3 0.1 collective-permute-start.1
  7.4 1.5 %collective-permute-done.1.mate_right_ref = bf16[512,256]{1,0:T(8,128)(2,1)S(1)} collective-permute-done((bf16[512,256]{1,0:T(8,128)(2,1)S(1)}, bf16[512,256]{1,0:T(8,128)(2,1)S(1)}, u32[]{:S(2)}, u32[]{:S(2)}) %collective-permute-start.1) | collective-permute-done | bytes 262176 | tf_op jit(solution)/shard_map/ppermute | solution.py:39
  8.8 0.4 shard_map.50
  9.3 5.0 %collective-permute-done.3 = f16[528,256]{1,0:T(8,128)(2,1)S(1)} collective-permute-done((f16[528,256]{1,0:T(8,128)(2,1)S(1)}, f16[528,256]{1,0:T(8,128)(2,1)S(1)}, u32[]{:S(2)}, u32[]{:S(2)}) %collective-permute-start.3) | collective-permute-done | bytes 270368 | tf_op jit(solution)/shard_map/ppermute | solution.py:39
  14.4 0.1 fusion.1.here_ref.refs_0_
  14.5 1.5 %collective-permute-done.4.there_ref.refs_1_ = bf16[512,256]{1,0:T(8,128)(2,1)S(1)} collective-permute-done((bf16[512,256]{1,0:T(8,128)(2,1)S(1)}, bf16[512,256]{1,0:T(8,128)(2,1)S(1)}, u32[]{:S(2)}, u32[]{:S(2)}) %collective-permute-start.4) | collective-permute-done | bytes 262176 | tf_op jit(solution)/shard_map/ppermute | solution.py:39
  16.1 0.4 shard_map.52
  16.4 1.8 %collective-permute-start.7 = (bf16[160,128]{1,0:T(8,128)(2,1)S(1)}, bf16[160,128]{1,0:T(8,128)(2,1)S(1)}, u32[]{:S(2)}, u32[]{:S(2)}) collective-permute-start(bf16[160,128]{1,0:T(8,128)(2,1)S(1)} %get-tuple-element.27), channel_id=1, source_target_pairs={{0,4},{1,5},{2,6},{3,7},{4,0},{5,1},{6,2},{7,3},{8,12},{9,13},{10,... | collective-permute-start | bytes 122888 | tf_op jit(solution)/shard_map/ppermute | solution.py:39
  18.2 1.5 %collective-permute-start.6 = (bf16[160,128]{1,0:T(8,128)(2,1)S(1)}, bf16[160,128]{1,0:T(8,128)(2,1)S(1)}, u32[]{:S(2)}, u32[]{:S(2)}) collective-permute-start(bf16[160,128]{1,0:T(8,128)(2,1)S(1)} %get-tuple-element.26), channel_id=1, source_target_pairs={{0,2},{1,3},{2,0},{3,1},{4,6},{5,7},{6,4},{7,5},{8,10},{9,11},{10,... | collective-permute-start | bytes 122888 | tf_op jit(solution)/shard_map/ppermute | solution.py:39
  19.7 0.2 collective-permute-start.5
  20.0 1.8 %collective-permute-start.11 = (bf16[512,256]{1,0:T(8,128)(2,1)S(1)}, bf16[512,256]{1,0:T(8,128)(2,1)S(1)}, u32[]{:S(2)}, u32[]{:S(2)}) collective-permute-start(bf16[512,256]{1,0:T(8,128)(2,1)S(1)} %fusion.1.here_ref.refs_0_), channel_id=1, source_target_pairs={{0,4},{1,5},{2,6},{3,7},{4,0},{5,1},{6,2},{7,3},{8,12},{9,13},{10,... | collective-permute-start | bytes 786440 | tf_op jit(solution)/shard_map/ppermute | solution.py:39
  21.7 1.5 %collective-permute-start.12 = (bf16[512,256]{1,0:T(8,128)(2,1)S(1)}, bf16[512,256]{1,0:T(8,128)(2,1)S(1)}, u32[]{:S(2)}, u32[]{:S(2)}) collective-permute-start(bf16[512,256]{1,0:T(8,128)(2,1)S(1)} %fusion.1.here_ref.refs_0_), channel_id=1, source_target_pairs={{0,2},{1,3},{2,0},{3,1},{4,6},{5,7},{6,4},{7,5},{8,10},{9,11},{10,... | collective-permute-start | bytes 786440 | tf_op jit(solution)/shard_map/ppermute | solution.py:39
  23.2 1.9 %collective-permute-done.5 = bf16[160,128]{1,0:T(8,128)(2,1)S(1)} collective-permute-done((bf16[160,128]{1,0:T(8,128)(2,1)S(1)}, bf16[160,128]{1,0:T(8,128)(2,1)S(1)}, u32[]{:S(2)}, u32[]{:S(2)}) %collective-permute-start.5) | collective-permute-done | bytes 40992 | tf_op jit(solution)/shard_map/ppermute | solution.py:39
  25.2 3.6 %collective-permute-start.10 = (bf16[160,128]{1,0:T(8,128)(2,1)S(1)}, bf16[160,128]{1,0:T(8,128)(2,1)S(1)}, u32[]{:S(2)}, u32[]{:S(2)}) collective-permute-start(bf16[160,128]{1,0:T(8,128)(2,1)S(1)} %convert_add_fusion), channel_id=1, source_target_pairs={{0,24},{1,25},{2,26},{3,27},{4,28},{5,29},{6,30},{7,31},{8,16},{9,... | collective-permute-start | bytes 122888 | tf_op jit(solution)/shard_map/ppermute | solution.py:39
  28.8 0.9 collective-permute-start.8
  29.6 1.4 %collective-permute-done.10 = bf16[160,128]{1,0:T(8,128)(2,1)S(1)} collective-permute-done((bf16[160,128]{1,0:T(8,128)(2,1)S(1)}, bf16[160,128]{1,0:T(8,128)(2,1)S(1)}, u32[]{:S(2)}, u32[]{:S(2)}) %collective-permute-start.10) | collective-permute-done | bytes 40992 | tf_op jit(solution)/shard_map/ppermute | solution.py:39
  31.1 0.1 collective-permute-start.16
  31.1 1.6 %collective-permute-done.9 = bf16[160,128]{1,0:T(8,128)(2,1)S(1)} collective-permute-done((bf16[160,128]{1,0:T(8,128)(2,1)S(1)}, bf16[160,128]{1,0:T(8,128)(2,1)S(1)}, u32[]{:S(2)}, u32[]{:S(2)}) %collective-permute-start.9) | collective-permute-done | bytes 40992 | tf_op jit(solution)/shard_map/ppermute | solution.py:39
  32.8 0.9 %collective-permute-done.8 = bf16[160,128]{1,0:T(8,128)(2,1)S(1)} collective-permute-done((bf16[160,128]{1,0:T(8,128)(2,1)S(1)}, bf16[160,128]{1,0:T(8,128)(2,1)S(1)}, u32[]{:S(2)}, u32[]{:S(2)}) %collective-permute-start.8) | collective-permute-done | bytes 40992 | tf_op jit(solution)/shard_map/ppermute | solution.py:39
  33.7 0.4 collective-permute-start.15
  34.1 1.5 %collective-permute-start.13 = (bf16[160,128]{1,0:T(8,128)(2,1)S(1)}, bf16[160,128]{1,0:T(8,128)(2,1)S(1)}, u32[]{:S(2)}, u32[]{:S(2)}) collective-permute-start(bf16[160,128]{1,0:T(8,128)(2,1)S(1)} %add_convert_fusion.2.refs_0_), channel_id=1, source_target_pairs={{0,2},{1,3},{2,0},{3,1},{4,6},{5,7},{6,4},{7,5},{8,10},{9,11},{10,... | collective-permute-start | bytes 122888 | tf_op jit(solution)/shard_map/ppermute | solution.py:39
  35.7 1.6 %collective-permute-start.14 = (bf16[160,128]{1,0:T(8,128)(2,1)S(1)}, bf16[160,128]{1,0:T(8,128)(2,1)S(1)}, u32[]{:S(2)}, u32[]{:S(2)}) collective-permute-start(bf16[160,128]{1,0:T(8,128)(2,1)S(1)} %add_convert_fusion.2.refs_0_), channel_id=1, source_target_pairs={{0,4},{1,5},{2,6},{3,7},{4,0},{5,1},{6,2},{7,3},{8,12},{9,13},{10,... | collective-permute-start | bytes 122888 | tf_op jit(solution)/shard_map/ppermute | solution.py:39
  37.2 1.6 %collective-permute-done.15.refs_3_ = bf16[160,128]{1,0:T(8,128)(2,1)S(1)} collective-permute-done((bf16[160,128]{1,0:T(8,128)(2,1)S(1)}, bf16[160,128]{1,0:T(8,128)(2,1)S(1)}, u32[]{:S(2)}, u32[]{:S(2)}) %collective-permute-start.15) | collective-permute-done | bytes 40992 | tf_op jit(solution)/shard_map/ppermute | solution.py:39
  38.9 0.8 collective-permute-done.14.refs_2_
  39.8 0.5 collective-permute-start.18
  40.3 0.1 collective-permute-start.19
  40.3 0.4 collective-permute-start.20
  40.8 0.4 collective-permute-done.17
  41.2 2.2 %shard_map.53 = (bf16[512,512]{1,0:T(8,128)(2,1)S(1)}, bf16[64,512]{1,0:T(8,128)(2,1)S(1)}) custom-call(bf16[160,128]{1,0:T(8,128)(2,1)S(1)} %add_convert_fusion.2.refs_0_, bf16[160,128]{1,0:T(8,128)(2,1)S(1)} %collective-permute-done.13.refs_1_, bf16[160,128]{1,0:T(8,128)(2,1)S(1)} %collective-permute-done.14.refs_2_, ...), custom_call_target="tpu_custom_call" | custom-call | tf_op jit(solution)/shard_map/pallas_call | solution.py:69
  43.4 1.3 %shard_map.54 = f32[64,512]{1,0:T(8,128)S(1)} custom-call(bf16[64,512]{1,0:T(8,128)(2,1)S(1)} %get-tuple-element.33.mixed_ref, bf16[512,512]{1,0:T(8,128)(2,1)S(1)} %get-tuple-element.39.whiten_ref, f32[64,512]{1,0:T(8,128)S(1)} %constant_dynamic-slice_fusion.refs_8_.weights_ref, bf16[512,256]{1,0:T(8,128)(2,1)S(1)} %fusion.1.here_ref.refs_0_, ...), custom_call_target="tpu_custom_call" | custom-call | tf_op jit(solution)/shard_map/pallas_call | solution.py:69
  44.8 3.1 %collective-permute-start.23 = (f16[64,512]{1,0:T(8,128)(2,1)S(1)}, f16[64,512]{1,0:T(8,128)(2,1)S(1)}, u32[]{:S(2)}, u32[]{:S(2)}) collective-permute-start(f16[64,512]{1,0:T(8,128)(2,1)S(1)} %convert_element_type.132), channel_id=1, source_target_pairs={{0,24},{1,25},{2,26},{3,27},{4,28},{5,29},{6,30},{7,31},{8,16},{9,... | collective-permute-start | bytes 196616 | tf_op jit(solution)/shard_map/ppermute | solution.py:39
  47.9 0.4 collective-permute-start.22
  48.3 0.9 %collective-permute-start.21 = (f16[64,512]{1,0:T(8,128)(2,1)S(1)}, f16[64,512]{1,0:T(8,128)(2,1)S(1)}, u32[]{:S(2)}, u32[]{:S(2)}) collective-permute-start(f16[64,512]{1,0:T(8,128)(2,1)S(1)} %convert_element_type.132), channel_id=1, source_target_pairs={{0,8},{1,9},{2,10},{3,11},{4,12},{5,13},{6,14},{7,15},{8,0},{9,1},... | collective-permute-start | bytes 196616 | tf_op jit(solution)/shard_map/ppermute | solution.py:39
  49.2 1.3 %shard_map.55 = (bf16[8,512,256]{2,1,0:T(8,128)(2,1)S(1)}, bf16[8,256,512]{2,1,0:T(8,128)(2,1)S(1)}) custom-call(bf16[512,512]{1,0:T(8,128)(2,1)S(1)} %get-tuple-element.39.whiten_ref, bf16[512,256]{1,0:T(8,128)(2,1)S(1)} %fusion.1.here_ref.refs_0_, bf16[512,256]{1,0:T(8,128)(2,1)S(1)} %collective-permute-done.4.there_ref.refs_1_, ...), custom_call_target="tpu_custom_call" | custom-call | flops 1073741824 | bytes 4194304 | tf_op jit(solution)/shard_map/pallas_call | solution.py:69
  50.5 1.1 %collective-permute-done.23 = f16[64,512]{1,0:T(8,128)(2,1)S(1)} collective-permute-done((f16[64,512]{1,0:T(8,128)(2,1)S(1)}, f16[64,512]{1,0:T(8,128)(2,1)S(1)}, u32[]{:S(2)}, u32[]{:S(2)}) %collective-permute-start.23) | collective-permute-done | bytes 65568 | tf_op jit(solution)/shard_map/ppermute | solution.py:39
  51.7 3.0 %collective-permute-done.22 = f16[64,512]{1,0:T(8,128)(2,1)S(1)} collective-permute-done((f16[64,512]{1,0:T(8,128)(2,1)S(1)}, f16[64,512]{1,0:T(8,128)(2,1)S(1)}, u32[]{:S(2)}, u32[]{:S(2)}) %collective-permute-start.22) | collective-permute-done | bytes 65568 | tf_op jit(solution)/shard_map/ppermute | solution.py:39
  54.7 1.6 %collective-permute-start.24 = (f16[64,512]{1,0:T(8,128)(2,1)S(1)}, f16[64,512]{1,0:T(8,128)(2,1)S(1)}, u32[]{:S(2)}, u32[]{:S(2)}) collective-permute-start(f16[64,512]{1,0:T(8,128)(2,1)S(1)} %get-tuple-element.47), channel_id=1, source_target_pairs={{0,6},{1,7},{2,4},{3,5},{4,2},{5,3},{6,0},{7,1},{8,14},{9,15},{10,... | collective-permute-start | bytes 196616 | tf_op jit(solution)/shard_map/ppermute | solution.py:39
  56.3 1.5 %collective-permute-start.25 = (f16[64,512]{1,0:T(8,128)(2,1)S(1)}, f16[64,512]{1,0:T(8,128)(2,1)S(1)}, u32[]{:S(2)}, u32[]{:S(2)}) collective-permute-start(f16[64,512]{1,0:T(8,128)(2,1)S(1)} %get-tuple-element.47), channel_id=1, source_target_pairs={{0,2},{1,3},{2,0},{3,1},{4,6},{5,7},{6,4},{7,5},{8,10},{9,11},{10,... | collective-permute-start | bytes 196616 | tf_op jit(solution)/shard_map/ppermute | solution.py:39
  57.8 0.4 collective-permute-start.26
  58.2 1.9 %collective-permute-done.24 = f16[64,512]{1,0:T(8,128)(2,1)S(1)} collective-permute-done((f16[64,512]{1,0:T(8,128)(2,1)S(1)}, f16[64,512]{1,0:T(8,128)(2,1)S(1)}, u32[]{:S(2)}, u32[]{:S(2)}) %collective-permute-start.24) | collective-permute-done | bytes 65568 | tf_op jit(solution)/shard_map/ppermute | solution.py:39
  60.1 0.8 collective-permute-done.25
  60.9 1.2 %collective-permute-done.26 = f16[64,512]{1,0:T(8,128)(2,1)S(1)} collective-permute-done((f16[64,512]{1,0:T(8,128)(2,1)S(1)}, f16[64,512]{1,0:T(8,128)(2,1)S(1)}, u32[]{:S(2)}, u32[]{:S(2)}) %collective-permute-start.26) | collective-permute-done | bytes 65568 | tf_op jit(solution)/shard_map/ppermute | solution.py:39
  62.2 1.1 %collective-permute-done.30 = f16[64,512]{1,0:T(8,128)(2,1)S(1)} collective-permute-done((f16[64,512]{1,0:T(8,128)(2,1)S(1)}, f16[64,512]{1,0:T(8,128)(2,1)S(1)}, u32[]{:S(2)}, u32[]{:S(2)}) %collective-permute-start.30) | collective-permute-done | bytes 65568 | tf_op jit(solution)/shard_map/ppermute | solution.py:39
  63.3 2.9 %shard_map.56 = f32[64,512]{1,0:T(8,128)S(1)} custom-call(f32[64,512]{1,0:T(8,128)S(1)} %get-tuple-element.46.refs_0_, f32[64,512]{1,0:T(8,128)S(1)} %convert_element_type.139.refs_1_, f32[64,512]{1,0:T(8,128)S(1)} %convert_element_type.140.refs_2_, f32[64,512]{1,0:T(8,128)S(1)} %convert_element_type.141.refs_3_, ...), custom_call_target="tpu_custom_call" | custom-call | tf_op jit(solution)/shard_map/pallas_call | solution.py:69
  66.3 1.3 %collective-permute-start.33 = (f16[64,512]{1,0:T(8,128)(2,1)S(1)}, f16[64,512]{1,0:T(8,128)(2,1)S(1)}, u32[]{:S(2)}, u32[]{:S(2)}) collective-permute-start(f16[64,512]{1,0:T(8,128)(2,1)S(1)} %convert_element_type.146), channel_id=1, source_target_pairs={{0,24},{1,25},{2,26},{3,27},{4,28},{5,29},{6,30},{7,31},{8,16},{9,... | collective-permute-start | bytes 196616 | tf_op jit(solution)/shard_map/ppermute | solution.py:39
  67.6 3.2 %collective-permute-start.31 = (f16[64,512]{1,0:T(8,128)(2,1)S(1)}, f16[64,512]{1,0:T(8,128)(2,1)S(1)}, u32[]{:S(2)}, u32[]{:S(2)}) collective-permute-start(f16[64,512]{1,0:T(8,128)(2,1)S(1)} %convert_element_type.146), channel_id=1, source_target_pairs={{0,8},{1,9},{2,10},{3,11},{4,12},{5,13},{6,14},{7,15},{8,0},{9,1},... | collective-permute-start | bytes 196616 | tf_op jit(solution)/shard_map/ppermute | solution.py:39
  70.8 2.4 %collective-permute-done.33 = f16[64,512]{1,0:T(8,128)(2,1)S(1)} collective-permute-done((f16[64,512]{1,0:T(8,128)(2,1)S(1)}, f16[64,512]{1,0:T(8,128)(2,1)S(1)}, u32[]{:S(2)}, u32[]{:S(2)}) %collective-permute-start.33) | collective-permute-done | bytes 65568 | tf_op jit(solution)/shard_map/ppermute | solution.py:39
  73.2 2.0 %collective-permute-done.32 = f16[64,512]{1,0:T(8,128)(2,1)S(1)} collective-permute-done((f16[64,512]{1,0:T(8,128)(2,1)S(1)}, f16[64,512]{1,0:T(8,128)(2,1)S(1)}, u32[]{:S(2)}, u32[]{:S(2)}) %collective-permute-start.32) | collective-permute-done | bytes 65568 | tf_op jit(solution)/shard_map/ppermute | solution.py:39
  75.2 0.7 collective-permute-start.34
  75.9 1.2 %collective-permute-start.35 = (f16[64,512]{1,0:T(8,128)(2,1)S(1)}, f16[64,512]{1,0:T(8,128)(2,1)S(1)}, u32[]{:S(2)}, u32[]{:S(2)}) collective-permute-start(f16[64,512]{1,0:T(8,128)(2,1)S(1)} %get-tuple-element.45), channel_id=1, source_target_pairs={{0,2},{1,3},{2,0},{3,1},{4,6},{5,7},{6,4},{7,5},{8,10},{9,11},{10,... | collective-permute-start | bytes 196616 | tf_op jit(solution)/shard_map/ppermute | solution.py:39
  77.1 1.6 %collective-permute-start.36 = (f16[64,512]{1,0:T(8,128)(2,1)S(1)}, f16[64,512]{1,0:T(8,128)(2,1)S(1)}, u32[]{:S(2)}, u32[]{:S(2)}) collective-permute-start(f16[64,512]{1,0:T(8,128)(2,1)S(1)} %get-tuple-element.45), channel_id=1, source_target_pairs={{0,4},{1,5},{2,6},{3,7},{4,0},{5,1},{6,2},{7,3},{8,12},{9,13},{10,... | collective-permute-start | bytes 196616 | tf_op jit(solution)/shard_map/ppermute | solution.py:39
  78.7 2.1 %collective-permute-done.34 = f16[64,512]{1,0:T(8,128)(2,1)S(1)} collective-permute-done((f16[64,512]{1,0:T(8,128)(2,1)S(1)}, f16[64,512]{1,0:T(8,128)(2,1)S(1)}, u32[]{:S(2)}, u32[]{:S(2)}) %collective-permute-start.34) | collective-permute-done | bytes 65568 | tf_op jit(solution)/shard_map/ppermute | solution.py:39
  80.9 0.5 collective-permute-start.39
  81.4 0.2 collective-permute-done.36
  81.6 0.5 collective-permute-done.38
  82.1 0.1 collective-permute-done.39
  82.3 0.5 collective-permute-done.40
  82.8 3.1 %shard_map.57 = (f32[128,512]{1,0:T(8,128)}, bf16[128,1024]{1,0:T(8,128)(2,1)}) custom-call(f32[64,512]{1,0:T(8,128)S(1)} %get-tuple-element.44.refs_0_, f32[64,512]{1,0:T(8,128)S(1)} %convert_element_type.153.refs_1_, f32[64,512]{1,0:T(8,128)S(1)} %convert_element_type.154.refs_2_, f32[64,512]{1,0:T(8,128)S(1)} %convert_element_type.155.refs_3_, ...), custom_call_target="tpu_custom_call" | custom-call | tf_op jit(solution)/shard_map/pallas_call | solution.py:69
  (58 shorter events, 0.7 us)
Async XLA Ops:
  0.6 40.1 %copy-start = (f32[128,512]{1,0:T(8,128)S(1)}, f32[128,512]{1,0:T(8,128)}, u32[]{:S(2)}) copy-start(f32[128,512]{1,0:T(8,128)} %param.5) | copy-start | bytes 786436
  0.6 3.4 %copy-start.1 = (bf16[512,512]{1,0:T(8,128)(2,1)S(1)}, bf16[512,512]{1,0:T(8,128)(2,1)}, u32[]{:S(2)}) copy-start(bf16[512,512]{1,0:T(8,128)(2,1)} %left_ref.3) | copy-start | bytes 1572868
  0.7 3.4 %collective-permute-start = (bf16[512,512]{1,0:T(8,128)(2,1)}, bf16[512,512]{1,0:T(8,128)(2,1)S(1)}, u32[]{:S(2)}, u32[]{:S(2)}) collective-permute-start(bf16[512,512]{1,0:T(8,128)(2,1)} %left_ref.3), channel_id=1, source_target_pairs={{0,1},{1,0},{2,3},{3,2},{4,5},{5,4},{6,7},{7,6},{8,9},{9,8},{10,11... | collective-permute-start | bytes 1572872 | tf_op jit(solution)/shard_map/ppermute | solution.py:39
  2.4 1.6 %collective-permute-start.2 = (bf16[512,256]{1,0:T(8,128)(2,1)S(1)}, bf16[512,256]{1,0:T(8,128)(2,1)S(1)}, u32[]{:S(2)}, u32[]{:S(2)}) collective-permute-start(bf16[512,256]{1,0:T(8,128)(2,1)S(1)} %get-tuple-element.48), channel_id=1, source_target_pairs={{0,1},{1,0},{2,3},{3,2},{4,5},{5,4},{6,7},{7,6},{8,9},{9,8},{10,11... | collective-permute-start | bytes 786440 | tf_op jit(solution)/shard_map/ppermute | solution.py:39
  4.6 9.7 %collective-permute-start.3 = (f16[528,256]{1,0:T(8,128)(2,1)S(1)}, f16[528,256]{1,0:T(8,128)(2,1)S(1)}, u32[]{:S(2)}, u32[]{:S(2)}) collective-permute-start(f16[528,256]{1,0:T(8,128)(2,1)S(1)} %convert_element_type.120), channel_id=1, source_target_pairs={{0,2},{1,3},{2,0},{3,1},{4,6},{5,7},{6,4},{7,5},{8,10},{9,11},{10,... | collective-permute-start | bytes 811016 | tf_op jit(solution)/shard_map/ppermute | solution.py:39
  7.3 1.5 %collective-permute-start.1 = (bf16[512,256]{1,0:T(8,128)(2,1)S(1)}, bf16[512,256]{1,0:T(8,128)(2,1)S(1)}, u32[]{:S(2)}, u32[]{:S(2)}) collective-permute-start(bf16[512,256]{1,0:T(8,128)(2,1)S(1)} %get-tuple-element.49), channel_id=1, source_target_pairs={{0,1},{1,0},{2,3},{3,2},{4,5},{5,4},{6,7},{7,6},{8,9},{9,8},{10,11... | collective-permute-start | bytes 786440 | tf_op jit(solution)/shard_map/ppermute | solution.py:39
  14.5 1.6 %collective-permute-start.4 = (bf16[512,256]{1,0:T(8,128)(2,1)S(1)}, bf16[512,256]{1,0:T(8,128)(2,1)S(1)}, u32[]{:S(2)}, u32[]{:S(2)}) collective-permute-start(bf16[512,256]{1,0:T(8,128)(2,1)S(1)} %fusion.1.here_ref.refs_0_), channel_id=1, source_target_pairs={{0,1},{1,0},{2,3},{3,2},{4,5},{5,4},{6,7},{7,6},{8,9},{9,8},{10,11... | collective-permute-start | bytes 786440 | tf_op jit(solution)/shard_map/ppermute | solution.py:39
  16.4 6.8 %collective-permute-start.7 = (bf16[160,128]{1,0:T(8,128)(2,1)S(1)}, bf16[160,128]{1,0:T(8,128)(2,1)S(1)}, u32[]{:S(2)}, u32[]{:S(2)}) collective-permute-start(bf16[160,128]{1,0:T(8,128)(2,1)S(1)} %get-tuple-element.27), channel_id=1, source_target_pairs={{0,4},{1,5},{2,6},{3,7},{4,0},{5,1},{6,2},{7,3},{8,12},{9,13},{10,... | collective-permute-start | bytes 122888 | tf_op jit(solution)/shard_map/ppermute | solution.py:39
  18.2 5.0 %collective-permute-start.6 = (bf16[160,128]{1,0:T(8,128)(2,1)S(1)}, bf16[160,128]{1,0:T(8,128)(2,1)S(1)}, u32[]{:S(2)}, u32[]{:S(2)}) collective-permute-start(bf16[160,128]{1,0:T(8,128)(2,1)S(1)} %get-tuple-element.26), channel_id=1, source_target_pairs={{0,2},{1,3},{2,0},{3,1},{4,6},{5,7},{6,4},{7,5},{8,10},{9,11},{10,... | collective-permute-start | bytes 122888 | tf_op jit(solution)/shard_map/ppermute | solution.py:39
  19.7 5.4 %collective-permute-start.5 = (bf16[160,128]{1,0:T(8,128)(2,1)S(1)}, bf16[160,128]{1,0:T(8,128)(2,1)S(1)}, u32[]{:S(2)}, u32[]{:S(2)}) collective-permute-start(bf16[160,128]{1,0:T(8,128)(2,1)S(1)} %get-tuple-element.25), channel_id=1, source_target_pairs={{0,6},{1,7},{2,4},{3,5},{4,2},{5,3},{6,0},{7,1},{8,14},{9,15},{10,... | collective-permute-start | bytes 122888 | tf_op jit(solution)/shard_map/ppermute | solution.py:39
  20.0 11.2 %collective-permute-start.11 = (bf16[512,256]{1,0:T(8,128)(2,1)S(1)}, bf16[512,256]{1,0:T(8,128)(2,1)S(1)}, u32[]{:S(2)}, u32[]{:S(2)}) collective-permute-start(bf16[512,256]{1,0:T(8,128)(2,1)S(1)} %fusion.1.here_ref.refs_0_), channel_id=1, source_target_pairs={{0,4},{1,5},{2,6},{3,7},{4,0},{5,1},{6,2},{7,3},{8,12},{9,13},{10,... | collective-permute-start | bytes 786440 | tf_op jit(solution)/shard_map/ppermute | solution.py:39
  21.7 9.4 %collective-permute-start.12 = (bf16[512,256]{1,0:T(8,128)(2,1)S(1)}, bf16[512,256]{1,0:T(8,128)(2,1)S(1)}, u32[]{:S(2)}, u32[]{:S(2)}) collective-permute-start(bf16[512,256]{1,0:T(8,128)(2,1)S(1)} %fusion.1.here_ref.refs_0_), channel_id=1, source_target_pairs={{0,2},{1,3},{2,0},{3,1},{4,6},{5,7},{6,4},{7,5},{8,10},{9,11},{10,... | collective-permute-start | bytes 786440 | tf_op jit(solution)/shard_map/ppermute | solution.py:39
  25.2 5.9 %collective-permute-start.10 = (bf16[160,128]{1,0:T(8,128)(2,1)S(1)}, bf16[160,128]{1,0:T(8,128)(2,1)S(1)}, u32[]{:S(2)}, u32[]{:S(2)}) collective-permute-start(bf16[160,128]{1,0:T(8,128)(2,1)S(1)} %convert_add_fusion), channel_id=1, source_target_pairs={{0,24},{1,25},{2,26},{3,27},{4,28},{5,29},{6,30},{7,31},{8,16},{9,... | collective-permute-start | bytes 122888 | tf_op jit(solution)/shard_map/ppermute | solution.py:39
  28.8 4.0 %collective-permute-start.9 = (bf16[160,128]{1,0:T(8,128)(2,1)S(1)}, bf16[160,128]{1,0:T(8,128)(2,1)S(1)}, u32[]{:S(2)}, u32[]{:S(2)}) collective-permute-start(bf16[160,128]{1,0:T(8,128)(2,1)S(1)} %convert_add_fusion), channel_id=1, source_target_pairs={{0,8},{1,9},{2,10},{3,11},{4,12},{5,13},{6,14},{7,15},{8,0},{9,1},... | collective-permute-start | bytes 122888 | tf_op jit(solution)/shard_map/ppermute | solution.py:39
  28.8 4.9 %collective-permute-start.8 = (bf16[160,128]{1,0:T(8,128)(2,1)S(1)}, bf16[160,128]{1,0:T(8,128)(2,1)S(1)}, u32[]{:S(2)}, u32[]{:S(2)}) collective-permute-start(bf16[160,128]{1,0:T(8,128)(2,1)S(1)} %convert_add_fusion), channel_id=1, source_target_pairs={{0,16},{1,17},{2,18},{3,19},{4,20},{5,21},{6,22},{7,23},{8,24},{9,... | collective-permute-start | bytes 122888 | tf_op jit(solution)/shard_map/ppermute | solution.py:39
  31.1 7.8 %collective-permute-start.16 = (bf16[512,256]{1,0:T(8,128)(2,1)S(1)}, bf16[512,256]{1,0:T(8,128)(2,1)S(1)}, u32[]{:S(2)}, u32[]{:S(2)}) collective-permute-start(bf16[512,256]{1,0:T(8,128)(2,1)S(1)} %fusion.1.here_ref.refs_0_), channel_id=1, source_target_pairs={{0,6},{1,7},{2,4},{3,5},{4,2},{5,3},{6,0},{7,1},{8,14},{9,15},{10,... | collective-permute-start | bytes 786440 | tf_op jit(solution)/shard_map/ppermute | solution.py:39
  33.7 5.2 %collective-permute-start.15 = (bf16[160,128]{1,0:T(8,128)(2,1)S(1)}, bf16[160,128]{1,0:T(8,128)(2,1)S(1)}, u32[]{:S(2)}, u32[]{:S(2)}) collective-permute-start(bf16[160,128]{1,0:T(8,128)(2,1)S(1)} %add_convert_fusion.2.refs_0_), channel_id=1, source_target_pairs={{0,6},{1,7},{2,4},{3,5},{4,2},{5,3},{6,0},{7,1},{8,14},{9,15},{10,... | collective-permute-start | bytes 122888 | tf_op jit(solution)/shard_map/ppermute | solution.py:39
  34.1 4.8 %collective-permute-start.13 = (bf16[160,128]{1,0:T(8,128)(2,1)S(1)}, bf16[160,128]{1,0:T(8,128)(2,1)S(1)}, u32[]{:S(2)}, u32[]{:S(2)}) collective-permute-start(bf16[160,128]{1,0:T(8,128)(2,1)S(1)} %add_convert_fusion.2.refs_0_), channel_id=1, source_target_pairs={{0,2},{1,3},{2,0},{3,1},{4,6},{5,7},{6,4},{7,5},{8,10},{9,11},{10,... | collective-permute-start | bytes 122888 | tf_op jit(solution)/shard_map/ppermute | solution.py:39
  35.7 4.0 %collective-permute-start.14 = (bf16[160,128]{1,0:T(8,128)(2,1)S(1)}, bf16[160,128]{1,0:T(8,128)(2,1)S(1)}, u32[]{:S(2)}, u32[]{:S(2)}) collective-permute-start(bf16[160,128]{1,0:T(8,128)(2,1)S(1)} %add_convert_fusion.2.refs_0_), channel_id=1, source_target_pairs={{0,4},{1,5},{2,6},{3,7},{4,0},{5,1},{6,2},{7,3},{8,12},{9,13},{10,... | collective-permute-start | bytes 122888 | tf_op jit(solution)/shard_map/ppermute | solution.py:39
  39.7 1.5 %collective-permute-start.17 = (bf16[4,160,128]{2,1,0:T(8,128)(2,1)S(1)}, bf16[4,160,128]{2,1,0:T(8,128)(2,1)S(1)}, u32[]{:S(2)}, u32[]{:S(2)}) collective-permute-start(bf16[4,160,128]{2,1,0:T(8,128)(2,1)S(1)} %pad_maximum_fusion), channel_id=1, source_target_pairs={{0,1},{1,0},{2,3},{3,2},{4,5},{5,4},{6,7},{7,6},{8,9},{9,8},{10,11... | collective-permute-start | bytes 491528 | tf_op jit(solution)/shard_map/ppermute | solution.py:39
  39.8 3.6 %collective-permute-start.18 = (bf16[512,256]{1,0:T(8,128)(2,1)S(1)}, bf16[512,256]{1,0:T(8,128)(2,1)S(1)}, u32[]{:S(2)}, u32[]{:S(2)}) collective-permute-start(bf16[512,256]{1,0:T(8,128)(2,1)S(1)} %collective-permute-done.12.refs_2_), channel_id=1, source_target_pairs={{0,1},{1,0},{2,3},{3,2},{4,5},{5,4},{6,7},{7,6},{8,9},{9,8},{10,11... | collective-permute-start | bytes 786440 | tf_op jit(solution)/shard_map/ppermute | solution.py:39
  40.3 3.1 %collective-permute-start.19 = (bf16[512,256]{1,0:T(8,128)(2,1)S(1)}, bf16[512,256]{1,0:T(8,128)(2,1)S(1)}, u32[]{:S(2)}, u32[]{:S(2)}) collective-permute-start(bf16[512,256]{1,0:T(8,128)(2,1)S(1)} %collective-permute-done.11.refs_4_), channel_id=1, source_target_pairs={{0,1},{1,0},{2,3},{3,2},{4,5},{5,4},{6,7},{7,6},{8,9},{9,8},{10,11... | collective-permute-start | bytes 786440 | tf_op jit(solution)/shard_map/ppermute | solution.py:39
  40.3 3.0 %collective-permute-start.20 = (bf16[512,256]{1,0:T(8,128)(2,1)S(1)}, bf16[512,256]{1,0:T(8,128)(2,1)S(1)}, u32[]{:S(2)}, u32[]{:S(2)}) collective-permute-start(bf16[512,256]{1,0:T(8,128)(2,1)S(1)} %collective-permute-done.16.refs_6_), channel_id=1, source_target_pairs={{0,1},{1,0},{2,3},{3,2},{4,5},{5,4},{6,7},{7,6},{8,9},{9,8},{10,11... | collective-permute-start | bytes 786440 | tf_op jit(solution)/shard_map/ppermute | solution.py:39
  44.8 6.9 %collective-permute-start.23 = (f16[64,512]{1,0:T(8,128)(2,1)S(1)}, f16[64,512]{1,0:T(8,128)(2,1)S(1)}, u32[]{:S(2)}, u32[]{:S(2)}) collective-permute-start(f16[64,512]{1,0:T(8,128)(2,1)S(1)} %convert_element_type.132), channel_id=1, source_target_pairs={{0,24},{1,25},{2,26},{3,27},{4,28},{5,29},{6,30},{7,31},{8,16},{9,... | collective-permute-start | bytes 196616 | tf_op jit(solution)/shard_map/ppermute | solution.py:39
  47.9 6.8 %collective-permute-start.22 = (f16[64,512]{1,0:T(8,128)(2,1)S(1)}, f16[64,512]{1,0:T(8,128)(2,1)S(1)}, u32[]{:S(2)}, u32[]{:S(2)}) collective-permute-start(f16[64,512]{1,0:T(8,128)(2,1)S(1)} %convert_element_type.132), channel_id=1, source_target_pairs={{0,16},{1,17},{2,18},{3,19},{4,20},{5,21},{6,22},{7,23},{8,24},{9,... | collective-permute-start | bytes 196616 | tf_op jit(solution)/shard_map/ppermute | solution.py:39
  48.3 6.3 %collective-permute-start.21 = (f16[64,512]{1,0:T(8,128)(2,1)S(1)}, f16[64,512]{1,0:T(8,128)(2,1)S(1)}, u32[]{:S(2)}, u32[]{:S(2)}) collective-permute-start(f16[64,512]{1,0:T(8,128)(2,1)S(1)} %convert_element_type.132), channel_id=1, source_target_pairs={{0,8},{1,9},{2,10},{3,11},{4,12},{5,13},{6,14},{7,15},{8,0},{9,1},... | collective-permute-start | bytes 196616 | tf_op jit(solution)/shard_map/ppermute | solution.py:39
  54.7 5.4 %collective-permute-start.24 = (f16[64,512]{1,0:T(8,128)(2,1)S(1)}, f16[64,512]{1,0:T(8,128)(2,1)S(1)}, u32[]{:S(2)}, u32[]{:S(2)}) collective-permute-start(f16[64,512]{1,0:T(8,128)(2,1)S(1)} %get-tuple-element.47), channel_id=1, source_target_pairs={{0,6},{1,7},{2,4},{3,5},{4,2},{5,3},{6,0},{7,1},{8,14},{9,15},{10,... | collective-permute-start | bytes 196616 | tf_op jit(solution)/shard_map/ppermute | solution.py:39
  56.3 4.6 %collective-permute-start.25 = (f16[64,512]{1,0:T(8,128)(2,1)S(1)}, f16[64,512]{1,0:T(8,128)(2,1)S(1)}, u32[]{:S(2)}, u32[]{:S(2)}) collective-permute-start(f16[64,512]{1,0:T(8,128)(2,1)S(1)} %get-tuple-element.47), channel_id=1, source_target_pairs={{0,2},{1,3},{2,0},{3,1},{4,6},{5,7},{6,4},{7,5},{8,10},{9,11},{10,... | collective-permute-start | bytes 196616 | tf_op jit(solution)/shard_map/ppermute | solution.py:39
  57.8 4.3 %collective-permute-start.26 = (f16[64,512]{1,0:T(8,128)(2,1)S(1)}, f16[64,512]{1,0:T(8,128)(2,1)S(1)}, u32[]{:S(2)}, u32[]{:S(2)}) collective-permute-start(f16[64,512]{1,0:T(8,128)(2,1)S(1)} %get-tuple-element.47), channel_id=1, source_target_pairs={{0,4},{1,5},{2,6},{3,7},{4,0},{5,1},{6,2},{7,3},{8,12},{9,13},{10,... | collective-permute-start | bytes 196616 | tf_op jit(solution)/shard_map/ppermute | solution.py:39
  58.2 3.9 %collective-permute-start.27 = (f16[64,512]{1,0:T(8,128)(2,1)S(1)}, f16[64,512]{1,0:T(8,128)(2,1)S(1)}, u32[]{:S(2)}, u32[]{:S(2)}) collective-permute-start(f16[64,512]{1,0:T(8,128)(2,1)S(1)} %get-tuple-element.47), channel_id=1, source_target_pairs={{0,1},{1,0},{2,3},{3,2},{4,5},{5,4},{6,7},{7,6},{8,9},{9,8},{10,11... | collective-permute-start | bytes 196616 | tf_op jit(solution)/shard_map/ppermute | solution.py:39
  60.1 2.1 %collective-permute-start.28 = (f16[64,512]{1,0:T(8,128)(2,1)S(1)}, f16[64,512]{1,0:T(8,128)(2,1)S(1)}, u32[]{:S(2)}, u32[]{:S(2)}) collective-permute-start(f16[64,512]{1,0:T(8,128)(2,1)S(1)} %collective-permute-done.24), channel_id=1, source_target_pairs={{0,1},{1,0},{2,3},{3,2},{4,5},{5,4},{6,7},{7,6},{8,9},{9,8},{10,11... | collective-permute-start | bytes 196616 | tf_op jit(solution)/shard_map/ppermute | solution.py:39
  60.9 1.3 %collective-permute-start.29 = (f16[64,512]{1,0:T(8,128)(2,1)S(1)}, f16[64,512]{1,0:T(8,128)(2,1)S(1)}, u32[]{:S(2)}, u32[]{:S(2)}) collective-permute-start(f16[64,512]{1,0:T(8,128)(2,1)S(1)} %collective-permute-done.25), channel_id=1, source_target_pairs={{0,1},{1,0},{2,3},{3,2},{4,5},{5,4},{6,7},{7,6},{8,9},{9,8},{10,11... | collective-permute-start | bytes 196616 | tf_op jit(solution)/shard_map/ppermute | solution.py:39
  62.1 1.3 %collective-permute-start.30 = (f16[64,512]{1,0:T(8,128)(2,1)S(1)}, f16[64,512]{1,0:T(8,128)(2,1)S(1)}, u32[]{:S(2)}, u32[]{:S(2)}) collective-permute-start(f16[64,512]{1,0:T(8,128)(2,1)S(1)} %collective-permute-done.26), channel_id=1, source_target_pairs={{0,1},{1,0},{2,3},{3,2},{4,5},{5,4},{6,7},{7,6},{8,9},{9,8},{10,11... | collective-permute-start | bytes 196616 | tf_op jit(solution)/shard_map/ppermute | solution.py:39
  66.3 6.9 %collective-permute-start.33 = (f16[64,512]{1,0:T(8,128)(2,1)S(1)}, f16[64,512]{1,0:T(8,128)(2,1)S(1)}, u32[]{:S(2)}, u32[]{:S(2)}) collective-permute-start(f16[64,512]{1,0:T(8,128)(2,1)S(1)} %convert_element_type.146), channel_id=1, source_target_pairs={{0,24},{1,25},{2,26},{3,27},{4,28},{5,29},{6,30},{7,31},{8,16},{9,... | collective-permute-start | bytes 196616 | tf_op jit(solution)/shard_map/ppermute | solution.py:39
  67.6 7.6 %collective-permute-start.32 = (f16[64,512]{1,0:T(8,128)(2,1)S(1)}, f16[64,512]{1,0:T(8,128)(2,1)S(1)}, u32[]{:S(2)}, u32[]{:S(2)}) collective-permute-start(f16[64,512]{1,0:T(8,128)(2,1)S(1)} %convert_element_type.146), channel_id=1, source_target_pairs={{0,16},{1,17},{2,18},{3,19},{4,20},{5,21},{6,22},{7,23},{8,24},{9,... | collective-permute-start | bytes 196616 | tf_op jit(solution)/shard_map/ppermute | solution.py:39
  67.6 7.6 %collective-permute-start.31 = (f16[64,512]{1,0:T(8,128)(2,1)S(1)}, f16[64,512]{1,0:T(8,128)(2,1)S(1)}, u32[]{:S(2)}, u32[]{:S(2)}) collective-permute-start(f16[64,512]{1,0:T(8,128)(2,1)S(1)} %convert_element_type.146), channel_id=1, source_target_pairs={{0,8},{1,9},{2,10},{3,11},{4,12},{5,13},{6,14},{7,15},{8,0},{9,1},... | collective-permute-start | bytes 196616 | tf_op jit(solution)/shard_map/ppermute | solution.py:39
  75.2 5.7 %collective-permute-start.34 = (f16[64,512]{1,0:T(8,128)(2,1)S(1)}, f16[64,512]{1,0:T(8,128)(2,1)S(1)}, u32[]{:S(2)}, u32[]{:S(2)}) collective-permute-start(f16[64,512]{1,0:T(8,128)(2,1)S(1)} %get-tuple-element.45), channel_id=1, source_target_pairs={{0,6},{1,7},{2,4},{3,5},{4,2},{5,3},{6,0},{7,1},{8,14},{9,15},{10,... | collective-permute-start | bytes 196616 | tf_op jit(solution)/shard_map/ppermute | solution.py:39
  75.9 5.0 %collective-permute-start.35 = (f16[64,512]{1,0:T(8,128)(2,1)S(1)}, f16[64,512]{1,0:T(8,128)(2,1)S(1)}, u32[]{:S(2)}, u32[]{:S(2)}) collective-permute-start(f16[64,512]{1,0:T(8,128)(2,1)S(1)} %get-tuple-element.45), channel_id=1, source_target_pairs={{0,2},{1,3},{2,0},{3,1},{4,6},{5,7},{6,4},{7,5},{8,10},{9,11},{10,... | collective-permute-start | bytes 196616 | tf_op jit(solution)/shard_map/ppermute | solution.py:39
  77.1 4.4 %collective-permute-start.36 = (f16[64,512]{1,0:T(8,128)(2,1)S(1)}, f16[64,512]{1,0:T(8,128)(2,1)S(1)}, u32[]{:S(2)}, u32[]{:S(2)}) collective-permute-start(f16[64,512]{1,0:T(8,128)(2,1)S(1)} %get-tuple-element.45), channel_id=1, source_target_pairs={{0,4},{1,5},{2,6},{3,7},{4,0},{5,1},{6,2},{7,3},{8,12},{9,13},{10,... | collective-permute-start | bytes 196616 | tf_op jit(solution)/shard_map/ppermute | solution.py:39
  78.7 2.9 %collective-permute-start.37 = (f16[64,512]{1,0:T(8,128)(2,1)S(1)}, f16[64,512]{1,0:T(8,128)(2,1)S(1)}, u32[]{:S(2)}, u32[]{:S(2)}) collective-permute-start(f16[64,512]{1,0:T(8,128)(2,1)S(1)} %get-tuple-element.45), channel_id=1, source_target_pairs={{0,1},{1,0},{2,3},{3,2},{4,5},{5,4},{6,7},{7,6},{8,9},{9,8},{10,11... | collective-permute-start | bytes 196616 | tf_op jit(solution)/shard_map/ppermute | solution.py:39
  80.9 1.3 %collective-permute-start.38 = (f16[64,512]{1,0:T(8,128)(2,1)S(1)}, f16[64,512]{1,0:T(8,128)(2,1)S(1)}, u32[]{:S(2)}, u32[]{:S(2)}) collective-permute-start(f16[64,512]{1,0:T(8,128)(2,1)S(1)} %collective-permute-done.34), channel_id=1, source_target_pairs={{0,1},{1,0},{2,3},{3,2},{4,5},{5,4},{6,7},{7,6},{8,9},{9,8},{10,11... | collective-permute-start | bytes 196616 | tf_op jit(solution)/shard_map/ppermute | solution.py:39
  80.9 1.4 %collective-permute-start.39 = (f16[64,512]{1,0:T(8,128)(2,1)S(1)}, f16[64,512]{1,0:T(8,128)(2,1)S(1)}, u32[]{:S(2)}, u32[]{:S(2)}) collective-permute-start(f16[64,512]{1,0:T(8,128)(2,1)S(1)} %collective-permute-done.35), channel_id=1, source_target_pairs={{0,1},{1,0},{2,3},{3,2},{4,5},{5,4},{6,7},{7,6},{8,9},{9,8},{10,11... | collective-permute-start | bytes 196616 | tf_op jit(solution)/shard_map/ppermute | solution.py:39
  81.6 1.3 %collective-permute-start.40 = (f16[64,512]{1,0:T(8,128)(2,1)S(1)}, f16[64,512]{1,0:T(8,128)(2,1)S(1)}, u32[]{:S(2)}, u32[]{:S(2)}) collective-permute-start(f16[64,512]{1,0:T(8,128)(2,1)S(1)} %collective-permute-done.36), channel_id=1, source_target_pairs={{0,1},{1,0},{2,3},{3,2},{4,5},{5,4},{6,7},{7,6},{8,9},{9,8},{10,11... | collective-permute-start | bytes 196616 | tf_op jit(solution)/shard_map/ppermute | solution.py:39
